TPU v7x, 32 devices: a whole 2x2x4 slice. The times are simulated.
32 devices in a mesh: ty: 4 (over x, core), tx: 8 (over z, y).
Axes of the slice: x: 2, y: 2, z: 4, core: 2. Of those that a mesh axis runs over, the one named last changes fastest.
Arguments:
- latent: float32 [384, 768], P('ty', 'tx'), may hold values from -6 to 6
- kernels: float32 [2, 12, 129, 129], replicated, may hold values from -0.046875 to 0.046875
- socs_weights: float32 [12], replicated, may hold values from 0.01 to 0.1
- dose_scale: float32 [8], replicated, may hold values from 0.8 to 1.25
- inv_slope: float32 [4, 2048], P('ty', 'tx'), may hold values from 1 to 8
- edge_pixels: int32 [4, 2048], P('ty', 'tx'), may hold values from 0 to 9215
- threshold_pick: int32 [1], replicated, may hold values from 0 to 65535
Outputs:
- steering: float32 [384, 768], P('ty', 'tx')
- tail_mean: float32 [1], replicated
Inputs may be any that keep to these rules, and one draw needn't show every extreme that they name: `edge_pixels`: each entry names a pixel of its own tile, numbered row by row.
All inputs are finite; a program needn't handle non-finite values.
Results may differ from a plain program's by a relative error of at most 0.0003.
Values sent between devices are 32-bit elements; how exact they have to be, the bound alone decides.
No kernel may reach another device: no remote copies, remote signals or barrier semaphores. Data moves between devices by JAX's collectives and lax.ppermute only.
A program may use at most 64 MiB of HBM per device.

v0:
```python
import functools
import math

import jax
import jax.numpy as jnp
import ml_dtypes
import numpy as np
from jax import lax
from jax.experimental import pallas as pl
from jax.experimental.pallas import tpu as pltpu
from jax.sharding import PartitionSpec as P

STEEPNESS = 4.0
RESIST_LEVEL = 0.7
SOFTNESS = 0.25
LANES = 128
F32 = jnp.float32
BF16 = jnp.bfloat16


def split(x):
    high = x.astype(BF16)
    return high, (x - high.astype(F32)).astype(BF16)


def split_table(table):
    high = table.astype(ml_dtypes.bfloat16)
    low = (table - high.astype(np.float64)).astype(ml_dtypes.bfloat16)
    return high, low


def dot(a, b):
    return jnp.dot(a, b, preferred_element_type=F32)


def dot3(a, b):
    return dot(a[0], b[0]) + dot(a[0], b[1]) + dot(a[1], b[0])


def load(pair):
    return pair[0][...], pair[1][...]


def waves(count, period):
    half = period // 2
    angle = (np.arange(half)[None, :] + 0.5) * np.arange(count)[:, None]
    angle = angle * (2.0 * math.pi / period)
    return np.cos(angle), np.sin(angle)


def on_lanes(count, period, rows):
    cos, sin = waves(count, period)
    half = period // 2
    out = np.zeros((rows, 2 * LANES))
    out[:count, :half] = cos
    out[:count, LANES : LANES + half] = sin
    return out


def on_rows(count, period):
    cos, sin = waves(count, period)
    return np.concatenate([cos, sin], axis=1).T


def halves(x):
    return x[:, :LANES], x[:, LANES:]


def spectra_kernel(kern, cb_hi, cb_lo, ca_hi, ca_lo, out_re, out_im):
    half = out_re.shape[1] // 2
    cols = load((cb_hi, cb_lo))
    rows = load((ca_hi, ca_lo))

    def step(k, carry):
        real_cos, real_sin = halves(dot3(split(kern[0, k]), cols))
        imag_cos, imag_sin = halves(dot3(split(kern[1, k]), cols))
        wide_re = jnp.concatenate([real_cos - imag_sin, real_cos + imag_sin], axis=1)
        wide_im = jnp.concatenate([real_sin + imag_cos, imag_cos - real_sin], axis=1)
        tall_re = dot3(rows, split(wide_re))
        tall_im = dot3(rows, split(wide_im))
        out_re[k, :half] = tall_re[:half] - tall_im[half:]
        out_re[k, half:] = tall_re[:half] + tall_im[half:]
        out_im[k, :half] = tall_im[:half] + tall_re[half:]
        out_im[k, half:] = tall_im[:half] - tall_re[half:]
        return carry

    lax.fori_loop(0, out_re.shape[0], step, 0)


def total_weight(weights, kernels):
    total = weights[0]
    for k in range(1, kernels):
        total = total + weights[k]
    return jnp.full((1, 1), total, F32)


def sample_places(pixels, tile):
    row = ((pixels.astype(F32) + 0.5) * (1.0 / tile)).astype(jnp.int32)
    return row, pixels - row * tile


def field_kernel(
    weights, spec_re, spec_im, middle, above, below, left, right, pixels, slopes,
    fj_hi, fj_lo, fi_hi, fi_lo, up_hi, up_lo, side_hi, side_lo,
    field_re, field_im, sampled, framed, mask,
):
    kernels, period, _ = spec_re.shape
    half = period // 2
    tile = field_re.shape[1]
    radius = above.shape[0]
    framed[:, period:] = jnp.zeros((period, 2 * LANES - period), F32)
    framed[:, :radius] = left[...]
    framed[:, radius + tile : period] = right[...]
    framed[:radius, radius : radius + tile] = above[...]
    framed[radius : radius + tile, radius : radius + tile] = middle[...]
    framed[radius + tile :, radius : radius + tile] = below[...]
    wide = dot3(split(framed[...]), load((fj_hi, fj_lo)))
    tall = dot3(load((fi_hi, fi_lo)), split(wide)) * (1.0 / (period * period))
    cos_cos, cos_sin = halves(tall[:half])
    sin_cos, sin_sin = halves(tall[half:])
    same, other = cos_cos - sin_sin, cos_cos + sin_sin
    joint, cross = sin_cos + cos_sin, sin_cos - cos_sin
    mask[0, :, :LANES], mask[0, :, LANES:] = same, other
    mask[1, :, :LANES], mask[1, :, LANES:] = -joint, -cross
    mask[2, :, :LANES], mask[2, :, LANES:] = other, same
    mask[3, :, :LANES], mask[3, :, LANES:] = cross, joint
    lift = load((up_hi, up_lo))
    across = load((side_hi, side_lo))

    def step(k, intensity):
        pos_re, pos_im = spec_re[k, :half], spec_im[k, :half]
        neg_re, neg_im = spec_re[k, half:], spec_im[k, half:]
        up_re = mask[0] * pos_re - mask[1] * pos_im
        up_im = mask[0] * pos_im + mask[1] * pos_re
        down_re = mask[2] * neg_re - mask[3] * neg_im
        down_im = mask[2] * neg_im + mask[3] * neg_re
        for_re = jnp.concatenate([up_re + down_re, down_im - up_im], axis=0)
        for_im = jnp.concatenate([up_im + down_im, up_re - down_re], axis=0)
        re_pos, re_neg = halves(dot3(lift, split(for_re)))
        im_pos, im_neg = halves(dot3(lift, split(for_im)))
        rows_re = jnp.concatenate([re_pos + re_neg, im_neg - im_pos], axis=1)
        rows_im = jnp.concatenate([im_pos + im_neg, re_pos - re_neg], axis=1)
        real = dot3(split(rows_re), across)
        imag = dot3(split(rows_im), across)
        field_re[k] = real
        field_im[k] = imag
        return intensity + weights[k] * (real * real + imag * imag)

    intensity = lax.fori_loop(0, kernels, step, jnp.zeros((tile, LANES), F32))
    intensity = intensity / total_weight(weights, kernels)
    samples = pixels.shape[1]
    row, col = sample_places(pixels[...], tile)
    in_col = lax.broadcasted_iota(jnp.int32, (LANES, samples), 0) == col
    one_hot = jnp.where(in_col, 1.0, 0.0).astype(BF16)
    high, rest = split(intensity)
    low = intensity - high.astype(F32) - rest.astype(F32)
    picked = dot(high, one_hot) + dot(rest, one_hot) + dot(low.astype(BF16), one_hot)
    in_row = lax.broadcasted_iota(jnp.int32, (tile, samples), 0) == row
    sampled[:, :samples] = jnp.sum(jnp.where(in_row, picked, 0.0), axis=0, keepdims=True)
    sampled[:, samples:] = slopes[...]


def sigmoid(x):
    return 1.0 / (1.0 + jnp.exp(-x))


def errors(intensity, slope, dose):
    resist = sigmoid(STEEPNESS * (dose * intensity - RESIST_LEVEL))
    offset = (resist - 0.5) * slope
    return resist, offset, offset * offset


def gradient_kernel(
    weights, doses, pick, me, gathered, pixels, spec_re, spec_im, field_re, field_im,
    sj_hi, sj_lo, si_hi, si_lo, bi_hi, bi_lo, bj_hi, bj_lo,
    left, middle, right, tail, total_re, total_im,
):
    kernels, period, _ = spec_re.shape
    half = period // 2
    tile = field_re.shape[1]
    radius = (period - tile) // 2
    samples = pixels.shape[1]
    devices = gathered.shape[0]
    corners = doses.shape[0]
    per_corner = devices * samples
    everyone, every_slope = gathered[:, :samples], gathered[:, samples:]
    pick_corner = pick[0] // per_corner
    remain = pick[0] - pick_corner * per_corner
    owner = lax.broadcasted_iota(jnp.int32, (devices, samples), 0) ^ me[0]
    place = owner * samples + lax.broadcasted_iota(jnp.int32, (devices, samples), 1)
    _, _, picked = errors(everyone, every_slope, doses[pick_corner])
    threshold = jnp.sum(jnp.where(place == remain, picked, 0.0), keepdims=True)

    def corner(c, sums):
        _, _, error = errors(everyone, every_slope, doses[c])
        soft = sigmoid((error - threshold) * (1.0 / SOFTNESS))
        return sums[0] + soft, sums[1] + error * soft

    zero = jnp.zeros((devices, samples), F32)
    soft_sum, error_sum = lax.fori_loop(0, corners, corner, (zero, zero))
    soft_total = jnp.sum(soft_sum, keepdims=True)
    tail_mean = jnp.sum(error_sum, keepdims=True) / soft_total
    tail[...] = tail_mean

    own, slope = gathered[:1, :samples], gathered[:1, samples:]
    which = lax.broadcasted_iota(jnp.int32, (corners, samples), 0)
    dose = jnp.zeros((corners, samples), F32)
    for c in range(corners):
        dose = jnp.where(which == c, doses[c], dose)
    resist, offset, error = errors(own, slope, dose)
    soft = sigmoid((error - threshold) * (1.0 / SOFTNESS))
    slope_soft = soft * (1.0 - soft) * (1.0 / SOFTNESS)
    chain = 2.0 * STEEPNESS * offset * slope * dose * resist * (1.0 - resist)
    coefficient = (soft + (error - tail_mean) * slope_soft) * (corners * per_corner / soft_total)
    summed = jnp.sum(coefficient * chain, axis=0, keepdims=True)
    summed = summed / total_weight(weights, kernels)

    row, col = sample_places(pixels[...], tile)
    in_row = lax.broadcasted_iota(jnp.int32, (tile, samples), 0) == row
    in_col = lax.broadcasted_iota(jnp.int32, (LANES, samples), 0) == col
    one_hot = jnp.where(in_col, 1.0, 0.0).astype(BF16)
    placed = jnp.where(in_row, summed, 0.0)
    high, rest = split(placed)
    low = (placed - high.astype(F32) - rest.astype(F32)).astype(BF16)
    grid = jnp.zeros((tile, LANES), F32)
    for part in (high, rest, low):
        grid = grid + lax.dot_general(
            part, one_hot, (((1,), (1,)), ((), ())), preferred_element_type=F32
        )

    cols = load((sj_hi, sj_lo))
    rows = load((si_hi, si_lo))
    total_re[...] = jnp.zeros((period, 2 * LANES), F32)
    total_im[...] = jnp.zeros((period, 2 * LANES), F32)

    def step(k, carry):
        weighted = grid * weights[k]
        real_cos, real_sin = halves(dot3(split(weighted * field_re[k]), cols))
        imag_cos, imag_sin = halves(dot3(split(weighted * field_im[k]), cols))
        wide_re = jnp.concatenate([real_cos + imag_sin, real_cos - imag_sin], axis=1)
        wide_im = jnp.concatenate([imag_cos - real_sin, imag_cos + real_sin], axis=1)
        tall_re = dot3(rows, split(wide_re))
        tall_im = dot3(rows, split(wide_im))
        for first, sign in ((0, 1.0), (half, -1.0)):
            part = slice(first, first + half)
            wave_re = tall_re[:half] + sign * tall_im[half:]
            wave_im = tall_im[:half] - sign * tall_re[half:]
            own_re, own_im = spec_re[k, part], spec_im[k, part]
            total_re[part] += own_re * wave_re + own_im * wave_im
            total_im[part] += own_re * wave_im - own_im * wave_re
        return carry

    lax.fori_loop(0, kernels, step, 0)
    pos_re, neg_re = total_re[:half], total_re[half:]
    pos_im, neg_im = total_im[:half], total_im[half:]
    back_rows = load((bi_hi, bi_lo))
    for_re = jnp.concatenate([pos_re + neg_re, neg_im - pos_im], axis=0)
    for_im = jnp.concatenate([pos_im + neg_im, pos_re - neg_re], axis=0)
    re_pos, re_neg = halves(dot3(back_rows, split(for_re)))
    im_pos, im_neg = halves(dot3(back_rows, split(for_im)))
    last = jnp.concatenate([re_pos + re_neg, im_neg - im_pos], axis=1)
    grad = dot3(split(last), load((bj_hi, bj_lo))) * (2.0 / (period * period))
    left[...] = grad[:, :radius]
    middle[...] = grad[:, radius : radius + tile]
    right[...] = grad[:, radius + tile : period]


VMEM = pl.BlockSpec(memory_space=pltpu.VMEM)
SMEM = pl.BlockSpec(memory_space=pltpu.SMEM)
PARAMS = pltpu.CompilerParams(vmem_limit_bytes=32 * 1024 * 1024)


def shape(*dims):
    return jax.ShapeDtypeStruct(dims, F32)


def shifted(x, axis, by):
    peers = lax.axis_size(axis)
    pairs = [(i, i + by) for i in range(peers) if 0 <= i + by < peers]
    return lax.ppermute(x, axis, pairs)


def gather_all(x):
    axes = ("ty", "tx")
    count = lax.axis_size("ty") * lax.axis_size("tx")
    step = 1
    while step < count:
        other = lax.ppermute(x, axes, [(i, i ^ step) for i in range(count)])
        x = jnp.concatenate([x, other], axis=0)
        step *= 2
    return x


def body(latent, kernels, socs_weights, dose_scale, inv_slope, edge_pixels, threshold_pick):
    tile = latent.shape[0]
    count, taps = kernels.shape[1], kernels.shape[-1]
    samples = edge_pixels.shape[1]
    radius = (taps - 1) // 2
    period = tile + 2 * radius
    half = period // 2

    transmit = 0.5 * (1.0 + jnp.tanh(latent))
    above = shifted(transmit[tile - radius :], "ty", 1)
    below = shifted(transmit[:radius], "ty", -1)

    spec_re, spec_im = pl.pallas_call(
        spectra_kernel,
        out_shape=[shape(count, period, 2 * LANES)] * 2,
        in_specs=[VMEM] * 5,
        out_specs=[VMEM] * 2,
        compiler_params=PARAMS,
        name="spectra",
    )(
        kernels,
        *split_table(on_lanes(taps, period, taps)),
        *split_table(on_rows(taps, period)),
    )

    column = jnp.concatenate([above, transmit, below], axis=0)
    left = shifted(column[:, tile - radius :], "tx", 1)
    right = shifted(column[:, :radius], "tx", -1)

    lift = on_rows(tile, period).T
    across = np.zeros((2 * LANES, LANES))
    across[:, :tile] = on_lanes(tile, period, tile).T
    field_re, field_im, sampled = pl.pallas_call(
        field_kernel,
        out_shape=[shape(count, tile, LANES)] * 2 + [shape(1, 2 * samples)],
        in_specs=[SMEM] + [VMEM] * 17,
        out_specs=[VMEM] * 3,
        scratch_shapes=[
            pltpu.VMEM((period, 2 * LANES), F32),
            pltpu.VMEM((4, half, 2 * LANES), F32),
        ],
        compiler_params=PARAMS,
        name="field",
    )(
        socs_weights, spec_re, spec_im, transmit, above, below, left, right,
        edge_pixels, inv_slope,
        *split_table(on_lanes(period, period, 2 * LANES)),
        *split_table(on_rows(period, period)),
        *split_table(lift),
        *split_table(across),
    )

    gathered = gather_all(sampled)
    me = lax.axis_index("ty") * lax.axis_size("tx") + lax.axis_index("tx")
    grad_left, grad_middle, grad_right, tail_mean = pl.pallas_call(
        gradient_kernel,
        out_shape=[shape(period, radius), shape(period, tile), shape(period, radius), shape(1, 1)],
        in_specs=[SMEM] * 4 + [VMEM] * 14,
        out_specs=[VMEM] * 4,
        scratch_shapes=[pltpu.VMEM((period, 2 * LANES), F32)] * 2,
        compiler_params=PARAMS,
        name="gradient",
    )(
        socs_weights, dose_scale, threshold_pick, me.astype(jnp.int32).reshape(1),
        gathered, edge_pixels, spec_re, spec_im, field_re, field_im,
        *split_table(on_lanes(tile, period, LANES)),
        *split_table(on_rows(tile, period)),
        *split_table(on_rows(period, period).T),
        *split_table(on_lanes(period, period, 2 * LANES).T),
    )

    from_left = shifted(grad_right, "tx", 1)
    from_right = shifted(grad_left, "tx", -1)
    rest = tile - radius
    column = (
        grad_middle
        + jnp.pad(from_left, ((0, 0), (0, rest)))
        + jnp.pad(from_right, ((0, 0), (rest, 0)))
    )
    from_above = shifted(column[radius + tile :], "ty", 1)
    from_below = shifted(column[:radius], "ty", -1)
    mask_grad = (
        column[radius : radius + tile]
        + jnp.pad(from_above, ((0, rest), (0, 0)))
        + jnp.pad(from_below, ((rest, 0), (0, 0)))
    )
    tanh_value = jnp.tanh(latent)
    steering = mask_grad * 0.5 * (1.0 - tanh_value * tanh_value)
    return (steering, tail_mean.reshape(1))


def solution(mesh):
    placed = (P("ty", "tx"), P(), P(), P(), P("ty", "tx"), P("ty", "tx"), P())
    return jax.shard_map(
        body, mesh=mesh, in_specs=placed, out_specs=(P("ty", "tx"), P()), check_vma=False
    )
```

profile of v0, /device:TPU:10, one launch (start us, length us, event | category | flops | bytes accessed | tf_op | source)
XLA Modules:
  0.0 90.1 jit_solution(15090795396708869897)
XLA Ops:
  1.5 1.9 %collective-permute-start = (f32[64,96]{1,0:T(8,128)S(1)}, f32[64,96]{1,0:T(8,128)S(1)}, u32[]{:S(2)}, u32[]{:S(2)}) collective-permute-start(f32[64,96]{1,0:T(8,128)S(1)} %get-tuple-element.25), channel_id=1, source_target_pairs={{0,8},{8,16},{16,24},{1,9},{9,17},{17,25},{2,10},{10,18},{18,26},{... | collective-permute-start | bytes 73736 | tf_op jit(solution)/shard_map/ppermute | solution.py:280
  3.4 3.6 %collective-permute-start.1 = (f32[64,96]{1,0:T(8,128)S(1)}, f32[64,96]{1,0:T(8,128)S(1)}, u32[]{:S(2)}, u32[]{:S(2)}) collective-permute-start(f32[64,96]{1,0:T(8,128)S(1)} %get-tuple-element.24), channel_id=1, source_target_pairs={{8,0},{16,8},{24,16},{9,1},{17,9},{25,17},{10,2},{18,10},{26,18},{... | collective-permute-start | bytes 73736 | tf_op jit(solution)/shard_map/ppermute | solution.py:280
  7.1 1.6 %collective-permute-done.1.below = f32[64,96]{1,0:T(8,128)S(1)} collective-permute-done((f32[64,96]{1,0:T(8,128)S(1)}, f32[64,96]{1,0:T(8,128)S(1)}, u32[]{:S(2)}, u32[]{:S(2)}) %collective-permute-start.1) | collective-permute-done | bytes 24608 | tf_op jit(solution)/shard_map/ppermute | solution.py:280
  8.7 3.4 %collective-permute-start.2 = (f32[224,64]{1,0:T(8,128)S(1)}, f32[224,64]{1,0:T(8,128)S(1)}, u32[]{:S(2)}, u32[]{:S(2)}) collective-permute-start(f32[224,64]{1,0:T(8,128)S(1)} %get-tuple-element.23), channel_id=1, source_target_pairs={{0,1},{1,2},{2,3},{3,4},{4,5},{5,6},{6,7},{8,9},{9,10},{10,11},{11... | collective-permute-start | bytes 172040 | tf_op jit(solution)/shard_map/ppermute | solution.py:280
  12.2 3.4 %collective-permute-start.3 = (f32[224,64]{1,0:T(8,128)S(1)}, f32[224,64]{1,0:T(8,128)S(1)}, u32[]{:S(2)}, u32[]{:S(2)}) collective-permute-start(f32[224,64]{1,0:T(8,128)S(1)} %get-tuple-element.22), channel_id=1, source_target_pairs={{1,0},{2,1},{3,2},{4,3},{5,4},{6,5},{7,6},{9,8},{10,9},{11,10},{12... | collective-permute-start | bytes 172040 | tf_op jit(solution)/shard_map/ppermute | solution.py:280
  15.7 2.2 %copy.29.kern = f32[2,12,129,129]{3,2,1,0:T(8,128)S(1)} copy(f32[2,12,129,129]{3,0,2,1:T(2,128)} %param.28) | data formatting | bytes 3195072 | tf_op args[1]
  18.1 7.1 %spectra.1 = (f32[12,224,256]{2,1,0:T(8,128)S(1)}, f32[12,224,256]{2,1,0:T(8,128)S(1)}) custom-call(f32[2,12,129,129]{3,2,1,0:T(8,128)S(1)} %copy.29.kern, bf16[129,256]{1,0:T(8,128)(2,1)S(1)} %copy-done.14, bf16[129,256]{1,0:T(8,128)(2,1)S(1)} %copy-done.15, bf16[224,129]{1,0:T(8,128)(2,1)S(1)} %copy-done.12, bf16[224,129]{1,0:T(8,128)(2,1)S(1)} %copy-done.13), custom_call_target="tpu_custom_call" | custom-call | tf_op jit(solution)/shard_map/spectra/pallas_call | solution.py:306
  25.4 7.7 %field.1 = (f32[12,96,128]{2,1,0:T(8,128)S(1)}, f32[12,96,128]{2,1,0:T(8,128)S(1)}, f32[1,512]{1,0:T(1,128)S(1)}) custom-call(f32[12]{0:T(128)S(1)} %copy-done.25, f32[12,224,256]{2,1,0:T(8,128)S(1)} %get-tuple-element.11.spec_re, f32[12,224,256]{2,1,0:T(8,128)S(1)} %get-tuple-element.12.spec_im, f32[96,96]{1,0:T(8,128)S(1)} %add_multiply_fusion.middle, ...), custom_call_target="tpu_custom_call" | custom-call | tf_op jit(solution)/shard_map/field/pallas_call | solution.py:326
  34.5 3.0 %collective-permute-done.4 = f32[1,512]{1,0:T(1,128)S(1)} collective-permute-done((f32[1,512]{1,0:T(1,128)S(1)}, f32[1,512]{1,0:T(1,128)S(1)}, u32[]{:S(2)}, u32[]{:S(2)}) %collective-permute-start.4) | collective-permute-done | bytes 2080 | tf_op jit(solution)/shard_map/ppermute | solution.py:288
  37.6 3.6 %collective-permute-done.5 = f32[2,512]{1,0:T(2,128)S(1)} collective-permute-done((f32[2,512]{1,0:T(2,128)S(1)}, f32[2,512]{1,0:T(2,128)S(1)}, u32[]{:S(2)}, u32[]{:S(2)}) %collective-permute-start.5) | collective-permute-done | bytes 4128 | tf_op jit(solution)/shard_map/ppermute | solution.py:288
  41.2 2.7 %collective-permute-start.6 = (f32[4,512]{1,0:T(4,128)S(1)}, f32[4,512]{1,0:T(4,128)S(1)}, u32[]{:S(2)}, u32[]{:S(2)}) collective-permute-start(f32[4,512]{1,0:T(4,128)S(1)} %pad_maximum_fusion.2), channel_id=1, source_target_pairs={{0,4},{1,5},{2,6},{3,7},{4,0},{5,1},{6,2},{7,3},{8,12},{9,13},{10,... | collective-permute-start | bytes 24584 | tf_op jit(solution)/shard_map/ppermute | solution.py:288
  43.9 2.0 %collective-permute-done.6 = f32[4,512]{1,0:T(4,128)S(1)} collective-permute-done((f32[4,512]{1,0:T(4,128)S(1)}, f32[4,512]{1,0:T(4,128)S(1)}, u32[]{:S(2)}, u32[]{:S(2)}) %collective-permute-start.6) | collective-permute-done | bytes 8224 | tf_op jit(solution)/shard_map/ppermute | solution.py:288
  45.9 1.2 %collective-permute-done.7 = f32[8,512]{1,0:T(8,128)S(1)} collective-permute-done((f32[8,512]{1,0:T(8,128)S(1)}, f32[8,512]{1,0:T(8,128)S(1)}, u32[]{:S(2)}, u32[]{:S(2)}) %collective-permute-start.7) | collective-permute-done | bytes 16416 | tf_op jit(solution)/shard_map/ppermute | solution.py:288
  47.9 3.3 %collective-permute-done.8 = f32[16,512]{1,0:T(8,128)} collective-permute-done((f32[16,512]{1,0:T(8,128)S(1)}, f32[16,512]{1,0:T(8,128)}, u32[]{:S(2)}, u32[]{:S(2)}) %collective-permute-start.8) | collective-permute-done | bytes 32800 | tf_op jit(solution)/shard_map/ppermute | solution.py:288
  51.2 2.2 %concatenate.27.gathered = f32[32,512]{1,0:T(8,128)S(1)} concatenate(f32[1,512]{1,0:T(1,128)S(1)} %get-tuple-element.13, f32[1,512]{1,0:T(1,128)} %copy-done.32, f32[2,512]{1,0:T(2,128)} %copy-done.30, f32[4,512]{1,0:T(4,128)} %copy-done.29, f32[8,512]{1,0:T(8,128)} %copy-done.31, f32[16,512]{1,0:T(8,128)} %collective-permute-done.8), dimensions={0} | concatenate | bytes 131072 | tf_op jit(solution)/shard_map/concatenate | solution.py:289
  53.4 1.8 %copy-done.1 = f32[12,224,256]{2,1,0:T(8,128)S(1)} copy-done((f32[12,224,256]{2,1,0:T(8,128)S(1)}, f32[12,224,256]{2,1,0:T(8,128)}, u32[]{:S(2)}) %copy-start.1) | copy-done | bytes 2752536
  62.3 9.9 %gradient.1 = (f32[224,64]{1,0:T(8,128)S(1)}, f32[224,96]{1,0:T(8,128)S(1)}, f32[224,64]{1,0:T(8,128)S(1)}, f32[1,1]{1,0:T(1,128)}) custom-call(f32[12]{0:T(128)S(1)} %copy-done.25, f32[8]{0:T(128)S(1)} %copy-done.27, s32[1]{0:T(128)S(6)} %copy.30.pick, s32[1]{0:T(128)} %bitcast.me, f32[32,512]{1,0:T(8,128)S(1)} %concatenate.27.gathered, ...), custom_call_target="tpu_custom_call" | custom-call | tf_op jit(solution)/shard_map/gradient/pallas_call | solution.py:348
  72.2 2.4 %collective-permute-start.10 = (f32[224,64]{1,0:T(8,128)S(1)}, f32[224,64]{1,0:T(8,128)S(1)}, u32[]{:S(2)}, u32[]{:S(2)}) collective-permute-start(f32[224,64]{1,0:T(8,128)S(1)} %get-tuple-element.18), channel_id=1, source_target_pairs={{1,0},{2,1},{3,2},{4,3},{5,4},{6,5},{7,6},{9,8},{10,9},{11,10},{12... | collective-permute-start | bytes 172040 | tf_op jit(solution)/shard_map/ppermute | solution.py:280
  74.6 3.4 %collective-permute-start.9 = (f32[224,64]{1,0:T(8,128)S(1)}, f32[224,64]{1,0:T(8,128)S(1)}, u32[]{:S(2)}, u32[]{:S(2)}) collective-permute-start(f32[224,64]{1,0:T(8,128)S(1)} %get-tuple-element.17), channel_id=1, source_target_pairs={{0,1},{1,2},{2,3},{3,4},{4,5},{5,6},{6,7},{8,9},{9,10},{10,11},{11... | collective-permute-start | bytes 172040 | tf_op jit(solution)/shard_map/ppermute | solution.py:280
  78.0 2.1 %collective-permute-done.10 = f32[224,64]{1,0:T(8,128)S(1)} collective-permute-done((f32[224,64]{1,0:T(8,128)S(1)}, f32[224,64]{1,0:T(8,128)S(1)}, u32[]{:S(2)}, u32[]{:S(2)}) %collective-permute-start.10) | collective-permute-done | bytes 57376 | tf_op jit(solution)/shard_map/ppermute | solution.py:280
  80.1 2.1 %collective-permute-done.9 = f32[224,64]{1,0:T(8,128)S(1)} collective-permute-done((f32[224,64]{1,0:T(8,128)S(1)}, f32[224,64]{1,0:T(8,128)S(1)}, u32[]{:S(2)}, u32[]{:S(2)}) %collective-permute-start.9) | collective-permute-done | bytes 57376 | tf_op jit(solution)/shard_map/ppermute | solution.py:280
  82.3 1.9 %collective-permute-start.12 = (f32[64,96]{1,0:T(8,128)S(1)}, f32[64,96]{1,0:T(8,128)S(1)}, u32[]{:S(2)}, u32[]{:S(2)}) collective-permute-start(f32[64,96]{1,0:T(8,128)S(1)} %get-tuple-element.21), channel_id=1, source_target_pairs={{8,0},{16,8},{24,16},{9,1},{17,9},{25,17},{10,2},{18,10},{26,18},{... | collective-permute-start | bytes 73736 | tf_op jit(solution)/shard_map/ppermute | solution.py:280
  84.2 2.4 %collective-permute-start.11 = (f32[64,96]{1,0:T(8,128)S(1)}, f32[64,96]{1,0:T(8,128)S(1)}, u32[]{:S(2)}, u32[]{:S(2)}) collective-permute-start(f32[64,96]{1,0:T(8,128)S(1)} %get-tuple-element.20), channel_id=1, source_target_pairs={{0,8},{8,16},{16,24},{1,9},{9,17},{17,25},{2,10},{10,18},{18,26},{... | collective-permute-start | bytes 73736 | tf_op jit(solution)/shard_map/ppermute | solution.py:280
  86.7 2.8 %collective-permute-done.11 = f32[64,96]{1,0:T(8,128)S(1)} collective-permute-done((f32[64,96]{1,0:T(8,128)S(1)}, f32[64,96]{1,0:T(8,128)S(1)}, u32[]{:S(2)}, u32[]{:S(2)}) %collective-permute-start.11) | collective-permute-done | bytes 24608 | tf_op jit(solution)/shard_map/ppermute | solution.py:280
  (84 shorter events, 10.6 us)
Async XLA Ops:
  1.5 5.6 %collective-permute-start = (f32[64,96]{1,0:T(8,128)S(1)}, f32[64,96]{1,0:T(8,128)S(1)}, u32[]{:S(2)}, u32[]{:S(2)}) collective-permute-start(f32[64,96]{1,0:T(8,128)S(1)} %get-tuple-element.25), channel_id=1, source_target_pairs={{0,8},{8,16},{16,24},{1,9},{9,17},{17,25},{2,10},{10,18},{18,26},{... | collective-permute-start | bytes 73736 | tf_op jit(solution)/shard_map/ppermute | solution.py:280
  3.4 5.2 %collective-permute-start.1 = (f32[64,96]{1,0:T(8,128)S(1)}, f32[64,96]{1,0:T(8,128)S(1)}, u32[]{:S(2)}, u32[]{:S(2)}) collective-permute-start(f32[64,96]{1,0:T(8,128)S(1)} %get-tuple-element.24), channel_id=1, source_target_pairs={{8,0},{16,8},{24,16},{9,1},{17,9},{25,17},{10,2},{18,10},{26,18},{... | collective-permute-start | bytes 73736 | tf_op jit(solution)/shard_map/ppermute | solution.py:280
  8.7 16.5 %collective-permute-start.2 = (f32[224,64]{1,0:T(8,128)S(1)}, f32[224,64]{1,0:T(8,128)S(1)}, u32[]{:S(2)}, u32[]{:S(2)}) collective-permute-start(f32[224,64]{1,0:T(8,128)S(1)} %get-tuple-element.23), channel_id=1, source_target_pairs={{0,1},{1,2},{2,3},{3,4},{4,5},{5,6},{6,7},{8,9},{9,10},{10,11},{11... | collective-permute-start | bytes 172040 | tf_op jit(solution)/shard_map/ppermute | solution.py:280
  12.2 13.0 %collective-permute-start.3 = (f32[224,64]{1,0:T(8,128)S(1)}, f32[224,64]{1,0:T(8,128)S(1)}, u32[]{:S(2)}, u32[]{:S(2)}) collective-permute-start(f32[224,64]{1,0:T(8,128)S(1)} %get-tuple-element.22), channel_id=1, source_target_pairs={{1,0},{2,1},{3,2},{4,3},{5,4},{6,5},{7,6},{9,8},{10,9},{11,10},{12... | collective-permute-start | bytes 172040 | tf_op jit(solution)/shard_map/ppermute | solution.py:280
  17.9 7.3 %copy-start.6 = (bf16[256,256]{1,0:T(8,128)(2,1)S(1)}, bf16[256,256]{1,0:T(8,128)(2,1)}, u32[]{:S(2)}) copy-start(bf16[256,256]{1,0:T(8,128)(2,1)} %constant.61.clone.fj_hi) | copy-start | bytes 393220
  18.0 7.3 %copy-start.7 = (bf16[256,256]{1,0:T(8,128)(2,1)S(1)}, bf16[256,256]{1,0:T(8,128)(2,1)}, u32[]{:S(2)}) copy-start(bf16[256,256]{1,0:T(8,128)(2,1)} %constant.62.clone.fj_lo) | copy-start | bytes 393220
  18.0 7.3 %copy-start.10 = (bf16[224,224]{1,0:T(8,128)(2,1)S(1)}, bf16[224,224]{1,0:T(8,128)(2,1)}, u32[]{:S(2)}) copy-start(bf16[224,224]{1,0:T(8,128)(2,1)} %constant.63.clone.fi_hi) | copy-start | bytes 301060
  18.0 7.3 %copy-start.11 = (bf16[224,224]{1,0:T(8,128)(2,1)S(1)}, bf16[224,224]{1,0:T(8,128)(2,1)}, u32[]{:S(2)}) copy-start(bf16[224,224]{1,0:T(8,128)(2,1)} %constant.64.clone.fi_lo) | copy-start | bytes 301060
  18.0 7.3 %copy-start.18 = (bf16[256,128]{1,0:T(8,128)(2,1)S(1)}, bf16[256,128]{1,0:T(8,128)(2,1)}, u32[]{:S(2)}) copy-start(bf16[256,128]{1,0:T(8,128)(2,1)} %constant.67.clone.side_hi) | copy-start | bytes 196612
  18.0 7.3 %copy-start.19 = (bf16[256,128]{1,0:T(8,128)(2,1)S(1)}, bf16[256,128]{1,0:T(8,128)(2,1)}, u32[]{:S(2)}) copy-start(bf16[256,128]{1,0:T(8,128)(2,1)} %constant.68.clone.side_lo) | copy-start | bytes 196612
  25.2 7.9 %copy-start = (f32[12,224,256]{2,1,0:T(8,128)}, f32[12,224,256]{2,1,0:T(8,128)S(1)}, u32[]{:S(2)}) copy-start(f32[12,224,256]{2,1,0:T(8,128)S(1)} %get-tuple-element.12.spec_im) | copy-start | bytes 8257540
  25.3 28.1 %copy-start.4 = (bf16[256,256]{1,0:T(8,128)(2,1)S(1)}, bf16[256,256]{1,0:T(8,128)(2,1)}, u32[]{:S(2)}) copy-start(bf16[256,256]{1,0:T(8,128)(2,1)} %constant.75.clone.bj_hi) | copy-start | bytes 393220
  25.3 28.1 %copy-start.27 = (f32[8]{0:T(128)S(1)}, f32[8]{0:T(128)}, u32[]{:S(2)}) copy-start(f32[8]{0:T(128)} %doses.1) | copy-start | bytes 100
  33.9 3.6 %collective-permute-start.4 = (f32[1,512]{1,0:T(1,128)S(1)}, f32[1,512]{1,0:T(1,128)S(1)}, u32[]{:S(2)}, u32[]{:S(2)}) collective-permute-start(f32[1,512]{1,0:T(1,128)S(1)} %get-tuple-element.13), channel_id=1, source_target_pairs={{0,1},{1,0},{2,3},{3,2},{4,5},{5,4},{6,7},{7,6},{8,9},{9,8},{10,11... | collective-permute-start | bytes 6152 | tf_op jit(solution)/shard_map/ppermute | solution.py:288
  37.5 10.3 %copy-start.32 = (f32[1,512]{1,0:T(1,128)}, f32[1,512]{1,0:T(1,128)S(1)}, u32[]{:S(2)}) copy-start(f32[1,512]{1,0:T(1,128)S(1)} %collective-permute-done.4) | copy-start | bytes 6148
  37.5 3.7 %collective-permute-start.5 = (f32[2,512]{1,0:T(2,128)S(1)}, f32[2,512]{1,0:T(2,128)S(1)}, u32[]{:S(2)}, u32[]{:S(2)}) collective-permute-start(f32[2,512]{1,0:T(2,128)S(1)} %pad_maximum_fusion.3), channel_id=1, source_target_pairs={{0,2},{1,3},{2,0},{3,1},{4,6},{5,7},{6,4},{7,5},{8,10},{9,11},{10,... | collective-permute-start | bytes 12296 | tf_op jit(solution)/shard_map/ppermute | solution.py:288
  41.2 4.6 %collective-permute-start.6 = (f32[4,512]{1,0:T(4,128)S(1)}, f32[4,512]{1,0:T(4,128)S(1)}, u32[]{:S(2)}, u32[]{:S(2)}) collective-permute-start(f32[4,512]{1,0:T(4,128)S(1)} %pad_maximum_fusion.2), channel_id=1, source_target_pairs={{0,4},{1,5},{2,6},{3,7},{4,0},{5,1},{6,2},{7,3},{8,12},{9,13},{10,... | collective-permute-start | bytes 24584 | tf_op jit(solution)/shard_map/ppermute | solution.py:288
  45.8 1.2 %collective-permute-start.7 = (f32[8,512]{1,0:T(8,128)S(1)}, f32[8,512]{1,0:T(8,128)S(1)}, u32[]{:S(2)}, u32[]{:S(2)}) collective-permute-start(f32[8,512]{1,0:T(8,128)S(1)} %pad_maximum_fusion.1), channel_id=1, source_target_pairs={{0,8},{1,9},{2,10},{3,11},{4,12},{5,13},{6,14},{7,15},{8,0},{9,1},... | collective-permute-start | bytes 49160 | tf_op jit(solution)/shard_map/ppermute | solution.py:288
  47.1 4.1 %collective-permute-start.8 = (f32[16,512]{1,0:T(8,128)S(1)}, f32[16,512]{1,0:T(8,128)}, u32[]{:S(2)}, u32[]{:S(2)}) collective-permute-start(f32[16,512]{1,0:T(8,128)S(1)} %concatenate.26), channel_id=1, source_target_pairs={{0,16},{1,17},{2,18},{3,19},{4,20},{5,21},{6,22},{7,23},{8,24},{9,... | collective-permute-start | bytes 98312 | tf_op jit(solution)/shard_map/ppermute | solution.py:288
  62.3 27.2 %copy-start.28 = (f32[96,96]{1,0:T(8,128)S(1)}, f32[96,96]{1,0:T(8,128)}, u32[]{:S(2)}) copy-start(f32[96,96]{1,0:T(8,128)} %param.27) | copy-start | bytes 110596
  72.2 7.9 %collective-permute-start.10 = (f32[224,64]{1,0:T(8,128)S(1)}, f32[224,64]{1,0:T(8,128)S(1)}, u32[]{:S(2)}, u32[]{:S(2)}) collective-permute-start(f32[224,64]{1,0:T(8,128)S(1)} %get-tuple-element.18), channel_id=1, source_target_pairs={{1,0},{2,1},{3,2},{4,3},{5,4},{6,5},{7,6},{9,8},{10,9},{11,10},{12... | collective-permute-start | bytes 172040 | tf_op jit(solution)/shard_map/ppermute | solution.py:280
  74.6 7.6 %collective-permute-start.9 = (f32[224,64]{1,0:T(8,128)S(1)}, f32[224,64]{1,0:T(8,128)S(1)}, u32[]{:S(2)}, u32[]{:S(2)}) collective-permute-start(f32[224,64]{1,0:T(8,128)S(1)} %get-tuple-element.17), channel_id=1, source_target_pairs={{0,1},{1,2},{2,3},{3,4},{4,5},{5,6},{6,7},{8,9},{9,10},{10,11},{11... | collective-permute-start | bytes 172040 | tf_op jit(solution)/shard_map/ppermute | solution.py:280
  82.3 4.3 %collective-permute-start.12 = (f32[64,96]{1,0:T(8,128)S(1)}, f32[64,96]{1,0:T(8,128)S(1)}, u32[]{:S(2)}, u32[]{:S(2)}) collective-permute-start(f32[64,96]{1,0:T(8,128)S(1)} %get-tuple-element.21), channel_id=1, source_target_pairs={{8,0},{16,8},{24,16},{9,1},{17,9},{25,17},{10,2},{18,10},{26,18},{... | collective-permute-start | bytes 73736 | tf_op jit(solution)/shard_map/ppermute | solution.py:280
  84.2 5.2 %collective-permute-start.11 = (f32[64,96]{1,0:T(8,128)S(1)}, f32[64,96]{1,0:T(8,128)S(1)}, u32[]{:S(2)}, u32[]{:S(2)}) collective-permute-start(f32[64,96]{1,0:T(8,128)S(1)} %get-tuple-element.20), channel_id=1, source_target_pairs={{0,8},{8,16},{16,24},{1,9},{9,17},{17,25},{2,10},{10,18},{18,26},{... | collective-permute-start | bytes 73736 | tf_op jit(solution)/shard_map/ppermute | solution.py:280
  (22 other events, 78.5 us)
where the time goes:
time: 91 us; the launch traced here: 90.1 us
  starting transfers between devices  26.1 us (29%)
  Pallas kernels  24.7 us (27%)
  waiting for transfers between devices  21.5 us (24%)
  local copies, waits for them, and re-layouts  14.4 us (16%)
  between operations  1.8 us (2%)
  other arithmetic  1.59 us (2%)
    ppermute x8, starting transfers between devices, shifted(): return lax.ppermute(x, axis, pairs)  22.6 us
    ppermute x5, waiting for transfers between devices, gather_all(): other = lax.ppermute(x, axes, [(i, i ^ step) for i in range(count)])  13 us
    unnamed x67, local copies, waits for them, and re-layouts  12 us
    pallas_call x1, Pallas kernels, body(): pl.pallas_call(gradient_kernel, out_shape=[shape(period, radius), shape(p...  9.9 us
    ppermute x8, waiting for transfers between devices, shifted(): return lax.ppermute(x, axis, pairs)  8.54 us
    pallas_call x1, Pallas kernels, body(): pl.pallas_call(field_kernel, out_shape=[shape(count, tile, LANES)] * 2 +...  7.71 us
    pallas_call x1, Pallas kernels, body(): pl.pallas_call(spectra_kernel, out_shape=[shape(count, period, 2 * LANES)...  7.1 us
    ppermute x5, starting transfers between devices, gather_all(): other = lax.ppermute(x, axes, [(i, i ^ step) for i in range(count)])  3.48 us
  transfers between devices with their start and end apart: 13, of which 9 were waited for; matrix products, arithmetic and copies ran while one was open for 2% of the time, Pallas kernels for 8%

commit v1 on v0

v1 whole, which is shorter than its diff:
```python
import functools
import math

import jax
import jax.numpy as jnp
import numpy as np
from jax import lax
from jax.experimental import pallas as pl
from jax.experimental.pallas import tpu as pltpu
from jax.sharding import PartitionSpec as P

STEEPNESS = 4.0
RESIST_LEVEL = 0.7
SOFTNESS = 0.25
LANES = 128
F32 = jnp.float32
BF16 = jnp.bfloat16


def split(x):
    high = x.astype(BF16)
    return high, (x - high.astype(F32)).astype(BF16)


def dot(a, b):
    return jnp.dot(a, b, preferred_element_type=F32)


def dot3(a, b):
    return dot(a[0], b[0]) + dot(a[0], b[1]) + dot(a[1], b[0])


def wave_tables(period):
    half = period // 2
    place = np.arange(period)
    angle = (np.arange(half)[None, :] + 0.5) * place[:, None] * (2.0 * math.pi / period)
    cos, sin = np.cos(angle), np.sin(angle)
    out = np.zeros((4, 2 * LANES, 2 * LANES))
    out[0, :period, :half] = cos
    out[0, :period, LANES : LANES + half] = sin
    out[1] = out[0].T
    out[2, :half, :period] = cos.T
    out[2, half:period, :period] = sin.T
    out[3] = out[2].T
    return out.astype(np.float32)


def halves(x):
    return x[:, :LANES], x[:, LANES:]


def edge_flags(axis):
    index, count = lax.axis_index(axis), lax.axis_size(axis)
    return lax.rem(index, 2) == 0, index > 0, index < count - 1


def sides(axis, first, second):
    even, lower, higher = edge_flags(axis)
    from_lower = jnp.where(lower, jnp.where(even, second, first), 0.0)
    from_higher = jnp.where(higher, jnp.where(even, first, second), 0.0)
    return from_lower, from_higher


def ordered(axis, for_lower, for_higher):
    even = lax.rem(lax.axis_index(axis), 2) == 0
    return jnp.where(even, for_higher, for_lower), jnp.where(even, for_lower, for_higher)


def exchange(axis, first, second):
    count = lax.axis_size(axis)
    out = []
    for offset, value in ((0, first), (1, second)):
        pairs = [(i, i) for i in range(count)]
        for low in range(offset, count - 1, 2):
            pairs[low], pairs[low + 1] = (low, low + 1), (low + 1, low)
        out.append(lax.ppermute(value, axis, pairs))
    return out


def spectra_kernel(start, kern, tables, *rest):
    out_re, out_im, token, planes, sems = rest[-5:]
    period = out_re.shape[1]
    half = period // 2
    taps = kern.shape[-1]
    parts = planes.shape[0]

    def fetch(k):
        return pltpu.make_async_copy(kern.at[:, start + k], planes.at[k], sems.at[k])

    for k in range(parts):
        fetch(k).start()
    cols = split(tables[0, :taps, :])
    rows = split(tables[2, :period, :taps])
    token[...] = jnp.zeros(token.shape, F32)

    def step(k, carry):
        fetch(k).wait()
        real_cos, real_sin = halves(dot3(split(planes[k, 0]), cols))
        imag_cos, imag_sin = halves(dot3(split(planes[k, 1]), cols))
        wide_re = jnp.concatenate([real_cos - imag_sin, real_cos + imag_sin], axis=1)
        wide_im = jnp.concatenate([real_sin + imag_cos, imag_cos - real_sin], axis=1)
        tall_re = dot3(rows, split(wide_re))
        tall_im = dot3(rows, split(wide_im))
        out_re[start + k, :half] = tall_re[:half] - tall_im[half:]
        out_re[start + k, half:] = tall_re[:half] + tall_im[half:]
        out_im[start + k, :half] = tall_im[:half] + tall_re[half:]
        out_im[start + k, half:] = tall_im[:half] - tall_re[half:]
        return carry

    lax.fori_loop(0, parts, step, 0)


def column_kernel(middle, first, second, after, column, next_first, next_second, token):
    tile = middle.shape[0]
    radius = first.shape[0]
    above, below = sides("ty", first[...], second[...])
    column[:radius] = above
    column[radius : radius + tile] = middle[...]
    column[radius + tile :] = below
    next_first[...], next_second[...] = ordered(
        "tx", column[:, :radius], column[:, tile - radius :]
    )
    token[...] = jnp.zeros(token.shape, F32)


def total_weight(weights, kernels):
    total = weights[0]
    for k in range(1, kernels):
        total = total + weights[k]
    return jnp.full((1, 1), total, F32)


def sample_places(pixels, tile):
    row = ((pixels.astype(F32) + 0.5) * (1.0 / tile)).astype(jnp.int32)
    return row, pixels - row * tile


def field_kernel(
    weights, spec_re, spec_im, column, first, second, pixels, slopes, tables,
    field_re, field_im, sampled, framed, mask,
):
    kernels, period, _ = spec_re.shape
    half = period // 2
    tile = field_re.shape[1]
    radius = first.shape[1]
    left, right = sides("tx", first[...], second[...])
    framed[:, period:] = jnp.zeros((period, 2 * LANES - period), F32)
    framed[:, :radius] = left
    framed[:, radius + tile : period] = right
    framed[:, radius : radius + tile] = column[...]
    wide = dot3(split(framed[...]), split(tables[0]))
    tall = dot3(split(tables[2, :period, :period]), split(wide)) * (1.0 / (period * period))
    cos_cos, cos_sin = halves(tall[:half])
    sin_cos, sin_sin = halves(tall[half:])
    same, other = cos_cos - sin_sin, cos_cos + sin_sin
    joint, cross = sin_cos + cos_sin, sin_cos - cos_sin
    mask[0, :, :LANES], mask[0, :, LANES:] = same, other
    mask[1, :, :LANES], mask[1, :, LANES:] = -joint, -cross
    mask[2, :, :LANES], mask[2, :, LANES:] = other, same
    mask[3, :, :LANES], mask[3, :, LANES:] = cross, joint
    lift = split(tables[3, :tile, :period])
    across = split(tables[1, :, :LANES])

    def step(k, intensity):
        pos_re, pos_im = spec_re[k, :half], spec_im[k, :half]
        neg_re, neg_im = spec_re[k, half:], spec_im[k, half:]
        up_re = mask[0] * pos_re - mask[1] * pos_im
        up_im = mask[0] * pos_im + mask[1] * pos_re
        down_re = mask[2] * neg_re - mask[3] * neg_im
        down_im = mask[2] * neg_im + mask[3] * neg_re
        for_re = jnp.concatenate([up_re + down_re, down_im - up_im], axis=0)
        for_im = jnp.concatenate([up_im + down_im, up_re - down_re], axis=0)
        re_pos, re_neg = halves(dot3(lift, split(for_re)))
        im_pos, im_neg = halves(dot3(lift, split(for_im)))
        rows_re = jnp.concatenate([re_pos + re_neg, im_neg - im_pos], axis=1)
        rows_im = jnp.concatenate([im_pos + im_neg, re_pos - re_neg], axis=1)
        real = dot3(split(rows_re), across)
        imag = dot3(split(rows_im), across)
        field_re[k] = real
        field_im[k] = imag
        return intensity + weights[k] * (real * real + imag * imag)

    intensity = lax.fori_loop(0, kernels, step, jnp.zeros((tile, LANES), F32))
    intensity = intensity / total_weight(weights, kernels)
    samples = pixels.shape[1]
    row, col = sample_places(pixels[...], tile)
    in_col = lax.broadcasted_iota(jnp.int32, (LANES, samples), 0) == col
    one_hot = jnp.where(in_col, 1.0, 0.0).astype(BF16)
    high, rest = split(intensity)
    low = intensity - high.astype(F32) - rest.astype(F32)
    picked = dot(high, one_hot) + dot(rest, one_hot) + dot(low.astype(BF16), one_hot)
    in_row = lax.broadcasted_iota(jnp.int32, (tile, samples), 0) == row
    sampled[:, :samples] = jnp.sum(jnp.where(in_row, picked, 0.0), axis=0, keepdims=True)
    sampled[:, samples:] = slopes[...]


def sigmoid(x):
    return 1.0 / (1.0 + jnp.exp(-x))


def errors(intensity, slope, dose):
    resist = sigmoid(STEEPNESS * (dose * intensity - RESIST_LEVEL))
    offset = (resist - 0.5) * slope
    return resist, offset, offset * offset


def gradient_kernel(
    weights, doses, pick, gathered, sampled, pixels, spec_re, spec_im, field_re, field_im,
    tables, middle, first, second, tail, total_re, total_im,
):
    kernels, period, _ = spec_re.shape
    half = period // 2
    tile = field_re.shape[1]
    radius = (period - tile) // 2
    samples = pixels.shape[1]
    devices = gathered.shape[0]
    corners = doses.shape[0]
    per_corner = devices * samples
    everyone, every_slope = gathered[:, :samples], gathered[:, samples:]
    pick_corner = pick[0] // per_corner
    remain = pick[0] - pick_corner * per_corner
    place = lax.broadcasted_iota(jnp.int32, (devices, samples), 0) * samples
    place = place + lax.broadcasted_iota(jnp.int32, (devices, samples), 1)
    _, _, picked = errors(everyone, every_slope, doses[pick_corner])
    threshold = jnp.sum(jnp.where(place == remain, picked, 0.0), keepdims=True)

    def corner(c, sums):
        _, _, error = errors(everyone, every_slope, doses[c])
        soft = sigmoid((error - threshold) * (1.0 / SOFTNESS))
        return sums[0] + soft, sums[1] + error * soft

    zero = jnp.zeros((devices, samples), F32)
    soft_sum, error_sum = lax.fori_loop(0, corners, corner, (zero, zero))
    soft_total = jnp.sum(soft_sum, keepdims=True)
    tail_mean = jnp.sum(error_sum, keepdims=True) / soft_total
    tail[...] = tail_mean

    own, slope = sampled[:, :samples], sampled[:, samples:]
    which = lax.broadcasted_iota(jnp.int32, (corners, samples), 0)
    dose = jnp.zeros((corners, samples), F32)
    for c in range(corners):
        dose = jnp.where(which == c, doses[c], dose)
    resist, offset, error = errors(own, slope, dose)
    soft = sigmoid((error - threshold) * (1.0 / SOFTNESS))
    slope_soft = soft * (1.0 - soft) * (1.0 / SOFTNESS)
    chain = 2.0 * STEEPNESS * offset * slope * dose * resist * (1.0 - resist)
    coefficient = (soft + (error - tail_mean) * slope_soft) * (corners * per_corner / soft_total)
    summed = jnp.sum(coefficient * chain, axis=0, keepdims=True)
    summed = summed / total_weight(weights, kernels)

    row, col = sample_places(pixels[...], tile)
    in_row = lax.broadcasted_iota(jnp.int32, (tile, samples), 0) == row
    in_col = lax.broadcasted_iota(jnp.int32, (LANES, samples), 0) == col
    one_hot = jnp.where(in_col, 1.0, 0.0).astype(BF16)
    placed = jnp.where(in_row, summed, 0.0)
    high, rest = split(placed)
    low = (placed - high.astype(F32) - rest.astype(F32)).astype(BF16)
    grid = jnp.zeros((tile, LANES), F32)
    for part in (high, rest, low):
        grid = grid + lax.dot_general(
            part, one_hot, (((1,), (1,)), ((), ())), preferred_element_type=F32
        )

    cols = split(tables[0, :LANES])
    rows = split(tables[2, :period, :tile])
    total_re[...] = jnp.zeros((period, 2 * LANES), F32)
    total_im[...] = jnp.zeros((period, 2 * LANES), F32)

    def step(k, carry):
        weighted = grid * weights[k]
        real_cos, real_sin = halves(dot3(split(weighted * field_re[k]), cols))
        imag_cos, imag_sin = halves(dot3(split(weighted * field_im[k]), cols))
        wide_re = jnp.concatenate([real_cos + imag_sin, real_cos - imag_sin], axis=1)
        wide_im = jnp.concatenate([imag_cos - real_sin, imag_cos + real_sin], axis=1)
        tall_re = dot3(rows, split(wide_re))
        tall_im = dot3(rows, split(wide_im))
        for start, sign in ((0, 1.0), (half, -1.0)):
            part = slice(start, start + half)
            wave_re = tall_re[:half] + sign * tall_im[half:]
            wave_im = tall_im[:half] - sign * tall_re[half:]
            own_re, own_im = spec_re[k, part], spec_im[k, part]
            total_re[part] += own_re * wave_re + own_im * wave_im
            total_im[part] += own_re * wave_im - own_im * wave_re
        return carry

    lax.fori_loop(0, kernels, step, 0)
    pos_re, neg_re = total_re[:half], total_re[half:]
    pos_im, neg_im = total_im[:half], total_im[half:]
    back_rows = split(tables[3, :period, :period])
    for_re = jnp.concatenate([pos_re + neg_re, neg_im - pos_im], axis=0)
    for_im = jnp.concatenate([pos_im + neg_im, pos_re - neg_re], axis=0)
    re_pos, re_neg = halves(dot3(back_rows, split(for_re)))
    im_pos, im_neg = halves(dot3(back_rows, split(for_im)))
    last = jnp.concatenate([re_pos + re_neg, im_neg - im_pos], axis=1)
    grad = dot3(split(last), split(tables[1])) * (2.0 / (period * period))
    middle[...] = grad[:, radius : radius + tile]
    first[...], second[...] = ordered("tx", grad[:, :radius], grad[:, radius + tile : period])


VMEM = pl.BlockSpec(memory_space=pltpu.VMEM)
SMEM = pl.BlockSpec(memory_space=pltpu.SMEM)
ANY = pl.BlockSpec(memory_space=pl.ANY)


def shape(*dims):
    return jax.ShapeDtypeStruct(dims, F32)


def call(kernel, name, out_shape, in_specs, scratch=(), aliases=None, micros=1):
    return pl.pallas_call(
        kernel,
        out_shape=out_shape,
        in_specs=in_specs,
        out_specs=[VMEM] * len(out_shape),
        scratch_shapes=scratch,
        input_output_aliases=aliases or {},
        compiler_params=pltpu.CompilerParams(vmem_limit_bytes=10 * 1024 * 1024),
        cost_estimate=pl.CostEstimate(
            flops=micros * 10**9, bytes_accessed=2**20, transcendentals=0
        ),
        name=name,
    )


def gather_all(x):
    return lax.all_gather(x, ("ty", "tx"), axis=0, tiled=True)


def body(latent, kernels, socs_weights, dose_scale, inv_slope, edge_pixels, threshold_pick):
    tile = latent.shape[0]
    count, taps = kernels.shape[1], kernels.shape[-1]
    samples = edge_pixels.shape[1]
    radius = (taps - 1) // 2
    period = tile + 2 * radius
    half = period // 2
    tables = jnp.asarray(wave_tables(period))
    token = shape(8, LANES)

    transmit = 0.5 * (1.0 + jnp.tanh(latent))
    rims = exchange("ty", *ordered("ty", transmit[:radius], transmit[tile - radius :]))

    parts = count // 2
    spec = []
    after = []
    for part in range(2):
        given = spec + after
        *spec, done = call(
            functools.partial(spectra_kernel, part * parts),
            "spectra",
            [shape(count, period, 2 * LANES)] * 2 + [token],
            [ANY, VMEM] + [ANY] * len(given),
            scratch=[
                pltpu.VMEM((parts, 2, taps, taps), F32),
                pltpu.SemaphoreType.DMA((parts,)),
            ],
            aliases={2: 0, 3: 1} if spec else None,
            micros=3,
        )(kernels, tables, *given)
        if part == 0:
            column, *rims, done = call(
                column_kernel,
                "column",
                [shape(period, tile)] + [shape(period, radius)] * 2 + [token],
                [VMEM] * 3 + [ANY],
            )(transmit, *rims, done)
            after = [done]
            rims = exchange("tx", *rims)

    field_re, field_im, sampled = call(
        field_kernel,
        "field",
        [shape(count, tile, LANES)] * 2 + [shape(1, 2 * samples)],
        [SMEM] + [VMEM] * 8,
        scratch=[
            pltpu.VMEM((period, 2 * LANES), F32),
            pltpu.VMEM((4, half, 2 * LANES), F32),
        ],
        micros=7,
    )(socs_weights, *spec, column, *rims, edge_pixels, inv_slope, tables)

    gathered = gather_all(sampled)
    grad_middle, first, second, tail_mean = call(
        gradient_kernel,
        "gradient",
        [shape(period, tile)] + [shape(period, radius)] * 2 + [shape(1, 1)],
        [SMEM] * 3 + [VMEM] * 8,
        scratch=[pltpu.VMEM((period, 2 * LANES), F32)] * 2,
        micros=9,
    )(
        socs_weights, dose_scale, threshold_pick, gathered, sampled, edge_pixels,
        *spec, field_re, field_im, tables,
    )

    rest = tile - radius
    from_left, from_right = sides("tx", *exchange("tx", first, second))
    column = (
        grad_middle
        + jnp.pad(from_left, ((0, 0), (0, rest)))
        + jnp.pad(from_right, ((0, 0), (rest, 0)))
    )
    rims = exchange("ty", *ordered("ty", column[:radius], column[radius + tile :]))
    from_above, from_below = sides("ty", *rims)
    mask_grad = (
        column[radius : radius + tile]
        + jnp.pad(from_above, ((0, rest), (0, 0)))
        + jnp.pad(from_below, ((rest, 0), (0, 0)))
    )
    tanh_value = jnp.tanh(latent)
    steering = mask_grad * 0.5 * (1.0 - tanh_value * tanh_value)
    return (steering, tail_mean.reshape(1))


def solution(mesh):
    placed = (P("ty", "tx"), P(), P(), P(), P("ty", "tx"), P("ty", "tx"), P())
    return jax.shard_map(
        body, mesh=mesh, in_specs=placed, out_specs=(P("ty", "tx"), P()), check_vma=False
    )
```

time: 91 us -> 116 us (1.27)
  the two profiles are of different devices: /device:TPU:10 before, /device:TPU:0 now
where the time goes in v1:
time: 116 us; the launch traced here: 115 us
  blocking collectives  67.9 us (59%)
  Pallas kernels  25.1 us (22%)
  starting transfers between devices  12.1 us (10%)
  waiting for transfers between devices  4.44 us (4%)
  local copies, waits for them, and re-layouts  2.28 us (2%)
  other arithmetic  1.6 us (1%)
  between operations  1.49 us (1%)
    all_gather x1, blocking collectives, gather_all(): return lax.all_gather(x, ('ty', 'tx'), axis=0, tiled=True)  67.9 us
    ppermute x8, starting transfers between devices, exchange(): out.append(lax.ppermute(value, axis, pairs))  12.1 us
    pallas_call x1, Pallas kernels, body(): call(gradient_kernel, 'gradient', [shape(period, tile)] + [shape(period,...  9.52 us
    pallas_call x1, Pallas kernels, body(): call(field_kernel, 'field', [shape(count, tile, LANES)] * 2 + [shape(1, 2...  7.81 us
    pallas_call x2, Pallas kernels, body(): call(functools.partial(spectra_kernel, part * parts), 'spectra', [shape(c...  7.57 us
    ppermute x8, waiting for transfers between devices, exchange(): out.append(lax.ppermute(value, axis, pairs))  4.44 us
  transfers between devices with their start and end apart: 8, of which 2 were waited for; matrix products, arithmetic and copies ran while one was open for 2% of the time, Pallas kernels for 7%

profile of v1, /device:TPU:0, one launch (start us, length us, event | category | flops | bytes accessed | tf_op | source)
XLA Modules:
  0.0 114.9 jit_solution(948632211988567169)
XLA Ops:
  0.6 0.8 add_multiply_fusion.middle
  1.5 0.5 collective-permute-start
  2.0 0.8 collective-permute-start.1
  2.8 2.2 %copy.15.kern = f32[2,12,129,129]{3,2,1,0:T(8,128)S(1)} copy(f32[2,12,129,129]{3,0,2,1:T(2,128)} %param.9) | data formatting | bytes 3195072 | tf_op args[1]
  5.0 3.8 %spectra.2 = (f32[12,224,256]{2,1,0:T(8,128)S(1)}, f32[12,224,256]{2,1,0:T(8,128)S(1)}, f32[8,128]{1,0:T(8,128)S(1)}) custom-call(f32[2,12,129,129]{3,2,1,0:T(8,128)S(1)} %copy.15.kern, f32[4,256,256]{2,1,0:T(8,128)S(1)} %copy-done.4), custom_call_target="tpu_custom_call" | custom-call | flops 3000000000 | bytes 1048576 | tf_op jit(solution)/shard_map/spectra/pallas_call | solution.py:347
  9.5 0.2 column.1
  9.7 2.6 %collective-permute-start.2 = (f32[224,64]{1,0:T(8,128)S(1)}, f32[224,64]{1,0:T(8,128)S(1)}, u32[]{:S(2)}, u32[]{:S(2)}) collective-permute-start(f32[224,64]{1,0:T(8,128)S(1)} %get-tuple-element.25), channel_id=1, source_target_pairs={{0,1},{1,0},{2,3},{3,2},{4,5},{5,4},{6,7},{7,6},{8,9},{9,8},{10,11... | collective-permute-start | bytes 172040 | tf_op jit(solution)/shard_map/ppermute | solution.py:76
  12.3 0.7 collective-permute-start.3
  12.9 0.0 copy-start
  13.0 0.0 copy-start.1
  13.0 0.0 copy-start.2
  13.0 3.8 %spectra.3 = (f32[12,224,256]{2,1,0:T(8,128)S(1)}, f32[12,224,256]{2,1,0:T(8,128)S(1)}, f32[8,128]{1,0:T(8,128)}) custom-call(f32[2,12,129,129]{3,2,1,0:T(8,128)S(1)} %copy.15.kern, f32[4,256,256]{2,1,0:T(8,128)S(1)} %copy-done.4, f32[12,224,256]{2,1,0:T(8,128)S(1)} %get-tuple-element.18.rest_0_, ...), custom_call_target="tpu_custom_call", output_to_operand_aliasing={{0}: (2, {}), {1}: (3, {})} | custom-call | flops 3000000000 | bytes 1048576 | tf_op jit(solution)/shard_map/spectra/pallas_call | solution.py:347
  16.8 7.8 %field.1 = (f32[12,96,128]{2,1,0:T(8,128)S(1)}, f32[12,96,128]{2,1,0:T(8,128)S(1)}, f32[1,512]{1,0:T(1,128)S(1)}) custom-call(f32[12]{0:T(128)S(1)} %copy-done.2, f32[12,224,256]{2,1,0:T(8,128)S(1)} %get-tuple-element.22.spec_re, f32[12,224,256]{2,1,0:T(8,128)S(1)} %get-tuple-element.23.spec_im, f32[224,96]{1,0:T(8,128)S(1)} %get-tuple-element.24.column, ...), custom_call_target="tpu_custom_call" | custom-call | flops 7000000000 | bytes 1048576 | tf_op jit(solution)/shard_map/field/pallas_call | solution.py:369
  24.7 67.9 %all-gather = f32[32,1,512]{2,1,0:T(1,128)S(1)} all-gather(f32[1,1,512]{2,1,0:T(1,128)S(1)} %bitcast.6), channel_id=1, replica_groups=mesh['ty'=4,'tx'=8] {'ty','tx'}, dimensions={0}, use_global_device_ids=true | all-gather | bytes 67584 | tf_op jit(solution)/shard_map/all_gather | solution.py:326
  92.6 0.0 copy-start.5
  92.6 9.5 %gradient.1 = (f32[224,96]{1,0:T(8,128)S(1)}, f32[224,64]{1,0:T(8,128)S(1)}, f32[224,64]{1,0:T(8,128)S(1)}, f32[1,1]{1,0:T(1,128)}) custom-call(f32[12]{0:T(128)S(1)} %copy-done.2, f32[8]{0:T(128)S(1)} %copy-done.3, s32[1]{0:T(128)S(6)} %copy.21.pick, f32[32,512]{1,0:T(8,128)S(1)} %bitcast.5, f32[1,512]{1,0:T(1,128)S(1)} %get-tuple-element.27.sampled, ...), custom_call_target="tpu_custom_call" | custom-call | flops 8999999488 | bytes 1048576 | tf_op jit(solution)/shard_map/gradient/pallas_call | solution.py:382
  102.1 0.7 collective-permute-start.4
  102.8 1.5 %collective-permute-start.5 = (f32[224,64]{1,0:T(8,128)S(1)}, f32[224,64]{1,0:T(8,128)S(1)}, u32[]{:S(2)}, u32[]{:S(2)}) collective-permute-start(f32[224,64]{1,0:T(8,128)S(1)} %get-tuple-element.32), channel_id=1, source_target_pairs={{0,1},{1,0},{2,3},{3,2},{4,5},{5,4},{6,7},{7,6},{8,9},{9,8},{10,11... | collective-permute-start | bytes 172040 | tf_op jit(solution)/shard_map/ppermute | solution.py:76
  104.3 3.6 %collective-permute-done.5 = f32[224,64]{1,0:T(8,128)S(1)} collective-permute-done((f32[224,64]{1,0:T(8,128)S(1)}, f32[224,64]{1,0:T(8,128)S(1)}, u32[]{:S(2)}, u32[]{:S(2)}) %collective-permute-start.5) | collective-permute-done | bytes 57376 | tf_op jit(solution)/shard_map/ppermute | solution.py:76
  107.9 0.1 pad_add_fusion
  108.0 0.7 collective-permute-start.6
  108.7 4.7 %collective-permute-start.7 = (f32[64,96]{1,0:T(8,128)S(1)}, f32[64,96]{1,0:T(8,128)S(1)}, u32[]{:S(2)}, u32[]{:S(2)}) collective-permute-start(f32[64,96]{1,0:T(8,128)S(1)} %get-tuple-element.37), channel_id=1, source_target_pairs={{0,8},{8,0},{16,24},{24,16},{1,9},{9,1},{17,25},{25,17},{2,10},{10... | collective-permute-start | bytes 73736 | tf_op jit(solution)/shard_map/ppermute | solution.py:76
  113.4 0.9 collective-permute-done.7
  114.3 0.6 fusion.2
  (19 shorter events, 0.1 us)
Async XLA Ops:
  1.5 8.0 %collective-permute-start = (f32[64,96]{1,0:T(8,128)S(1)}, f32[64,96]{1,0:T(8,128)S(1)}, u32[]{:S(2)}, u32[]{:S(2)}) collective-permute-start(f32[64,96]{1,0:T(8,128)S(1)} %get-tuple-element.41), channel_id=1, source_target_pairs={{0,8},{8,0},{16,24},{24,16},{1,9},{9,1},{17,25},{25,17},{2,10},{10... | collective-permute-start | bytes 73736 | tf_op jit(solution)/shard_map/ppermute | solution.py:76
  2.0 3.0 %copy-start.4 = (f32[4,256,256]{2,1,0:T(8,128)S(1)}, f32[4,256,256]{2,1,0:T(8,128)}, u32[]{:S(2)}) copy-start(f32[4,256,256]{2,1,0:T(8,128)} %constant.29.clone.tables) | copy-start | bytes 3145732
  2.0 7.5 %collective-permute-start.1 = (f32[64,96]{1,0:T(8,128)S(1)}, f32[64,96]{1,0:T(8,128)S(1)}, u32[]{:S(2)}, u32[]{:S(2)}) collective-permute-start(f32[64,96]{1,0:T(8,128)S(1)} %get-tuple-element.40), channel_id=1, source_target_pairs={{0,0},{8,16},{16,8},{24,24},{1,1},{9,17},{17,9},{25,25},{2,2},{10,... | collective-permute-start | bytes 73736 | tf_op jit(solution)/shard_map/ppermute | solution.py:76
  9.7 7.1 %collective-permute-start.2 = (f32[224,64]{1,0:T(8,128)S(1)}, f32[224,64]{1,0:T(8,128)S(1)}, u32[]{:S(2)}, u32[]{:S(2)}) collective-permute-start(f32[224,64]{1,0:T(8,128)S(1)} %get-tuple-element.25), channel_id=1, source_target_pairs={{0,1},{1,0},{2,3},{3,2},{4,5},{5,4},{6,7},{7,6},{8,9},{9,8},{10,11... | collective-permute-start | bytes 172040 | tf_op jit(solution)/shard_map/ppermute | solution.py:76
  12.3 4.5 %collective-permute-start.3 = (f32[224,64]{1,0:T(8,128)S(1)}, f32[224,64]{1,0:T(8,128)S(1)}, u32[]{:S(2)}, u32[]{:S(2)}) collective-permute-start(f32[224,64]{1,0:T(8,128)S(1)} %get-tuple-element.26), channel_id=1, source_target_pairs={{0,0},{1,2},{2,1},{3,4},{4,3},{5,6},{6,5},{7,7},{8,8},{9,10},{10,9... | collective-permute-start | bytes 172040 | tf_op jit(solution)/shard_map/ppermute | solution.py:76
  12.9 3.9 %copy-start = (f32[1,256]{1,0:T(1,128)S(1)}, f32[1,256]{1,0:T(1,128)}, u32[]{:S(2)}) copy-start(f32[1,256]{1,0:T(1,128)} %slopes.1) | copy-start | bytes 3076
  13.0 3.9 %copy-start.1 = (s32[1,256]{1,0:T(1,128)S(1)}, s32[1,256]{1,0:T(1,128)}, u32[]{:S(2)}) copy-start(s32[1,256]{1,0:T(1,128)} %pixels.3) | copy-start | bytes 3076
  13.0 3.9 %copy-start.2 = (f32[12]{0:T(128)S(1)}, f32[12]{0:T(128)}, u32[]{:S(2)}) copy-start(f32[12]{0:T(128)} %weights.3) | copy-start | bytes 148
  16.8 75.7 %copy-start.3 = (f32[8]{0:T(128)S(1)}, f32[8]{0:T(128)}, u32[]{:S(2)}) copy-start(f32[8]{0:T(128)} %doses.1) | copy-start | bytes 100
  92.6 21.7 %copy-start.5 = (f32[96,96]{1,0:T(8,128)S(1)}, f32[96,96]{1,0:T(8,128)}, u32[]{:S(2)}) copy-start(f32[96,96]{1,0:T(8,128)} %param.8) | copy-start | bytes 110596
  102.1 2.2 %collective-permute-start.4 = (f32[224,64]{1,0:T(8,128)S(1)}, f32[224,64]{1,0:T(8,128)S(1)}, u32[]{:S(2)}, u32[]{:S(2)}) collective-permute-start(f32[224,64]{1,0:T(8,128)S(1)} %get-tuple-element.31), channel_id=1, source_target_pairs={{0,0},{1,2},{2,1},{3,4},{4,3},{5,6},{6,5},{7,7},{8,8},{9,10},{10,9... | collective-permute-start | bytes 172040 | tf_op jit(solution)/shard_map/ppermute | solution.py:76
  102.8 5.1 %collective-permute-start.5 = (f32[224,64]{1,0:T(8,128)S(1)}, f32[224,64]{1,0:T(8,128)S(1)}, u32[]{:S(2)}, u32[]{:S(2)}) collective-permute-start(f32[224,64]{1,0:T(8,128)S(1)} %get-tuple-element.32), channel_id=1, source_target_pairs={{0,1},{1,0},{2,3},{3,2},{4,5},{5,4},{6,7},{7,6},{8,9},{9,8},{10,11... | collective-permute-start | bytes 172040 | tf_op jit(solution)/shard_map/ppermute | solution.py:76
  108.0 5.4 %collective-permute-start.6 = (f32[64,96]{1,0:T(8,128)S(1)}, f32[64,96]{1,0:T(8,128)S(1)}, u32[]{:S(2)}, u32[]{:S(2)}) collective-permute-start(f32[64,96]{1,0:T(8,128)S(1)} %get-tuple-element.36), channel_id=1, source_target_pairs={{0,0},{8,16},{16,8},{24,24},{1,1},{9,17},{17,9},{25,25},{2,2},{10,... | collective-permute-start | bytes 73736 | tf_op jit(solution)/shard_map/ppermute | solution.py:76
  108.7 5.6 %collective-permute-start.7 = (f32[64,96]{1,0:T(8,128)S(1)}, f32[64,96]{1,0:T(8,128)S(1)}, u32[]{:S(2)}, u32[]{:S(2)}) collective-permute-start(f32[64,96]{1,0:T(8,128)S(1)} %get-tuple-element.37), channel_id=1, source_target_pairs={{0,8},{8,0},{16,24},{24,16},{1,9},{9,1},{17,25},{25,17},{2,10},{10... | collective-permute-start | bytes 73736 | tf_op jit(solution)/shard_map/ppermute | solution.py:76

commit v2 on v1

--- a/solution.py
+++ b/solution.py
@@ -323,7 +323,9 @@
 
 
 def gather_all(x):
-    return lax.all_gather(x, ("ty", "tx"), axis=0, tiled=True)
+    count = lax.axis_size("ty") * lax.axis_size("tx")
+    copies = jnp.broadcast_to(x, (count, x.shape[1]))
+    return lax.all_to_all(copies, ("ty", "tx"), 0, 0, tiled=True)
 
 
 def body(latent, kernels, socs_weights, dose_scale, inv_slope, edge_pixels, threshold_pick):

time: 116 us -> 69.6 us (0.60)
  the two profiles are of different devices: /device:TPU:0 before, /device:TPU:5 now
where the time goes in v2:
time: 69.6 us; the launch traced here: 69.2 us
  Pallas kernels  25 us (36%)
  starting transfers between devices  18.8 us (27%)
  waiting for transfers between devices  15.7 us (23%)
  local copies, waits for them, and re-layouts  6.49 us (9%)
  other arithmetic  1.6 us (2%)
  between operations  1.57 us (2%)
    ppermute x8, starting transfers between devices, exchange(): out.append(lax.ppermute(value, axis, pairs))  13.7 us
    ppermute x8, waiting for transfers between devices, exchange(): out.append(lax.ppermute(value, axis, pairs))  10.1 us
    pallas_call x1, Pallas kernels, body(): call(gradient_kernel, 'gradient', [shape(period, tile)] + [shape(period,...  9.55 us
    pallas_call x1, Pallas kernels, body(): call(field_kernel, 'field', [shape(count, tile, LANES)] * 2 + [shape(1, 2...  7.71 us
    pallas_call x2, Pallas kernels, body(): call(functools.partial(spectra_kernel, part * parts), 'spectra', [shape(c...  7.57 us
    unnamed x22, local copies, waits for them, and re-layouts  5.83 us
    all_to_all x1, waiting for transfers between devices, gather_all(): return lax.all_to_all(copies, ('ty', 'tx'), 0, 0, tiled=True)  5.61 us
    all_to_all x1, starting transfers between devices, gather_all(): return lax.all_to_all(copies, ('ty', 'tx'), 0, 0, tiled=True)  5.13 us
  transfers between devices with their start and end apart: 9, of which 4 were waited for; matrix products, arithmetic and copies ran while one was open for 3% of the time, Pallas kernels for 11%

profile of v2, /device:TPU:5, one launch (start us, length us, event | category | flops | bytes accessed | tf_op | source)
XLA Modules:
  0.0 69.2 jit_solution(1386410867047042415)
XLA Ops:
  0.6 0.8 %add_multiply_fusion.middle = f32[96,96]{1,0:T(8,128)S(1)} fusion(f32[96,96]{1,0:T(8,128)} %param.8), kind=kLoop, calls=%fused_computation.8 | loop fusion | flops 18432 | bytes 73728 | tf_op jit(solution)/shard_map/mul | solution.py:341
  1.5 0.7 %collective-permute-start = (f32[64,96]{1,0:T(8,128)S(1)}, f32[64,96]{1,0:T(8,128)S(1)}, u32[]{:S(2)}, u32[]{:S(2)}) collective-permute-start(f32[64,96]{1,0:T(8,128)S(1)} %get-tuple-element.41), channel_id=1, source_target_pairs={{0,8},{8,0},{16,24},{24,16},{1,9},{9,1},{17,25},{25,17},{2,10},{10... | collective-permute-start | bytes 73736 | tf_op jit(solution)/shard_map/ppermute | solution.py:76
  2.2 3.2 %collective-permute-start.1 = (f32[64,96]{1,0:T(8,128)S(1)}, f32[64,96]{1,0:T(8,128)S(1)}, u32[]{:S(2)}, u32[]{:S(2)}) collective-permute-start(f32[64,96]{1,0:T(8,128)S(1)} %get-tuple-element.40), channel_id=1, source_target_pairs={{0,0},{8,16},{16,8},{24,24},{1,1},{9,17},{17,9},{25,25},{2,2},{10,... | collective-permute-start | bytes 73736 | tf_op jit(solution)/shard_map/ppermute | solution.py:76
  5.4 2.2 %copy.15.kern = f32[2,12,129,129]{3,2,1,0:T(8,128)S(1)} copy(f32[2,12,129,129]{3,0,2,1:T(2,128)} %param.9) | data formatting | bytes 3195072 | tf_op args[1]
  7.6 3.8 %spectra.2 = (f32[12,224,256]{2,1,0:T(8,128)S(1)}, f32[12,224,256]{2,1,0:T(8,128)S(1)}, f32[8,128]{1,0:T(8,128)S(1)}) custom-call(f32[2,12,129,129]{3,2,1,0:T(8,128)S(1)} %copy.15.kern, f32[4,256,256]{2,1,0:T(8,128)S(1)} %copy-done.4), custom_call_target="tpu_custom_call" | custom-call | flops 3000000000 | bytes 1048576 | tf_op jit(solution)/shard_map/spectra/pallas_call | solution.py:349
  11.4 0.2 column.1
  11.6 0.3 collective-permute-start.2
  11.9 4.1 %collective-permute-start.3 = (f32[224,64]{1,0:T(8,128)S(1)}, f32[224,64]{1,0:T(8,128)S(1)}, u32[]{:S(2)}, u32[]{:S(2)}) collective-permute-start(f32[224,64]{1,0:T(8,128)S(1)} %get-tuple-element.26), channel_id=1, source_target_pairs={{0,0},{1,2},{2,1},{3,4},{4,3},{5,6},{6,5},{7,7},{8,8},{9,10},{10,9... | collective-permute-start | bytes 172040 | tf_op jit(solution)/shard_map/ppermute | solution.py:76
  16.1 3.8 %spectra.3 = (f32[12,224,256]{2,1,0:T(8,128)S(1)}, f32[12,224,256]{2,1,0:T(8,128)S(1)}, f32[8,128]{1,0:T(8,128)}) custom-call(f32[2,12,129,129]{3,2,1,0:T(8,128)S(1)} %copy.15.kern, f32[4,256,256]{2,1,0:T(8,128)S(1)} %copy-done.4, f32[12,224,256]{2,1,0:T(8,128)S(1)} %get-tuple-element.18.rest_0_, ...), custom_call_target="tpu_custom_call", output_to_operand_aliasing={{0}: (2, {}), {1}: (3, {})} | custom-call | flops 3000000000 | bytes 1048576 | tf_op jit(solution)/shard_map/spectra/pallas_call | solution.py:349
  20.0 7.7 %field.1 = (f32[12,96,128]{2,1,0:T(8,128)S(1)}, f32[12,96,128]{2,1,0:T(8,128)S(1)}, f32[1,512]{1,0:T(1,128)S(1)}) custom-call(f32[12]{0:T(128)S(1)} %copy-done.2, f32[12,224,256]{2,1,0:T(8,128)S(1)} %get-tuple-element.22.spec_re, f32[12,224,256]{2,1,0:T(8,128)S(1)} %get-tuple-element.23.spec_im, f32[224,96]{1,0:T(8,128)S(1)} %get-tuple-element.24.column, ...), custom_call_target="tpu_custom_call" | custom-call | flops 7000000000 | bytes 1048576 | tf_op jit(solution)/shard_map/field/pallas_call | solution.py:371
  27.7 0.7 broadcast_in_dim.15
  28.4 5.1 %all-to-all-start = ((f32[32,1,512]{2,1,0:T(1,128)}), f32[32,1,512]{2,1,0:T(1,128)S(1)}, u32[]{:S(2)}, u32[]{:S(2)}) async-start(f32[32,1,512]{2,1,0:T(1,128)} %broadcast_in_dim.15), calls=%async_computation | async-start | bytes 131072 | tf_op jit(solution)/shard_map/all_to_all | solution.py:328
  34.2 5.6 %all-to-all-done = f32[32,1,512]{2,1,0:T(1,128)S(1)} async-done(((f32[32,1,512]{2,1,0:T(1,128)}), f32[32,1,512]{2,1,0:T(1,128)S(1)}, u32[]{:S(2)}, u32[]{:S(2)}) %all-to-all-start) | async-done | bytes 65568 | tf_op jit(solution)/shard_map/all_to_all | solution.py:328
  39.8 1.8 %copy-done.6 = f32[12,224,256]{2,1,0:T(8,128)S(1)} copy-done((f32[12,224,256]{2,1,0:T(8,128)S(1)}, f32[12,224,256]{2,1,0:T(8,128)}, u32[]{:S(2)}) %copy-start.6) | copy-done | bytes 2752536
  41.6 1.8 %copy-done.8 = f32[12,224,256]{2,1,0:T(8,128)S(1)} copy-done((f32[12,224,256]{2,1,0:T(8,128)S(1)}, f32[12,224,256]{2,1,0:T(8,128)}, u32[]{:S(2)}) %copy-start.8) | copy-done | bytes 2752536
  43.3 9.5 %gradient.1 = (f32[224,96]{1,0:T(8,128)S(1)}, f32[224,64]{1,0:T(8,128)S(1)}, f32[224,64]{1,0:T(8,128)S(1)}, f32[1,1]{1,0:T(1,128)}) custom-call(f32[12]{0:T(128)S(1)} %copy-done.2, f32[8]{0:T(128)S(1)} %copy-done.3, s32[1]{0:T(128)S(6)} %copy.21.pick, f32[32,512]{1,0:T(8,128)S(1)} %bitcast.5, f32[1,512]{1,0:T(1,128)S(1)} %get-tuple-element.27.sampled, ...), custom_call_target="tpu_custom_call" | custom-call | flops 8999999488 | bytes 1048576 | tf_op jit(solution)/shard_map/gradient/pallas_call | solution.py:384
  52.9 2.7 %collective-permute-start.4 = (f32[224,64]{1,0:T(8,128)S(1)}, f32[224,64]{1,0:T(8,128)S(1)}, u32[]{:S(2)}, u32[]{:S(2)}) collective-permute-start(f32[224,64]{1,0:T(8,128)S(1)} %get-tuple-element.31), channel_id=1, source_target_pairs={{0,0},{1,2},{2,1},{3,4},{4,3},{5,6},{6,5},{7,7},{8,8},{9,10},{10,9... | collective-permute-start | bytes 172040 | tf_op jit(solution)/shard_map/ppermute | solution.py:76
  55.6 0.1 collective-permute-start.5
  55.7 4.4 %collective-permute-done.4 = f32[224,64]{1,0:T(8,128)S(1)} collective-permute-done((f32[224,64]{1,0:T(8,128)S(1)}, f32[224,64]{1,0:T(8,128)S(1)}, u32[]{:S(2)}, u32[]{:S(2)}) %collective-permute-start.4) | collective-permute-done | bytes 57376 | tf_op jit(solution)/shard_map/ppermute | solution.py:76
  60.1 3.1 %collective-permute-done.5 = f32[224,64]{1,0:T(8,128)S(1)} collective-permute-done((f32[224,64]{1,0:T(8,128)S(1)}, f32[224,64]{1,0:T(8,128)S(1)}, u32[]{:S(2)}, u32[]{:S(2)}) %collective-permute-start.5) | collective-permute-done | bytes 57376 | tf_op jit(solution)/shard_map/ppermute | solution.py:76
  63.2 0.1 pad_add_fusion
  63.3 2.5 %collective-permute-start.6 = (f32[64,96]{1,0:T(8,128)S(1)}, f32[64,96]{1,0:T(8,128)S(1)}, u32[]{:S(2)}, u32[]{:S(2)}) collective-permute-start(f32[64,96]{1,0:T(8,128)S(1)} %get-tuple-element.36), channel_id=1, source_target_pairs={{0,0},{8,16},{16,8},{24,24},{1,1},{9,17},{17,9},{25,25},{2,2},{10,... | collective-permute-start | bytes 73736 | tf_op jit(solution)/shard_map/ppermute | solution.py:76
  66.0 2.6 %collective-permute-done.6 = f32[64,96]{1,0:T(8,128)S(1)} collective-permute-done((f32[64,96]{1,0:T(8,128)S(1)}, f32[64,96]{1,0:T(8,128)S(1)}, u32[]{:S(2)}, u32[]{:S(2)}) %collective-permute-start.6) | collective-permute-done | bytes 24608 | tf_op jit(solution)/shard_map/ppermute | solution.py:76
  68.6 0.6 fusion.2
  (29 shorter events, 0.2 us)
Async XLA Ops:
  1.5 10.0 %collective-permute-start = (f32[64,96]{1,0:T(8,128)S(1)}, f32[64,96]{1,0:T(8,128)S(1)}, u32[]{:S(2)}, u32[]{:S(2)}) collective-permute-start(f32[64,96]{1,0:T(8,128)S(1)} %get-tuple-element.41), channel_id=1, source_target_pairs={{0,8},{8,0},{16,24},{24,16},{1,9},{9,1},{17,25},{25,17},{2,10},{10... | collective-permute-start | bytes 73736 | tf_op jit(solution)/shard_map/ppermute | solution.py:76
  2.2 5.4 %copy-start.4 = (f32[4,256,256]{2,1,0:T(8,128)S(1)}, f32[4,256,256]{2,1,0:T(8,128)}, u32[]{:S(2)}) copy-start(f32[4,256,256]{2,1,0:T(8,128)} %constant.29.clone.tables) | copy-start | bytes 3145732
  2.2 9.2 %collective-permute-start.1 = (f32[64,96]{1,0:T(8,128)S(1)}, f32[64,96]{1,0:T(8,128)S(1)}, u32[]{:S(2)}, u32[]{:S(2)}) collective-permute-start(f32[64,96]{1,0:T(8,128)S(1)} %get-tuple-element.40), channel_id=1, source_target_pairs={{0,0},{8,16},{16,8},{24,24},{1,1},{9,17},{17,9},{25,25},{2,2},{10,... | collective-permute-start | bytes 73736 | tf_op jit(solution)/shard_map/ppermute | solution.py:76
  11.6 8.3 %collective-permute-start.2 = (f32[224,64]{1,0:T(8,128)S(1)}, f32[224,64]{1,0:T(8,128)S(1)}, u32[]{:S(2)}, u32[]{:S(2)}) collective-permute-start(f32[224,64]{1,0:T(8,128)S(1)} %get-tuple-element.25), channel_id=1, source_target_pairs={{0,1},{1,0},{2,3},{3,2},{4,5},{5,4},{6,7},{7,6},{8,9},{9,8},{10,11... | collective-permute-start | bytes 172040 | tf_op jit(solution)/shard_map/ppermute | solution.py:76
  11.9 8.0 %collective-permute-start.3 = (f32[224,64]{1,0:T(8,128)S(1)}, f32[224,64]{1,0:T(8,128)S(1)}, u32[]{:S(2)}, u32[]{:S(2)}) collective-permute-start(f32[224,64]{1,0:T(8,128)S(1)} %get-tuple-element.26), channel_id=1, source_target_pairs={{0,0},{1,2},{2,1},{3,4},{4,3},{5,6},{6,5},{7,7},{8,8},{9,10},{10,9... | collective-permute-start | bytes 172040 | tf_op jit(solution)/shard_map/ppermute | solution.py:76
  16.1 3.9 %copy-start = (f32[1,256]{1,0:T(1,128)S(1)}, f32[1,256]{1,0:T(1,128)}, u32[]{:S(2)}) copy-start(f32[1,256]{1,0:T(1,128)} %slopes.1) | copy-start | bytes 3076
  16.1 3.9 %copy-start.1 = (s32[1,256]{1,0:T(1,128)S(1)}, s32[1,256]{1,0:T(1,128)}, u32[]{:S(2)}) copy-start(s32[1,256]{1,0:T(1,128)} %pixels.3) | copy-start | bytes 3076
  16.1 3.9 %copy-start.2 = (f32[12]{0:T(128)S(1)}, f32[12]{0:T(128)}, u32[]{:S(2)}) copy-start(f32[12]{0:T(128)} %weights.3) | copy-start | bytes 148
  19.9 7.8 %copy-start.5 = (f32[12,224,256]{2,1,0:T(8,128)}, f32[12,224,256]{2,1,0:T(8,128)S(1)}, u32[]{:S(2)}) copy-start(f32[12,224,256]{2,1,0:T(8,128)S(1)} %get-tuple-element.22.spec_re) | copy-start | bytes 8257540
  19.9 7.8 %copy-start.7 = (f32[12,224,256]{2,1,0:T(8,128)}, f32[12,224,256]{2,1,0:T(8,128)S(1)}, u32[]{:S(2)}) copy-start(f32[12,224,256]{2,1,0:T(8,128)S(1)} %get-tuple-element.23.spec_im) | copy-start | bytes 8257540
  20.0 19.8 %copy-start.3 = (f32[8]{0:T(128)S(1)}, f32[8]{0:T(128)}, u32[]{:S(2)}) copy-start(f32[8]{0:T(128)} %doses.1) | copy-start | bytes 100
  28.4 11.4 %all-to-all-start = ((f32[32,1,512]{2,1,0:T(1,128)}), f32[32,1,512]{2,1,0:T(1,128)S(1)}, u32[]{:S(2)}, u32[]{:S(2)}) async-start(f32[32,1,512]{2,1,0:T(1,128)} %broadcast_in_dim.15), calls=%async_computation | async-start | bytes 131072 | tf_op jit(solution)/shard_map/all_to_all | solution.py:328
  39.8 1.8 %copy-start.6 = (f32[12,224,256]{2,1,0:T(8,128)S(1)}, f32[12,224,256]{2,1,0:T(8,128)}, u32[]{:S(2)}) copy-start(f32[12,224,256]{2,1,0:T(8,128)} %copy-done.5) | copy-start | bytes 8257540
  41.6 1.8 %copy-start.8 = (f32[12,224,256]{2,1,0:T(8,128)S(1)}, f32[12,224,256]{2,1,0:T(8,128)}, u32[]{:S(2)}) copy-start(f32[12,224,256]{2,1,0:T(8,128)} %copy-done.7) | copy-start | bytes 8257540
  43.3 25.2 %copy-start.9 = (f32[96,96]{1,0:T(8,128)S(1)}, f32[96,96]{1,0:T(8,128)}, u32[]{:S(2)}) copy-start(f32[96,96]{1,0:T(8,128)} %param.8) | copy-start | bytes 110596
  52.9 7.2 %collective-permute-start.4 = (f32[224,64]{1,0:T(8,128)S(1)}, f32[224,64]{1,0:T(8,128)S(1)}, u32[]{:S(2)}, u32[]{:S(2)}) collective-permute-start(f32[224,64]{1,0:T(8,128)S(1)} %get-tuple-element.31), channel_id=1, source_target_pairs={{0,0},{1,2},{2,1},{3,4},{4,3},{5,6},{6,5},{7,7},{8,8},{9,10},{10,9... | collective-permute-start | bytes 172040 | tf_op jit(solution)/shard_map/ppermute | solution.py:76
  55.6 7.6 %collective-permute-start.5 = (f32[224,64]{1,0:T(8,128)S(1)}, f32[224,64]{1,0:T(8,128)S(1)}, u32[]{:S(2)}, u32[]{:S(2)}) collective-permute-start(f32[224,64]{1,0:T(8,128)S(1)} %get-tuple-element.32), channel_id=1, source_target_pairs={{0,1},{1,0},{2,3},{3,2},{4,5},{5,4},{6,7},{7,6},{8,9},{9,8},{10,11... | collective-permute-start | bytes 172040 | tf_op jit(solution)/shard_map/ppermute | solution.py:76
  63.3 5.2 %collective-permute-start.6 = (f32[64,96]{1,0:T(8,128)S(1)}, f32[64,96]{1,0:T(8,128)S(1)}, u32[]{:S(2)}, u32[]{:S(2)}) collective-permute-start(f32[64,96]{1,0:T(8,128)S(1)} %get-tuple-element.36), channel_id=1, source_target_pairs={{0,0},{8,16},{16,8},{24,24},{1,1},{9,17},{17,9},{25,25},{2,2},{10,... | collective-permute-start | bytes 73736 | tf_op jit(solution)/shard_map/ppermute | solution.py:76
  65.9 2.7 %collective-permute-start.7 = (f32[64,96]{1,0:T(8,128)S(1)}, f32[64,96]{1,0:T(8,128)S(1)}, u32[]{:S(2)}, u32[]{:S(2)}) collective-permute-start(f32[64,96]{1,0:T(8,128)S(1)} %get-tuple-element.37), channel_id=1, source_target_pairs={{0,8},{8,0},{16,24},{24,16},{1,9},{9,1},{17,25},{25,17},{2,10},{10... | collective-permute-start | bytes 73736 | tf_op jit(solution)/shard_map/ppermute | solution.py:76

commit v3 on v2

--- a/solution.py
+++ b/solution.py
@@ -13,6 +13,7 @@
 RESIST_LEVEL = 0.7
 SOFTNESS = 0.25
 LANES = 128
+UNROLL = 3
 F32 = jnp.float32
 BF16 = jnp.bfloat16
 
@@ -28,6 +29,17 @@
 
 def dot3(a, b):
     return dot(a[0], b[0]) + dot(a[0], b[1]) + dot(a[1], b[0])
+
+
+def stacked(pair):
+    return jnp.concatenate(pair, axis=0)
+
+
+def dot3_stacked(a, b):
+    high, both = a
+    count = high.shape[0]
+    tall = dot(both, b[0])
+    return tall[:count] + tall[count:] + dot(high, b[1])
 
 
 def wave_tables(period):
@@ -77,50 +89,93 @@
     return out
 
 
-def spectra_kernel(start, kern, tables, *rest):
-    out_re, out_im, token, planes, sems = rest[-5:]
+def spectra_kernel(start, parts, kern, tables, *rest):
+    out_re, out_im, token = rest[-3:]
     period = out_re.shape[1]
     half = period // 2
     taps = kern.shape[-1]
-    parts = planes.shape[0]
-
-    def fetch(k):
-        return pltpu.make_async_copy(kern.at[:, start + k], planes.at[k], sems.at[k])
-
-    for k in range(parts):
-        fetch(k).start()
     cols = split(tables[0, :taps, :])
     rows = split(tables[2, :period, :taps])
+    rows = (rows[0], stacked(rows))
     token[...] = jnp.zeros(token.shape, F32)
 
     def step(k, carry):
-        fetch(k).wait()
-        real_cos, real_sin = halves(dot3(split(planes[k, 0]), cols))
-        imag_cos, imag_sin = halves(dot3(split(planes[k, 1]), cols))
+        real_cos, real_sin = halves(dot3(split(kern[0, start + k]), cols))
+        imag_cos, imag_sin = halves(dot3(split(kern[1, start + k]), cols))
         wide_re = jnp.concatenate([real_cos - imag_sin, real_cos + imag_sin], axis=1)
         wide_im = jnp.concatenate([real_sin + imag_cos, imag_cos - real_sin], axis=1)
-        tall_re = dot3(rows, split(wide_re))
-        tall_im = dot3(rows, split(wide_im))
+        tall_re = dot3_stacked(rows, split(wide_re))
+        tall_im = dot3_stacked(rows, split(wide_im))
         out_re[start + k, :half] = tall_re[:half] - tall_im[half:]
         out_re[start + k, half:] = tall_re[:half] + tall_im[half:]
         out_im[start + k, :half] = tall_im[:half] + tall_re[half:]
         out_im[start + k, half:] = tall_im[:half] - tall_re[half:]
         return carry
 
-    lax.fori_loop(0, parts, step, 0)
-
-
-def column_kernel(middle, first, second, after, column, next_first, next_second, token):
+    lax.fori_loop(0, parts, step, 0, unroll=UNROLL)
+
+
+def pack(x):
+    count = x.shape[0] // 2
+    return jnp.concatenate([x[:count], x[count:]], axis=1)
+
+
+def unpack(x):
+    width = x.shape[1] // 2
+    return jnp.concatenate([x[:, :width], x[:, width:]], axis=0)
+
+
+def start_kernel(latent, transmit, first, second):
+    tile = latent.shape[0]
+    radius = first.shape[1] // 2
+    value = 0.5 * (1.0 + jnp.tanh(latent[...]))
+    transmit[...] = value
+    first[...], second[...] = ordered(
+        "tx", pack(value[:, :radius]), pack(value[:, tile - radius :])
+    )
+
+
+def band_kernel(middle, first, second, after, band, next_first, next_second, token):
     tile = middle.shape[0]
+    radius = first.shape[1] // 2
+    left, right = sides("tx", first[...], second[...])
+    band[:, :radius] = unpack(left)
+    band[:, radius : radius + tile] = middle[...]
+    band[:, radius + tile :] = unpack(right)
+    next_first[...], next_second[...] = ordered(
+        "ty", band[:radius], band[tile - radius :]
+    )
+    token[...] = jnp.zeros(token.shape, F32)
+
+
+def join_kernel(own, other, out):
+    count = own.shape[0]
+    out[:count] = own[...]
+    out[count:] = other[...]
+
+
+def fold_kernel(grad, first, second, band, next_first, next_second):
+    tile = band.shape[0]
     radius = first.shape[0]
     above, below = sides("ty", first[...], second[...])
-    column[:radius] = above
-    column[radius : radius + tile] = middle[...]
-    column[radius + tile :] = below
+    band[...] = grad[radius : radius + tile]
+    band[:radius] += above
+    band[tile - radius :] += below
+    period = band.shape[1]
     next_first[...], next_second[...] = ordered(
-        "tx", column[:, :radius], column[:, tile - radius :]
-    )
-    token[...] = jnp.zeros(token.shape, F32)
+        "tx", pack(band[:, :radius]), pack(band[:, period - radius :])
+    )
+
+
+def finish_kernel(band, first, second, latent, steering):
+    tile = latent.shape[0]
+    radius = first.shape[1] // 2
+    left, right = sides("tx", first[...], second[...])
+    steering[...] = band[:, radius : radius + tile]
+    steering[:, :radius] += unpack(left)
+    steering[:, tile - radius :] += unpack(right)
+    value = jnp.tanh(latent[...])
+    steering[...] = steering[...] * 0.5 * (1.0 - value * value)
 
 
 def total_weight(weights, kernels):
@@ -136,19 +191,18 @@
 
 
 def field_kernel(
-    weights, spec_re, spec_im, column, first, second, pixels, slopes, tables,
+    weights, spec_re, spec_im, band, first, second, pixels, slopes, tables,
     field_re, field_im, sampled, framed, mask,
 ):
     kernels, period, _ = spec_re.shape
     half = period // 2
     tile = field_re.shape[1]
-    radius = first.shape[1]
-    left, right = sides("tx", first[...], second[...])
-    framed[:, period:] = jnp.zeros((period, 2 * LANES - period), F32)
-    framed[:, :radius] = left
-    framed[:, radius + tile : period] = right
-    framed[:, radius : radius + tile] = column[...]
-    wide = dot3(split(framed[...]), split(tables[0]))
+    radius = first.shape[0]
+    above, below = sides("ty", first[...], second[...])
+    framed[:radius] = above
+    framed[radius + tile :] = below
+    framed[radius : radius + tile] = band[...]
+    wide = dot3(split(framed[...]), split(tables[0, :period]))
     tall = dot3(split(tables[2, :period, :period]), split(wide)) * (1.0 / (period * period))
     cos_cos, cos_sin = halves(tall[:half])
     sin_cos, sin_sin = halves(tall[half:])
@@ -159,6 +213,7 @@
     mask[2, :, :LANES], mask[2, :, LANES:] = other, same
     mask[3, :, :LANES], mask[3, :, LANES:] = cross, joint
     lift = split(tables[3, :tile, :period])
+    lift = (lift[0], stacked(lift))
     across = split(tables[1, :, :LANES])
 
     def step(k, intensity):
@@ -170,17 +225,19 @@
         down_im = mask[2] * neg_im + mask[3] * neg_re
         for_re = jnp.concatenate([up_re + down_re, down_im - up_im], axis=0)
         for_im = jnp.concatenate([up_im + down_im, up_re - down_re], axis=0)
-        re_pos, re_neg = halves(dot3(lift, split(for_re)))
-        im_pos, im_neg = halves(dot3(lift, split(for_im)))
+        re_pos, re_neg = halves(dot3_stacked(lift, split(for_re)))
+        im_pos, im_neg = halves(dot3_stacked(lift, split(for_im)))
         rows_re = jnp.concatenate([re_pos + re_neg, im_neg - im_pos], axis=1)
         rows_im = jnp.concatenate([im_pos + im_neg, re_pos - re_neg], axis=1)
-        real = dot3(split(rows_re), across)
-        imag = dot3(split(rows_im), across)
+        both = dot3(split(stacked((rows_re, rows_im))), across)
+        real, imag = both[:tile], both[tile:]
         field_re[k] = real
         field_im[k] = imag
         return intensity + weights[k] * (real * real + imag * imag)
 
-    intensity = lax.fori_loop(0, kernels, step, jnp.zeros((tile, LANES), F32))
+    intensity = lax.fori_loop(
+        0, kernels, step, jnp.zeros((tile, LANES), F32), unroll=UNROLL
+    )
     intensity = intensity / total_weight(weights, kernels)
     samples = pixels.shape[1]
     row, col = sample_places(pixels[...], tile)
@@ -206,7 +263,7 @@
 
 def gradient_kernel(
     weights, doses, pick, gathered, sampled, pixels, spec_re, spec_im, field_re, field_im,
-    tables, middle, first, second, tail, total_re, total_im,
+    tables, grad, first, second, tail, total_re, total_im,
 ):
     kernels, period, _ = spec_re.shape
     half = period // 2
@@ -219,7 +276,8 @@
     everyone, every_slope = gathered[:, :samples], gathered[:, samples:]
     pick_corner = pick[0] // per_corner
     remain = pick[0] - pick_corner * per_corner
-    place = lax.broadcasted_iota(jnp.int32, (devices, samples), 0) * samples
+    me = lax.axis_index("ty") * lax.axis_size("tx") + lax.axis_index("tx")
+    place = (lax.broadcasted_iota(jnp.int32, (devices, samples), 0) ^ me) * samples
     place = place + lax.broadcasted_iota(jnp.int32, (devices, samples), 1)
     _, _, picked = errors(everyone, every_slope, doses[pick_corner])
     threshold = jnp.sum(jnp.where(place == remain, picked, 0.0), keepdims=True)
@@ -230,7 +288,9 @@
         return sums[0] + soft, sums[1] + error * soft
 
     zero = jnp.zeros((devices, samples), F32)
-    soft_sum, error_sum = lax.fori_loop(0, corners, corner, (zero, zero))
+    soft_sum, error_sum = lax.fori_loop(
+        0, corners, corner, (zero, zero), unroll=4 if devices <= 32 else 1
+    )
     soft_total = jnp.sum(soft_sum, keepdims=True)
     tail_mean = jnp.sum(error_sum, keepdims=True) / soft_total
     tail[...] = tail_mean
@@ -263,17 +323,20 @@
 
     cols = split(tables[0, :LANES])
     rows = split(tables[2, :period, :tile])
+    rows = (rows[0], stacked(rows))
     total_re[...] = jnp.zeros((period, 2 * LANES), F32)
     total_im[...] = jnp.zeros((period, 2 * LANES), F32)
 
     def step(k, carry):
         weighted = grid * weights[k]
-        real_cos, real_sin = halves(dot3(split(weighted * field_re[k]), cols))
-        imag_cos, imag_sin = halves(dot3(split(weighted * field_im[k]), cols))
+        source = stacked((weighted * field_re[k], weighted * field_im[k]))
+        both = dot3(split(source), cols)
+        real_cos, real_sin = halves(both[:tile])
+        imag_cos, imag_sin = halves(both[tile:])
         wide_re = jnp.concatenate([real_cos + imag_sin, real_cos - imag_sin], axis=1)
         wide_im = jnp.concatenate([imag_cos - real_sin, imag_cos + real_sin], axis=1)
-        tall_re = dot3(rows, split(wide_re))
-        tall_im = dot3(rows, split(wide_im))
+        tall_re = dot3_stacked(rows, split(wide_re))
+        tall_im = dot3_stacked(rows, split(wide_im))
         for start, sign in ((0, 1.0), (half, -1.0)):
             part = slice(start, start + half)
             wave_re = tall_re[:half] + sign * tall_im[half:]
@@ -283,7 +346,7 @@
             total_im[part] += own_re * wave_im - own_im * wave_re
         return carry
 
-    lax.fori_loop(0, kernels, step, 0)
+    lax.fori_loop(0, kernels, step, 0, unroll=UNROLL)
     pos_re, neg_re = total_re[:half], total_re[half:]
     pos_im, neg_im = total_im[:half], total_im[half:]
     back_rows = split(tables[3, :period, :period])
@@ -292,9 +355,9 @@
     re_pos, re_neg = halves(dot3(back_rows, split(for_re)))
     im_pos, im_neg = halves(dot3(back_rows, split(for_im)))
     last = jnp.concatenate([re_pos + re_neg, im_neg - im_pos], axis=1)
-    grad = dot3(split(last), split(tables[1])) * (2.0 / (period * period))
-    middle[...] = grad[:, radius : radius + tile]
-    first[...], second[...] = ordered("tx", grad[:, :radius], grad[:, radius + tile : period])
+    framed = dot3(split(last), split(tables[1, :, :period])) * (2.0 / (period * period))
+    grad[...] = framed
+    first[...], second[...] = ordered("ty", framed[:radius], framed[radius + tile :])
 
 
 VMEM = pl.BlockSpec(memory_space=pltpu.VMEM)
@@ -324,8 +387,13 @@
 
 def gather_all(x):
     count = lax.axis_size("ty") * lax.axis_size("tx")
-    copies = jnp.broadcast_to(x, (count, x.shape[1]))
-    return lax.all_to_all(copies, ("ty", "tx"), 0, 0, tiled=True)
+    step = 1
+    while step < count:
+        other = lax.ppermute(x, ("ty", "tx"), [(i, i ^ step) for i in range(count)])
+        joined = [shape(2 * step, x.shape[1])]
+        (x,) = call(join_kernel, "join", joined, [VMEM] * 2)(x, other)
+        step *= 2
+    return x
 
 
 def body(latent, kernels, socs_weights, dose_scale, inv_slope, edge_pixels, threshold_pick):
@@ -337,9 +405,13 @@
     half = period // 2
     tables = jnp.asarray(wave_tables(period))
     token = shape(8, LANES)
-
-    transmit = 0.5 * (1.0 + jnp.tanh(latent))
-    rims = exchange("ty", *ordered("ty", transmit[:radius], transmit[tile - radius :]))
+    packed = [shape(tile // 2, 2 * radius)] * 2
+    rim = [shape(radius, period)] * 2
+
+    transmit, *rims = call(
+        start_kernel, "start", [shape(tile, tile)] + packed, [VMEM]
+    )(latent)
+    rims = exchange("tx", *rims)
 
     parts = count // 2
     spec = []
@@ -347,26 +419,22 @@
     for part in range(2):
         given = spec + after
         *spec, done = call(
-            functools.partial(spectra_kernel, part * parts),
+            functools.partial(spectra_kernel, part * parts, parts),
             "spectra",
             [shape(count, period, 2 * LANES)] * 2 + [token],
-            [ANY, VMEM] + [ANY] * len(given),
-            scratch=[
-                pltpu.VMEM((parts, 2, taps, taps), F32),
-                pltpu.SemaphoreType.DMA((parts,)),
-            ],
+            [VMEM] * 2 + [ANY] * len(given),
             aliases={2: 0, 3: 1} if spec else None,
             micros=3,
         )(kernels, tables, *given)
         if part == 0:
-            column, *rims, done = call(
-                column_kernel,
-                "column",
-                [shape(period, tile)] + [shape(period, radius)] * 2 + [token],
+            band, *rims, done = call(
+                band_kernel,
+                "band",
+                [shape(tile, period)] + rim + [token],
                 [VMEM] * 3 + [ANY],
             )(transmit, *rims, done)
             after = [done]
-            rims = exchange("tx", *rims)
+            rims = exchange("ty", *rims)
 
     field_re, field_im, sampled = call(
         field_kernel,
@@ -374,17 +442,17 @@
         [shape(count, tile, LANES)] * 2 + [shape(1, 2 * samples)],
         [SMEM] + [VMEM] * 8,
         scratch=[
-            pltpu.VMEM((period, 2 * LANES), F32),
+            pltpu.VMEM((period, period), F32),
             pltpu.VMEM((4, half, 2 * LANES), F32),
         ],
         micros=7,
-    )(socs_weights, *spec, column, *rims, edge_pixels, inv_slope, tables)
+    )(socs_weights, *spec, band, *rims, edge_pixels, inv_slope, tables)
 
     gathered = gather_all(sampled)
-    grad_middle, first, second, tail_mean = call(
+    grad, *rims, tail_mean = call(
         gradient_kernel,
         "gradient",
-        [shape(period, tile)] + [shape(period, radius)] * 2 + [shape(1, 1)],
+        [shape(period, period)] + rim + [shape(1, 1)],
         [SMEM] * 3 + [VMEM] * 8,
         scratch=[pltpu.VMEM((period, 2 * LANES), F32)] * 2,
         micros=9,
@@ -393,22 +461,14 @@
         *spec, field_re, field_im, tables,
     )
 
-    rest = tile - radius
-    from_left, from_right = sides("tx", *exchange("tx", first, second))
-    column = (
-        grad_middle
-        + jnp.pad(from_left, ((0, 0), (0, rest)))
-        + jnp.pad(from_right, ((0, 0), (rest, 0)))
-    )
-    rims = exchange("ty", *ordered("ty", column[:radius], column[radius + tile :]))
-    from_above, from_below = sides("ty", *rims)
-    mask_grad = (
-        column[radius : radius + tile]
-        + jnp.pad(from_above, ((0, rest), (0, 0)))
-        + jnp.pad(from_below, ((rest, 0), (0, 0)))
-    )
-    tanh_value = jnp.tanh(latent)
-    steering = mask_grad * 0.5 * (1.0 - tanh_value * tanh_value)
+    rims = exchange("ty", *rims)
+    band, *rims = call(
+        fold_kernel, "fold", [shape(tile, period)] + packed, [VMEM] * 3
+    )(grad, *rims)
+    rims = exchange("tx", *rims)
+    (steering,) = call(
+        finish_kernel, "finish", [shape(tile, tile)], [VMEM] * 4
+    )(band, *rims, latent)
     return (steering, tail_mean.reshape(1))
 
 

time: 69.6 us -> 62.4 us (0.90)
  the two profiles are of different devices: /device:TPU:5 before, /device:TPU:18 now
where the time goes in v3:
time: 62.4 us; the launch traced here: 62.1 us
  waiting for transfers between devices  22 us (35%)
  Pallas kernels  21.6 us (35%)
  starting transfers between devices  15.9 us (25%)
  between operations  1.48 us (2%)
  local copies, waits for them, and re-layouts  1.17 us (2%)
    ppermute x5, waiting for transfers between devices, gather_all(): other = lax.ppermute(x, ('ty', 'tx'), [(i, i ^ step) for i in range(count)])  12.9 us
    ppermute x8, starting transfers between devices, exchange(): out.append(lax.ppermute(value, axis, pairs))  12.6 us
    ppermute x8, waiting for transfers between devices, exchange(): out.append(lax.ppermute(value, axis, pairs))  9.1 us
    pallas_call x1, Pallas kernels, body(): call(gradient_kernel, 'gradient', [shape(period, period)] + rim + [shape(...  8.62 us
    pallas_call x1, Pallas kernels, body(): call(field_kernel, 'field', [shape(count, tile, LANES)] * 2 + [shape(1, 2...  5.93 us
    pallas_call x2, Pallas kernels, body(): call(functools.partial(spectra_kernel, part * parts, parts), 'spectra', [...  5.86 us
    ppermute x5, starting transfers between devices, gather_all(): other = lax.ppermute(x, ('ty', 'tx'), [(i, i ^ step) for i in range(count)])  3.33 us
  transfers between devices with their start and end apart: 13, of which 9 were waited for; matrix products, arithmetic and copies ran while one was open for 1% of the time, Pallas kernels for 9%

profile of v3, /device:TPU:18, one launch (start us, length us, event | category | flops | bytes accessed | tf_op | source)
XLA Modules:
  0.0 62.1 jit_solution(726318801121618488)
XLA Ops:
  0.6 0.8 %copy-done = f32[96,96]{1,0:T(8,128)S(1)} copy-done((f32[96,96]{1,0:T(8,128)S(1)}, f32[96,96]{1,0:T(8,128)}, u32[]{:S(2)}) %copy-start) | copy-done | bytes 36888
  1.5 1.6 %collective-permute-start = (f32[48,128]{1,0:T(8,128)S(1)}, f32[48,128]{1,0:T(8,128)S(1)}, u32[]{:S(2)}, u32[]{:S(2)}) collective-permute-start(f32[48,128]{1,0:T(8,128)S(1)} %get-tuple-element.27), channel_id=1, source_target_pairs={{0,1},{1,0},{2,3},{3,2},{4,5},{5,4},{6,7},{7,6},{8,9},{9,8},{10,11... | collective-permute-start | bytes 73736 | tf_op jit(solution)/shard_map/ppermute | solution.py:88
  3.1 2.4 %collective-permute-start.1 = (f32[48,128]{1,0:T(8,128)S(1)}, f32[48,128]{1,0:T(8,128)S(1)}, u32[]{:S(2)}, u32[]{:S(2)}) collective-permute-start(f32[48,128]{1,0:T(8,128)S(1)} %get-tuple-element.28), channel_id=1, source_target_pairs={{0,0},{1,2},{2,1},{3,4},{4,3},{5,6},{6,5},{7,7},{8,8},{9,10},{10,9... | collective-permute-start | bytes 73736 | tf_op jit(solution)/shard_map/ppermute | solution.py:88
  5.6 0.3 copy.13.kern
  5.9 2.9 %spectra.2 = (f32[12,224,256]{2,1,0:T(8,128)S(1)}, f32[12,224,256]{2,1,0:T(8,128)S(1)}, f32[8,128]{1,0:T(8,128)S(1)}) custom-call(f32[2,12,129,129]{3,2,1,0:T(8,128)S(1)} %copy.13.kern, f32[4,256,256]{2,1,0:T(8,128)S(1)} %copy-done.6), custom_call_target="tpu_custom_call" | custom-call | flops 3000000000 | bytes 1048576 | tf_op jit(solution)/shard_map/spectra/pallas_call | solution.py:421
  8.9 1.0 %collective-permute-done.1.second = f32[48,128]{1,0:T(8,128)S(1)} collective-permute-done((f32[48,128]{1,0:T(8,128)S(1)}, f32[48,128]{1,0:T(8,128)S(1)}, u32[]{:S(2)}, u32[]{:S(2)}) %collective-permute-start.1) | collective-permute-done | bytes 24608 | tf_op jit(solution)/shard_map/ppermute | solution.py:88
  9.9 0.1 band.1
  10.1 2.5 %collective-permute-start.3 = (f32[64,224]{1,0:T(8,128)S(1)}, f32[64,224]{1,0:T(8,128)S(1)}, u32[]{:S(2)}, u32[]{:S(2)}) collective-permute-start(f32[64,224]{1,0:T(8,128)S(1)} %get-tuple-element.35), channel_id=1, source_target_pairs={{0,0},{8,16},{16,8},{24,24},{1,1},{9,17},{17,9},{25,25},{2,2},{10,... | collective-permute-start | bytes 172040 | tf_op jit(solution)/shard_map/ppermute | solution.py:88
  12.7 2.9 %spectra.3 = (f32[12,224,256]{2,1,0:T(8,128)S(1)}, f32[12,224,256]{2,1,0:T(8,128)S(1)}, f32[8,128]{1,0:T(8,128)}) custom-call(f32[2,12,129,129]{3,2,1,0:T(8,128)S(1)} %copy.13.kern, f32[4,256,256]{2,1,0:T(8,128)S(1)} %copy-done.6, f32[12,224,256]{2,1,0:T(8,128)S(1)} %get-tuple-element.24.rest_0_, ...), custom_call_target="tpu_custom_call", output_to_operand_aliasing={{0}: (2, {}), {1}: (3, {})} | custom-call | flops 3000000000 | bytes 1048576 | tf_op jit(solution)/shard_map/spectra/pallas_call | solution.py:421
  15.7 5.9 %field.1 = (f32[12,96,128]{2,1,0:T(8,128)S(1)}, f32[12,96,128]{2,1,0:T(8,128)S(1)}, f32[1,512]{1,0:T(1,128)S(1)}) custom-call(f32[12]{0:T(128)S(1)} %copy-done.4, f32[12,224,256]{2,1,0:T(8,128)S(1)} %get-tuple-element.31.spec_re, f32[12,224,256]{2,1,0:T(8,128)S(1)} %get-tuple-element.32.spec_im, f32[96,224]{1,0:T(8,128)S(1)} %get-tuple-element.33.band, ...), custom_call_target="tpu_custom_call" | custom-call | flops 7000000000 | bytes 1048576 | tf_op jit(solution)/shard_map/field/pallas_call | solution.py:439
  21.6 1.7 %collective-permute-start.4 = (f32[1,512]{1,0:T(1,128)S(1)}, f32[1,512]{1,0:T(1,128)S(1)}, u32[]{:S(2)}, u32[]{:S(2)}) collective-permute-start(f32[1,512]{1,0:T(1,128)S(1)} %get-tuple-element.36.own.sampled), channel_id=1, source_target_pairs={{0,1},{1,0},{2,3},{3,2},{4,5},{5,4},{6,7},{7,6},{8,9},{9,8},{10,11... | collective-permute-start | bytes 6152 | tf_op jit(solution)/shard_map/ppermute | solution.py:392
  23.4 1.9 %collective-permute-done.4.other = f32[1,512]{1,0:T(1,128)S(1)} collective-permute-done((f32[1,512]{1,0:T(1,128)S(1)}, f32[1,512]{1,0:T(1,128)S(1)}, u32[]{:S(2)}, u32[]{:S(2)}) %collective-permute-start.4) | collective-permute-done | bytes 2080 | tf_op jit(solution)/shard_map/ppermute | solution.py:392
  25.3 1.6 %collective-permute-start.5 = (f32[2,512]{1,0:T(2,128)S(1)}, f32[2,512]{1,0:T(2,128)S(1)}, u32[]{:S(2)}, u32[]{:S(2)}) collective-permute-start(f32[2,512]{1,0:T(2,128)S(1)} %join.5.own), channel_id=1, source_target_pairs={{0,2},{1,3},{2,0},{3,1},{4,6},{5,7},{6,4},{7,5},{8,10},{9,11},{10,... | collective-permute-start | bytes 12296 | tf_op jit(solution)/shard_map/ppermute | solution.py:392
  26.8 2.0 %collective-permute-done.5.other = f32[2,512]{1,0:T(2,128)S(1)} collective-permute-done((f32[2,512]{1,0:T(2,128)S(1)}, f32[2,512]{1,0:T(2,128)S(1)}, u32[]{:S(2)}, u32[]{:S(2)}) %collective-permute-start.5) | collective-permute-done | bytes 4128 | tf_op jit(solution)/shard_map/ppermute | solution.py:392
  28.9 4.5 %collective-permute-done.6.other = f32[4,512]{1,0:T(4,128)S(1)} collective-permute-done((f32[4,512]{1,0:T(4,128)S(1)}, f32[4,512]{1,0:T(4,128)S(1)}, u32[]{:S(2)}, u32[]{:S(2)}) %collective-permute-start.6) | collective-permute-done | bytes 8224 | tf_op jit(solution)/shard_map/ppermute | solution.py:392
  33.4 1.2 %collective-permute-done.7.other = f32[8,512]{1,0:T(8,128)S(1)} collective-permute-done((f32[8,512]{1,0:T(8,128)S(1)}, f32[8,512]{1,0:T(8,128)S(1)}, u32[]{:S(2)}, u32[]{:S(2)}) %collective-permute-start.7) | collective-permute-done | bytes 16416 | tf_op jit(solution)/shard_map/ppermute | solution.py:392
  35.3 3.2 %collective-permute-done.8.other = f32[16,512]{1,0:T(8,128)S(1)} collective-permute-done((f32[16,512]{1,0:T(8,128)S(1)}, f32[16,512]{1,0:T(8,128)S(1)}, u32[]{:S(2)}, u32[]{:S(2)}) %collective-permute-start.8) | collective-permute-done | bytes 32800 | tf_op jit(solution)/shard_map/ppermute | solution.py:392
  38.5 8.6 %gradient.1 = (f32[224,224]{1,0:T(8,128)S(1)}, f32[64,224]{1,0:T(8,128)S(1)}, f32[64,224]{1,0:T(8,128)S(1)}, f32[1,1]{1,0:T(1,128)}) custom-call(f32[12]{0:T(128)S(1)} %copy-done.4, f32[8]{0:T(128)S(1)} %copy-done.5, s32[1]{0:T(128)S(6)} %copy.16.pick, f32[32,512]{1,0:T(8,128)S(1)} %join.9.gathered, f32[1,512]{1,0:T(1,128)S(1)} %get-tuple-element.36.own.sampled, ...), custom_call_target="tpu_custom_call" | custom-call | flops 8999999488 | bytes 1048576 | tf_op jit(solution)/shard_map/gradient/pallas_call | solution.py:452
  47.2 2.0 %collective-permute-start.10 = (f32[64,224]{1,0:T(8,128)S(1)}, f32[64,224]{1,0:T(8,128)S(1)}, u32[]{:S(2)}, u32[]{:S(2)}) collective-permute-start(f32[64,224]{1,0:T(8,128)S(1)} %get-tuple-element.41), channel_id=1, source_target_pairs={{0,0},{8,16},{16,8},{24,24},{1,1},{9,17},{17,9},{25,25},{2,2},{10,... | collective-permute-start | bytes 172040 | tf_op jit(solution)/shard_map/ppermute | solution.py:88
  49.3 3.6 %collective-permute-done.10.second = f32[64,224]{1,0:T(8,128)S(1)} collective-permute-done((f32[64,224]{1,0:T(8,128)S(1)}, f32[64,224]{1,0:T(8,128)S(1)}, u32[]{:S(2)}, u32[]{:S(2)}) %collective-permute-start.10) | collective-permute-done | bytes 57376 | tf_op jit(solution)/shard_map/ppermute | solution.py:88
  53.0 1.7 %collective-permute-start.11 = (f32[48,128]{1,0:T(8,128)S(1)}, f32[48,128]{1,0:T(8,128)S(1)}, u32[]{:S(2)}, u32[]{:S(2)}) collective-permute-start(f32[48,128]{1,0:T(8,128)S(1)} %get-tuple-element.43), channel_id=1, source_target_pairs={{0,1},{1,0},{2,3},{3,2},{4,5},{5,4},{6,7},{7,6},{8,9},{9,8},{10,11... | collective-permute-start | bytes 73736 | tf_op jit(solution)/shard_map/ppermute | solution.py:88
  54.7 2.1 %collective-permute-start.12 = (f32[48,128]{1,0:T(8,128)S(1)}, f32[48,128]{1,0:T(8,128)S(1)}, u32[]{:S(2)}, u32[]{:S(2)}) collective-permute-start(f32[48,128]{1,0:T(8,128)S(1)} %get-tuple-element.44), channel_id=1, source_target_pairs={{0,0},{1,2},{2,1},{3,4},{4,3},{5,6},{6,5},{7,7},{8,8},{9,10},{10,9... | collective-permute-start | bytes 73736 | tf_op jit(solution)/shard_map/ppermute | solution.py:88
  56.9 4.5 %collective-permute-done.12.second = f32[48,128]{1,0:T(8,128)S(1)} collective-permute-done((f32[48,128]{1,0:T(8,128)S(1)}, f32[48,128]{1,0:T(8,128)S(1)}, u32[]{:S(2)}, u32[]{:S(2)}) %collective-permute-start.12) | collective-permute-done | bytes 24608 | tf_op jit(solution)/shard_map/ppermute | solution.py:88
  61.3 0.8 %finish.1 = f32[96,96]{1,0:T(8,128)} custom-call(f32[96,224]{1,0:T(8,128)S(1)} %get-tuple-element.42.band, f32[48,128]{1,0:T(8,128)S(1)} %collective-permute-done.11.first, f32[48,128]{1,0:T(8,128)S(1)} %collective-permute-done.12.second, f32[96,96]{1,0:T(8,128)S(1)} %copy-done.1), custom_call_target="tpu_custom_call" | custom-call | flops 1000000000 | bytes 1048576 | tf_op jit(solution)/shard_map/finish/pallas_call | solution.py:469
  (32 shorter events, 0.5 us)
Async XLA Ops:
  0.6 0.8 %copy-start = (f32[96,96]{1,0:T(8,128)S(1)}, f32[96,96]{1,0:T(8,128)}, u32[]{:S(2)}) copy-start(f32[96,96]{1,0:T(8,128)} %latent.3) | copy-start | bytes 110596
  1.4 4.1 %copy-start.7 = (f32[2,12,129,129]{3,0,2,1:T(2,128)S(1)}, f32[2,12,129,129]{3,0,2,1:T(2,128)}, u32[]{:S(2)}) copy-start(f32[2,12,129,129]{3,0,2,1:T(2,128)} %param.9) | copy-start | bytes 4792612
  1.5 7.3 %collective-permute-start = (f32[48,128]{1,0:T(8,128)S(1)}, f32[48,128]{1,0:T(8,128)S(1)}, u32[]{:S(2)}, u32[]{:S(2)}) collective-permute-start(f32[48,128]{1,0:T(8,128)S(1)} %get-tuple-element.27), channel_id=1, source_target_pairs={{0,1},{1,0},{2,3},{3,2},{4,5},{5,4},{6,7},{7,6},{8,9},{9,8},{10,11... | collective-permute-start | bytes 73736 | tf_op jit(solution)/shard_map/ppermute | solution.py:88
  3.1 2.8 %copy-start.6 = (f32[4,256,256]{2,1,0:T(8,128)S(1)}, f32[4,256,256]{2,1,0:T(8,128)}, u32[]{:S(2)}) copy-start(f32[4,256,256]{2,1,0:T(8,128)} %constant.2.clone.tables) | copy-start | bytes 3145732
  3.1 6.7 %collective-permute-start.1 = (f32[48,128]{1,0:T(8,128)S(1)}, f32[48,128]{1,0:T(8,128)S(1)}, u32[]{:S(2)}, u32[]{:S(2)}) collective-permute-start(f32[48,128]{1,0:T(8,128)S(1)} %get-tuple-element.28), channel_id=1, source_target_pairs={{0,0},{1,2},{2,1},{3,4},{4,3},{5,6},{6,5},{7,7},{8,8},{9,10},{10,9... | collective-permute-start | bytes 73736 | tf_op jit(solution)/shard_map/ppermute | solution.py:88
  10.0 5.6 %collective-permute-start.2 = (f32[64,224]{1,0:T(8,128)S(1)}, f32[64,224]{1,0:T(8,128)S(1)}, u32[]{:S(2)}, u32[]{:S(2)}) collective-permute-start(f32[64,224]{1,0:T(8,128)S(1)} %get-tuple-element.34), channel_id=1, source_target_pairs={{0,8},{8,0},{16,24},{24,16},{1,9},{9,1},{17,25},{25,17},{2,10},{10... | collective-permute-start | bytes 172040 | tf_op jit(solution)/shard_map/ppermute | solution.py:88
  10.1 5.6 %collective-permute-start.3 = (f32[64,224]{1,0:T(8,128)S(1)}, f32[64,224]{1,0:T(8,128)S(1)}, u32[]{:S(2)}, u32[]{:S(2)}) collective-permute-start(f32[64,224]{1,0:T(8,128)S(1)} %get-tuple-element.35), channel_id=1, source_target_pairs={{0,0},{8,16},{16,8},{24,24},{1,1},{9,17},{17,9},{25,25},{2,2},{10,... | collective-permute-start | bytes 172040 | tf_op jit(solution)/shard_map/ppermute | solution.py:88
  12.6 3.0 %copy-start.2 = (f32[1,256]{1,0:T(1,128)S(1)}, f32[1,256]{1,0:T(1,128)}, u32[]{:S(2)}) copy-start(f32[1,256]{1,0:T(1,128)} %slopes.1) | copy-start | bytes 3076
  12.6 3.0 %copy-start.3 = (s32[1,256]{1,0:T(1,128)S(1)}, s32[1,256]{1,0:T(1,128)}, u32[]{:S(2)}) copy-start(s32[1,256]{1,0:T(1,128)} %pixels.3) | copy-start | bytes 3076
  12.6 3.0 %copy-start.4 = (f32[12]{0:T(128)S(1)}, f32[12]{0:T(128)}, u32[]{:S(2)}) copy-start(f32[12]{0:T(128)} %weights.3) | copy-start | bytes 148
  21.6 3.7 %collective-permute-start.4 = (f32[1,512]{1,0:T(1,128)S(1)}, f32[1,512]{1,0:T(1,128)S(1)}, u32[]{:S(2)}, u32[]{:S(2)}) collective-permute-start(f32[1,512]{1,0:T(1,128)S(1)} %get-tuple-element.36.own.sampled), channel_id=1, source_target_pairs={{0,1},{1,0},{2,3},{3,2},{4,5},{5,4},{6,7},{7,6},{8,9},{9,8},{10,11... | collective-permute-start | bytes 6152 | tf_op jit(solution)/shard_map/ppermute | solution.py:392
  25.3 3.6 %collective-permute-start.5 = (f32[2,512]{1,0:T(2,128)S(1)}, f32[2,512]{1,0:T(2,128)S(1)}, u32[]{:S(2)}, u32[]{:S(2)}) collective-permute-start(f32[2,512]{1,0:T(2,128)S(1)} %join.5.own), channel_id=1, source_target_pairs={{0,2},{1,3},{2,0},{3,1},{4,6},{5,7},{6,4},{7,5},{8,10},{9,11},{10,... | collective-permute-start | bytes 12296 | tf_op jit(solution)/shard_map/ppermute | solution.py:392
  28.9 4.5 %collective-permute-start.6 = (f32[4,512]{1,0:T(4,128)S(1)}, f32[4,512]{1,0:T(4,128)S(1)}, u32[]{:S(2)}, u32[]{:S(2)}) collective-permute-start(f32[4,512]{1,0:T(4,128)S(1)} %join.6.own), channel_id=1, source_target_pairs={{0,4},{1,5},{2,6},{3,7},{4,0},{5,1},{6,2},{7,3},{8,12},{9,13},{10,... | collective-permute-start | bytes 24584 | tf_op jit(solution)/shard_map/ppermute | solution.py:392
  33.4 1.2 %collective-permute-start.7 = (f32[8,512]{1,0:T(8,128)S(1)}, f32[8,512]{1,0:T(8,128)S(1)}, u32[]{:S(2)}, u32[]{:S(2)}) collective-permute-start(f32[8,512]{1,0:T(8,128)S(1)} %join.7.own), channel_id=1, source_target_pairs={{0,8},{1,9},{2,10},{3,11},{4,12},{5,13},{6,14},{7,15},{8,0},{9,1},... | collective-permute-start | bytes 49160 | tf_op jit(solution)/shard_map/ppermute | solution.py:392
  34.6 3.9 %copy-start.5 = (f32[8]{0:T(128)S(1)}, f32[8]{0:T(128)}, u32[]{:S(2)}) copy-start(f32[8]{0:T(128)} %doses.1) | copy-start | bytes 100
  34.6 3.9 %collective-permute-start.8 = (f32[16,512]{1,0:T(8,128)S(1)}, f32[16,512]{1,0:T(8,128)S(1)}, u32[]{:S(2)}, u32[]{:S(2)}) collective-permute-start(f32[16,512]{1,0:T(8,128)S(1)} %join.8.own), channel_id=1, source_target_pairs={{0,16},{1,17},{2,18},{3,19},{4,20},{5,21},{6,22},{7,23},{8,24},{9,... | collective-permute-start | bytes 98312 | tf_op jit(solution)/shard_map/ppermute | solution.py:392
  47.2 14.2 %copy-start.1 = (f32[96,96]{1,0:T(8,128)S(1)}, f32[96,96]{1,0:T(8,128)}, u32[]{:S(2)}) copy-start(f32[96,96]{1,0:T(8,128)} %latent.3) | copy-start | bytes 110596
  47.2 5.7 %collective-permute-start.10 = (f32[64,224]{1,0:T(8,128)S(1)}, f32[64,224]{1,0:T(8,128)S(1)}, u32[]{:S(2)}, u32[]{:S(2)}) collective-permute-start(f32[64,224]{1,0:T(8,128)S(1)} %get-tuple-element.41), channel_id=1, source_target_pairs={{0,0},{8,16},{16,8},{24,24},{1,1},{9,17},{17,9},{25,25},{2,2},{10,... | collective-permute-start | bytes 172040 | tf_op jit(solution)/shard_map/ppermute | solution.py:88
  49.2 3.7 %collective-permute-start.9 = (f32[64,224]{1,0:T(8,128)S(1)}, f32[64,224]{1,0:T(8,128)S(1)}, u32[]{:S(2)}, u32[]{:S(2)}) collective-permute-start(f32[64,224]{1,0:T(8,128)S(1)} %get-tuple-element.40), channel_id=1, source_target_pairs={{0,8},{8,0},{16,24},{24,16},{1,9},{9,1},{17,25},{25,17},{2,10},{10... | collective-permute-start | bytes 172040 | tf_op jit(solution)/shard_map/ppermute | solution.py:88
  53.0 3.9 %collective-permute-start.11 = (f32[48,128]{1,0:T(8,128)S(1)}, f32[48,128]{1,0:T(8,128)S(1)}, u32[]{:S(2)}, u32[]{:S(2)}) collective-permute-start(f32[48,128]{1,0:T(8,128)S(1)} %get-tuple-element.43), channel_id=1, source_target_pairs={{0,1},{1,0},{2,3},{3,2},{4,5},{5,4},{6,7},{7,6},{8,9},{9,8},{10,11... | collective-permute-start | bytes 73736 | tf_op jit(solution)/shard_map/ppermute | solution.py:88
  54.7 6.6 %collective-permute-start.12 = (f32[48,128]{1,0:T(8,128)S(1)}, f32[48,128]{1,0:T(8,128)S(1)}, u32[]{:S(2)}, u32[]{:S(2)}) collective-permute-start(f32[48,128]{1,0:T(8,128)S(1)} %get-tuple-element.44), channel_id=1, source_target_pairs={{0,0},{1,2},{2,1},{3,4},{4,3},{5,6},{6,5},{7,7},{8,8},{9,10},{10,9... | collective-permute-start | bytes 73736 | tf_op jit(solution)/shard_map/ppermute | solution.py:88

commit v4 on v3

--- a/solution.py
+++ b/solution.py
@@ -148,10 +148,9 @@
     token[...] = jnp.zeros(token.shape, F32)
 
 
-def join_kernel(own, other, out):
-    count = own.shape[0]
-    out[:count] = own[...]
-    out[count:] = other[...]
+def repeat_kernel(rows, out):
+    for r in range(rows.shape[0]):
+        out[:, r] = jnp.broadcast_to(rows[r], (out.shape[0], out.shape[2]))
 
 
 def fold_kernel(grad, first, second, band, next_first, next_second):
@@ -192,7 +191,7 @@
 
 def field_kernel(
     weights, spec_re, spec_im, band, first, second, pixels, slopes, tables,
-    field_re, field_im, sampled, framed, mask,
+    field_re, field_im, sampled, copies, framed, mask,
 ):
     kernels, period, _ = spec_re.shape
     half = period // 2
@@ -247,8 +246,9 @@
     low = intensity - high.astype(F32) - rest.astype(F32)
     picked = dot(high, one_hot) + dot(rest, one_hot) + dot(low.astype(BF16), one_hot)
     in_row = lax.broadcasted_iota(jnp.int32, (tile, samples), 0) == row
-    sampled[:, :samples] = jnp.sum(jnp.where(in_row, picked, 0.0), axis=0, keepdims=True)
-    sampled[:, samples:] = slopes[...]
+    own = jnp.sum(jnp.where(in_row, picked, 0.0), axis=0, keepdims=True)
+    sampled[...] = jnp.concatenate([own, slopes[...]], axis=1)
+    copies[...] = jnp.broadcast_to(sampled[...][None], copies.shape)
 
 
 def sigmoid(x):
@@ -270,14 +270,15 @@
     tile = field_re.shape[1]
     radius = (period - tile) // 2
     samples = pixels.shape[1]
-    devices = gathered.shape[0]
+    groups, members, _ = gathered.shape
+    devices = groups * members
     corners = doses.shape[0]
     per_corner = devices * samples
-    everyone, every_slope = gathered[:, :samples], gathered[:, samples:]
+    rows = gathered[...].reshape(devices, 2 * samples)
+    everyone, every_slope = rows[:, :samples], rows[:, samples:]
     pick_corner = pick[0] // per_corner
     remain = pick[0] - pick_corner * per_corner
-    me = lax.axis_index("ty") * lax.axis_size("tx") + lax.axis_index("tx")
-    place = (lax.broadcasted_iota(jnp.int32, (devices, samples), 0) ^ me) * samples
+    place = lax.broadcasted_iota(jnp.int32, (devices, samples), 0) * samples
     place = place + lax.broadcasted_iota(jnp.int32, (devices, samples), 1)
     _, _, picked = errors(everyone, every_slope, doses[pick_corner])
     threshold = jnp.sum(jnp.where(place == remain, picked, 0.0), keepdims=True)
@@ -385,15 +386,11 @@
     )
 
 
-def gather_all(x):
-    count = lax.axis_size("ty") * lax.axis_size("tx")
-    step = 1
-    while step < count:
-        other = lax.ppermute(x, ("ty", "tx"), [(i, i ^ step) for i in range(count)])
-        joined = [shape(2 * step, x.shape[1])]
-        (x,) = call(join_kernel, "join", joined, [VMEM] * 2)(x, other)
-        step *= 2
-    return x
+def gather_all(copies):
+    group = lax.all_to_all(copies, "tx", 0, 0, tiled=True)
+    repeated = [shape(lax.axis_size("ty"), group.shape[0], group.shape[2])]
+    (groups,) = call(repeat_kernel, "repeat", repeated, [VMEM])(group)
+    return lax.all_to_all(groups, "ty", 0, 0, tiled=True)
 
 
 def body(latent, kernels, socs_weights, dose_scale, inv_slope, edge_pixels, threshold_pick):
@@ -436,10 +433,12 @@
             after = [done]
             rims = exchange("ty", *rims)
 
-    field_re, field_im, sampled = call(
+    across = lax.axis_size("tx")
+    field_re, field_im, sampled, copies = call(
         field_kernel,
         "field",
-        [shape(count, tile, LANES)] * 2 + [shape(1, 2 * samples)],
+        [shape(count, tile, LANES)] * 2
+        + [shape(1, 2 * samples), shape(across, 1, 2 * samples)],
         [SMEM] + [VMEM] * 8,
         scratch=[
             pltpu.VMEM((period, period), F32),
@@ -448,7 +447,7 @@
         micros=7,
     )(socs_weights, *spec, band, *rims, edge_pixels, inv_slope, tables)
 
-    gathered = gather_all(sampled)
+    gathered = gather_all(copies)
     grad, *rims, tail_mean = call(
         gradient_kernel,
         "gradient",

time: 62.4 us -> 66.1 us (1.059)
  the two profiles are of different devices: /device:TPU:18 before, /device:TPU:5 now
where the time goes in v4:
time: 66.1 us; the launch traced here: 65.6 us
  Pallas kernels  22.2 us (34%)
  starting transfers between devices  18.9 us (29%)
  waiting for transfers between devices  9.51 us (14%)
  blocking collectives  8.77 us (13%)
  local copies, waits for them, and re-layouts  4.74 us (7%)
  between operations  1.54 us (2%)
    ppermute x8, starting transfers between devices, exchange(): out.append(lax.ppermute(value, axis, pairs))  15.1 us
    all_to_all x1, blocking collectives, gather_all(): group = lax.all_to_all(copies, 'tx', 0, 0, tiled=True)  8.77 us
    pallas_call x1, Pallas kernels, body(): call(gradient_kernel, 'gradient', [shape(period, period)] + rim + [shape(...  8.53 us
    ppermute x8, waiting for transfers between devices, exchange(): out.append(lax.ppermute(value, axis, pairs))  6.9 us
    pallas_call x1, Pallas kernels, body(): call(field_kernel, 'field', [shape(count, tile, LANES)] * 2 + [shape(1, 2...  6.06 us
    pallas_call x2, Pallas kernels, body(): call(functools.partial(spectra_kernel, part * parts, parts), 'spectra', [...  5.86 us
    unnamed x25, local copies, waits for them, and re-layouts  4.74 us
    all_to_all x1, starting transfers between devices, gather_all(): return lax.all_to_all(groups, 'ty', 0, 0, tiled=True)  3.72 us
  transfers between devices with their start and end apart: 9, of which 3 were waited for; matrix products, arithmetic and copies ran while one was open for 1% of the time, Pallas kernels for 9%

profile of v4, /device:TPU:5, one launch (start us, length us, event | category | flops | bytes accessed | tf_op | source)
XLA Modules:
  0.0 65.6 jit_solution(13574260927521870891)
XLA Ops:
  0.6 0.8 %copy-done = f32[96,96]{1,0:T(8,128)S(1)} copy-done((f32[96,96]{1,0:T(8,128)S(1)}, f32[96,96]{1,0:T(8,128)}, u32[]{:S(2)}) %copy-start) | copy-done | bytes 36888
  1.6 4.5 %collective-permute-start.1 = (f32[48,128]{1,0:T(8,128)S(1)}, f32[48,128]{1,0:T(8,128)S(1)}, u32[]{:S(2)}, u32[]{:S(2)}) collective-permute-start(f32[48,128]{1,0:T(8,128)S(1)} %get-tuple-element.29), channel_id=1, source_target_pairs={{0,0},{1,2},{2,1},{3,4},{4,3},{5,6},{6,5},{7,7},{8,8},{9,10},{10,9... | collective-permute-start | bytes 73736 | tf_op jit(solution)/shard_map/ppermute | solution.py:88
  6.1 0.3 copy.13.kern
  6.5 2.9 %spectra.2 = (f32[12,224,256]{2,1,0:T(8,128)S(1)}, f32[12,224,256]{2,1,0:T(8,128)S(1)}, f32[8,128]{1,0:T(8,128)S(1)}) custom-call(f32[2,12,129,129]{3,2,1,0:T(8,128)S(1)} %copy.13.kern, f32[4,256,256]{2,1,0:T(8,128)S(1)} %copy-done.6), custom_call_target="tpu_custom_call" | custom-call | flops 3000000000 | bytes 1048576 | tf_op jit(solution)/shard_map/spectra/pallas_call | solution.py:418
  9.4 0.2 band.1
  9.6 1.3 %collective-permute-start.2 = (f32[64,224]{1,0:T(8,128)S(1)}, f32[64,224]{1,0:T(8,128)S(1)}, u32[]{:S(2)}, u32[]{:S(2)}) collective-permute-start(f32[64,224]{1,0:T(8,128)S(1)} %get-tuple-element.35), channel_id=1, source_target_pairs={{0,8},{8,0},{16,24},{24,16},{1,9},{9,1},{17,25},{25,17},{2,10},{10... | collective-permute-start | bytes 172040 | tf_op jit(solution)/shard_map/ppermute | solution.py:88
  10.9 3.0 %collective-permute-start.3 = (f32[64,224]{1,0:T(8,128)S(1)}, f32[64,224]{1,0:T(8,128)S(1)}, u32[]{:S(2)}, u32[]{:S(2)}) collective-permute-start(f32[64,224]{1,0:T(8,128)S(1)} %get-tuple-element.36), channel_id=1, source_target_pairs={{0,0},{8,16},{16,8},{24,24},{1,1},{9,17},{17,9},{25,25},{2,2},{10,... | collective-permute-start | bytes 172040 | tf_op jit(solution)/shard_map/ppermute | solution.py:88
  14.0 2.9 %spectra.3 = (f32[12,224,256]{2,1,0:T(8,128)S(1)}, f32[12,224,256]{2,1,0:T(8,128)S(1)}, f32[8,128]{1,0:T(8,128)}) custom-call(f32[2,12,129,129]{3,2,1,0:T(8,128)S(1)} %copy.13.kern, f32[4,256,256]{2,1,0:T(8,128)S(1)} %copy-done.6, f32[12,224,256]{2,1,0:T(8,128)S(1)} %get-tuple-element.25.rest_0_, ...), custom_call_target="tpu_custom_call", output_to_operand_aliasing={{0}: (2, {}), {1}: (3, {})} | custom-call | flops 3000000000 | bytes 1048576 | tf_op jit(solution)/shard_map/spectra/pallas_call | solution.py:418
  17.0 6.1 %field.1 = (f32[12,96,128]{2,1,0:T(8,128)S(1)}, f32[12,96,128]{2,1,0:T(8,128)S(1)}, f32[1,512]{1,0:T(1,128)S(1)}, f32[8,1,512]{2,1,0:T(1,128)S(1)}) custom-call(f32[12]{0:T(128)S(1)} %copy-done.4, f32[12,224,256]{2,1,0:T(8,128)S(1)} %get-tuple-element.32.spec_re, f32[12,224,256]{2,1,0:T(8,128)S(1)} %get-tuple-element.33.spec_im, ...), custom_call_target="tpu_custom_call" | custom-call | flops 7000000000 | bytes 1048576 | tf_op jit(solution)/shard_map/field/pallas_call | solution.py:437
  23.1 8.8 %all_to_all.10.rows = f32[8,1,512]{2,1,0:T(1,128)S(1)} all-to-all(f32[8,1,512]{2,1,0:T(1,128)S(1)} %get-tuple-element.37), channel_id=1, replica_groups=mesh['ty'=4,'tx'=8] {'tx'}, dimensions={0} | all-to-all | bytes 32768 | tf_op jit(solution)/shard_map/all_to_all | solution.py:390
  31.8 0.6 repeat.1
  32.5 3.7 %all-to-all-start.1 = ((f32[4,8,512]{2,1,0:T(8,128)}), f32[4,8,512]{2,1,0:T(8,128)S(1)}, u32[]{:S(2)}, u32[]{:S(2)}) async-start(f32[4,8,512]{2,1,0:T(8,128)} %repeat.1), calls=%async_computation.1 | async-start | bytes 131072 | tf_op jit(solution)/shard_map/all_to_all | solution.py:393
  36.8 2.6 %all-to-all-done.1.gathered = f32[4,8,512]{2,1,0:T(8,128)S(1)} async-done(((f32[4,8,512]{2,1,0:T(8,128)}), f32[4,8,512]{2,1,0:T(8,128)S(1)}, u32[]{:S(2)}, u32[]{:S(2)}) %all-to-all-start.1) | async-done | bytes 65568 | tf_op jit(solution)/shard_map/all_to_all | solution.py:393
  39.5 1.8 %copy-done.8 = f32[12,224,256]{2,1,0:T(8,128)S(1)} copy-done((f32[12,224,256]{2,1,0:T(8,128)S(1)}, f32[12,224,256]{2,1,0:T(8,128)}, u32[]{:S(2)}) %copy-start.8) | copy-done | bytes 2752536
  41.2 1.8 %copy-done.10 = f32[12,224,256]{2,1,0:T(8,128)S(1)} copy-done((f32[12,224,256]{2,1,0:T(8,128)S(1)}, f32[12,224,256]{2,1,0:T(8,128)}, u32[]{:S(2)}) %copy-start.10) | copy-done | bytes 2752536
  43.0 8.5 %gradient.1 = (f32[224,224]{1,0:T(8,128)S(1)}, f32[64,224]{1,0:T(8,128)S(1)}, f32[64,224]{1,0:T(8,128)S(1)}, f32[1,1]{1,0:T(1,128)}) custom-call(f32[12]{0:T(128)S(1)} %copy-done.4, f32[8]{0:T(128)S(1)} %copy-done.5, s32[1]{0:T(128)S(6)} %copy.16.pick, f32[4,8,512]{2,1,0:T(8,128)S(1)} %all-to-all-done.1.gathered, f32[1,512]{1,0:T(1,128)S(1)} %get-tuple-element.38.sampled, ...), custom_call_target="tpu_custom_call" | custom-call | flops 8999999488 | bytes 1048576 | tf_op jit(solution)/shard_map/gradient/pallas_call | solution.py:451
  51.5 0.9 %collective-permute-start.4 = (f32[64,224]{1,0:T(8,128)S(1)}, f32[64,224]{1,0:T(8,128)S(1)}, u32[]{:S(2)}, u32[]{:S(2)}) collective-permute-start(f32[64,224]{1,0:T(8,128)S(1)} %get-tuple-element.42), channel_id=1, source_target_pairs={{0,8},{8,0},{16,24},{24,16},{1,9},{9,1},{17,25},{25,17},{2,10},{10... | collective-permute-start | bytes 172040 | tf_op jit(solution)/shard_map/ppermute | solution.py:88
  52.4 1.9 %collective-permute-start.5 = (f32[64,224]{1,0:T(8,128)S(1)}, f32[64,224]{1,0:T(8,128)S(1)}, u32[]{:S(2)}, u32[]{:S(2)}) collective-permute-start(f32[64,224]{1,0:T(8,128)S(1)} %get-tuple-element.43), channel_id=1, source_target_pairs={{0,0},{8,16},{16,8},{24,24},{1,1},{9,17},{17,9},{25,25},{2,2},{10,... | collective-permute-start | bytes 172040 | tf_op jit(solution)/shard_map/ppermute | solution.py:88
  54.3 3.6 %collective-permute-done.5.second = f32[64,224]{1,0:T(8,128)S(1)} collective-permute-done((f32[64,224]{1,0:T(8,128)S(1)}, f32[64,224]{1,0:T(8,128)S(1)}, u32[]{:S(2)}, u32[]{:S(2)}) %collective-permute-start.5) | collective-permute-done | bytes 57376 | tf_op jit(solution)/shard_map/ppermute | solution.py:88
  58.0 0.1 fold.1
  58.1 1.3 %collective-permute-start.6 = (f32[48,128]{1,0:T(8,128)S(1)}, f32[48,128]{1,0:T(8,128)S(1)}, u32[]{:S(2)}, u32[]{:S(2)}) collective-permute-start(f32[48,128]{1,0:T(8,128)S(1)} %get-tuple-element.45), channel_id=1, source_target_pairs={{0,1},{1,0},{2,3},{3,2},{4,5},{5,4},{6,7},{7,6},{8,9},{9,8},{10,11... | collective-permute-start | bytes 73736 | tf_op jit(solution)/shard_map/ppermute | solution.py:88
  59.4 2.2 %collective-permute-start.7 = (f32[48,128]{1,0:T(8,128)S(1)}, f32[48,128]{1,0:T(8,128)S(1)}, u32[]{:S(2)}, u32[]{:S(2)}) collective-permute-start(f32[48,128]{1,0:T(8,128)S(1)} %get-tuple-element.46), channel_id=1, source_target_pairs={{0,0},{1,2},{2,1},{3,4},{4,3},{5,6},{6,5},{7,7},{8,8},{9,10},{10,9... | collective-permute-start | bytes 73736 | tf_op jit(solution)/shard_map/ppermute | solution.py:88
  61.6 3.2 %collective-permute-done.7.second = f32[48,128]{1,0:T(8,128)S(1)} collective-permute-done((f32[48,128]{1,0:T(8,128)S(1)}, f32[48,128]{1,0:T(8,128)S(1)}, u32[]{:S(2)}, u32[]{:S(2)}) %collective-permute-start.7) | collective-permute-done | bytes 24608 | tf_op jit(solution)/shard_map/ppermute | solution.py:88
  64.8 0.8 %finish.1 = f32[96,96]{1,0:T(8,128)} custom-call(f32[96,224]{1,0:T(8,128)S(1)} %get-tuple-element.44.band, f32[48,128]{1,0:T(8,128)S(1)} %collective-permute-done.6.first, f32[48,128]{1,0:T(8,128)S(1)} %collective-permute-done.7.second, f32[96,96]{1,0:T(8,128)S(1)} %copy-done.1), custom_call_target="tpu_custom_call" | custom-call | flops 1000000000 | bytes 1048576 | tf_op jit(solution)/shard_map/finish/pallas_call | solution.py:468
  (29 shorter events, 0.2 us)
Async XLA Ops:
  0.6 0.8 %copy-start = (f32[96,96]{1,0:T(8,128)S(1)}, f32[96,96]{1,0:T(8,128)}, u32[]{:S(2)}) copy-start(f32[96,96]{1,0:T(8,128)} %latent.3) | copy-start | bytes 110596
  1.4 4.7 %copy-start.11 = (f32[2,12,129,129]{3,0,2,1:T(2,128)S(1)}, f32[2,12,129,129]{3,0,2,1:T(2,128)}, u32[]{:S(2)}) copy-start(f32[2,12,129,129]{3,0,2,1:T(2,128)} %param.9) | copy-start | bytes 4792612
  1.5 7.9 %collective-permute-start = (f32[48,128]{1,0:T(8,128)S(1)}, f32[48,128]{1,0:T(8,128)S(1)}, u32[]{:S(2)}, u32[]{:S(2)}) collective-permute-start(f32[48,128]{1,0:T(8,128)S(1)} %get-tuple-element.28), channel_id=1, source_target_pairs={{0,1},{1,0},{2,3},{3,2},{4,5},{5,4},{6,7},{7,6},{8,9},{9,8},{10,11... | collective-permute-start | bytes 73736 | tf_op jit(solution)/shard_map/ppermute | solution.py:88
  1.6 4.9 %copy-start.6 = (f32[4,256,256]{2,1,0:T(8,128)S(1)}, f32[4,256,256]{2,1,0:T(8,128)}, u32[]{:S(2)}) copy-start(f32[4,256,256]{2,1,0:T(8,128)} %constant.2.clone.tables) | copy-start | bytes 3145732
  1.6 7.8 %collective-permute-start.1 = (f32[48,128]{1,0:T(8,128)S(1)}, f32[48,128]{1,0:T(8,128)S(1)}, u32[]{:S(2)}, u32[]{:S(2)}) collective-permute-start(f32[48,128]{1,0:T(8,128)S(1)} %get-tuple-element.29), channel_id=1, source_target_pairs={{0,0},{1,2},{2,1},{3,4},{4,3},{5,6},{6,5},{7,7},{8,8},{9,10},{10,9... | collective-permute-start | bytes 73736 | tf_op jit(solution)/shard_map/ppermute | solution.py:88
  9.6 7.3 %collective-permute-start.2 = (f32[64,224]{1,0:T(8,128)S(1)}, f32[64,224]{1,0:T(8,128)S(1)}, u32[]{:S(2)}, u32[]{:S(2)}) collective-permute-start(f32[64,224]{1,0:T(8,128)S(1)} %get-tuple-element.35), channel_id=1, source_target_pairs={{0,8},{8,0},{16,24},{24,16},{1,9},{9,1},{17,25},{25,17},{2,10},{10... | collective-permute-start | bytes 172040 | tf_op jit(solution)/shard_map/ppermute | solution.py:88
  10.9 6.0 %collective-permute-start.3 = (f32[64,224]{1,0:T(8,128)S(1)}, f32[64,224]{1,0:T(8,128)S(1)}, u32[]{:S(2)}, u32[]{:S(2)}) collective-permute-start(f32[64,224]{1,0:T(8,128)S(1)} %get-tuple-element.36), channel_id=1, source_target_pairs={{0,0},{8,16},{16,8},{24,24},{1,1},{9,17},{17,9},{25,25},{2,2},{10,... | collective-permute-start | bytes 172040 | tf_op jit(solution)/shard_map/ppermute | solution.py:88
  13.9 3.0 %copy-start.2 = (f32[1,256]{1,0:T(1,128)S(1)}, f32[1,256]{1,0:T(1,128)}, u32[]{:S(2)}) copy-start(f32[1,256]{1,0:T(1,128)} %slopes.1) | copy-start | bytes 3076
  13.9 3.0 %copy-start.3 = (s32[1,256]{1,0:T(1,128)S(1)}, s32[1,256]{1,0:T(1,128)}, u32[]{:S(2)}) copy-start(s32[1,256]{1,0:T(1,128)} %pixels.3) | copy-start | bytes 3076
  13.9 3.0 %copy-start.4 = (f32[12]{0:T(128)S(1)}, f32[12]{0:T(128)}, u32[]{:S(2)}) copy-start(f32[12]{0:T(128)} %weights.3) | copy-start | bytes 148
  16.9 6.1 %copy-start.7 = (f32[12,224,256]{2,1,0:T(8,128)}, f32[12,224,256]{2,1,0:T(8,128)S(1)}, u32[]{:S(2)}) copy-start(f32[12,224,256]{2,1,0:T(8,128)S(1)} %get-tuple-element.32.spec_re) | copy-start | bytes 8257540
  16.9 6.1 %copy-start.9 = (f32[12,224,256]{2,1,0:T(8,128)}, f32[12,224,256]{2,1,0:T(8,128)S(1)}, u32[]{:S(2)}) copy-start(f32[12,224,256]{2,1,0:T(8,128)S(1)} %get-tuple-element.33.spec_im) | copy-start | bytes 8257540
  23.1 16.4 %copy-start.5 = (f32[8]{0:T(128)S(1)}, f32[8]{0:T(128)}, u32[]{:S(2)}) copy-start(f32[8]{0:T(128)} %doses.1) | copy-start | bytes 100
  32.5 7.0 %all-to-all-start.1 = ((f32[4,8,512]{2,1,0:T(8,128)}), f32[4,8,512]{2,1,0:T(8,128)S(1)}, u32[]{:S(2)}, u32[]{:S(2)}) async-start(f32[4,8,512]{2,1,0:T(8,128)} %repeat.1), calls=%async_computation.1 | async-start | bytes 131072 | tf_op jit(solution)/shard_map/all_to_all | solution.py:393
  39.5 1.8 %copy-start.8 = (f32[12,224,256]{2,1,0:T(8,128)S(1)}, f32[12,224,256]{2,1,0:T(8,128)}, u32[]{:S(2)}) copy-start(f32[12,224,256]{2,1,0:T(8,128)} %copy-done.7) | copy-start | bytes 8257540
  41.2 1.8 %copy-start.10 = (f32[12,224,256]{2,1,0:T(8,128)S(1)}, f32[12,224,256]{2,1,0:T(8,128)}, u32[]{:S(2)}) copy-start(f32[12,224,256]{2,1,0:T(8,128)} %copy-done.9) | copy-start | bytes 8257540
  51.5 13.3 %copy-start.1 = (f32[96,96]{1,0:T(8,128)S(1)}, f32[96,96]{1,0:T(8,128)}, u32[]{:S(2)}) copy-start(f32[96,96]{1,0:T(8,128)} %latent.3) | copy-start | bytes 110596
  51.5 2.8 %collective-permute-start.4 = (f32[64,224]{1,0:T(8,128)S(1)}, f32[64,224]{1,0:T(8,128)S(1)}, u32[]{:S(2)}, u32[]{:S(2)}) collective-permute-start(f32[64,224]{1,0:T(8,128)S(1)} %get-tuple-element.42), channel_id=1, source_target_pairs={{0,8},{8,0},{16,24},{24,16},{1,9},{9,1},{17,25},{25,17},{2,10},{10... | collective-permute-start | bytes 172040 | tf_op jit(solution)/shard_map/ppermute | solution.py:88
  52.4 5.6 %collective-permute-start.5 = (f32[64,224]{1,0:T(8,128)S(1)}, f32[64,224]{1,0:T(8,128)S(1)}, u32[]{:S(2)}, u32[]{:S(2)}) collective-permute-start(f32[64,224]{1,0:T(8,128)S(1)} %get-tuple-element.43), channel_id=1, source_target_pairs={{0,0},{8,16},{16,8},{24,24},{1,1},{9,17},{17,9},{25,25},{2,2},{10,... | collective-permute-start | bytes 172040 | tf_op jit(solution)/shard_map/ppermute | solution.py:88
  58.1 3.5 %collective-permute-start.6 = (f32[48,128]{1,0:T(8,128)S(1)}, f32[48,128]{1,0:T(8,128)S(1)}, u32[]{:S(2)}, u32[]{:S(2)}) collective-permute-start(f32[48,128]{1,0:T(8,128)S(1)} %get-tuple-element.45), channel_id=1, source_target_pairs={{0,1},{1,0},{2,3},{3,2},{4,5},{5,4},{6,7},{7,6},{8,9},{9,8},{10,11... | collective-permute-start | bytes 73736 | tf_op jit(solution)/shard_map/ppermute | solution.py:88
  59.4 5.5 %collective-permute-start.7 = (f32[48,128]{1,0:T(8,128)S(1)}, f32[48,128]{1,0:T(8,128)S(1)}, u32[]{:S(2)}, u32[]{:S(2)}) collective-permute-start(f32[48,128]{1,0:T(8,128)S(1)} %get-tuple-element.46), channel_id=1, source_target_pairs={{0,0},{1,2},{2,1},{3,4},{4,3},{5,6},{6,5},{7,7},{8,8},{9,10},{10,9... | collective-permute-start | bytes 73736 | tf_op jit(solution)/shard_map/ppermute | solution.py:88

commit v5 on v4

--- a/solution.py
+++ b/solution.py
@@ -3,6 +3,7 @@
 
 import jax
 import jax.numpy as jnp
+import ml_dtypes
 import numpy as np
 from jax import lax
 from jax.experimental import pallas as pl
@@ -42,19 +43,33 @@
     return tall[:count] + tall[count:] + dot(high, b[1])
 
 
-def wave_tables(period):
+def wave_tables(period, tile):
     half = period // 2
     place = np.arange(period)
     angle = (np.arange(half)[None, :] + 0.5) * place[:, None] * (2.0 * math.pi / period)
     cos, sin = np.cos(angle), np.sin(angle)
-    out = np.zeros((4, 2 * LANES, 2 * LANES))
-    out[0, :period, :half] = cos
-    out[0, :period, LANES : LANES + half] = sin
-    out[1] = out[0].T
-    out[2, :half, :period] = cos.T
-    out[2, half:period, :period] = sin.T
-    out[3] = out[2].T
-    return out.astype(np.float32)
+    wide = np.zeros((2 * LANES, 2 * LANES))
+    tall = np.zeros((2 * LANES, 2 * LANES))
+    wide[:period, :half] = cos
+    wide[:period, LANES : LANES + half] = sin
+    tall[:half, :period] = cos.T
+    tall[half:period, :period] = sin.T
+    out = np.zeros((10, 2 * LANES, 2 * LANES), ml_dtypes.bfloat16)
+    for first, table in ((0, wide), (2, tall), (4, wide.T), (6, tall.T)):
+        out[first] = table.astype(ml_dtypes.bfloat16)
+        out[first + 1] = (table - out[first].astype(np.float64)).astype(ml_dtypes.bfloat16)
+    out[8, :, :tile] = out[2, :, :tile]
+    out[8, :, tile : 2 * tile] = out[2, :, :tile]
+    out[9, :, :tile] = out[3, :, :tile]
+    return out
+
+
+def pair(tables, first, rows, cols):
+    return tables[first, :rows, :cols], tables[first + 1, :rows, :cols]
+
+
+def whole(parts):
+    return parts[0].astype(F32) + parts[1].astype(F32)
 
 
 def halves(x):
@@ -90,22 +105,43 @@
 
 
 def spectra_kernel(start, parts, kern, tables, *rest):
-    out_re, out_im, token = rest[-3:]
+    out_re, out_im, token, edge = rest[-4:]
     period = out_re.shape[1]
     half = period // 2
-    taps = kern.shape[-1]
-    cols = split(tables[0, :taps, :])
-    rows = split(tables[2, :period, :taps])
-    rows = (rows[0], stacked(rows))
+    last = kern.shape[-1] - 1
+    cols = pair(tables, 0, last, 2 * LANES)
+    cols = (stacked((cols[0], cols[0])), cols[1])
+    end_row = whole((tables[0, last : last + 16, :], tables[1, last : last + 16, :]))[:1]
+    high, low = pair(tables, 2, period, last)
+    rows = stacked(
+        (
+            jnp.concatenate([high, high], axis=1),
+            jnp.concatenate([low, jnp.zeros_like(low)], axis=1),
+        )
+    )
+    end_col = whole(pair(tables, 2, period, 2 * LANES))[:, last : last + 1]
+    edge[...] = jnp.broadcast_to(end_col, edge.shape)
+
+    def along_lanes(plane):
+        high, low = split(plane[:, :last])
+        out = dot(jnp.concatenate([high, low], axis=1), cols[0]) + dot(high, cols[1])
+        return halves(out + plane[:, last:] * end_row)
+
+    def along_rows(wide):
+        tall = dot(rows, stacked(split(wide[:last])))
+        tail = wide[last:]
+        outer = [edge[...] * tail[:, :LANES], edge[...] * tail[:, LANES:]]
+        return tall[:period] + tall[period:] + jnp.concatenate(outer, axis=1)
+
     token[...] = jnp.zeros(token.shape, F32)
 
     def step(k, carry):
-        real_cos, real_sin = halves(dot3(split(kern[0, start + k]), cols))
-        imag_cos, imag_sin = halves(dot3(split(kern[1, start + k]), cols))
+        real_cos, real_sin = along_lanes(kern[0, start + k])
+        imag_cos, imag_sin = along_lanes(kern[1, start + k])
         wide_re = jnp.concatenate([real_cos - imag_sin, real_cos + imag_sin], axis=1)
         wide_im = jnp.concatenate([real_sin + imag_cos, imag_cos - real_sin], axis=1)
-        tall_re = dot3_stacked(rows, split(wide_re))
-        tall_im = dot3_stacked(rows, split(wide_im))
+        tall_re = along_rows(wide_re)
+        tall_im = along_rows(wide_im)
         out_re[start + k, :half] = tall_re[:half] - tall_im[half:]
         out_re[start + k, half:] = tall_re[:half] + tall_im[half:]
         out_im[start + k, :half] = tall_im[:half] + tall_re[half:]
@@ -146,11 +182,6 @@
         "ty", band[:radius], band[tile - radius :]
     )
     token[...] = jnp.zeros(token.shape, F32)
-
-
-def repeat_kernel(rows, out):
-    for r in range(rows.shape[0]):
-        out[:, r] = jnp.broadcast_to(rows[r], (out.shape[0], out.shape[2]))
 
 
 def fold_kernel(grad, first, second, band, next_first, next_second):
@@ -201,8 +232,8 @@
     framed[:radius] = above
     framed[radius + tile :] = below
     framed[radius : radius + tile] = band[...]
-    wide = dot3(split(framed[...]), split(tables[0, :period]))
-    tall = dot3(split(tables[2, :period, :period]), split(wide)) * (1.0 / (period * period))
+    wide = dot3(split(framed[...]), pair(tables, 0, period, 2 * LANES))
+    tall = dot3(pair(tables, 2, period, period), split(wide)) * (1.0 / (period * period))
     cos_cos, cos_sin = halves(tall[:half])
     sin_cos, sin_sin = halves(tall[half:])
     same, other = cos_cos - sin_sin, cos_cos + sin_sin
@@ -211,9 +242,10 @@
     mask[1, :, :LANES], mask[1, :, LANES:] = -joint, -cross
     mask[2, :, :LANES], mask[2, :, LANES:] = other, same
     mask[3, :, :LANES], mask[3, :, LANES:] = cross, joint
-    lift = split(tables[3, :tile, :period])
+    lift = pair(tables, 6, tile, period)
     lift = (lift[0], stacked(lift))
-    across = split(tables[1, :, :LANES])
+    across = pair(tables, 4, 2 * LANES, LANES)
+    across = (across[0], jnp.concatenate(across, axis=1))
 
     def step(k, intensity):
         pos_re, pos_im = spec_re[k, :half], spec_im[k, :half]
@@ -228,7 +260,9 @@
         im_pos, im_neg = halves(dot3_stacked(lift, split(for_im)))
         rows_re = jnp.concatenate([re_pos + re_neg, im_neg - im_pos], axis=1)
         rows_im = jnp.concatenate([im_pos + im_neg, re_pos - re_neg], axis=1)
-        both = dot3(split(stacked((rows_re, rows_im))), across)
+        high, low = split(stacked((rows_re, rows_im)))
+        first, second = halves(dot(high, across[1]))
+        both = first + second + dot(low, across[0])
         real, imag = both[:tile], both[tile:]
         field_re[k] = real
         field_im[k] = imag
@@ -256,26 +290,34 @@
 
 
 def errors(intensity, slope, dose):
-    resist = sigmoid(STEEPNESS * (dose * intensity - RESIST_LEVEL))
-    offset = (resist - 0.5) * slope
+    resist = 0.5 * jnp.tanh(0.5 * STEEPNESS * (dose * intensity - RESIST_LEVEL))
+    offset = resist * slope
     return resist, offset, offset * offset
 
 
 def gradient_kernel(
     weights, doses, pick, gathered, sampled, pixels, spec_re, spec_im, field_re, field_im,
-    tables, grad, first, second, tail, total_re, total_im,
+    tables, grad, first, second, tail, total_re, total_im, held, sems,
 ):
     kernels, period, _ = spec_re.shape
+
+    def fetch(k):
+        return [
+            pltpu.make_async_copy(source.at[k], held.at[i, k], sems.at[i, k])
+            for i, source in enumerate((spec_re, spec_im))
+        ]
+
+    for k in range(kernels):
+        for copy in fetch(k):
+            copy.start()
     half = period // 2
     tile = field_re.shape[1]
     radius = (period - tile) // 2
     samples = pixels.shape[1]
-    groups, members, _ = gathered.shape
-    devices = groups * members
+    devices = gathered.shape[0]
     corners = doses.shape[0]
     per_corner = devices * samples
-    rows = gathered[...].reshape(devices, 2 * samples)
-    everyone, every_slope = rows[:, :samples], rows[:, samples:]
+    everyone, every_slope = gathered[:, :samples], gathered[:, samples:]
     pick_corner = pick[0] // per_corner
     remain = pick[0] - pick_corner * per_corner
     place = lax.broadcasted_iota(jnp.int32, (devices, samples), 0) * samples
@@ -304,7 +346,7 @@
     resist, offset, error = errors(own, slope, dose)
     soft = sigmoid((error - threshold) * (1.0 / SOFTNESS))
     slope_soft = soft * (1.0 - soft) * (1.0 / SOFTNESS)
-    chain = 2.0 * STEEPNESS * offset * slope * dose * resist * (1.0 - resist)
+    chain = 2.0 * STEEPNESS * offset * slope * dose * (0.25 - resist * resist)
     coefficient = (soft + (error - tail_mean) * slope_soft) * (corners * per_corner / soft_total)
     summed = jnp.sum(coefficient * chain, axis=0, keepdims=True)
     summed = summed / total_weight(weights, kernels)
@@ -322,27 +364,32 @@
             part, one_hot, (((1,), (1,)), ((), ())), preferred_element_type=F32
         )
 
-    cols = split(tables[0, :LANES])
-    rows = split(tables[2, :period, :tile])
-    rows = (rows[0], stacked(rows))
+    cols = pair(tables, 0, LANES, 2 * LANES)
+    cols = (stacked((cols[0], cols[0])), cols[1])
+    rows = stacked(pair(tables, 8, period, 2 * tile))
     total_re[...] = jnp.zeros((period, 2 * LANES), F32)
     total_im[...] = jnp.zeros((period, 2 * LANES), F32)
 
     def step(k, carry):
         weighted = grid * weights[k]
         source = stacked((weighted * field_re[k], weighted * field_im[k]))
-        both = dot3(split(source), cols)
+        high, low = split(source)
+        both = dot(jnp.concatenate([high, low], axis=1), cols[0]) + dot(high, cols[1])
         real_cos, real_sin = halves(both[:tile])
         imag_cos, imag_sin = halves(both[tile:])
         wide_re = jnp.concatenate([real_cos + imag_sin, real_cos - imag_sin], axis=1)
         wide_im = jnp.concatenate([imag_cos - real_sin, imag_cos + real_sin], axis=1)
-        tall_re = dot3_stacked(rows, split(wide_re))
-        tall_im = dot3_stacked(rows, split(wide_im))
+        tall_re = dot(rows, stacked(split(wide_re)))
+        tall_im = dot(rows, stacked(split(wide_im)))
+        tall_re = tall_re[:period] + tall_re[period:]
+        tall_im = tall_im[:period] + tall_im[period:]
+        for copy in fetch(k):
+            copy.wait()
         for start, sign in ((0, 1.0), (half, -1.0)):
             part = slice(start, start + half)
             wave_re = tall_re[:half] + sign * tall_im[half:]
             wave_im = tall_im[:half] - sign * tall_re[half:]
-            own_re, own_im = spec_re[k, part], spec_im[k, part]
+            own_re, own_im = held[0, k, part], held[1, k, part]
             total_re[part] += own_re * wave_re + own_im * wave_im
             total_im[part] += own_re * wave_im - own_im * wave_re
         return carry
@@ -350,13 +397,14 @@
     lax.fori_loop(0, kernels, step, 0, unroll=UNROLL)
     pos_re, neg_re = total_re[:half], total_re[half:]
     pos_im, neg_im = total_im[:half], total_im[half:]
-    back_rows = split(tables[3, :period, :period])
+    back_rows = pair(tables, 6, period, period)
+    back_rows = (back_rows[0], stacked(back_rows))
     for_re = jnp.concatenate([pos_re + neg_re, neg_im - pos_im], axis=0)
     for_im = jnp.concatenate([pos_im + neg_im, pos_re - neg_re], axis=0)
-    re_pos, re_neg = halves(dot3(back_rows, split(for_re)))
-    im_pos, im_neg = halves(dot3(back_rows, split(for_im)))
+    re_pos, re_neg = halves(dot3_stacked(back_rows, split(for_re)))
+    im_pos, im_neg = halves(dot3_stacked(back_rows, split(for_im)))
     last = jnp.concatenate([re_pos + re_neg, im_neg - im_pos], axis=1)
-    framed = dot3(split(last), split(tables[1, :, :period])) * (2.0 / (period * period))
+    framed = dot3(split(last), pair(tables, 4, 2 * LANES, period)) * (2.0 / (period * period))
     grad[...] = framed
     first[...], second[...] = ordered("ty", framed[:radius], framed[radius + tile :])
 
@@ -364,6 +412,7 @@
 VMEM = pl.BlockSpec(memory_space=pltpu.VMEM)
 SMEM = pl.BlockSpec(memory_space=pltpu.SMEM)
 ANY = pl.BlockSpec(memory_space=pl.ANY)
+HBM = pl.BlockSpec(memory_space=pltpu.HBM)
 
 
 def shape(*dims):
@@ -378,7 +427,7 @@
         out_specs=[VMEM] * len(out_shape),
         scratch_shapes=scratch,
         input_output_aliases=aliases or {},
-        compiler_params=pltpu.CompilerParams(vmem_limit_bytes=10 * 1024 * 1024),
+        compiler_params=pltpu.CompilerParams(vmem_limit_bytes=16 * 1024 * 1024),
         cost_estimate=pl.CostEstimate(
             flops=micros * 10**9, bytes_accessed=2**20, transcendentals=0
         ),
@@ -387,10 +436,7 @@
 
 
 def gather_all(copies):
-    group = lax.all_to_all(copies, "tx", 0, 0, tiled=True)
-    repeated = [shape(lax.axis_size("ty"), group.shape[0], group.shape[2])]
-    (groups,) = call(repeat_kernel, "repeat", repeated, [VMEM])(group)
-    return lax.all_to_all(groups, "ty", 0, 0, tiled=True)
+    return lax.all_to_all(copies, ("ty", "tx"), 0, 0, tiled=True)
 
 
 def body(latent, kernels, socs_weights, dose_scale, inv_slope, edge_pixels, threshold_pick):
@@ -400,7 +446,7 @@
     radius = (taps - 1) // 2
     period = tile + 2 * radius
     half = period // 2
-    tables = jnp.asarray(wave_tables(period))
+    tables = jnp.asarray(wave_tables(period, tile))
     token = shape(8, LANES)
     packed = [shape(tile // 2, 2 * radius)] * 2
     rim = [shape(radius, period)] * 2
@@ -420,6 +466,7 @@
             "spectra",
             [shape(count, period, 2 * LANES)] * 2 + [token],
             [VMEM] * 2 + [ANY] * len(given),
+            scratch=[pltpu.VMEM((period, LANES), F32)],
             aliases={2: 0, 3: 1} if spec else None,
             micros=3,
         )(kernels, tables, *given)
@@ -433,12 +480,12 @@
             after = [done]
             rims = exchange("ty", *rims)
 
-    across = lax.axis_size("tx")
+    devices = lax.axis_size("ty") * lax.axis_size("tx")
     field_re, field_im, sampled, copies = call(
         field_kernel,
         "field",
         [shape(count, tile, LANES)] * 2
-        + [shape(1, 2 * samples), shape(across, 1, 2 * samples)],
+        + [shape(1, 2 * samples), shape(devices, 1, 2 * samples)],
         [SMEM] + [VMEM] * 8,
         scratch=[
             pltpu.VMEM((period, period), F32),
@@ -447,13 +494,17 @@
         micros=7,
     )(socs_weights, *spec, band, *rims, edge_pixels, inv_slope, tables)
 
-    gathered = gather_all(copies)
+    gathered = gather_all(copies).reshape(devices, 2 * samples)
     grad, *rims, tail_mean = call(
         gradient_kernel,
         "gradient",
         [shape(period, period)] + rim + [shape(1, 1)],
-        [SMEM] * 3 + [VMEM] * 8,
-        scratch=[pltpu.VMEM((period, 2 * LANES), F32)] * 2,
+        [SMEM] * 3 + [VMEM] * 3 + [HBM] * 2 + [VMEM] * 3,
+        scratch=[pltpu.VMEM((period, 2 * LANES), F32)] * 2
+        + [
+            pltpu.VMEM((2, count, period, 2 * LANES), F32),
+            pltpu.SemaphoreType.DMA((2, count)),
+        ],
         micros=9,
     )(
         socs_weights, dose_scale, threshold_pick, gathered, sampled, edge_pixels,

time: 66.1 us -> 67.9 us (1.027)
  blocking collectives: 8.77 us -> 0 us
  Pallas kernels: 22.2 us -> 29.2 us
  waiting for transfers between devices: 9.51 us -> 12 us
  starting transfers between devices: 18.9 us -> 20 us
    all_to_all x1 -> x0, blocking collectives: 8.77 us -> none  [gather_all(): group = lax.all_to_all(copies, 'tx', 0, 0, tiled=True)]
    pallas_call x1, Pallas kernels: 8.53 us -> 17 us  [body(): call(gradient_kernel, 'gradient', [shape(period, period)] + rim + [shape(...]
    all_to_all x1, waiting for transfers between devices: 2.61 us -> 5.61 us  [gather_all(): return lax.all_to_all(copies, ('ty', 'tx'), 0, 0, tiled=True)]
    all_to_all x1, starting transfers between devices: 3.72 us -> 5.02 us  [gather_all(): return lax.all_to_all(copies, ('ty', 'tx'), 0, 0, tiled=True)]
    pallas_call x2, Pallas kernels: 5.86 us -> 5.01 us  [body(): call(functools.partial(spectra_kernel, part * parts, parts), 'spectra', [...]
    unnamed x25 -> x26, local copies, waits for them, and re-layouts: 4.74 us -> 4.74 us
  transfers between devices with their start and end apart: 9 -> 9, of which waited for: 3 -> 3; matrix products, arithmetic and copies ran while one was open for 1% -> 1% of each run, Pallas kernels for 9% -> 7%
where the time goes in v5:
time: 67.9 us; the launch traced here: 67.5 us
  Pallas kernels  29.2 us (43%)
  starting transfers between devices  20 us (29%)
  waiting for transfers between devices  12 us (18%)
  local copies, waits for them, and re-layouts  4.74 us (7%)
  between operations  1.55 us (2%)
    pallas_call x1, Pallas kernels, body(): call(gradient_kernel, 'gradient', [shape(period, period)] + rim + [shape(...  17 us
    ppermute x8, starting transfers between devices, exchange(): out.append(lax.ppermute(value, axis, pairs))  15 us
    ppermute x8, waiting for transfers between devices, exchange(): out.append(lax.ppermute(value, axis, pairs))  6.4 us
    pallas_call x1, Pallas kernels, body(): call(field_kernel, 'field', [shape(count, tile, LANES)] * 2 + [shape(1, 2...  6.1 us
    all_to_all x1, waiting for transfers between devices, gather_all(): return lax.all_to_all(copies, ('ty', 'tx'), 0, 0, tiled=True)  5.61 us
    all_to_all x1, starting transfers between devices, gather_all(): return lax.all_to_all(copies, ('ty', 'tx'), 0, 0, tiled=True)  5.02 us
    pallas_call x2, Pallas kernels, body(): call(functools.partial(spectra_kernel, part * parts, parts), 'spectra', [...  5.01 us
    unnamed x26, local copies, waits for them, and re-layouts  4.74 us
  transfers between devices with their start and end apart: 9, of which 3 were waited for; matrix products, arithmetic and copies ran while one was open for 1% of the time, Pallas kernels for 7%

profile of v5, /device:TPU:5, one launch (start us, length us, event | category | flops | bytes accessed | tf_op | source)
XLA Modules:
  0.0 67.5 jit_solution(5502900058800648484)
XLA Ops:
  0.6 0.8 %copy-done = f32[96,96]{1,0:T(8,128)S(1)} copy-done((f32[96,96]{1,0:T(8,128)S(1)}, f32[96,96]{1,0:T(8,128)}, u32[]{:S(2)}) %copy-start) | copy-done | bytes 36888
  1.4 0.1 start.1
  1.5 0.1 collective-permute-start
  1.6 4.5 %collective-permute-start.1 = (f32[48,128]{1,0:T(8,128)S(1)}, f32[48,128]{1,0:T(8,128)S(1)}, u32[]{:S(2)}, u32[]{:S(2)}) collective-permute-start(f32[48,128]{1,0:T(8,128)S(1)} %get-tuple-element.29), channel_id=1, source_target_pairs={{0,0},{1,2},{2,1},{3,4},{4,3},{5,6},{6,5},{7,7},{8,8},{9,10},{10,9... | collective-permute-start | bytes 73736 | tf_op jit(solution)/shard_map/ppermute | solution.py:103
  6.1 0.3 copy.16.kern
  6.5 2.5 %spectra.2 = (f32[12,224,256]{2,1,0:T(8,128)S(1)}, f32[12,224,256]{2,1,0:T(8,128)S(1)}, f32[8,128]{1,0:T(8,128)S(1)}) custom-call(f32[2,12,129,129]{3,2,1,0:T(8,128)S(1)} %copy.16.kern, bf16[10,256,256]{2,1,0:T(8,128)(2,1)S(1)} %copy-done.6), custom_call_target="tpu_custom_call" | custom-call | flops 3000000000 | bytes 1048576 | tf_op jit(solution)/shard_map/spectra/pallas_call | solution.py:464
  9.0 0.2 band.1
  9.2 1.3 %collective-permute-start.2 = (f32[64,224]{1,0:T(8,128)S(1)}, f32[64,224]{1,0:T(8,128)S(1)}, u32[]{:S(2)}, u32[]{:S(2)}) collective-permute-start(f32[64,224]{1,0:T(8,128)S(1)} %get-tuple-element.35), channel_id=1, source_target_pairs={{0,8},{8,0},{16,24},{24,16},{1,9},{9,1},{17,25},{25,17},{2,10},{10... | collective-permute-start | bytes 172040 | tf_op jit(solution)/shard_map/ppermute | solution.py:103
  10.5 3.0 %collective-permute-start.3 = (f32[64,224]{1,0:T(8,128)S(1)}, f32[64,224]{1,0:T(8,128)S(1)}, u32[]{:S(2)}, u32[]{:S(2)}) collective-permute-start(f32[64,224]{1,0:T(8,128)S(1)} %get-tuple-element.36), channel_id=1, source_target_pairs={{0,0},{8,16},{16,8},{24,24},{1,1},{9,17},{17,9},{25,25},{2,2},{10,... | collective-permute-start | bytes 172040 | tf_op jit(solution)/shard_map/ppermute | solution.py:103
  13.5 2.5 %spectra.3 = (f32[12,224,256]{2,1,0:T(8,128)S(1)}, f32[12,224,256]{2,1,0:T(8,128)S(1)}, f32[8,128]{1,0:T(8,128)}) custom-call(f32[2,12,129,129]{3,2,1,0:T(8,128)S(1)} %copy.16.kern, bf16[10,256,256]{2,1,0:T(8,128)(2,1)S(1)} %copy-done.6, f32[12,224,256]{2,1,0:T(8,128)S(1)} %get-tuple-element.25.rest_0_, ...), custom_call_target="tpu_custom_call", output_to_operand_aliasing={{0}: (2, {}), {1}: (3, {})} | custom-call | flops 3000000000 | bytes 1048576 | tf_op jit(solution)/shard_map/spectra/pallas_call | solution.py:464
  16.1 6.1 %field.1 = (f32[12,96,128]{2,1,0:T(8,128)S(1)}, f32[12,96,128]{2,1,0:T(8,128)S(1)}, f32[1,512]{1,0:T(1,128)S(1)}, f32[32,1,512]{2,1,0:T(1,128)}) custom-call(f32[12]{0:T(128)S(1)} %copy-done.4, f32[12,224,256]{2,1,0:T(8,128)S(1)} %get-tuple-element.32.spec_re, f32[12,224,256]{2,1,0:T(8,128)S(1)} %get-tuple-element.33.spec_im, ...), custom_call_target="tpu_custom_call" | custom-call | flops 7000000000 | bytes 1048576 | tf_op jit(solution)/shard_map/field/pallas_call | solution.py:484
  22.2 5.0 %all-to-all-start = ((f32[32,1,512]{2,1,0:T(1,128)}), f32[32,1,512]{2,1,0:T(1,128)S(1)}, u32[]{:S(2)}, u32[]{:S(2)}) async-start(f32[32,1,512]{2,1,0:T(1,128)} %get-tuple-element.37), calls=%async_computation | async-start | bytes 131072 | tf_op jit(solution)/shard_map/all_to_all | solution.py:439
  27.9 5.6 %all-to-all-done = f32[32,1,512]{2,1,0:T(1,128)S(1)} async-done(((f32[32,1,512]{2,1,0:T(1,128)}), f32[32,1,512]{2,1,0:T(1,128)S(1)}, u32[]{:S(2)}, u32[]{:S(2)}) %all-to-all-start) | async-done | bytes 65568 | tf_op jit(solution)/shard_map/all_to_all | solution.py:439
  33.5 1.8 %copy-done.8 = f32[12,224,256]{2,1,0:T(8,128)S(1)} copy-done((f32[12,224,256]{2,1,0:T(8,128)S(1)}, f32[12,224,256]{2,1,0:T(8,128)}, u32[]{:S(2)}) %copy-start.8) | copy-done | bytes 2752536
  35.3 1.8 %copy-done.10 = f32[12,224,256]{2,1,0:T(8,128)S(1)} copy-done((f32[12,224,256]{2,1,0:T(8,128)S(1)}, f32[12,224,256]{2,1,0:T(8,128)}, u32[]{:S(2)}) %copy-start.10) | copy-done | bytes 2752536
  37.1 17.0 %gradient.1 = (f32[224,224]{1,0:T(8,128)S(1)}, f32[64,224]{1,0:T(8,128)S(1)}, f32[64,224]{1,0:T(8,128)S(1)}, f32[1,1]{1,0:T(1,128)}) custom-call(f32[12]{0:T(128)S(1)} %copy-done.4, f32[8]{0:T(128)S(1)} %copy-done.5, s32[1]{0:T(128)S(6)} %copy.22.pick, f32[32,512]{1,0:T(8,128)S(1)} %bitcast.4, f32[1,512]{1,0:T(1,128)S(1)} %get-tuple-element.38.sampled, ...), custom_call_target="tpu_custom_call" | custom-call | flops 8999999488 | bytes 1048576 | tf_op jit(solution)/shard_map/gradient/pallas_call | solution.py:498
  54.1 0.5 collective-permute-start.4
  54.6 2.2 %collective-permute-start.5 = (f32[64,224]{1,0:T(8,128)S(1)}, f32[64,224]{1,0:T(8,128)S(1)}, u32[]{:S(2)}, u32[]{:S(2)}) collective-permute-start(f32[64,224]{1,0:T(8,128)S(1)} %get-tuple-element.43), channel_id=1, source_target_pairs={{0,0},{8,16},{16,8},{24,24},{1,1},{9,17},{17,9},{25,25},{2,2},{10,... | collective-permute-start | bytes 172040 | tf_op jit(solution)/shard_map/ppermute | solution.py:103
  56.8 3.4 %collective-permute-done.5.second = f32[64,224]{1,0:T(8,128)S(1)} collective-permute-done((f32[64,224]{1,0:T(8,128)S(1)}, f32[64,224]{1,0:T(8,128)S(1)}, u32[]{:S(2)}, u32[]{:S(2)}) %collective-permute-start.5) | collective-permute-done | bytes 57376 | tf_op jit(solution)/shard_map/ppermute | solution.py:103
  60.1 0.1 fold.1
  60.3 1.0 %collective-permute-start.6 = (f32[48,128]{1,0:T(8,128)S(1)}, f32[48,128]{1,0:T(8,128)S(1)}, u32[]{:S(2)}, u32[]{:S(2)}) collective-permute-start(f32[48,128]{1,0:T(8,128)S(1)} %get-tuple-element.45), channel_id=1, source_target_pairs={{0,1},{1,0},{2,3},{3,2},{4,5},{5,4},{6,7},{7,6},{8,9},{9,8},{10,11... | collective-permute-start | bytes 73736 | tf_op jit(solution)/shard_map/ppermute | solution.py:103
  61.3 2.4 %collective-permute-start.7 = (f32[48,128]{1,0:T(8,128)S(1)}, f32[48,128]{1,0:T(8,128)S(1)}, u32[]{:S(2)}, u32[]{:S(2)}) collective-permute-start(f32[48,128]{1,0:T(8,128)S(1)} %get-tuple-element.46), channel_id=1, source_target_pairs={{0,0},{1,2},{2,1},{3,4},{4,3},{5,6},{6,5},{7,7},{8,8},{9,10},{10,9... | collective-permute-start | bytes 73736 | tf_op jit(solution)/shard_map/ppermute | solution.py:103
  63.7 3.0 %collective-permute-done.7.second = f32[48,128]{1,0:T(8,128)S(1)} collective-permute-done((f32[48,128]{1,0:T(8,128)S(1)}, f32[48,128]{1,0:T(8,128)S(1)}, u32[]{:S(2)}, u32[]{:S(2)}) %collective-permute-start.7) | collective-permute-done | bytes 24608 | tf_op jit(solution)/shard_map/ppermute | solution.py:103
  66.7 0.8 %finish.1 = f32[96,96]{1,0:T(8,128)} custom-call(f32[96,224]{1,0:T(8,128)S(1)} %get-tuple-element.44.band, f32[48,128]{1,0:T(8,128)S(1)} %collective-permute-done.6.first, f32[48,128]{1,0:T(8,128)S(1)} %collective-permute-done.7.second, f32[96,96]{1,0:T(8,128)S(1)} %copy-done.1), custom_call_target="tpu_custom_call" | custom-call | flops 1000000000 | bytes 1048576 | tf_op jit(solution)/shard_map/finish/pallas_call | solution.py:519
  (28 shorter events, 0.1 us)
Async XLA Ops:
  0.6 0.8 %copy-start = (f32[96,96]{1,0:T(8,128)S(1)}, f32[96,96]{1,0:T(8,128)}, u32[]{:S(2)}) copy-start(f32[96,96]{1,0:T(8,128)} %latent.3) | copy-start | bytes 110596
  1.4 4.7 %copy-start.11 = (f32[2,12,129,129]{3,0,2,1:T(2,128)S(1)}, f32[2,12,129,129]{3,0,2,1:T(2,128)}, u32[]{:S(2)}) copy-start(f32[2,12,129,129]{3,0,2,1:T(2,128)} %param.9) | copy-start | bytes 4792612
  1.5 7.5 %collective-permute-start = (f32[48,128]{1,0:T(8,128)S(1)}, f32[48,128]{1,0:T(8,128)S(1)}, u32[]{:S(2)}, u32[]{:S(2)}) collective-permute-start(f32[48,128]{1,0:T(8,128)S(1)} %get-tuple-element.28), channel_id=1, source_target_pairs={{0,1},{1,0},{2,3},{3,2},{4,5},{5,4},{6,7},{7,6},{8,9},{9,8},{10,11... | collective-permute-start | bytes 73736 | tf_op jit(solution)/shard_map/ppermute | solution.py:103
  1.6 4.9 %copy-start.6 = (bf16[10,256,256]{2,1,0:T(8,128)(2,1)S(1)}, bf16[10,256,256]{2,1,0:T(8,128)(2,1)}, u32[]{:S(2)}) copy-start(bf16[10,256,256]{2,1,0:T(8,128)(2,1)} %constant.2.clone.tables) | copy-start | bytes 3932164
  1.6 7.4 %collective-permute-start.1 = (f32[48,128]{1,0:T(8,128)S(1)}, f32[48,128]{1,0:T(8,128)S(1)}, u32[]{:S(2)}, u32[]{:S(2)}) collective-permute-start(f32[48,128]{1,0:T(8,128)S(1)} %get-tuple-element.29), channel_id=1, source_target_pairs={{0,0},{1,2},{2,1},{3,4},{4,3},{5,6},{6,5},{7,7},{8,8},{9,10},{10,9... | collective-permute-start | bytes 73736 | tf_op jit(solution)/shard_map/ppermute | solution.py:103
  9.2 6.9 %collective-permute-start.2 = (f32[64,224]{1,0:T(8,128)S(1)}, f32[64,224]{1,0:T(8,128)S(1)}, u32[]{:S(2)}, u32[]{:S(2)}) collective-permute-start(f32[64,224]{1,0:T(8,128)S(1)} %get-tuple-element.35), channel_id=1, source_target_pairs={{0,8},{8,0},{16,24},{24,16},{1,9},{9,1},{17,25},{25,17},{2,10},{10... | collective-permute-start | bytes 172040 | tf_op jit(solution)/shard_map/ppermute | solution.py:103
  10.5 5.6 %collective-permute-start.3 = (f32[64,224]{1,0:T(8,128)S(1)}, f32[64,224]{1,0:T(8,128)S(1)}, u32[]{:S(2)}, u32[]{:S(2)}) collective-permute-start(f32[64,224]{1,0:T(8,128)S(1)} %get-tuple-element.36), channel_id=1, source_target_pairs={{0,0},{8,16},{16,8},{24,24},{1,1},{9,17},{17,9},{25,25},{2,2},{10,... | collective-permute-start | bytes 172040 | tf_op jit(solution)/shard_map/ppermute | solution.py:103
  13.5 2.6 %copy-start.2 = (f32[1,256]{1,0:T(1,128)S(1)}, f32[1,256]{1,0:T(1,128)}, u32[]{:S(2)}) copy-start(f32[1,256]{1,0:T(1,128)} %slopes.1) | copy-start | bytes 3076
  13.5 2.6 %copy-start.3 = (s32[1,256]{1,0:T(1,128)S(1)}, s32[1,256]{1,0:T(1,128)}, u32[]{:S(2)}) copy-start(s32[1,256]{1,0:T(1,128)} %pixels.3) | copy-start | bytes 3076
  13.5 2.6 %copy-start.4 = (f32[12]{0:T(128)S(1)}, f32[12]{0:T(128)}, u32[]{:S(2)}) copy-start(f32[12]{0:T(128)} %weights.3) | copy-start | bytes 148
  16.1 6.2 %copy-start.7 = (f32[12,224,256]{2,1,0:T(8,128)}, f32[12,224,256]{2,1,0:T(8,128)S(1)}, u32[]{:S(2)}) copy-start(f32[12,224,256]{2,1,0:T(8,128)S(1)} %get-tuple-element.32.spec_re) | copy-start | bytes 8257540
  16.1 6.2 %copy-start.9 = (f32[12,224,256]{2,1,0:T(8,128)}, f32[12,224,256]{2,1,0:T(8,128)S(1)}, u32[]{:S(2)}) copy-start(f32[12,224,256]{2,1,0:T(8,128)S(1)} %get-tuple-element.33.spec_im) | copy-start | bytes 8257540
  16.1 17.4 %copy-start.5 = (f32[8]{0:T(128)S(1)}, f32[8]{0:T(128)}, u32[]{:S(2)}) copy-start(f32[8]{0:T(128)} %doses.1) | copy-start | bytes 100
  22.2 11.3 %all-to-all-start = ((f32[32,1,512]{2,1,0:T(1,128)}), f32[32,1,512]{2,1,0:T(1,128)S(1)}, u32[]{:S(2)}, u32[]{:S(2)}) async-start(f32[32,1,512]{2,1,0:T(1,128)} %get-tuple-element.37), calls=%async_computation | async-start | bytes 131072 | tf_op jit(solution)/shard_map/all_to_all | solution.py:439
  33.5 1.8 %copy-start.8 = (f32[12,224,256]{2,1,0:T(8,128)S(1)}, f32[12,224,256]{2,1,0:T(8,128)}, u32[]{:S(2)}) copy-start(f32[12,224,256]{2,1,0:T(8,128)} %copy-done.7) | copy-start | bytes 8257540
  35.3 1.8 %copy-start.10 = (f32[12,224,256]{2,1,0:T(8,128)S(1)}, f32[12,224,256]{2,1,0:T(8,128)}, u32[]{:S(2)}) copy-start(f32[12,224,256]{2,1,0:T(8,128)} %copy-done.9) | copy-start | bytes 8257540
  54.1 12.6 %copy-start.1 = (f32[96,96]{1,0:T(8,128)S(1)}, f32[96,96]{1,0:T(8,128)}, u32[]{:S(2)}) copy-start(f32[96,96]{1,0:T(8,128)} %latent.3) | copy-start | bytes 110596
  54.1 2.6 %collective-permute-start.4 = (f32[64,224]{1,0:T(8,128)S(1)}, f32[64,224]{1,0:T(8,128)S(1)}, u32[]{:S(2)}, u32[]{:S(2)}) collective-permute-start(f32[64,224]{1,0:T(8,128)S(1)} %get-tuple-element.42), channel_id=1, source_target_pairs={{0,8},{8,0},{16,24},{24,16},{1,9},{9,1},{17,25},{25,17},{2,10},{10... | collective-permute-start | bytes 172040 | tf_op jit(solution)/shard_map/ppermute | solution.py:103
  54.6 5.6 %collective-permute-start.5 = (f32[64,224]{1,0:T(8,128)S(1)}, f32[64,224]{1,0:T(8,128)S(1)}, u32[]{:S(2)}, u32[]{:S(2)}) collective-permute-start(f32[64,224]{1,0:T(8,128)S(1)} %get-tuple-element.43), channel_id=1, source_target_pairs={{0,0},{8,16},{16,8},{24,24},{1,1},{9,17},{17,9},{25,25},{2,2},{10,... | collective-permute-start | bytes 172040 | tf_op jit(solution)/shard_map/ppermute | solution.py:103
  60.3 3.5 %collective-permute-start.6 = (f32[48,128]{1,0:T(8,128)S(1)}, f32[48,128]{1,0:T(8,128)S(1)}, u32[]{:S(2)}, u32[]{:S(2)}) collective-permute-start(f32[48,128]{1,0:T(8,128)S(1)} %get-tuple-element.45), channel_id=1, source_target_pairs={{0,1},{1,0},{2,3},{3,2},{4,5},{5,4},{6,7},{7,6},{8,9},{9,8},{10,11... | collective-permute-start | bytes 73736 | tf_op jit(solution)/shard_map/ppermute | solution.py:103
  61.3 5.5 %collective-permute-start.7 = (f32[48,128]{1,0:T(8,128)S(1)}, f32[48,128]{1,0:T(8,128)S(1)}, u32[]{:S(2)}, u32[]{:S(2)}) collective-permute-start(f32[48,128]{1,0:T(8,128)S(1)} %get-tuple-element.46), channel_id=1, source_target_pairs={{0,0},{1,2},{2,1},{3,4},{4,3},{5,6},{6,5},{7,7},{8,8},{9,10},{10,9... | collective-permute-start | bytes 73736 | tf_op jit(solution)/shard_map/ppermute | solution.py:103

commit v6 on v5

--- a/solution.py
+++ b/solution.py
@@ -76,32 +76,21 @@
     return x[:, :LANES], x[:, LANES:]
 
 
-def edge_flags(axis):
+def place_in_pair(axis):
     index, count = lax.axis_index(axis), lax.axis_size(axis)
-    return lax.rem(index, 2) == 0, index > 0, index < count - 1
-
-
-def sides(axis, first, second):
-    even, lower, higher = edge_flags(axis)
-    from_lower = jnp.where(lower, jnp.where(even, second, first), 0.0)
-    from_higher = jnp.where(higher, jnp.where(even, first, second), 0.0)
-    return from_lower, from_higher
-
-
-def ordered(axis, for_lower, for_higher):
-    even = lax.rem(lax.axis_index(axis), 2) == 0
-    return jnp.where(even, for_higher, for_lower), jnp.where(even, for_lower, for_higher)
-
-
-def exchange(axis, first, second):
+    lower = lax.rem(index, 2) == 0
+    return lower, jnp.where(lower, index > 0, index < count - 1)
+
+
+def swap(axis, x):
+    return lax.ppermute(x, axis, [(i, i ^ 1) for i in range(lax.axis_size(axis))])
+
+
+def ring(axis, x, back=False):
     count = lax.axis_size(axis)
-    out = []
-    for offset, value in ((0, first), (1, second)):
-        pairs = [(i, i) for i in range(count)]
-        for low in range(offset, count - 1, 2):
-            pairs[low], pairs[low + 1] = (low, low + 1), (low + 1, low)
-        out.append(lax.ppermute(value, axis, pairs))
-    return out
+    cycle = list(range(0, count, 2)) + list(range(count - 1, 0, -2))
+    pairs = list(zip(cycle, cycle[1:] + cycle[:1]))
+    return lax.ppermute(x, axis, [(b, a) if back else (a, b) for a, b in pairs])
 
 
 def spectra_kernel(start, parts, kern, tables, *rest):
@@ -161,51 +150,83 @@
     return jnp.concatenate([x[:, :width], x[:, width:]], axis=0)
 
 
-def start_kernel(latent, transmit, first, second):
+def start_kernel(latent, transmit):
+    transmit[...] = 0.5 * (1.0 + jnp.tanh(latent[...]))
+
+
+def relay_columns_kernel(partner, after, rim, token):
+    radius = rim.shape[1] // 2
+    tile = partner.shape[1]
+    lower, _ = place_in_pair("tx")
+    rim[...] = jnp.where(
+        lower, pack(partner[:, tile - radius :]), pack(partner[:, :radius])
+    )
+    token[...] = jnp.zeros(token.shape, F32)
+
+
+def band_kernel(middle, partner, rim, after, band, token):
+    tile = middle.shape[0]
+    radius = rim.shape[1] // 2
+    lower, other = place_in_pair("tx")
+    outer = jnp.where(other, unpack(rim[...]), 0.0)
+    band[:, :radius] = jnp.where(lower, outer, partner[:, tile - radius :])
+    band[:, radius : radius + tile] = middle[...]
+    band[:, radius + tile :] = jnp.where(lower, partner[:, :radius], outer)
+    token[...] = jnp.zeros(token.shape, F32)
+
+
+def relay_rows_kernel(partner, after, rim, token):
+    radius = rim.shape[0]
+    tile = partner.shape[0]
+    lower, _ = place_in_pair("ty")
+    rim[...] = jnp.where(lower, partner[tile - radius :], partner[:radius])
+    token[...] = jnp.zeros(token.shape, F32)
+
+
+def fold_rows_kernel(grad, rim, out):
+    radius = rim.shape[0]
+    tile = out.shape[0]
+    lower, _ = place_in_pair("ty")
+    count, index = lax.axis_size("ty"), lax.axis_index("ty")
+    comes = jnp.where(lower, index < count - 2, index > 1)
+    outer = jnp.where(comes, rim[...], 0.0)
+    top = jnp.where(lower, grad[radius + tile :], outer)
+    bottom = jnp.where(lower, outer, grad[:radius])
+    out[:radius] = top
+    out[radius:] = jnp.zeros((tile - radius, out.shape[1]), F32)
+    out[tile - radius :] += bottom
+
+
+def fold_band_kernel(grad, partner, band, rim):
+    tile = band.shape[0]
+    radius = rim.shape[1] // 2
+    lower, _ = place_in_pair("tx")
+    band[...] = grad[radius : radius + tile] + partner[...]
+    rim[...] = jnp.where(
+        lower, pack(band[:, :radius]), pack(band[:, radius + tile :])
+    )
+
+
+def fold_columns_kernel(band, rim, out):
+    radius = rim.shape[1] // 2
+    tile = out.shape[1]
+    lower, _ = place_in_pair("tx")
+    count, index = lax.axis_size("tx"), lax.axis_index("tx")
+    comes = jnp.where(lower, index < count - 2, index > 1)
+    outer = jnp.where(comes, unpack(rim[...]), 0.0)
+    left = jnp.where(lower, band[:, radius + tile :], outer)
+    right = jnp.where(lower, outer, band[:, :radius])
+    out[:, :radius] = left
+    out[:, radius:] = jnp.zeros((out.shape[0], tile - radius), F32)
+    out[:, tile - radius :] += right
+
+
+def finish_kernel(band, partner, latent, steering):
     tile = latent.shape[0]
-    radius = first.shape[1] // 2
-    value = 0.5 * (1.0 + jnp.tanh(latent[...]))
-    transmit[...] = value
-    first[...], second[...] = ordered(
-        "tx", pack(value[:, :radius]), pack(value[:, tile - radius :])
-    )
-
-
-def band_kernel(middle, first, second, after, band, next_first, next_second, token):
-    tile = middle.shape[0]
-    radius = first.shape[1] // 2
-    left, right = sides("tx", first[...], second[...])
-    band[:, :radius] = unpack(left)
-    band[:, radius : radius + tile] = middle[...]
-    band[:, radius + tile :] = unpack(right)
-    next_first[...], next_second[...] = ordered(
-        "ty", band[:radius], band[tile - radius :]
-    )
-    token[...] = jnp.zeros(token.shape, F32)
-
-
-def fold_kernel(grad, first, second, band, next_first, next_second):
-    tile = band.shape[0]
-    radius = first.shape[0]
-    above, below = sides("ty", first[...], second[...])
-    band[...] = grad[radius : radius + tile]
-    band[:radius] += above
-    band[tile - radius :] += below
-    period = band.shape[1]
-    next_first[...], next_second[...] = ordered(
-        "tx", pack(band[:, :radius]), pack(band[:, period - radius :])
-    )
-
-
-def finish_kernel(band, first, second, latent, steering):
-    tile = latent.shape[0]
-    radius = first.shape[1] // 2
-    left, right = sides("tx", first[...], second[...])
-    steering[...] = band[:, radius : radius + tile]
-    steering[:, :radius] += unpack(left)
-    steering[:, tile - radius :] += unpack(right)
+    radius = (band.shape[1] - tile) // 2
     value = jnp.tanh(latent[...])
-    steering[...] = steering[...] * 0.5 * (1.0 - value * value)
+    total = band[:, radius : radius + tile] + partner[...]
+    steering[...] = total * 0.5 * (1.0 - value * value)
 
 
 def total_weight(weights, kernels):
@@ -221,16 +242,17 @@
 
 
 def field_kernel(
-    weights, spec_re, spec_im, band, first, second, pixels, slopes, tables,
+    weights, spec_re, spec_im, band, partner, rim, pixels, slopes, tables,
     field_re, field_im, sampled, copies, framed, mask,
 ):
     kernels, period, _ = spec_re.shape
     half = period // 2
     tile = field_re.shape[1]
-    radius = first.shape[0]
-    above, below = sides("ty", first[...], second[...])
-    framed[:radius] = above
-    framed[radius + tile :] = below
+    radius = rim.shape[0]
+    lower, other = place_in_pair("ty")
+    outer = jnp.where(other, rim[...], 0.0)
+    framed[:radius] = jnp.where(lower, outer, partner[tile - radius :])
+    framed[radius + tile :] = jnp.where(lower, partner[:radius], outer)
     framed[radius : radius + tile] = band[...]
     wide = dot3(split(framed[...]), pair(tables, 0, period, 2 * LANES))
     tall = dot3(pair(tables, 2, period, period), split(wide)) * (1.0 / (period * period))
@@ -297,7 +319,7 @@
 
 def gradient_kernel(
     weights, doses, pick, gathered, sampled, pixels, spec_re, spec_im, field_re, field_im,
-    tables, grad, first, second, tail, total_re, total_im, held, sems,
+    tables, grad, rim, tail, total_re, total_im, held, sems,
 ):
     kernels, period, _ = spec_re.shape
 
@@ -406,7 +428,8 @@
     last = jnp.concatenate([re_pos + re_neg, im_neg - im_pos], axis=1)
     framed = dot3(split(last), pair(tables, 4, 2 * LANES, period)) * (2.0 / (period * period))
     grad[...] = framed
-    first[...], second[...] = ordered("ty", framed[:radius], framed[radius + tile :])
+    lower, _ = place_in_pair("ty")
+    rim[...] = jnp.where(lower, framed[:radius], framed[radius + tile :])
 
 
 VMEM = pl.BlockSpec(memory_space=pltpu.VMEM)
@@ -419,7 +442,7 @@
     return jax.ShapeDtypeStruct(dims, F32)
 
 
-def call(kernel, name, out_shape, in_specs, scratch=(), aliases=None, micros=1):
+def call(kernel, name, out_shape, in_specs, scratch=(), aliases=None, micros=1, vmem=10):
     return pl.pallas_call(
         kernel,
         out_shape=out_shape,
@@ -427,7 +450,7 @@
         out_specs=[VMEM] * len(out_shape),
         scratch_shapes=scratch,
         input_output_aliases=aliases or {},
-        compiler_params=pltpu.CompilerParams(vmem_limit_bytes=16 * 1024 * 1024),
+        compiler_params=pltpu.CompilerParams(vmem_limit_bytes=vmem * 1024 * 1024),
         cost_estimate=pl.CostEstimate(
             flops=micros * 10**9, bytes_accessed=2**20, transcendentals=0
         ),
@@ -448,39 +471,46 @@
     half = period // 2
     tables = jnp.asarray(wave_tables(period, tile))
     token = shape(8, LANES)
-    packed = [shape(tile // 2, 2 * radius)] * 2
-    rim = [shape(radius, period)] * 2
-
-    transmit, *rims = call(
-        start_kernel, "start", [shape(tile, tile)] + packed, [VMEM]
-    )(latent)
-    rims = exchange("tx", *rims)
-
-    parts = count // 2
+    packed = shape(tile // 2, 2 * radius)
+    devices = lax.axis_size("ty") * lax.axis_size("tx")
+
+    steps = 4
+    parts = count // steps
     spec = []
-    after = []
-    for part in range(2):
-        given = spec + after
-        *spec, done = call(
-            functools.partial(spectra_kernel, part * parts, parts),
+
+    def spectra(step, *after):
+        given = spec + list(after)
+        *out, done = call(
+            functools.partial(spectra_kernel, step * parts, parts),
             "spectra",
             [shape(count, period, 2 * LANES)] * 2 + [token],
             [VMEM] * 2 + [ANY] * len(given),
             scratch=[pltpu.VMEM((period, LANES), F32)],
             aliases={2: 0, 3: 1} if spec else None,
-            micros=3,
+            micros=2,
         )(kernels, tables, *given)
-        if part == 0:
-            band, *rims, done = call(
-                band_kernel,
-                "band",
-                [shape(tile, period)] + rim + [token],
-                [VMEM] * 3 + [ANY],
-            )(transmit, *rims, done)
-            after = [done]
-            rims = exchange("ty", *rims)
-
-    devices = lax.axis_size("ty") * lax.axis_size("tx")
+        spec[:] = out
+        return done
+
+    (transmit,) = call(start_kernel, "start", [shape(tile, tile)], [VMEM])(latent)
+    partner = swap("tx", transmit)
+    done = spectra(0)
+    rim, done = call(relay_columns_kernel, "relay", [packed, token], [VMEM, ANY])(
+        partner, done
+    )
+    rim = ring("tx", rim)
+    done = spectra(1, done)
+    band, done = call(
+        band_kernel, "band", [shape(tile, period), token], [VMEM] * 3 + [ANY]
+    )(transmit, partner, rim, done)
+    partner = swap("ty", band)
+    done = spectra(2, done)
+    rim, done = call(
+        relay_rows_kernel, "relay", [shape(radius, period), token], [VMEM, ANY]
+    )(partner, done)
+    rim = ring("ty", rim)
+    spectra(3, done)
+
     field_re, field_im, sampled, copies = call(
         field_kernel,
         "field",
@@ -492,13 +522,13 @@
             pltpu.VMEM((4, half, 2 * LANES), F32),
         ],
         micros=7,
-    )(socs_weights, *spec, band, *rims, edge_pixels, inv_slope, tables)
+    )(socs_weights, *spec, band, partner, rim, edge_pixels, inv_slope, tables)
 
     gathered = gather_all(copies).reshape(devices, 2 * samples)
-    grad, *rims, tail_mean = call(
+    grad, rim, tail_mean = call(
         gradient_kernel,
         "gradient",
-        [shape(period, period)] + rim + [shape(1, 1)],
+        [shape(period, period), shape(radius, period), shape(1, 1)],
         [SMEM] * 3 + [VMEM] * 3 + [HBM] * 2 + [VMEM] * 3,
         scratch=[pltpu.VMEM((period, 2 * LANES), F32)] * 2
         + [
@@ -506,19 +536,28 @@
             pltpu.SemaphoreType.DMA((2, count)),
         ],
         micros=9,
+        vmem=60,
     )(
         socs_weights, dose_scale, threshold_pick, gathered, sampled, edge_pixels,
         *spec, field_re, field_im, tables,
     )
 
-    rims = exchange("ty", *rims)
-    band, *rims = call(
-        fold_kernel, "fold", [shape(tile, period)] + packed, [VMEM] * 3
-    )(grad, *rims)
-    rims = exchange("tx", *rims)
-    (steering,) = call(
-        finish_kernel, "finish", [shape(tile, tile)], [VMEM] * 4
-    )(band, *rims, latent)
+    rim = ring("ty", rim, back=True)
+    (partner,) = call(fold_rows_kernel, "fold", [shape(tile, period)], [VMEM] * 2)(
+        grad, rim
+    )
+    partner = swap("ty", partner)
+    band, rim = call(
+        fold_band_kernel, "fold", [shape(tile, period), packed], [VMEM] * 2
+    )(grad, partner)
+    rim = ring("tx", rim, back=True)
+    (partner,) = call(fold_columns_kernel, "fold", [shape(tile, tile)], [VMEM] * 2)(
+        band, rim
+    )
+    partner = swap("tx", partner)
+    (steering,) = call(finish_kernel, "finish", [shape(tile, tile)], [VMEM] * 3)(
+        band, partner, latent
+    )
     return (steering, tail_mean.reshape(1))
 
 

time: 67.9 us -> 66.6 us (0.981)
  the two profiles are of different devices: /device:TPU:5 before, /device:TPU:0 now
where the time goes in v6:
time: 66.6 us; the launch traced here: 66.3 us
  Pallas kernels  24 us (36%)
  waiting for transfers between devices  20.1 us (30%)
  starting transfers between devices  15.8 us (24%)
  local copies, waits for them, and re-layouts  4.97 us (7%)
  between operations  1.42 us (2%)
    pallas_call x1, Pallas kernels, body(): call(gradient_kernel, 'gradient', [shape(period, period), shape(radius, p...  11.5 us
    ppermute x4, waiting for transfers between devices, ring(): return lax.ppermute(x, axis, [(b, a) if back else (a, b) for a, b in pairs])  8.31 us
    all_to_all x1, starting transfers between devices, gather_all(): return lax.all_to_all(copies, ('ty', 'tx'), 0, 0, tiled=True)  6.73 us
    all_to_all x1, waiting for transfers between devices, gather_all(): return lax.all_to_all(copies, ('ty', 'tx'), 0, 0, tiled=True)  6.63 us
    pallas_call x1, Pallas kernels, body(): call(field_kernel, 'field', [shape(count, tile, LANES)] * 2 + [shape(1, 2...  6.02 us
    ppermute x4, waiting for transfers between devices, swap(): lax.ppermute(x, axis, [(i, i ^ 1) for i in range(lax.axis_size(axis))])  5.17 us
    pallas_call x4, Pallas kernels, spectra(): call(functools.partial(spectra_kernel, step * parts, parts), 'spectra', [...  5.13 us
    ppermute x4, starting transfers between devices, ring(): return lax.ppermute(x, axis, [(b, a) if back else (a, b) for a, b in pairs])  5.1 us
  transfers between devices with their start and end apart: 9, of which 9 were waited for; matrix products, arithmetic and copies ran while one was open for 1% of the time, Pallas kernels for 8%

profile of v6, /device:TPU:0, one launch (start us, length us, event | category | flops | bytes accessed | tf_op | source)
XLA Modules:
  0.0 66.3 jit_solution(8120460944508167298)
XLA Ops:
  0.6 0.8 %copy-done.3 = f32[96,96]{1,0:T(8,128)S(1)} copy-done((f32[96,96]{1,0:T(8,128)S(1)}, f32[96,96]{1,0:T(8,128)}, u32[]{:S(2)}) %copy-start.3) | copy-done | bytes 36888
  1.5 3.0 %collective-permute-start = (f32[96,96]{1,0:T(8,128)S(1)}, f32[96,96]{1,0:T(8,128)S(1)}, u32[]{:S(2)}, u32[]{:S(2)}) collective-permute-start(f32[96,96]{1,0:T(8,128)S(1)} %start.1.middle), channel_id=1, source_target_pairs={{0,1},{1,0},{2,3},{3,2},{4,5},{5,4},{6,7},{7,6},{8,9},{9,8},{10,11... | collective-permute-start | bytes 110600 | tf_op jit(solution)/shard_map/ppermute | solution.py:86
  4.9 1.2 %spectra.4 = (f32[12,224,256]{2,1,0:T(8,128)S(1)}, f32[12,224,256]{2,1,0:T(8,128)S(1)}, f32[8,128]{1,0:T(8,128)S(1)}) custom-call(f32[2,12,129,129]{3,2,1,0:T(8,128)S(1)} %copy.24.kern, bf16[10,256,256]{2,1,0:T(8,128)(2,1)S(1)} %copy-done.2), custom_call_target="tpu_custom_call" | custom-call | flops 2000000000 | bytes 1048576 | tf_op jit(solution)/shard_map/spectra/pallas_call | solution.py:483
  6.7 2.1 %collective-permute-start.1 = (f32[48,128]{1,0:T(8,128)S(1)}, f32[48,128]{1,0:T(8,128)S(1)}, u32[]{:S(2)}, u32[]{:S(2)}) collective-permute-start(f32[48,128]{1,0:T(8,128)S(1)} %get-tuple-element.34), channel_id=1, source_target_pairs={{0,2},{2,4},{4,6},{6,7},{7,5},{5,3},{3,1},{1,0},{8,10},{10,12},{12... | collective-permute-start | bytes 73736 | tf_op jit(solution)/shard_map/ppermute | solution.py:93
  8.8 1.2 %spectra.5 = (f32[12,224,256]{2,1,0:T(8,128)S(1)}, f32[12,224,256]{2,1,0:T(8,128)S(1)}, f32[8,128]{1,0:T(8,128)S(1)}) custom-call(f32[2,12,129,129]{3,2,1,0:T(8,128)S(1)} %copy.24.kern, bf16[10,256,256]{2,1,0:T(8,128)(2,1)S(1)} %copy-done.2, f32[12,224,256]{2,1,0:T(8,128)S(1)} %get-tuple-element.28.rest_0_, ...), custom_call_target="tpu_custom_call", output_to_operand_aliasing={{0}: (2, {}), {1}: (3, {})} | custom-call | flops 2000000000 | bytes 1048576 | tf_op jit(solution)/shard_map/spectra/pallas_call | solution.py:483
  10.7 1.2 %spectra.6 = (f32[12,224,256]{2,1,0:T(8,128)S(1)}, f32[12,224,256]{2,1,0:T(8,128)S(1)}, f32[8,128]{1,0:T(8,128)S(1)}) custom-call(f32[2,12,129,129]{3,2,1,0:T(8,128)S(1)} %copy.24.kern, bf16[10,256,256]{2,1,0:T(8,128)(2,1)S(1)} %copy-done.2, f32[12,224,256]{2,1,0:T(8,128)S(1)} %get-tuple-element.32.rest_0_, ...), custom_call_target="tpu_custom_call", output_to_operand_aliasing={{0}: (2, {}), {1}: (3, {})} | custom-call | flops 2000000000 | bytes 1048576 | tf_op jit(solution)/shard_map/spectra/pallas_call | solution.py:483
  12.0 2.0 %collective-permute-start.3 = (f32[64,224]{1,0:T(8,128)S(1)}, f32[64,224]{1,0:T(8,128)S(1)}, u32[]{:S(2)}, u32[]{:S(2)}) collective-permute-start(f32[64,224]{1,0:T(8,128)S(1)} %get-tuple-element.44), channel_id=1, source_target_pairs={{0,16},{16,24},{24,8},{8,0},{1,17},{17,25},{25,9},{9,1},{2,18},{18... | collective-permute-start | bytes 172040 | tf_op jit(solution)/shard_map/ppermute | solution.py:93
  14.0 1.5 %spectra.7 = (f32[12,224,256]{2,1,0:T(8,128)S(1)}, f32[12,224,256]{2,1,0:T(8,128)S(1)}, f32[8,128]{1,0:T(8,128)}) custom-call(f32[2,12,129,129]{3,2,1,0:T(8,128)S(1)} %copy.24.kern, bf16[10,256,256]{2,1,0:T(8,128)(2,1)S(1)} %copy-done.2, f32[12,224,256]{2,1,0:T(8,128)S(1)} %get-tuple-element.37.rest_0_, ...), custom_call_target="tpu_custom_call", output_to_operand_aliasing={{0}: (2, {}), {1}: (3, {})} | custom-call | flops 2000000000 | bytes 1048576 | tf_op jit(solution)/shard_map/spectra/pallas_call | solution.py:483
  15.9 6.0 %field.1 = (f32[12,96,128]{2,1,0:T(8,128)S(1)}, f32[12,96,128]{2,1,0:T(8,128)S(1)}, f32[1,512]{1,0:T(1,128)S(1)}, f32[32,1,512]{2,1,0:T(1,128)}) custom-call(f32[12]{0:T(128)S(1)} %copy-done.7, f32[12,224,256]{2,1,0:T(8,128)S(1)} %get-tuple-element.42.spec_re, f32[12,224,256]{2,1,0:T(8,128)S(1)} %get-tuple-element.43.spec_im, ...), custom_call_target="tpu_custom_call" | custom-call | flops 7000000000 | bytes 1048576 | tf_op jit(solution)/shard_map/field/pallas_call | solution.py:514
  22.0 0.8 %copy-done.9 = f32[12,96,128]{2,1,0:T(8,128)} copy-done((f32[12,96,128]{2,1,0:T(8,128)}, f32[12,96,128]{2,1,0:T(8,128)S(1)}, u32[]{:S(2)}) %copy-start.9) | copy-done | bytes 589848
  22.8 0.8 %copy-done.10 = f32[12,96,128]{2,1,0:T(8,128)} copy-done((f32[12,96,128]{2,1,0:T(8,128)}, f32[12,96,128]{2,1,0:T(8,128)S(1)}, u32[]{:S(2)}) %copy-start.10) | copy-done | bytes 589848
  23.6 0.6 copy-done.11
  24.2 6.7 %all-to-all-start = ((f32[32,1,512]{2,1,0:T(1,128)}), f32[32,1,512]{2,1,0:T(1,128)S(1)}, u32[]{:S(2)}, u32[]{:S(2)}) async-start(f32[32,1,512]{2,1,0:T(1,128)} %get-tuple-element.45), calls=%async_computation | async-start | bytes 131072 | tf_op jit(solution)/shard_map/all_to_all | solution.py:462
  31.6 6.6 %all-to-all-done = f32[32,1,512]{2,1,0:T(1,128)S(1)} async-done(((f32[32,1,512]{2,1,0:T(1,128)}), f32[32,1,512]{2,1,0:T(1,128)S(1)}, u32[]{:S(2)}, u32[]{:S(2)}) %all-to-all-start) | async-done | bytes 65568 | tf_op jit(solution)/shard_map/all_to_all | solution.py:462
  38.2 0.6 copy.27
  38.8 11.5 %gradient.1 = (f32[224,224]{1,0:T(8,128)}, f32[64,224]{1,0:T(8,128)}, f32[1,1]{1,0:T(1,128)}) custom-call(f32[12]{0:T(128)} %weights.3, f32[8]{0:T(128)} %doses.1, s32[1]{0:T(128)S(6)} %copy.34.pick, f32[32,512]{1,0:T(8,128)} %bitcast.4, f32[1,512]{1,0:T(1,128)} %copy-done.11, s32[1,256]{1,0:T(1,128)} %pixels.3, f32[12,224,256]{2,1,0:T(8,128)} %copy-done, ...), custom_call_target="tpu_custom_call" | custom-call | flops 8999999488 | bytes 1048576 | tf_op jit(solution)/shard_map/gradient/pallas_call | solution.py:528
  50.5 4.4 %collective-permute-done.4.rim = f32[64,224]{1,0:T(8,128)S(1)} collective-permute-done((f32[64,224]{1,0:T(8,128)}, f32[64,224]{1,0:T(8,128)S(1)}, u32[]{:S(2)}, u32[]{:S(2)}) %collective-permute-start.4) | collective-permute-done | bytes 57376 | tf_op jit(solution)/shard_map/ppermute | solution.py:93
  54.9 0.9 %copy-done.8 = f32[224,224]{1,0:T(8,128)S(1)} copy-done((f32[224,224]{1,0:T(8,128)S(1)}, f32[224,224]{1,0:T(8,128)}, u32[]{:S(2)}) %copy-start.8) | copy-done | bytes 200728
  55.9 1.3 %collective-permute-done.5.partner = f32[96,224]{1,0:T(8,128)S(1)} collective-permute-done((f32[96,224]{1,0:T(8,128)S(1)}, f32[96,224]{1,0:T(8,128)S(1)}, u32[]{:S(2)}, u32[]{:S(2)}) %collective-permute-start.5) | collective-permute-done | bytes 86048 | tf_op jit(solution)/shard_map/ppermute | solution.py:86
  57.3 0.8 %collective-permute-start.6 = (f32[48,128]{1,0:T(8,128)S(1)}, f32[48,128]{1,0:T(8,128)S(1)}, u32[]{:S(2)}, u32[]{:S(2)}) collective-permute-start(f32[48,128]{1,0:T(8,128)S(1)} %get-tuple-element.52), channel_id=1, source_target_pairs={{2,0},{4,2},{6,4},{7,6},{5,7},{3,5},{1,3},{0,1},{10,8},{12,10},{14... | collective-permute-start | bytes 73736 | tf_op jit(solution)/shard_map/ppermute | solution.py:93
  58.1 3.0 %collective-permute-done.6.rim = f32[48,128]{1,0:T(8,128)S(1)} collective-permute-done((f32[48,128]{1,0:T(8,128)S(1)}, f32[48,128]{1,0:T(8,128)S(1)}, u32[]{:S(2)}, u32[]{:S(2)}) %collective-permute-start.6) | collective-permute-done | bytes 24608 | tf_op jit(solution)/shard_map/ppermute | solution.py:93
  61.4 0.9 %collective-permute-start.7 = (f32[96,96]{1,0:T(8,128)S(1)}, f32[96,96]{1,0:T(8,128)S(1)}, u32[]{:S(2)}, u32[]{:S(2)}) collective-permute-start(f32[96,96]{1,0:T(8,128)S(1)} %fold.5), channel_id=1, source_target_pairs={{0,1},{1,0},{2,3},{3,2},{4,5},{5,4},{6,7},{7,6},{8,9},{9,8},{10,11... | collective-permute-start | bytes 110600 | tf_op jit(solution)/shard_map/ppermute | solution.py:86
  62.2 3.3 %collective-permute-done.7.partner = f32[96,96]{1,0:T(8,128)S(1)} collective-permute-done((f32[96,96]{1,0:T(8,128)S(1)}, f32[96,96]{1,0:T(8,128)S(1)}, u32[]{:S(2)}, u32[]{:S(2)}) %collective-permute-start.7) | collective-permute-done | bytes 36896 | tf_op jit(solution)/shard_map/ppermute | solution.py:86
  65.6 0.8 %finish.1 = f32[96,96]{1,0:T(8,128)} custom-call(f32[96,224]{1,0:T(8,128)S(1)} %get-tuple-element.51.band, f32[96,96]{1,0:T(8,128)S(1)} %collective-permute-done.7.partner, f32[96,96]{1,0:T(8,128)S(1)} %copy-done.4), custom_call_target="tpu_custom_call" | custom-call | flops 1000000000 | bytes 1048576 | tf_op jit(solution)/shard_map/finish/pallas_call | solution.py:558
  (36 shorter events, 2.7 us)
Async XLA Ops:
  0.6 0.8 %copy-start.3 = (f32[96,96]{1,0:T(8,128)S(1)}, f32[96,96]{1,0:T(8,128)}, u32[]{:S(2)}) copy-start(f32[96,96]{1,0:T(8,128)} %latent.3) | copy-start | bytes 110596
  1.4 3.1 %copy-start.12 = (f32[2,12,129,129]{3,0,2,1:T(2,128)S(1)}, f32[2,12,129,129]{3,0,2,1:T(2,128)}, u32[]{:S(2)}) copy-start(f32[2,12,129,129]{3,0,2,1:T(2,128)} %param.9) | copy-start | bytes 4792612
  1.5 3.4 %copy-start.2 = (bf16[10,256,256]{2,1,0:T(8,128)(2,1)S(1)}, bf16[10,256,256]{2,1,0:T(8,128)(2,1)}, u32[]{:S(2)}) copy-start(bf16[10,256,256]{2,1,0:T(8,128)(2,1)} %constant.2.clone.tables) | copy-start | bytes 3932164
  1.5 5.1 %collective-permute-start = (f32[96,96]{1,0:T(8,128)S(1)}, f32[96,96]{1,0:T(8,128)S(1)}, u32[]{:S(2)}, u32[]{:S(2)}) collective-permute-start(f32[96,96]{1,0:T(8,128)S(1)} %start.1.middle), channel_id=1, source_target_pairs={{0,1},{1,0},{2,3},{3,2},{4,5},{5,4},{6,7},{7,6},{8,9},{9,8},{10,11... | collective-permute-start | bytes 110600 | tf_op jit(solution)/shard_map/ppermute | solution.py:86
  6.7 3.9 %collective-permute-start.1 = (f32[48,128]{1,0:T(8,128)S(1)}, f32[48,128]{1,0:T(8,128)S(1)}, u32[]{:S(2)}, u32[]{:S(2)}) collective-permute-start(f32[48,128]{1,0:T(8,128)S(1)} %get-tuple-element.34), channel_id=1, source_target_pairs={{0,2},{2,4},{4,6},{6,7},{7,5},{5,3},{3,1},{1,0},{8,10},{10,12},{12... | collective-permute-start | bytes 73736 | tf_op jit(solution)/shard_map/ppermute | solution.py:93
  10.7 1.3 %collective-permute-start.2 = (f32[96,224]{1,0:T(8,128)S(1)}, f32[96,224]{1,0:T(8,128)S(1)}, u32[]{:S(2)}, u32[]{:S(2)}) collective-permute-start(f32[96,224]{1,0:T(8,128)S(1)} %get-tuple-element.39.band), channel_id=1, source_target_pairs={{0,8},{8,0},{16,24},{24,16},{1,9},{9,1},{17,25},{25,17},{2,10},{10... | collective-permute-start | bytes 258056 | tf_op jit(solution)/shard_map/ppermute | solution.py:86
  12.0 3.9 %collective-permute-start.3 = (f32[64,224]{1,0:T(8,128)S(1)}, f32[64,224]{1,0:T(8,128)S(1)}, u32[]{:S(2)}, u32[]{:S(2)}) collective-permute-start(f32[64,224]{1,0:T(8,128)S(1)} %get-tuple-element.44), channel_id=1, source_target_pairs={{0,16},{16,24},{24,8},{8,0},{1,17},{17,25},{25,9},{9,1},{2,18},{18... | collective-permute-start | bytes 172040 | tf_op jit(solution)/shard_map/ppermute | solution.py:93
  14.0 1.9 %copy-start.5 = (f32[1,256]{1,0:T(1,128)S(1)}, f32[1,256]{1,0:T(1,128)}, u32[]{:S(2)}) copy-start(f32[1,256]{1,0:T(1,128)} %slopes.1) | copy-start | bytes 3076
  14.0 1.9 %copy-start.6 = (s32[1,256]{1,0:T(1,128)S(1)}, s32[1,256]{1,0:T(1,128)}, u32[]{:S(2)}) copy-start(s32[1,256]{1,0:T(1,128)} %pixels.3) | copy-start | bytes 3076
  14.0 1.9 %copy-start.7 = (f32[12]{0:T(128)S(1)}, f32[12]{0:T(128)}, u32[]{:S(2)}) copy-start(f32[12]{0:T(128)} %weights.3) | copy-start | bytes 148
  15.6 6.4 %copy-start = (f32[12,224,256]{2,1,0:T(8,128)}, f32[12,224,256]{2,1,0:T(8,128)S(1)}, u32[]{:S(2)}) copy-start(f32[12,224,256]{2,1,0:T(8,128)S(1)} %get-tuple-element.42.spec_re) | copy-start | bytes 8257540
  15.6 6.4 %copy-start.1 = (f32[12,224,256]{2,1,0:T(8,128)}, f32[12,224,256]{2,1,0:T(8,128)S(1)}, u32[]{:S(2)}) copy-start(f32[12,224,256]{2,1,0:T(8,128)S(1)} %get-tuple-element.43.spec_im) | copy-start | bytes 8257540
  22.0 0.8 %copy-start.9 = (f32[12,96,128]{2,1,0:T(8,128)}, f32[12,96,128]{2,1,0:T(8,128)S(1)}, u32[]{:S(2)}) copy-start(f32[12,96,128]{2,1,0:T(8,128)S(1)} %get-tuple-element.47.field_re) | copy-start | bytes 1769476
  22.8 0.8 %copy-start.10 = (f32[12,96,128]{2,1,0:T(8,128)}, f32[12,96,128]{2,1,0:T(8,128)S(1)}, u32[]{:S(2)}) copy-start(f32[12,96,128]{2,1,0:T(8,128)S(1)} %get-tuple-element.48.field_im) | copy-start | bytes 1769476
  23.6 0.6 copy-start.11
  24.2 14.0 %all-to-all-start = ((f32[32,1,512]{2,1,0:T(1,128)}), f32[32,1,512]{2,1,0:T(1,128)S(1)}, u32[]{:S(2)}, u32[]{:S(2)}) async-start(f32[32,1,512]{2,1,0:T(1,128)} %get-tuple-element.45), calls=%async_computation | async-start | bytes 131072 | tf_op jit(solution)/shard_map/all_to_all | solution.py:462
  50.4 4.5 %collective-permute-start.4 = (f32[64,224]{1,0:T(8,128)}, f32[64,224]{1,0:T(8,128)S(1)}, u32[]{:S(2)}, u32[]{:S(2)}) collective-permute-start(f32[64,224]{1,0:T(8,128)} %get-tuple-element.50), channel_id=1, source_target_pairs={{16,0},{24,16},{8,24},{0,8},{17,1},{25,17},{9,25},{1,9},{18,2},{26... | collective-permute-start | bytes 172040 | tf_op jit(solution)/shard_map/ppermute | solution.py:93
  54.9 0.9 %copy-start.8 = (f32[224,224]{1,0:T(8,128)S(1)}, f32[224,224]{1,0:T(8,128)}, u32[]{:S(2)}) copy-start(f32[224,224]{1,0:T(8,128)} %get-tuple-element.49.grad) | copy-start | bytes 602116
  55.8 1.4 %collective-permute-start.5 = (f32[96,224]{1,0:T(8,128)S(1)}, f32[96,224]{1,0:T(8,128)S(1)}, u32[]{:S(2)}, u32[]{:S(2)}) collective-permute-start(f32[96,224]{1,0:T(8,128)S(1)} %fold.3), channel_id=1, source_target_pairs={{0,8},{8,0},{16,24},{24,16},{1,9},{9,1},{17,25},{25,17},{2,10},{10... | collective-permute-start | bytes 258056 | tf_op jit(solution)/shard_map/ppermute | solution.py:86
  57.3 8.3 %copy-start.4 = (f32[96,96]{1,0:T(8,128)S(1)}, f32[96,96]{1,0:T(8,128)}, u32[]{:S(2)}) copy-start(f32[96,96]{1,0:T(8,128)} %latent.3) | copy-start | bytes 110596
  57.3 3.9 %collective-permute-start.6 = (f32[48,128]{1,0:T(8,128)S(1)}, f32[48,128]{1,0:T(8,128)S(1)}, u32[]{:S(2)}, u32[]{:S(2)}) collective-permute-start(f32[48,128]{1,0:T(8,128)S(1)} %get-tuple-element.52), channel_id=1, source_target_pairs={{2,0},{4,2},{6,4},{7,6},{5,7},{3,5},{1,3},{0,1},{10,8},{12,10},{14... | collective-permute-start | bytes 73736 | tf_op jit(solution)/shard_map/ppermute | solution.py:93
  61.4 4.2 %collective-permute-start.7 = (f32[96,96]{1,0:T(8,128)S(1)}, f32[96,96]{1,0:T(8,128)S(1)}, u32[]{:S(2)}, u32[]{:S(2)}) collective-permute-start(f32[96,96]{1,0:T(8,128)S(1)} %fold.5), channel_id=1, source_target_pairs={{0,1},{1,0},{2,3},{3,2},{4,5},{5,4},{6,7},{7,6},{8,9},{9,8},{10,11... | collective-permute-start | bytes 110600 | tf_op jit(solution)/shard_map/ppermute | solution.py:86

commit v7 on v6

--- a/solution.py
+++ b/solution.py
@@ -14,7 +14,7 @@
 RESIST_LEVEL = 0.7
 SOFTNESS = 0.25
 LANES = 128
-UNROLL = 3
+BATCH = 3
 F32 = jnp.float32
 BF16 = jnp.bfloat16
 
@@ -86,6 +86,14 @@
     return lax.ppermute(x, axis, [(i, i ^ 1) for i in range(lax.axis_size(axis))])
 
 
+def swap_outside(axis, x):
+    count = lax.axis_size(axis)
+    pairs = [(0, 0), (count - 1, count - 1)]
+    for low in range(1, count - 1, 2):
+        pairs += [(low, low + 1), (low + 1, low)]
+    return lax.ppermute(x, axis, pairs)
+
+
 def ring(axis, x, back=False):
     count = lax.axis_size(axis)
     cycle = list(range(0, count, 2)) + list(range(count - 1, 0, -2))
@@ -111,33 +119,50 @@
     end_col = whole(pair(tables, 2, period, 2 * LANES))[:, last : last + 1]
     edge[...] = jnp.broadcast_to(end_col, edge.shape)
 
-    def along_lanes(plane):
-        high, low = split(plane[:, :last])
+    def along_lanes(planes):
+        main = stacked([plane[:last] for plane in planes])
+        tail = stacked([plane[last:] for plane in planes])
+        tail = jnp.concatenate([tail, jnp.zeros((-tail.shape[0] % 16, last + 1), F32)], axis=0)
+        both = stacked((main, tail))
+        high, low = split(both[:, :last])
         out = dot(jnp.concatenate([high, low], axis=1), cols[0]) + dot(high, cols[1])
-        return halves(out + plane[:, last:] * end_row)
-
-    def along_rows(wide):
-        tall = dot(rows, stacked(split(wide[:last])))
-        tail = wide[last:]
+        out = out + both[:, last:] * end_row
+        first = len(planes) * last
+        return [
+            (out[i * last : (i + 1) * last], out[first + i : first + i + 1])
+            for i in range(len(planes))
+        ]
+
+    def along_rows(wide, tail):
+        tall = dot(rows, stacked(split(wide)))
         outer = [edge[...] * tail[:, :LANES], edge[...] * tail[:, LANES:]]
         return tall[:period] + tall[period:] + jnp.concatenate(outer, axis=1)
 
-    token[...] = jnp.zeros(token.shape, F32)
-
-    def step(k, carry):
-        real_cos, real_sin = along_lanes(kern[0, start + k])
-        imag_cos, imag_sin = along_lanes(kern[1, start + k])
-        wide_re = jnp.concatenate([real_cos - imag_sin, real_cos + imag_sin], axis=1)
-        wide_im = jnp.concatenate([real_sin + imag_cos, imag_cos - real_sin], axis=1)
-        tall_re = along_rows(wide_re)
-        tall_im = along_rows(wide_im)
-        out_re[start + k, :half] = tall_re[:half] - tall_im[half:]
-        out_re[start + k, half:] = tall_re[:half] + tall_im[half:]
-        out_im[start + k, :half] = tall_im[:half] + tall_re[half:]
-        out_im[start + k, half:] = tall_im[:half] - tall_re[half:]
+    def mixed(real, imag):
+        real_cos, real_sin = halves(real)
+        imag_cos, imag_sin = halves(imag)
+        return (
+            jnp.concatenate([real_cos - imag_sin, real_cos + imag_sin], axis=1),
+            jnp.concatenate([real_sin + imag_cos, imag_cos - real_sin], axis=1),
+        )
+
+    def step(group, carry):
+        first = start + group * BATCH
+        planes = along_lanes([kern[c, first + i] for i in range(BATCH) for c in range(2)])
+        for i in range(BATCH):
+            k = first + i
+            (real, real_tail), (imag, imag_tail) = planes[2 * i : 2 * i + 2]
+            wide_re, wide_im = mixed(real, imag)
+            tail_re, tail_im = mixed(real_tail, imag_tail)
+            tall_re = along_rows(wide_re, tail_re)
+            tall_im = along_rows(wide_im, tail_im)
+            out_re[k, :half] = tall_re[:half] - tall_im[half:]
+            out_re[k, half:] = tall_re[:half] + tall_im[half:]
+            out_im[k, :half] = tall_im[:half] + tall_re[half:]
+            out_im[k, half:] = tall_im[:half] - tall_re[half:]
         return carry
 
-    lax.fori_loop(0, parts, step, 0, unroll=UNROLL)
+    lax.fori_loop(0, parts // BATCH, step, 0)
 
 
 def pack(x):
@@ -150,28 +175,20 @@
     return jnp.concatenate([x[:, :width], x[:, width:]], axis=0)
 
 
-def start_kernel(latent, transmit):
-    transmit[...] = 0.5 * (1.0 + jnp.tanh(latent[...]))
-
-
-def relay_columns_kernel(partner, after, rim, token):
-    radius = rim.shape[1] // 2
-    tile = partner.shape[1]
-    lower, _ = place_in_pair("tx")
-    rim[...] = jnp.where(
-        lower, pack(partner[:, tile - radius :]), pack(partner[:, :radius])
-    )
-    token[...] = jnp.zeros(token.shape, F32)
-
-
-def band_kernel(middle, partner, rim, after, band, token):
+def band_kernel(middle, partner, outside, after, band, token):
     tile = middle.shape[0]
-    radius = rim.shape[1] // 2
+    radius = (band.shape[1] - tile) // 2
     lower, other = place_in_pair("tx")
-    outer = jnp.where(other, unpack(rim[...]), 0.0)
-    band[:, :radius] = jnp.where(lower, outer, partner[:, tile - radius :])
-    band[:, radius : radius + tile] = middle[...]
-    band[:, radius + tile :] = jnp.where(lower, partner[:, :radius], outer)
+
+    def transmit(x):
+        return 0.5 * (1.0 + jnp.tanh(x))
+
+    near = transmit(jnp.where(lower, partner[:, :radius], partner[:, tile - radius :]))
+    far = transmit(jnp.where(lower, outside[:, tile - radius :], outside[:, :radius]))
+    far = jnp.where(other, far, 0.0)
+    band[:, :radius] = jnp.where(lower, far, near)
+    band[:, radius : radius + tile] = transmit(middle[...])
+    band[:, radius + tile :] = jnp.where(lower, near, far)
     token[...] = jnp.zeros(token.shape, F32)
 
 
@@ -197,36 +214,27 @@
     out[tile - radius :] += bottom
 
 
-def fold_band_kernel(grad, partner, band, rim):
+def fold_band_kernel(grad, partner, band, near, far):
     tile = band.shape[0]
-    radius = rim.shape[1] // 2
+    radius = near.shape[1] // 2
     lower, _ = place_in_pair("tx")
     band[...] = grad[radius : radius + tile] + partner[...]
-    rim[...] = jnp.where(
-        lower, pack(band[:, :radius]), pack(band[:, radius + tile :])
-    )
-
-
-def fold_columns_kernel(band, rim, out):
-    radius = rim.shape[1] // 2
-    tile = out.shape[1]
-    lower, _ = place_in_pair("tx")
-    count, index = lax.axis_size("tx"), lax.axis_index("tx")
-    comes = jnp.where(lower, index < count - 2, index > 1)
-    outer = jnp.where(comes, unpack(rim[...]), 0.0)
-    left = jnp.where(lower, band[:, radius + tile :], outer)
-    right = jnp.where(lower, outer, band[:, :radius])
-    out[:, :radius] = left
-    out[:, radius:] = jnp.zeros((out.shape[0], tile - radius), F32)
-    out[:, tile - radius :] += right
-
-
-def finish_kernel(band, partner, latent, steering):
+    left, right = pack(band[:, :radius]), pack(band[:, radius + tile :])
+    near[...] = jnp.where(lower, right, left)
+    far[...] = jnp.where(lower, left, right)
+
+
+def finish_kernel(band, near, far, latent, steering):
     tile = latent.shape[0]
     radius = (band.shape[1] - tile) // 2
+    lower, other = place_in_pair("tx")
+    inner = unpack(near[...])
+    outer = jnp.where(other, unpack(far[...]), 0.0)
+    steering[...] = band[:, radius : radius + tile]
+    steering[:, :radius] += jnp.where(lower, outer, inner)
+    steering[:, tile - radius :] += jnp.where(lower, inner, outer)
     value = jnp.tanh(latent[...])
-    total = band[:, radius : radius + tile] + partner[...]
-    steering[...] = total * 0.5 * (1.0 - value * value)
+    steering[...] = steering[...] * 0.5 * (1.0 - value * value)
 
 
 def total_weight(weights, kernels):
@@ -269,7 +277,7 @@
     across = pair(tables, 4, 2 * LANES, LANES)
     across = (across[0], jnp.concatenate(across, axis=1))
 
-    def step(k, intensity):
+    def lifted(k):
         pos_re, pos_im = spec_re[k, :half], spec_im[k, :half]
         neg_re, neg_im = spec_re[k, half:], spec_im[k, half:]
         up_re = mask[0] * pos_re - mask[1] * pos_im
@@ -282,16 +290,24 @@
         im_pos, im_neg = halves(dot3_stacked(lift, split(for_im)))
         rows_re = jnp.concatenate([re_pos + re_neg, im_neg - im_pos], axis=1)
         rows_im = jnp.concatenate([im_pos + im_neg, re_pos - re_neg], axis=1)
-        high, low = split(stacked((rows_re, rows_im)))
-        first, second = halves(dot(high, across[1]))
-        both = first + second + dot(low, across[0])
-        real, imag = both[:tile], both[tile:]
-        field_re[k] = real
-        field_im[k] = imag
-        return intensity + weights[k] * (real * real + imag * imag)
+        return [rows_re, rows_im]
+
+    def step(group, intensity):
+        first = group * BATCH
+        rows = stacked([row for i in range(BATCH) for row in lifted(first + i)])
+        high, low = split(rows)
+        by_high, by_low = halves(dot(high, across[1]))
+        both = by_high + by_low + dot(low, across[0])
+        for i in range(BATCH):
+            real = both[2 * i * tile : (2 * i + 1) * tile]
+            imag = both[(2 * i + 1) * tile : (2 * i + 2) * tile]
+            field_re[first + i] = real
+            field_im[first + i] = imag
+            intensity = intensity + weights[first + i] * (real * real + imag * imag)
+        return intensity
 
     intensity = lax.fori_loop(
-        0, kernels, step, jnp.zeros((tile, LANES), F32), unroll=UNROLL
+        0, kernels // BATCH, step, jnp.zeros((tile, LANES), F32)
     )
     intensity = intensity / total_weight(weights, kernels)
     samples = pixels.shape[1]
@@ -317,24 +333,9 @@
     return resist, offset, offset * offset
 
 
-def gradient_kernel(
-    weights, doses, pick, gathered, sampled, pixels, spec_re, spec_im, field_re, field_im,
-    tables, grad, rim, tail, total_re, total_im, held, sems,
-):
-    kernels, period, _ = spec_re.shape
-
-    def fetch(k):
-        return [
-            pltpu.make_async_copy(source.at[k], held.at[i, k], sems.at[i, k])
-            for i, source in enumerate((spec_re, spec_im))
-        ]
-
-    for k in range(kernels):
-        for copy in fetch(k):
-            copy.start()
-    half = period // 2
-    tile = field_re.shape[1]
-    radius = (period - tile) // 2
+def source_kernel(weights, doses, pick, gathered, sampled, pixels, placed_sum, tail):
+    kernels = weights.shape[0]
+    tile = placed_sum.shape[0]
     samples = pixels.shape[1]
     devices = gathered.shape[0]
     corners = doses.shape[0]
@@ -386,37 +387,51 @@
             part, one_hot, (((1,), (1,)), ((), ())), preferred_element_type=F32
         )
 
+    placed_sum[...] = grid
+
+
+def gradient_kernel(
+    weights, grid, spec_re, spec_im, field_re, field_im, tables,
+    grad, rim, total_re, total_im,
+):
+    kernels, period, _ = spec_re.shape
+    half = period // 2
+    tile = field_re.shape[1]
+    radius = (period - tile) // 2
     cols = pair(tables, 0, LANES, 2 * LANES)
     cols = (stacked((cols[0], cols[0])), cols[1])
     rows = stacked(pair(tables, 8, period, 2 * tile))
     total_re[...] = jnp.zeros((period, 2 * LANES), F32)
     total_im[...] = jnp.zeros((period, 2 * LANES), F32)
 
-    def step(k, carry):
-        weighted = grid * weights[k]
-        source = stacked((weighted * field_re[k], weighted * field_im[k]))
-        high, low = split(source)
+    def step(group, carry):
+        sources = []
+        for i in range(BATCH):
+            k = group * BATCH + i
+            weighted = grid[...] * weights[k]
+            sources += [weighted * field_re[k], weighted * field_im[k]]
+        high, low = split(stacked(sources))
         both = dot(jnp.concatenate([high, low], axis=1), cols[0]) + dot(high, cols[1])
-        real_cos, real_sin = halves(both[:tile])
-        imag_cos, imag_sin = halves(both[tile:])
-        wide_re = jnp.concatenate([real_cos + imag_sin, real_cos - imag_sin], axis=1)
-        wide_im = jnp.concatenate([imag_cos - real_sin, imag_cos + real_sin], axis=1)
-        tall_re = dot(rows, stacked(split(wide_re)))
-        tall_im = dot(rows, stacked(split(wide_im)))
-        tall_re = tall_re[:period] + tall_re[period:]
-        tall_im = tall_im[:period] + tall_im[period:]
-        for copy in fetch(k):
-            copy.wait()
-        for start, sign in ((0, 1.0), (half, -1.0)):
-            part = slice(start, start + half)
-            wave_re = tall_re[:half] + sign * tall_im[half:]
-            wave_im = tall_im[:half] - sign * tall_re[half:]
-            own_re, own_im = held[0, k, part], held[1, k, part]
-            total_re[part] += own_re * wave_re + own_im * wave_im
-            total_im[part] += own_re * wave_im - own_im * wave_re
+        for i in range(BATCH):
+            k = group * BATCH + i
+            real_cos, real_sin = halves(both[2 * i * tile : (2 * i + 1) * tile])
+            imag_cos, imag_sin = halves(both[(2 * i + 1) * tile : (2 * i + 2) * tile])
+            wide_re = jnp.concatenate([real_cos + imag_sin, real_cos - imag_sin], axis=1)
+            wide_im = jnp.concatenate([imag_cos - real_sin, imag_cos + real_sin], axis=1)
+            tall_re = dot(rows, stacked(split(wide_re)))
+            tall_im = dot(rows, stacked(split(wide_im)))
+            tall_re = tall_re[:period] + tall_re[period:]
+            tall_im = tall_im[:period] + tall_im[period:]
+            for start, sign in ((0, 1.0), (half, -1.0)):
+                part = slice(start, start + half)
+                wave_re = tall_re[:half] + sign * tall_im[half:]
+                wave_im = tall_im[:half] - sign * tall_re[half:]
+                own_re, own_im = spec_re[k, part], spec_im[k, part]
+                total_re[part] += own_re * wave_re + own_im * wave_im
+                total_im[part] += own_re * wave_im - own_im * wave_re
         return carry
 
-    lax.fori_loop(0, kernels, step, 0, unroll=UNROLL)
+    lax.fori_loop(0, kernels // BATCH, step, 0)
     pos_re, neg_re = total_re[:half], total_re[half:]
     pos_im, neg_im = total_im[:half], total_im[half:]
     back_rows = pair(tables, 6, period, period)
@@ -435,14 +450,13 @@
 VMEM = pl.BlockSpec(memory_space=pltpu.VMEM)
 SMEM = pl.BlockSpec(memory_space=pltpu.SMEM)
 ANY = pl.BlockSpec(memory_space=pl.ANY)
-HBM = pl.BlockSpec(memory_space=pltpu.HBM)
 
 
 def shape(*dims):
     return jax.ShapeDtypeStruct(dims, F32)
 
 
-def call(kernel, name, out_shape, in_specs, scratch=(), aliases=None, micros=1, vmem=10):
+def call(kernel, name, out_shape, in_specs, scratch=(), aliases=None, micros=1):
     return pl.pallas_call(
         kernel,
         out_shape=out_shape,
@@ -450,7 +464,7 @@
         out_specs=[VMEM] * len(out_shape),
         scratch_shapes=scratch,
         input_output_aliases=aliases or {},
-        compiler_params=pltpu.CompilerParams(vmem_limit_bytes=vmem * 1024 * 1024),
+        compiler_params=pltpu.CompilerParams(vmem_limit_bytes=10 * 1024 * 1024),
         cost_estimate=pl.CostEstimate(
             flops=micros * 10**9, bytes_accessed=2**20, transcendentals=0
         ),
@@ -474,14 +488,12 @@
     packed = shape(tile // 2, 2 * radius)
     devices = lax.axis_size("ty") * lax.axis_size("tx")
 
-    steps = 4
-    parts = count // steps
     spec = []
 
-    def spectra(step, *after):
+    def spectra(start, parts, *after):
         given = spec + list(after)
         *out, done = call(
-            functools.partial(spectra_kernel, step * parts, parts),
+            functools.partial(spectra_kernel, start, parts),
             "spectra",
             [shape(count, period, 2 * LANES)] * 2 + [token],
             [VMEM] * 2 + [ANY] * len(given),
@@ -492,24 +504,19 @@
         spec[:] = out
         return done
 
-    (transmit,) = call(start_kernel, "start", [shape(tile, tile)], [VMEM])(latent)
-    partner = swap("tx", transmit)
-    done = spectra(0)
-    rim, done = call(relay_columns_kernel, "relay", [packed, token], [VMEM, ANY])(
-        partner, done
-    )
-    rim = ring("tx", rim)
-    done = spectra(1, done)
+    partner, outside = swap("tx", latent), swap_outside("tx", latent)
+    quarter = count // 4
+    done = spectra(0, quarter)
     band, done = call(
         band_kernel, "band", [shape(tile, period), token], [VMEM] * 3 + [ANY]
-    )(transmit, partner, rim, done)
+    )(latent, partner, outside, done)
     partner = swap("ty", band)
-    done = spectra(2, done)
+    done = spectra(quarter, quarter, done)
     rim, done = call(
         relay_rows_kernel, "relay", [shape(radius, period), token], [VMEM, ANY]
     )(partner, done)
     rim = ring("ty", rim)
-    spectra(3, done)
+    spectra(2 * quarter, count - 2 * quarter, done)
 
     field_re, field_im, sampled, copies = call(
         field_kernel,
@@ -525,38 +532,33 @@
     )(socs_weights, *spec, band, partner, rim, edge_pixels, inv_slope, tables)
 
     gathered = gather_all(copies).reshape(devices, 2 * samples)
-    grad, rim, tail_mean = call(
+    grid, tail_mean = call(
+        source_kernel,
+        "source",
+        [shape(tile, LANES), shape(1, 1)],
+        [SMEM] * 3 + [VMEM] * 3,
+        micros=2,
+    )(socs_weights, dose_scale, threshold_pick, gathered, sampled, edge_pixels)
+    grad, rim = call(
         gradient_kernel,
         "gradient",
-        [shape(period, period), shape(radius, period), shape(1, 1)],
-        [SMEM] * 3 + [VMEM] * 3 + [HBM] * 2 + [VMEM] * 3,
-        scratch=[pltpu.VMEM((period, 2 * LANES), F32)] * 2
-        + [
-            pltpu.VMEM((2, count, period, 2 * LANES), F32),
-            pltpu.SemaphoreType.DMA((2, count)),
-        ],
-        micros=9,
-        vmem=60,
-    )(
-        socs_weights, dose_scale, threshold_pick, gathered, sampled, edge_pixels,
-        *spec, field_re, field_im, tables,
-    )
+        [shape(period, period), shape(radius, period)],
+        [SMEM] + [VMEM] * 6,
+        scratch=[pltpu.VMEM((period, 2 * LANES), F32)] * 2,
+        micros=6,
+    )(socs_weights, grid, *spec, field_re, field_im, tables)
 
     rim = ring("ty", rim, back=True)
     (partner,) = call(fold_rows_kernel, "fold", [shape(tile, period)], [VMEM] * 2)(
         grad, rim
     )
     partner = swap("ty", partner)
-    band, rim = call(
-        fold_band_kernel, "fold", [shape(tile, period), packed], [VMEM] * 2
+    band, near, far = call(
+        fold_band_kernel, "fold", [shape(tile, period)] + [packed] * 2, [VMEM] * 2
     )(grad, partner)
-    rim = ring("tx", rim, back=True)
-    (partner,) = call(fold_columns_kernel, "fold", [shape(tile, tile)], [VMEM] * 2)(
-        band, rim
-    )
-    partner = swap("tx", partner)
-    (steering,) = call(finish_kernel, "finish", [shape(tile, tile)], [VMEM] * 3)(
-        band, partner, latent
+    near, far = swap("tx", near), swap_outside("tx", far)
+    (steering,) = call(finish_kernel, "finish", [shape(tile, tile)], [VMEM] * 4)(
+        band, near, far, latent
     )
     return (steering, tail_mean.reshape(1))
 

time: 66.6 us -> 55 us (0.83)
  the two profiles are of different devices: /device:TPU:0 before, /device:TPU:4 now
where the time goes in v7:
time: 55 us; the launch traced here: 54.8 us
  Pallas kernels  17.7 us (32%)
  starting transfers between devices  16.5 us (30%)
  waiting for transfers between devices  15.1 us (27%)
  local copies, waits for them, and re-layouts  3.86 us (7%)
  between operations  1.52 us (3%)
    ppermute x2, starting transfers between devices, swap_outside(): return lax.ppermute(x, axis, pairs)  7.63 us
    all_to_all x1, starting transfers between devices, gather_all(): return lax.all_to_all(copies, ('ty', 'tx'), 0, 0, tiled=True)  5.75 us
    all_to_all x1, waiting for transfers between devices, gather_all(): return lax.all_to_all(copies, ('ty', 'tx'), 0, 0, tiled=True)  5.64 us
    pallas_call x1, Pallas kernels, body(): call(gradient_kernel, 'gradient', [shape(period, period), shape(radius, p...  5.29 us
    pallas_call x1, Pallas kernels, body(): call(field_kernel, 'field', [shape(count, tile, LANES)] * 2 + [shape(1, 2...  5.2 us
    pallas_call x3, Pallas kernels, spectra(): call(functools.partial(spectra_kernel, start, parts), 'spectra', [shape(c...  4.58 us
    ppermute x2, waiting for transfers between devices, ring(): return lax.ppermute(x, axis, [(b, a) if back else (a, b) for a, b in pairs])  4.15 us
    ppermute x2, waiting for transfers between devices, swap_outside(): return lax.ppermute(x, axis, pairs)  3.88 us
  transfers between devices with their start and end apart: 9, of which 5 were waited for; matrix products, arithmetic and copies ran while one was open for 4% of the time, Pallas kernels for 8%

profile of v7, /device:TPU:4, one launch (start us, length us, event | category | flops | bytes accessed | tf_op | source)
XLA Modules:
  0.0 54.8 jit_solution(7444648185438852042)
XLA Ops:
  0.7 4.9 %collective-permute-start.1 = (f32[96,96]{1,0:T(8,128)}, f32[96,96]{1,0:T(8,128)S(1)}, u32[]{:S(2)}, u32[]{:S(2)}) collective-permute-start(f32[96,96]{1,0:T(8,128)} %latent.1), channel_id=1, source_target_pairs={{0,0},{7,7},{1,2},{2,1},{3,4},{4,3},{5,6},{6,5},{8,8},{15,15},{9,1... | collective-permute-start | bytes 110600 | tf_op jit(solution)/shard_map/ppermute | solution.py:94
  5.7 2.2 %copy.20.kern = f32[2,12,129,129]{3,2,1,0:T(8,128)S(1)} copy(f32[2,12,129,129]{3,0,2,1:T(2,128)} %param.9) | data formatting | bytes 3195072 | tf_op args[1]
  7.9 1.1 %spectra.3 = (f32[12,224,256]{2,1,0:T(8,128)S(1)}, f32[12,224,256]{2,1,0:T(8,128)S(1)}, f32[8,128]{1,0:T(8,128)S(1)}) custom-call(f32[2,12,129,129]{3,2,1,0:T(8,128)S(1)} %copy.20.kern, bf16[10,256,256]{2,1,0:T(8,128)(2,1)S(1)} %copy-done.2), custom_call_target="tpu_custom_call" | custom-call | flops 2000000000 | bytes 1048576 | tf_op jit(solution)/shard_map/spectra/pallas_call | solution.py:495
  9.1 0.2 band.1
  9.4 1.1 %spectra.4 = (f32[12,224,256]{2,1,0:T(8,128)S(1)}, f32[12,224,256]{2,1,0:T(8,128)S(1)}, f32[8,128]{1,0:T(8,128)S(1)}) custom-call(f32[2,12,129,129]{3,2,1,0:T(8,128)S(1)} %copy.20.kern, bf16[10,256,256]{2,1,0:T(8,128)(2,1)S(1)} %copy-done.2, f32[12,224,256]{2,1,0:T(8,128)S(1)} %get-tuple-element.25.rest_0_, ...), custom_call_target="tpu_custom_call", output_to_operand_aliasing={{0}: (2, {}), {1}: (3, {})} | custom-call | flops 2000000000 | bytes 1048576 | tf_op jit(solution)/shard_map/spectra/pallas_call | solution.py:495
  10.5 0.2 collective-permute-done.2.partner
  10.7 1.5 %collective-permute-start.3 = (f32[64,224]{1,0:T(8,128)S(1)}, f32[64,224]{1,0:T(8,128)S(1)}, u32[]{:S(2)}, u32[]{:S(2)}) collective-permute-start(f32[64,224]{1,0:T(8,128)S(1)} %get-tuple-element.36), channel_id=1, source_target_pairs={{0,16},{16,24},{24,8},{8,0},{1,17},{17,25},{25,9},{9,1},{2,18},{18... | collective-permute-start | bytes 172040 | tf_op jit(solution)/shard_map/ppermute | solution.py:101
  12.2 2.3 %spectra.5 = (f32[12,224,256]{2,1,0:T(8,128)S(1)}, f32[12,224,256]{2,1,0:T(8,128)S(1)}, f32[8,128]{1,0:T(8,128)}) custom-call(f32[2,12,129,129]{3,2,1,0:T(8,128)S(1)} %copy.20.kern, bf16[10,256,256]{2,1,0:T(8,128)(2,1)S(1)} %copy-done.2, f32[12,224,256]{2,1,0:T(8,128)S(1)} %get-tuple-element.29.rest_0_, ...), custom_call_target="tpu_custom_call", output_to_operand_aliasing={{0}: (2, {}), {1}: (3, {})} | custom-call | flops 2000000000 | bytes 1048576 | tf_op jit(solution)/shard_map/spectra/pallas_call | solution.py:495
  14.6 5.2 %field.1 = (f32[12,96,128]{2,1,0:T(8,128)S(1)}, f32[12,96,128]{2,1,0:T(8,128)S(1)}, f32[1,512]{1,0:T(1,128)S(1)}, f32[32,1,512]{2,1,0:T(1,128)}) custom-call(f32[12]{0:T(128)S(1)} %copy-done.8, f32[12,224,256]{2,1,0:T(8,128)S(1)} %get-tuple-element.34.spec_re, f32[12,224,256]{2,1,0:T(8,128)S(1)} %get-tuple-element.35.spec_im, ...), custom_call_target="tpu_custom_call" | custom-call | flops 7000000000 | bytes 1048576 | tf_op jit(solution)/shard_map/field/pallas_call | solution.py:521
  19.8 0.8 %copy-done.9 = f32[12,96,128]{2,1,0:T(8,128)} copy-done((f32[12,96,128]{2,1,0:T(8,128)}, f32[12,96,128]{2,1,0:T(8,128)S(1)}, u32[]{:S(2)}) %copy-start.9) | copy-done | bytes 589848
  20.6 5.8 %all-to-all-start = ((f32[32,1,512]{2,1,0:T(1,128)}), f32[32,1,512]{2,1,0:T(1,128)S(1)}, u32[]{:S(2)}, u32[]{:S(2)}) async-start(f32[32,1,512]{2,1,0:T(1,128)} %get-tuple-element.37), calls=%async_computation | async-start | bytes 131072 | tf_op jit(solution)/shard_map/all_to_all | solution.py:476
  27.1 5.6 %all-to-all-done = f32[32,1,512]{2,1,0:T(1,128)S(1)} async-done(((f32[32,1,512]{2,1,0:T(1,128)}), f32[32,1,512]{2,1,0:T(1,128)S(1)}, u32[]{:S(2)}, u32[]{:S(2)}) %all-to-all-start) | async-done | bytes 65568 | tf_op jit(solution)/shard_map/all_to_all | solution.py:476
  32.7 1.5 %source.1 = (f32[96,128]{1,0:T(8,128)S(1)}, f32[1,1]{1,0:T(1,128)}) custom-call(f32[12]{0:T(128)S(1)} %copy-done.8, f32[8]{0:T(128)S(1)} %copy-done.7, s32[1]{0:T(128)S(6)} %copy.28.pick, f32[32,512]{1,0:T(8,128)S(1)} %bitcast.4, f32[1,512]{1,0:T(1,128)S(1)} %get-tuple-element.38.sampled, s32[1,256]{1,0:T(1,128)S(1)} %copy-done.6), custom_call_target="tpu_custom_call" | custom-call | flops 2000000000 | bytes 1048576 | tf_op jit(solution)/shard_map/source/pallas_call | solution.py:535
  34.2 0.3 copy-done.1
  34.5 0.4 copy-done.3
  34.9 0.1 copy-done.10
  35.0 5.3 %gradient.1 = (f32[224,224]{1,0:T(8,128)S(1)}, f32[64,224]{1,0:T(8,128)S(1)}) custom-call(f32[12]{0:T(128)S(1)} %copy-done.8, f32[96,128]{1,0:T(8,128)S(1)} %get-tuple-element.39.grid, f32[12,224,256]{2,1,0:T(8,128)S(1)} %get-tuple-element.34.spec_re, f32[12,224,256]{2,1,0:T(8,128)S(1)} %copy-done.1, f32[12,96,128]{2,1,0:T(8,128)S(1)} %get-tuple-element.40.field_re, ...), custom_call_target="tpu_custom_call" | custom-call | flops 6000000000 | bytes 1048576 | tf_op jit(solution)/shard_map/gradient/pallas_call | solution.py:542
  40.3 0.1 collective-permute-start.4
  40.4 4.2 %collective-permute-done.4.rim = f32[64,224]{1,0:T(8,128)S(1)} collective-permute-done((f32[64,224]{1,0:T(8,128)S(1)}, f32[64,224]{1,0:T(8,128)S(1)}, u32[]{:S(2)}, u32[]{:S(2)}) %collective-permute-start.4) | collective-permute-done | bytes 57376 | tf_op jit(solution)/shard_map/ppermute | solution.py:101
  44.7 1.3 %collective-permute-done.5.partner = f32[96,224]{1,0:T(8,128)S(1)} collective-permute-done((f32[96,224]{1,0:T(8,128)S(1)}, f32[96,224]{1,0:T(8,128)S(1)}, u32[]{:S(2)}, u32[]{:S(2)}) %collective-permute-start.5) | collective-permute-done | bytes 86048 | tf_op jit(solution)/shard_map/ppermute | solution.py:86
  46.1 1.3 %collective-permute-start.6 = (f32[48,128]{1,0:T(8,128)S(1)}, f32[48,128]{1,0:T(8,128)S(1)}, u32[]{:S(2)}, u32[]{:S(2)}) collective-permute-start(f32[48,128]{1,0:T(8,128)S(1)} %get-tuple-element.45), channel_id=1, source_target_pairs={{0,1},{1,0},{2,3},{3,2},{4,5},{5,4},{6,7},{7,6},{8,9},{9,8},{10,11... | collective-permute-start | bytes 73736 | tf_op jit(solution)/shard_map/ppermute | solution.py:86
  47.4 2.7 %collective-permute-start.7 = (f32[48,128]{1,0:T(8,128)S(1)}, f32[48,128]{1,0:T(8,128)S(1)}, u32[]{:S(2)}, u32[]{:S(2)}) collective-permute-start(f32[48,128]{1,0:T(8,128)S(1)} %get-tuple-element.46), channel_id=1, source_target_pairs={{0,0},{7,7},{1,2},{2,1},{3,4},{4,3},{5,6},{6,5},{8,8},{15,15},{9,1... | collective-permute-start | bytes 73736 | tf_op jit(solution)/shard_map/ppermute | solution.py:94
  50.1 3.9 %collective-permute-done.7.far = f32[48,128]{1,0:T(8,128)S(1)} collective-permute-done((f32[48,128]{1,0:T(8,128)S(1)}, f32[48,128]{1,0:T(8,128)S(1)}, u32[]{:S(2)}, u32[]{:S(2)}) %collective-permute-start.7) | collective-permute-done | bytes 24608 | tf_op jit(solution)/shard_map/ppermute | solution.py:94
  54.0 0.8 %finish.1 = f32[96,96]{1,0:T(8,128)} custom-call(f32[96,224]{1,0:T(8,128)S(1)} %get-tuple-element.44.band, f32[48,128]{1,0:T(8,128)S(1)} %collective-permute-done.6.near, f32[48,128]{1,0:T(8,128)S(1)} %collective-permute-done.7.far, f32[96,96]{1,0:T(8,128)S(1)} %copy-done.4), custom_call_target="tpu_custom_call" | custom-call | flops 1000000000 | bytes 1048576 | tf_op jit(solution)/shard_map/finish/pallas_call | solution.py:560
  (29 shorter events, 0.4 us)
Async XLA Ops:
  0.6 7.3 %copy-start.2 = (bf16[10,256,256]{2,1,0:T(8,128)(2,1)S(1)}, bf16[10,256,256]{2,1,0:T(8,128)(2,1)}, u32[]{:S(2)}) copy-start(bf16[10,256,256]{2,1,0:T(8,128)(2,1)} %constant.2.clone.tables) | copy-start | bytes 3932164
  0.6 8.4 %collective-permute-start = (f32[96,96]{1,0:T(8,128)}, f32[96,96]{1,0:T(8,128)S(1)}, u32[]{:S(2)}, u32[]{:S(2)}) collective-permute-start(f32[96,96]{1,0:T(8,128)} %latent.1), channel_id=1, source_target_pairs={{0,1},{1,0},{2,3},{3,2},{4,5},{5,4},{6,7},{7,6},{8,9},{9,8},{10,11... | collective-permute-start | bytes 110600 | tf_op jit(solution)/shard_map/ppermute | solution.py:86
  0.7 8.3 %collective-permute-start.1 = (f32[96,96]{1,0:T(8,128)}, f32[96,96]{1,0:T(8,128)S(1)}, u32[]{:S(2)}, u32[]{:S(2)}) collective-permute-start(f32[96,96]{1,0:T(8,128)} %latent.1), channel_id=1, source_target_pairs={{0,0},{7,7},{1,2},{2,1},{3,4},{4,3},{5,6},{6,5},{8,8},{15,15},{9,1... | collective-permute-start | bytes 110600 | tf_op jit(solution)/shard_map/ppermute | solution.py:94
  7.9 1.2 %copy-start.4 = (f32[96,96]{1,0:T(8,128)S(1)}, f32[96,96]{1,0:T(8,128)}, u32[]{:S(2)}) copy-start(f32[96,96]{1,0:T(8,128)} %latent.1) | copy-start | bytes 110596
  9.3 1.4 %collective-permute-start.2 = (f32[96,224]{1,0:T(8,128)S(1)}, f32[96,224]{1,0:T(8,128)S(1)}, u32[]{:S(2)}, u32[]{:S(2)}) collective-permute-start(f32[96,224]{1,0:T(8,128)S(1)} %get-tuple-element.31.band), channel_id=1, source_target_pairs={{0,8},{8,0},{16,24},{24,16},{1,9},{9,1},{17,25},{25,17},{2,10},{10... | collective-permute-start | bytes 258056 | tf_op jit(solution)/shard_map/ppermute | solution.py:86
  10.7 3.9 %collective-permute-start.3 = (f32[64,224]{1,0:T(8,128)S(1)}, f32[64,224]{1,0:T(8,128)S(1)}, u32[]{:S(2)}, u32[]{:S(2)}) collective-permute-start(f32[64,224]{1,0:T(8,128)S(1)} %get-tuple-element.36), channel_id=1, source_target_pairs={{0,16},{16,24},{24,8},{8,0},{1,17},{17,25},{25,9},{9,1},{2,18},{18... | collective-permute-start | bytes 172040 | tf_op jit(solution)/shard_map/ppermute | solution.py:101
  12.2 2.4 %copy-start.5 = (f32[1,256]{1,0:T(1,128)S(1)}, f32[1,256]{1,0:T(1,128)}, u32[]{:S(2)}) copy-start(f32[1,256]{1,0:T(1,128)} %slopes.1) | copy-start | bytes 3076
  12.2 2.4 %copy-start.6 = (s32[1,256]{1,0:T(1,128)S(1)}, s32[1,256]{1,0:T(1,128)}, u32[]{:S(2)}) copy-start(s32[1,256]{1,0:T(1,128)} %pixels.3) | copy-start | bytes 3076
  12.2 2.4 %copy-start.8 = (f32[12]{0:T(128)S(1)}, f32[12]{0:T(128)}, u32[]{:S(2)}) copy-start(f32[12]{0:T(128)} %weights.5) | copy-start | bytes 148
  14.6 5.3 %copy-start = (f32[12,224,256]{2,1,0:T(8,128)}, f32[12,224,256]{2,1,0:T(8,128)S(1)}, u32[]{:S(2)}) copy-start(f32[12,224,256]{2,1,0:T(8,128)S(1)} %get-tuple-element.35.spec_im) | copy-start | bytes 8257540
  14.6 18.1 %copy-start.7 = (f32[8]{0:T(128)S(1)}, f32[8]{0:T(128)}, u32[]{:S(2)}) copy-start(f32[8]{0:T(128)} %doses.1) | copy-start | bytes 100
  19.8 0.8 %copy-start.9 = (f32[12,96,128]{2,1,0:T(8,128)}, f32[12,96,128]{2,1,0:T(8,128)S(1)}, u32[]{:S(2)}) copy-start(f32[12,96,128]{2,1,0:T(8,128)S(1)} %get-tuple-element.41.field_im) | copy-start | bytes 1769476
  20.6 12.1 %all-to-all-start = ((f32[32,1,512]{2,1,0:T(1,128)}), f32[32,1,512]{2,1,0:T(1,128)S(1)}, u32[]{:S(2)}, u32[]{:S(2)}) async-start(f32[32,1,512]{2,1,0:T(1,128)} %get-tuple-element.37), calls=%async_computation | async-start | bytes 131072 | tf_op jit(solution)/shard_map/all_to_all | solution.py:476
  32.7 1.8 %copy-start.1 = (f32[12,224,256]{2,1,0:T(8,128)S(1)}, f32[12,224,256]{2,1,0:T(8,128)}, u32[]{:S(2)}) copy-start(f32[12,224,256]{2,1,0:T(8,128)} %copy-done) | copy-start | bytes 8257540
  32.7 2.1 %copy-start.3 = (bf16[10,256,256]{2,1,0:T(8,128)(2,1)S(1)}, bf16[10,256,256]{2,1,0:T(8,128)(2,1)}, u32[]{:S(2)}) copy-start(bf16[10,256,256]{2,1,0:T(8,128)(2,1)} %constant.2.clone.tables) | copy-start | bytes 3932164
  32.7 2.3 %copy-start.10 = (f32[12,96,128]{2,1,0:T(8,128)S(1)}, f32[12,96,128]{2,1,0:T(8,128)}, u32[]{:S(2)}) copy-start(f32[12,96,128]{2,1,0:T(8,128)} %copy-done.9) | copy-start | bytes 1769476
  40.3 4.3 %collective-permute-start.4 = (f32[64,224]{1,0:T(8,128)S(1)}, f32[64,224]{1,0:T(8,128)S(1)}, u32[]{:S(2)}, u32[]{:S(2)}) collective-permute-start(f32[64,224]{1,0:T(8,128)S(1)} %get-tuple-element.43), channel_id=1, source_target_pairs={{16,0},{24,16},{8,24},{0,8},{17,1},{25,17},{9,25},{1,9},{18,2},{26... | collective-permute-start | bytes 172040 | tf_op jit(solution)/shard_map/ppermute | solution.py:101
  44.6 1.4 %collective-permute-start.5 = (f32[96,224]{1,0:T(8,128)S(1)}, f32[96,224]{1,0:T(8,128)S(1)}, u32[]{:S(2)}, u32[]{:S(2)}) collective-permute-start(f32[96,224]{1,0:T(8,128)S(1)} %fold.2), channel_id=1, source_target_pairs={{0,8},{8,0},{16,24},{24,16},{1,9},{9,1},{17,25},{25,17},{2,10},{10... | collective-permute-start | bytes 258056 | tf_op jit(solution)/shard_map/ppermute | solution.py:86
  46.1 4.0 %collective-permute-start.6 = (f32[48,128]{1,0:T(8,128)S(1)}, f32[48,128]{1,0:T(8,128)S(1)}, u32[]{:S(2)}, u32[]{:S(2)}) collective-permute-start(f32[48,128]{1,0:T(8,128)S(1)} %get-tuple-element.45), channel_id=1, source_target_pairs={{0,1},{1,0},{2,3},{3,2},{4,5},{5,4},{6,7},{7,6},{8,9},{9,8},{10,11... | collective-permute-start | bytes 73736 | tf_op jit(solution)/shard_map/ppermute | solution.py:86
  47.4 6.6 %collective-permute-start.7 = (f32[48,128]{1,0:T(8,128)S(1)}, f32[48,128]{1,0:T(8,128)S(1)}, u32[]{:S(2)}, u32[]{:S(2)}) collective-permute-start(f32[48,128]{1,0:T(8,128)S(1)} %get-tuple-element.46), channel_id=1, source_target_pairs={{0,0},{7,7},{1,2},{2,1},{3,4},{4,3},{5,6},{6,5},{8,8},{15,15},{9,1... | collective-permute-start | bytes 73736 | tf_op jit(solution)/shard_map/ppermute | solution.py:94

commit v8 on v7

--- a/solution.py
+++ b/solution.py
@@ -45,22 +45,43 @@
 
 def wave_tables(period, tile):
     half = period // 2
+    turn = (np.arange(half) + 0.5) * (2.0 * math.pi / period)
+    size = 2 * LANES
+
+    def parts(table):
+        high = table.astype(ml_dtypes.bfloat16)
+        return high, (table - high.astype(np.float64)).astype(ml_dtypes.bfloat16)
+
+    def both(places):
+        angle = turn[:, None] * places[None, :]
+        return np.cos(angle), np.sin(angle)
+
+    def whole_table(places, by_lane):
+        cos, sin = both(places)
+        out = np.zeros((size, size))
+        out[:half, : len(places)] = cos
+        start = LANES if by_lane else half
+        out[start : start + half, : len(places)] = sin
+        return out
+
     place = np.arange(period)
-    angle = (np.arange(half)[None, :] + 0.5) * place[:, None] * (2.0 * math.pi / period)
-    cos, sin = np.cos(angle), np.sin(angle)
-    wide = np.zeros((2 * LANES, 2 * LANES))
-    tall = np.zeros((2 * LANES, 2 * LANES))
-    wide[:period, :half] = cos
-    wide[:period, LANES : LANES + half] = sin
-    tall[:half, :period] = cos.T
-    tall[half:period, :period] = sin.T
-    out = np.zeros((10, 2 * LANES, 2 * LANES), ml_dtypes.bfloat16)
-    for first, table in ((0, wide), (2, tall), (4, wide.T), (6, tall.T)):
-        out[first] = table.astype(ml_dtypes.bfloat16)
-        out[first + 1] = (table - out[first].astype(np.float64)).astype(ml_dtypes.bfloat16)
-    out[8, :, :tile] = out[2, :, :tile]
-    out[8, :, tile : 2 * tile] = out[2, :, :tile]
-    out[9, :, :tile] = out[3, :, :tile]
+    wide = whole_table(place, True)
+    tall = whole_table(place, False)
+    centred = whole_table(place - (tile - 1) / 2, False)
+    out = np.zeros((12, size, size), ml_dtypes.bfloat16)
+    for first, table in ((0, wide.T), (2, tall), (4, wide), (6, centred), (8, centred.T)):
+        out[first], out[first + 1] = parts(table)
+    rows = tile // 2
+    for i, table in enumerate(both(np.arange(rows) + 0.5)):
+        high, low = parts(table)
+        top = 2 * rows * i
+        out[10, top : top + rows, :half] = high.T
+        out[10, top : top + rows, half:period] = high.T
+        out[10, top + rows : top + 2 * rows, :half] = low.T
+        top = half * i
+        out[11, top : top + half, :rows] = high
+        out[11, top : top + half, rows : 2 * rows] = high
+        out[11, top : top + half, 2 * rows : 3 * rows] = low
     return out
 
 
@@ -148,7 +169,7 @@
 
     def step(group, carry):
         first = start + group * BATCH
-        planes = along_lanes([kern[c, first + i] for i in range(BATCH) for c in range(2)])
+        planes = along_lanes([kern[c, group * BATCH + i] for i in range(BATCH) for c in range(2)])
         for i in range(BATCH):
             k = first + i
             (real, real_tail), (imag, imag_tail) = planes[2 * i : 2 * i + 2]
@@ -214,14 +235,19 @@
     out[tile - radius :] += bottom
 
 
-def fold_band_kernel(grad, partner, band, near, far):
+def fold_band_kernel(grad, partner, band, far):
+    tile = band.shape[0]
+    radius = far.shape[1] // 2
+    lower, _ = place_in_pair("tx")
+    band[...] = grad[radius : radius + tile] + partner[...]
+    far[...] = jnp.where(lower, pack(band[:, :radius]), pack(band[:, radius + tile :]))
+
+
+def near_rim_kernel(band, near):
     tile = band.shape[0]
     radius = near.shape[1] // 2
     lower, _ = place_in_pair("tx")
-    band[...] = grad[radius : radius + tile] + partner[...]
-    left, right = pack(band[:, :radius]), pack(band[:, radius + tile :])
-    near[...] = jnp.where(lower, right, left)
-    far[...] = jnp.where(lower, left, right)
+    near[...] = jnp.where(lower, pack(band[:, radius + tile :]), pack(band[:, :radius]))
 
 
 def finish_kernel(band, near, far, latent, steering):
@@ -246,7 +272,8 @@
 
 def sample_places(pixels, tile):
     row = ((pixels.astype(F32) + 0.5) * (1.0 / tile)).astype(jnp.int32)
-    return row, pixels - row * tile
+    held = jnp.where(row < tile // 2, tile - 1 - row, row - tile // 2)
+    return held, pixels - row * tile
 
 
 def field_kernel(
@@ -263,7 +290,7 @@
     framed[radius + tile :] = jnp.where(lower, partner[:radius], outer)
     framed[radius : radius + tile] = band[...]
     wide = dot3(split(framed[...]), pair(tables, 0, period, 2 * LANES))
-    tall = dot3(pair(tables, 2, period, period), split(wide)) * (1.0 / (period * period))
+    tall = dot3(pair(tables, 6, period, period), split(wide)) * (1.0 / (period * period))
     cos_cos, cos_sin = halves(tall[:half])
     sin_cos, sin_sin = halves(tall[half:])
     same, other = cos_cos - sin_sin, cos_cos + sin_sin
@@ -272,8 +299,14 @@
     mask[1, :, :LANES], mask[1, :, LANES:] = -joint, -cross
     mask[2, :, :LANES], mask[2, :, LANES:] = other, same
     mask[3, :, :LANES], mask[3, :, LANES:] = cross, joint
-    lift = pair(tables, 6, tile, period)
-    lift = (lift[0], stacked(lift))
+    cos_lift = tables[10, :tile, :period]
+    sin_lift = tables[10, tile : 2 * tile, :period]
+    rows = tile // 2
+
+    def lift(table, x):
+        out = dot(table, stacked(split(x)))
+        return out[:rows] + out[rows:]
+
     across = pair(tables, 4, 2 * LANES, LANES)
     across = (across[0], jnp.concatenate(across, axis=1))
 
@@ -284,10 +317,12 @@
         up_im = mask[0] * pos_im + mask[1] * pos_re
         down_re = mask[2] * neg_re - mask[3] * neg_im
         down_im = mask[2] * neg_im + mask[3] * neg_re
-        for_re = jnp.concatenate([up_re + down_re, down_im - up_im], axis=0)
-        for_im = jnp.concatenate([up_im + down_im, up_re - down_re], axis=0)
-        re_pos, re_neg = halves(dot3_stacked(lift, split(for_re)))
-        im_pos, im_neg = halves(dot3_stacked(lift, split(for_im)))
+        even_re = lift(cos_lift, up_re + down_re)
+        even_im = lift(cos_lift, up_im + down_im)
+        odd_re = lift(sin_lift, up_im - down_im)
+        odd_im = lift(sin_lift, up_re - down_re)
+        re_pos, re_neg = halves(stacked((even_re - odd_re, even_re + odd_re)))
+        im_pos, im_neg = halves(stacked((even_im + odd_im, even_im - odd_im)))
         rows_re = jnp.concatenate([re_pos + re_neg, im_neg - im_pos], axis=1)
         rows_im = jnp.concatenate([im_pos + im_neg, re_pos - re_neg], axis=1)
         return [rows_re, rows_im]
@@ -400,7 +435,20 @@
     radius = (period - tile) // 2
     cols = pair(tables, 0, LANES, 2 * LANES)
     cols = (stacked((cols[0], cols[0])), cols[1])
-    rows = stacked(pair(tables, 8, period, 2 * tile))
+    rows = tile // 2
+    cos_rows = tables[11, :half, : 3 * rows]
+    sin_rows = tables[11, half:period, : 3 * rows]
+
+    def along_rows(wide):
+        out = []
+        for table, x in (
+            (cos_rows, wide[:rows] + wide[rows:]),
+            (sin_rows, wide[:rows] - wide[rows:]),
+        ):
+            high, low = split(x)
+            out.append(dot(table, stacked((high, low, high))))
+        return out
+
     total_re[...] = jnp.zeros((period, 2 * LANES), F32)
     total_im[...] = jnp.zeros((period, 2 * LANES), F32)
 
@@ -418,14 +466,12 @@
             imag_cos, imag_sin = halves(both[(2 * i + 1) * tile : (2 * i + 2) * tile])
             wide_re = jnp.concatenate([real_cos + imag_sin, real_cos - imag_sin], axis=1)
             wide_im = jnp.concatenate([imag_cos - real_sin, imag_cos + real_sin], axis=1)
-            tall_re = dot(rows, stacked(split(wide_re)))
-            tall_im = dot(rows, stacked(split(wide_im)))
-            tall_re = tall_re[:period] + tall_re[period:]
-            tall_im = tall_im[:period] + tall_im[period:]
+            cos_re, sin_re = along_rows(wide_re)
+            cos_im, sin_im = along_rows(wide_im)
             for start, sign in ((0, 1.0), (half, -1.0)):
                 part = slice(start, start + half)
-                wave_re = tall_re[:half] + sign * tall_im[half:]
-                wave_im = tall_im[:half] - sign * tall_re[half:]
+                wave_re = cos_re + sign * sin_im
+                wave_im = cos_im - sign * sin_re
                 own_re, own_im = spec_re[k, part], spec_im[k, part]
                 total_re[part] += own_re * wave_re + own_im * wave_im
                 total_im[part] += own_re * wave_im - own_im * wave_re
@@ -434,7 +480,7 @@
     lax.fori_loop(0, kernels // BATCH, step, 0)
     pos_re, neg_re = total_re[:half], total_re[half:]
     pos_im, neg_im = total_im[:half], total_im[half:]
-    back_rows = pair(tables, 6, period, period)
+    back_rows = pair(tables, 8, period, period)
     back_rows = (back_rows[0], stacked(back_rows))
     for_re = jnp.concatenate([pos_re + neg_re, neg_im - pos_im], axis=0)
     for_im = jnp.concatenate([pos_im + neg_im, pos_re - neg_re], axis=0)
@@ -500,7 +546,7 @@
             scratch=[pltpu.VMEM((period, LANES), F32)],
             aliases={2: 0, 3: 1} if spec else None,
             micros=2,
-        )(kernels, tables, *given)
+        )(kernels[:, start : start + parts], tables, *given)
         spec[:] = out
         return done
 
@@ -553,10 +599,12 @@
         grad, rim
     )
     partner = swap("ty", partner)
-    band, near, far = call(
-        fold_band_kernel, "fold", [shape(tile, period)] + [packed] * 2, [VMEM] * 2
+    band, far = call(
+        fold_band_kernel, "fold", [shape(tile, period), packed], [VMEM] * 2
     )(grad, partner)
-    near, far = swap("tx", near), swap_outside("tx", far)
+    far = swap_outside("tx", far)
+    (near,) = call(near_rim_kernel, "near", [packed], [VMEM])(band)
+    near = swap("tx", near)
     (steering,) = call(finish_kernel, "finish", [shape(tile, tile)], [VMEM] * 4)(
         band, near, far, latent
     )

time: 55 us -> 56 us (1.018)
  local copies, waits for them, and re-layouts: 3.86 us -> 5.26 us
    slice x0 -> x3, local copies, waits for them, and re-layouts: none -> 3.24 us  [spectra(): kernels[:, start:start + parts]]
    unnamed x24 -> x26, local copies, waits for them, and re-layouts: 3.86 us -> 2.02 us
where the time goes in v8:
time: 56 us; the launch traced here: 55.7 us
  Pallas kernels  17.5 us (31%)
  starting transfers between devices  16.3 us (29%)
  waiting for transfers between devices  15.1 us (27%)
  local copies, waits for them, and re-layouts  5.26 us (9%)
  between operations  1.56 us (3%)
    ppermute x2, starting transfers between devices, swap_outside(): return lax.ppermute(x, axis, pairs)  7.63 us
    all_to_all x1, waiting for transfers between devices, gather_all(): return lax.all_to_all(copies, ('ty', 'tx'), 0, 0, tiled=True)  5.64 us
    all_to_all x1, starting transfers between devices, gather_all(): return lax.all_to_all(copies, ('ty', 'tx'), 0, 0, tiled=True)  5.47 us
    pallas_call x1, Pallas kernels, body(): call(field_kernel, 'field', [shape(count, tile, LANES)] * 2 + [shape(1, 2...  5.15 us
    pallas_call x1, Pallas kernels, body(): call(gradient_kernel, 'gradient', [shape(period, period), shape(radius, p...  5.01 us
    pallas_call x3, Pallas kernels, spectra(): call(functools.partial(spectra_kernel, start, parts), 'spectra', [shape(c...  4.6 us
    ppermute x2, waiting for transfers between devices, ring(): return lax.ppermute(x, axis, [(b, a) if back else (a, b) for a, b in pairs])  4.15 us
    ppermute x2, waiting for transfers between devices, swap_outside(): return lax.ppermute(x, axis, pairs)  3.88 us
  transfers between devices with their start and end apart: 9, of which 5 were waited for; matrix products, arithmetic and copies ran while one was open for 4% of the time, Pallas kernels for 8%

profile of v8, /device:TPU:4, one launch (start us, length us, event | category | flops | bytes accessed | tf_op | source)
XLA Modules:
  0.0 55.7 jit_solution(10423648038702185416)
XLA Ops:
  0.7 4.9 %collective-permute-start.1 = (f32[96,96]{1,0:T(8,128)}, f32[96,96]{1,0:T(8,128)S(1)}, u32[]{:S(2)}, u32[]{:S(2)}) collective-permute-start(f32[96,96]{1,0:T(8,128)} %latent.1), channel_id=1, source_target_pairs={{0,0},{7,7},{1,2},{2,1},{3,4},{4,3},{5,6},{6,5},{8,8},{15,15},{9,1... | collective-permute-start | bytes 110600 | tf_op jit(solution)/shard_map/ppermute | solution.py:115
  5.7 1.9 %fusion = (f32[2,3,129,129]{3,0,2,1:T(2,128)S(1)}, f32[2,3,129,129]{3,0,2,1:T(2,128)S(1)}) fusion(f32[2,12,129,129]{3,0,2,1:T(2,128)} %param.9), kind=kLoop, calls=%fused_computation.1 | loop fusion | bytes 1597536 | tf_op jit(solution)/shard_map/slice | solution.py:549
  7.7 1.1 %spectra.3 = (f32[12,224,256]{2,1,0:T(8,128)S(1)}, f32[12,224,256]{2,1,0:T(8,128)S(1)}, f32[8,128]{1,0:T(8,128)S(1)}) custom-call(f32[2,3,129,129]{3,2,1,0:T(8,128)S(1)} %copy.24.kern, bf16[12,256,256]{2,1,0:T(8,128)(2,1)S(1)} %copy-done.2), custom_call_target="tpu_custom_call" | custom-call | flops 2000000000 | bytes 1048576 | tf_op jit(solution)/shard_map/spectra/pallas_call | solution.py:541
  8.9 1.3 %slice-done = f32[2,6,129,129]{3,0,2,1:T(2,128)S(1)} async-done(((f32[2,12,129,129]{3,0,2,1:T(2,128)}), f32[2,6,129,129]{3,0,2,1:T(2,128)S(1)}, s32[]{:S(2)}) %slice-start) | async-done | bytes 798792 | tf_op jit(solution)/shard_map/slice | solution.py:549
  10.2 0.2 copy.22.kern
  10.4 0.2 band.1
  10.7 1.1 %spectra.4 = (f32[12,224,256]{2,1,0:T(8,128)S(1)}, f32[12,224,256]{2,1,0:T(8,128)S(1)}, f32[8,128]{1,0:T(8,128)S(1)}) custom-call(f32[2,3,129,129]{3,2,1,0:T(8,128)S(1)} %copy.23.kern, bf16[12,256,256]{2,1,0:T(8,128)(2,1)S(1)} %copy-done.2, f32[12,224,256]{2,1,0:T(8,128)S(1)} %get-tuple-element.24.rest_0_, ...), custom_call_target="tpu_custom_call", output_to_operand_aliasing={{0}: (2, {}), {1}: (3, {})} | custom-call | flops 2000000000 | bytes 1048576 | tf_op jit(solution)/shard_map/spectra/pallas_call | solution.py:541
  11.9 0.1 collective-permute-done.2.partner
  12.0 1.5 %collective-permute-start.3 = (f32[64,224]{1,0:T(8,128)S(1)}, f32[64,224]{1,0:T(8,128)S(1)}, u32[]{:S(2)}, u32[]{:S(2)}) collective-permute-start(f32[64,224]{1,0:T(8,128)S(1)} %get-tuple-element.35), channel_id=1, source_target_pairs={{0,16},{16,24},{24,8},{8,0},{1,17},{17,25},{25,9},{9,1},{2,18},{18... | collective-permute-start | bytes 172040 | tf_op jit(solution)/shard_map/ppermute | solution.py:122
  13.6 2.3 %spectra.5 = (f32[12,224,256]{2,1,0:T(8,128)S(1)}, f32[12,224,256]{2,1,0:T(8,128)S(1)}, f32[8,128]{1,0:T(8,128)}) custom-call(f32[2,6,129,129]{3,2,1,0:T(8,128)S(1)} %copy.22.kern, bf16[12,256,256]{2,1,0:T(8,128)(2,1)S(1)} %copy-done.2, f32[12,224,256]{2,1,0:T(8,128)S(1)} %get-tuple-element.28.rest_0_, ...), custom_call_target="tpu_custom_call", output_to_operand_aliasing={{0}: (2, {}), {1}: (3, {})} | custom-call | flops 2000000000 | bytes 1048576 | tf_op jit(solution)/shard_map/spectra/pallas_call | solution.py:541
  16.0 5.1 %field.1 = (f32[12,96,128]{2,1,0:T(8,128)S(1)}, f32[12,96,128]{2,1,0:T(8,128)S(1)}, f32[1,512]{1,0:T(1,128)S(1)}, f32[32,1,512]{2,1,0:T(1,128)}) custom-call(f32[12]{0:T(128)S(1)} %copy-done.8, f32[12,224,256]{2,1,0:T(8,128)S(1)} %get-tuple-element.33.spec_re, f32[12,224,256]{2,1,0:T(8,128)S(1)} %get-tuple-element.34.spec_im, ...), custom_call_target="tpu_custom_call" | custom-call | flops 7000000000 | bytes 1048576 | tf_op jit(solution)/shard_map/field/pallas_call | solution.py:567
  21.1 0.8 %copy-done.9 = f32[12,96,128]{2,1,0:T(8,128)} copy-done((f32[12,96,128]{2,1,0:T(8,128)}, f32[12,96,128]{2,1,0:T(8,128)S(1)}, u32[]{:S(2)}) %copy-start.9) | copy-done | bytes 589848
  21.9 5.5 %all-to-all-start = ((f32[32,1,512]{2,1,0:T(1,128)}), f32[32,1,512]{2,1,0:T(1,128)S(1)}, u32[]{:S(2)}, u32[]{:S(2)}) async-start(f32[32,1,512]{2,1,0:T(1,128)} %get-tuple-element.36), calls=%async_computation | async-start | bytes 131072 | tf_op jit(solution)/shard_map/all_to_all | solution.py:522
  28.1 5.6 %all-to-all-done = f32[32,1,512]{2,1,0:T(1,128)S(1)} async-done(((f32[32,1,512]{2,1,0:T(1,128)}), f32[32,1,512]{2,1,0:T(1,128)S(1)}, u32[]{:S(2)}, u32[]{:S(2)}) %all-to-all-start) | async-done | bytes 65568 | tf_op jit(solution)/shard_map/all_to_all | solution.py:522
  33.8 1.5 %source.1 = (f32[96,128]{1,0:T(8,128)S(1)}, f32[1,1]{1,0:T(1,128)}) custom-call(f32[12]{0:T(128)S(1)} %copy-done.8, f32[8]{0:T(128)S(1)} %copy-done.7, s32[1]{0:T(128)S(6)} %copy.31.pick, f32[32,512]{1,0:T(8,128)S(1)} %bitcast.4, f32[1,512]{1,0:T(1,128)S(1)} %get-tuple-element.37.sampled, s32[1,256]{1,0:T(1,128)S(1)} %copy-done.6), custom_call_target="tpu_custom_call" | custom-call | flops 2000000000 | bytes 1048576 | tf_op jit(solution)/shard_map/source/pallas_call | solution.py:581
  35.3 0.3 copy-done.1
  35.5 0.5 copy-done.3
  36.1 5.0 %gradient.1 = (f32[224,224]{1,0:T(8,128)S(1)}, f32[64,224]{1,0:T(8,128)S(1)}) custom-call(f32[12]{0:T(128)S(1)} %copy-done.8, f32[96,128]{1,0:T(8,128)S(1)} %get-tuple-element.38.grid, f32[12,224,256]{2,1,0:T(8,128)S(1)} %get-tuple-element.33.spec_re, f32[12,224,256]{2,1,0:T(8,128)S(1)} %copy-done.1, f32[12,96,128]{2,1,0:T(8,128)S(1)} %get-tuple-element.39.field_re, ...), custom_call_target="tpu_custom_call" | custom-call | flops 6000000000 | bytes 1048576 | tf_op jit(solution)/shard_map/gradient/pallas_call | solution.py:588
  41.2 4.2 %collective-permute-done.4.rim = f32[64,224]{1,0:T(8,128)S(1)} collective-permute-done((f32[64,224]{1,0:T(8,128)S(1)}, f32[64,224]{1,0:T(8,128)S(1)}, u32[]{:S(2)}, u32[]{:S(2)}) %collective-permute-start.4) | collective-permute-done | bytes 57376 | tf_op jit(solution)/shard_map/ppermute | solution.py:122
  45.5 1.3 %collective-permute-done.5.partner = f32[96,224]{1,0:T(8,128)S(1)} collective-permute-done((f32[96,224]{1,0:T(8,128)S(1)}, f32[96,224]{1,0:T(8,128)S(1)}, u32[]{:S(2)}, u32[]{:S(2)}) %collective-permute-start.5) | collective-permute-done | bytes 86048 | tf_op jit(solution)/shard_map/ppermute | solution.py:107
  47.0 1.3 %collective-permute-start.6 = (f32[48,128]{1,0:T(8,128)S(1)}, f32[48,128]{1,0:T(8,128)S(1)}, u32[]{:S(2)}, u32[]{:S(2)}) collective-permute-start(f32[48,128]{1,0:T(8,128)S(1)} %near.1), channel_id=1, source_target_pairs={{0,1},{1,0},{2,3},{3,2},{4,5},{5,4},{6,7},{7,6},{8,9},{9,8},{10,11... | collective-permute-start | bytes 73736 | tf_op jit(solution)/shard_map/ppermute | solution.py:107
  48.3 2.7 %collective-permute-start.7 = (f32[48,128]{1,0:T(8,128)S(1)}, f32[48,128]{1,0:T(8,128)S(1)}, u32[]{:S(2)}, u32[]{:S(2)}) collective-permute-start(f32[48,128]{1,0:T(8,128)S(1)} %get-tuple-element.44), channel_id=1, source_target_pairs={{0,0},{7,7},{1,2},{2,1},{3,4},{4,3},{5,6},{6,5},{8,8},{15,15},{9,1... | collective-permute-start | bytes 73736 | tf_op jit(solution)/shard_map/ppermute | solution.py:115
  51.0 3.9 %collective-permute-done.7.far = f32[48,128]{1,0:T(8,128)S(1)} collective-permute-done((f32[48,128]{1,0:T(8,128)S(1)}, f32[48,128]{1,0:T(8,128)S(1)}, u32[]{:S(2)}, u32[]{:S(2)}) %collective-permute-start.7) | collective-permute-done | bytes 24608 | tf_op jit(solution)/shard_map/ppermute | solution.py:115
  54.9 0.8 %finish.1 = f32[96,96]{1,0:T(8,128)} custom-call(f32[96,224]{1,0:T(8,128)S(1)} %get-tuple-element.43.band, f32[48,128]{1,0:T(8,128)S(1)} %collective-permute-done.6.near, f32[48,128]{1,0:T(8,128)S(1)} %collective-permute-done.7.far, f32[96,96]{1,0:T(8,128)S(1)} %copy-done.4), custom_call_target="tpu_custom_call" | custom-call | flops 1000000000 | bytes 1048576 | tf_op jit(solution)/shard_map/finish/pallas_call | solution.py:608
  (35 shorter events, 0.9 us)
Async XLA Ops:
  0.6 7.0 %copy-start.2 = (bf16[12,256,256]{2,1,0:T(8,128)(2,1)S(1)}, bf16[12,256,256]{2,1,0:T(8,128)(2,1)}, u32[]{:S(2)}) copy-start(bf16[12,256,256]{2,1,0:T(8,128)(2,1)} %constant.2.clone.tables) | copy-start | bytes 4718596
  0.6 9.7 %collective-permute-start = (f32[96,96]{1,0:T(8,128)}, f32[96,96]{1,0:T(8,128)S(1)}, u32[]{:S(2)}, u32[]{:S(2)}) collective-permute-start(f32[96,96]{1,0:T(8,128)} %latent.1), channel_id=1, source_target_pairs={{0,1},{1,0},{2,3},{3,2},{4,5},{5,4},{6,7},{7,6},{8,9},{9,8},{10,11... | collective-permute-start | bytes 110600 | tf_op jit(solution)/shard_map/ppermute | solution.py:107
  0.7 9.7 %collective-permute-start.1 = (f32[96,96]{1,0:T(8,128)}, f32[96,96]{1,0:T(8,128)S(1)}, u32[]{:S(2)}, u32[]{:S(2)}) collective-permute-start(f32[96,96]{1,0:T(8,128)} %latent.1), channel_id=1, source_target_pairs={{0,0},{7,7},{1,2},{2,1},{3,4},{4,3},{5,6},{6,5},{8,8},{15,15},{9,1... | collective-permute-start | bytes 110600 | tf_op jit(solution)/shard_map/ppermute | solution.py:115
  8.8 1.4 %slice-start = ((f32[2,12,129,129]{3,0,2,1:T(2,128)}), f32[2,6,129,129]{3,0,2,1:T(2,128)S(1)}, s32[]{:S(2)}) async-start(f32[2,12,129,129]{3,0,2,1:T(2,128)} %param.9), calls=%async_computation.1 | async-start | bytes 3170304 | tf_op jit(solution)/shard_map/slice | solution.py:549
  8.8 1.6 %copy-start.4 = (f32[96,96]{1,0:T(8,128)S(1)}, f32[96,96]{1,0:T(8,128)}, u32[]{:S(2)}) copy-start(f32[96,96]{1,0:T(8,128)} %latent.1) | copy-start | bytes 110596
  10.7 1.4 %collective-permute-start.2 = (f32[96,224]{1,0:T(8,128)S(1)}, f32[96,224]{1,0:T(8,128)S(1)}, u32[]{:S(2)}, u32[]{:S(2)}) collective-permute-start(f32[96,224]{1,0:T(8,128)S(1)} %get-tuple-element.30.band), channel_id=1, source_target_pairs={{0,8},{8,0},{16,24},{24,16},{1,9},{9,1},{17,25},{25,17},{2,10},{10... | collective-permute-start | bytes 258056 | tf_op jit(solution)/shard_map/ppermute | solution.py:107
  12.0 3.9 %collective-permute-start.3 = (f32[64,224]{1,0:T(8,128)S(1)}, f32[64,224]{1,0:T(8,128)S(1)}, u32[]{:S(2)}, u32[]{:S(2)}) collective-permute-start(f32[64,224]{1,0:T(8,128)S(1)} %get-tuple-element.35), channel_id=1, source_target_pairs={{0,16},{16,24},{24,8},{8,0},{1,17},{17,25},{25,9},{9,1},{2,18},{18... | collective-permute-start | bytes 172040 | tf_op jit(solution)/shard_map/ppermute | solution.py:122
  13.5 2.4 %copy-start.5 = (f32[1,256]{1,0:T(1,128)S(1)}, f32[1,256]{1,0:T(1,128)}, u32[]{:S(2)}) copy-start(f32[1,256]{1,0:T(1,128)} %slopes.1) | copy-start | bytes 3076
  13.5 2.4 %copy-start.6 = (s32[1,256]{1,0:T(1,128)S(1)}, s32[1,256]{1,0:T(1,128)}, u32[]{:S(2)}) copy-start(s32[1,256]{1,0:T(1,128)} %pixels.3) | copy-start | bytes 3076
  13.6 2.4 %copy-start.8 = (f32[12]{0:T(128)S(1)}, f32[12]{0:T(128)}, u32[]{:S(2)}) copy-start(f32[12]{0:T(128)} %weights.5) | copy-start | bytes 148
  15.9 5.2 %copy-start = (f32[12,224,256]{2,1,0:T(8,128)}, f32[12,224,256]{2,1,0:T(8,128)S(1)}, u32[]{:S(2)}) copy-start(f32[12,224,256]{2,1,0:T(8,128)S(1)} %get-tuple-element.34.spec_im) | copy-start | bytes 8257540
  16.0 17.8 %copy-start.7 = (f32[8]{0:T(128)S(1)}, f32[8]{0:T(128)}, u32[]{:S(2)}) copy-start(f32[8]{0:T(128)} %doses.1) | copy-start | bytes 100
  21.1 0.8 %copy-start.9 = (f32[12,96,128]{2,1,0:T(8,128)}, f32[12,96,128]{2,1,0:T(8,128)S(1)}, u32[]{:S(2)}) copy-start(f32[12,96,128]{2,1,0:T(8,128)S(1)} %get-tuple-element.40.field_im) | copy-start | bytes 1769476
  21.9 11.8 %all-to-all-start = ((f32[32,1,512]{2,1,0:T(1,128)}), f32[32,1,512]{2,1,0:T(1,128)S(1)}, u32[]{:S(2)}, u32[]{:S(2)}) async-start(f32[32,1,512]{2,1,0:T(1,128)} %get-tuple-element.36), calls=%async_computation | async-start | bytes 131072 | tf_op jit(solution)/shard_map/all_to_all | solution.py:522
  33.7 1.8 %copy-start.1 = (f32[12,224,256]{2,1,0:T(8,128)S(1)}, f32[12,224,256]{2,1,0:T(8,128)}, u32[]{:S(2)}) copy-start(f32[12,224,256]{2,1,0:T(8,128)} %copy-done) | copy-start | bytes 8257540
  33.7 2.2 %copy-start.3 = (bf16[12,256,256]{2,1,0:T(8,128)(2,1)S(1)}, bf16[12,256,256]{2,1,0:T(8,128)(2,1)}, u32[]{:S(2)}) copy-start(bf16[12,256,256]{2,1,0:T(8,128)(2,1)} %constant.2.clone.tables) | copy-start | bytes 4718596
  33.8 2.3 %copy-start.10 = (f32[12,96,128]{2,1,0:T(8,128)S(1)}, f32[12,96,128]{2,1,0:T(8,128)}, u32[]{:S(2)}) copy-start(f32[12,96,128]{2,1,0:T(8,128)} %copy-done.9) | copy-start | bytes 1769476
  41.1 4.3 %collective-permute-start.4 = (f32[64,224]{1,0:T(8,128)S(1)}, f32[64,224]{1,0:T(8,128)S(1)}, u32[]{:S(2)}, u32[]{:S(2)}) collective-permute-start(f32[64,224]{1,0:T(8,128)S(1)} %get-tuple-element.42), channel_id=1, source_target_pairs={{16,0},{24,16},{8,24},{0,8},{17,1},{25,17},{9,25},{1,9},{18,2},{26... | collective-permute-start | bytes 172040 | tf_op jit(solution)/shard_map/ppermute | solution.py:122
  45.4 1.4 %collective-permute-start.5 = (f32[96,224]{1,0:T(8,128)S(1)}, f32[96,224]{1,0:T(8,128)S(1)}, u32[]{:S(2)}, u32[]{:S(2)}) collective-permute-start(f32[96,224]{1,0:T(8,128)S(1)} %fold.2), channel_id=1, source_target_pairs={{0,8},{8,0},{16,24},{24,16},{1,9},{9,1},{17,25},{25,17},{2,10},{10... | collective-permute-start | bytes 258056 | tf_op jit(solution)/shard_map/ppermute | solution.py:107
  47.0 4.0 %collective-permute-start.6 = (f32[48,128]{1,0:T(8,128)S(1)}, f32[48,128]{1,0:T(8,128)S(1)}, u32[]{:S(2)}, u32[]{:S(2)}) collective-permute-start(f32[48,128]{1,0:T(8,128)S(1)} %near.1), channel_id=1, source_target_pairs={{0,1},{1,0},{2,3},{3,2},{4,5},{5,4},{6,7},{7,6},{8,9},{9,8},{10,11... | collective-permute-start | bytes 73736 | tf_op jit(solution)/shard_map/ppermute | solution.py:107
  48.3 6.6 %collective-permute-start.7 = (f32[48,128]{1,0:T(8,128)S(1)}, f32[48,128]{1,0:T(8,128)S(1)}, u32[]{:S(2)}, u32[]{:S(2)}) collective-permute-start(f32[48,128]{1,0:T(8,128)S(1)} %get-tuple-element.44), channel_id=1, source_target_pairs={{0,0},{7,7},{1,2},{2,1},{3,4},{4,3},{5,6},{6,5},{8,8},{15,15},{9,1... | collective-permute-start | bytes 73736 | tf_op jit(solution)/shard_map/ppermute | solution.py:115

commit v9 on v8

--- a/solution.py
+++ b/solution.py
@@ -122,9 +122,9 @@
     return lax.ppermute(x, axis, [(b, a) if back else (a, b) for a, b in pairs])
 
 
-def spectra_kernel(start, parts, kern, tables, *rest):
-    out_re, out_im, token, edge = rest[-4:]
-    period = out_re.shape[1]
+def spectra_kernel(start, groups, kern, tables, *rest):
+    *outs, token, edge = rest[-2 - groups :]
+    period = outs[0].shape[2]
     half = period // 2
     last = kern.shape[-1] - 1
     cols = pair(tables, 0, last, 2 * LANES)
@@ -167,23 +167,19 @@
             jnp.concatenate([real_sin + imag_cos, imag_cos - real_sin], axis=1),
         )
 
-    def step(group, carry):
+    for group, out in enumerate(outs):
         first = start + group * BATCH
-        planes = along_lanes([kern[c, group * BATCH + i] for i in range(BATCH) for c in range(2)])
-        for i in range(BATCH):
-            k = first + i
-            (real, real_tail), (imag, imag_tail) = planes[2 * i : 2 * i + 2]
+        planes = along_lanes([kern[c, first + k] for k in range(BATCH) for c in range(2)])
+        for k in range(BATCH):
+            (real, real_tail), (imag, imag_tail) = planes[2 * k : 2 * k + 2]
             wide_re, wide_im = mixed(real, imag)
             tail_re, tail_im = mixed(real_tail, imag_tail)
             tall_re = along_rows(wide_re, tail_re)
             tall_im = along_rows(wide_im, tail_im)
-            out_re[k, :half] = tall_re[:half] - tall_im[half:]
-            out_re[k, half:] = tall_re[:half] + tall_im[half:]
-            out_im[k, :half] = tall_im[:half] + tall_re[half:]
-            out_im[k, half:] = tall_im[:half] - tall_re[half:]
-        return carry
-
-    lax.fori_loop(0, parts // BATCH, step, 0)
+            out[0, k, :half] = tall_re[:half] - tall_im[half:]
+            out[0, k, half:] = tall_re[:half] + tall_im[half:]
+            out[1, k, :half] = tall_im[:half] + tall_re[half:]
+            out[1, k, half:] = tall_im[:half] - tall_re[half:]
 
 
 def pack(x):
@@ -194,6 +190,11 @@
 def unpack(x):
     width = x.shape[1] // 2
     return jnp.concatenate([x[:, :width], x[:, width:]], axis=0)
+
+
+def own_kernel(latent, transmit, token):
+    transmit[...] = 0.5 * (1.0 + jnp.tanh(latent[...]))
+    token[...] = jnp.zeros(token.shape, F32)
 
 
 def band_kernel(middle, partner, outside, after, band, token):
@@ -208,7 +209,7 @@
     far = transmit(jnp.where(lower, outside[:, tile - radius :], outside[:, :radius]))
     far = jnp.where(other, far, 0.0)
     band[:, :radius] = jnp.where(lower, far, near)
-    band[:, radius : radius + tile] = transmit(middle[...])
+    band[:, radius : radius + tile] = middle[...]
     band[:, radius + tile :] = jnp.where(lower, near, far)
     token[...] = jnp.zeros(token.shape, F32)
 
@@ -250,15 +251,24 @@
     near[...] = jnp.where(lower, pack(band[:, radius + tile :]), pack(band[:, :radius]))
 
 
-def finish_kernel(band, near, far, latent, steering):
-    tile = latent.shape[0]
+def far_side_kernel(band, far, out):
+    tile = out.shape[0]
     radius = (band.shape[1] - tile) // 2
     lower, other = place_in_pair("tx")
+    outer = jnp.where(other, unpack(far[...]), 0.0)
+    out[...] = band[:, radius : radius + tile]
+    out[:, :radius] += jnp.where(lower, outer, 0.0)
+    out[:, tile - radius :] += jnp.where(lower, 0.0, outer)
+
+
+def finish_kernel(total, near, latent, steering):
+    tile = latent.shape[0]
+    radius = near.shape[1] // 2
+    lower, _ = place_in_pair("tx")
     inner = unpack(near[...])
-    outer = jnp.where(other, unpack(far[...]), 0.0)
-    steering[...] = band[:, radius : radius + tile]
-    steering[:, :radius] += jnp.where(lower, outer, inner)
-    steering[:, tile - radius :] += jnp.where(lower, inner, outer)
+    steering[...] = total[...]
+    steering[:, :radius] += jnp.where(lower, 0.0, inner)
+    steering[:, tile - radius :] += jnp.where(lower, inner, 0.0)
     value = jnp.tanh(latent[...])
     steering[...] = steering[...] * 0.5 * (1.0 - value * value)
 
@@ -276,11 +286,10 @@
     return held, pixels - row * tile
 
 
-def field_kernel(
-    weights, spec_re, spec_im, band, partner, rim, pixels, slopes, tables,
-    field_re, field_im, sampled, copies, framed, mask,
-):
-    kernels, period, _ = spec_re.shape
+def field_kernel(weights, band, partner, rim, pixels, slopes, tables, *rest):
+    *spec, field_re, field_im, sampled, copies, framed, mask = rest
+    kernels = weights.shape[0]
+    period = band.shape[1]
     half = period // 2
     tile = field_re.shape[1]
     radius = rim.shape[0]
@@ -310,9 +319,9 @@
     across = pair(tables, 4, 2 * LANES, LANES)
     across = (across[0], jnp.concatenate(across, axis=1))
 
-    def lifted(k):
-        pos_re, pos_im = spec_re[k, :half], spec_im[k, :half]
-        neg_re, neg_im = spec_re[k, half:], spec_im[k, half:]
+    def lifted(own, k):
+        pos_re, pos_im = own[0, k, :half], own[1, k, :half]
+        neg_re, neg_im = own[0, k, half:], own[1, k, half:]
         up_re = mask[0] * pos_re - mask[1] * pos_im
         up_im = mask[0] * pos_im + mask[1] * pos_re
         down_re = mask[2] * neg_re - mask[3] * neg_im
@@ -327,10 +336,11 @@
         rows_im = jnp.concatenate([im_pos + im_neg, re_pos - re_neg], axis=1)
         return [rows_re, rows_im]
 
-    def step(group, intensity):
+    intensity = jnp.zeros((tile, LANES), F32)
+    for group, own in enumerate(spec):
         first = group * BATCH
-        rows = stacked([row for i in range(BATCH) for row in lifted(first + i)])
-        high, low = split(rows)
+        lines = stacked([line for i in range(BATCH) for line in lifted(own, i)])
+        high, low = split(lines)
         by_high, by_low = halves(dot(high, across[1]))
         both = by_high + by_low + dot(low, across[0])
         for i in range(BATCH):
@@ -339,11 +349,6 @@
             field_re[first + i] = real
             field_im[first + i] = imag
             intensity = intensity + weights[first + i] * (real * real + imag * imag)
-        return intensity
-
-    intensity = lax.fori_loop(
-        0, kernels // BATCH, step, jnp.zeros((tile, LANES), F32)
-    )
     intensity = intensity / total_weight(weights, kernels)
     samples = pixels.shape[1]
     row, col = sample_places(pixels[...], tile)
@@ -425,19 +430,17 @@
     placed_sum[...] = grid
 
 
-def gradient_kernel(
-    weights, grid, spec_re, spec_im, field_re, field_im, tables,
-    grad, rim, total_re, total_im,
-):
-    kernels, period, _ = spec_re.shape
+def gradient_kernel(weights, grid, field_re, field_im, tables, *rest):
+    *spec, grad, rim, total_re, total_im = rest
+    period = grad.shape[0]
     half = period // 2
     tile = field_re.shape[1]
     radius = (period - tile) // 2
     cols = pair(tables, 0, LANES, 2 * LANES)
     cols = (stacked((cols[0], cols[0])), cols[1])
     rows = tile // 2
-    cos_rows = tables[11, :half, : 3 * rows]
-    sin_rows = tables[11, half:period, : 3 * rows]
+    cos_rows = tables[6, :half, : 3 * rows]
+    sin_rows = tables[6, half:period, : 3 * rows]
 
     def along_rows(wide):
         out = []
@@ -452,7 +455,7 @@
     total_re[...] = jnp.zeros((period, 2 * LANES), F32)
     total_im[...] = jnp.zeros((period, 2 * LANES), F32)
 
-    def step(group, carry):
+    for group, own in enumerate(spec):
         sources = []
         for i in range(BATCH):
             k = group * BATCH + i
@@ -472,22 +475,20 @@
                 part = slice(start, start + half)
                 wave_re = cos_re + sign * sin_im
                 wave_im = cos_im - sign * sin_re
-                own_re, own_im = spec_re[k, part], spec_im[k, part]
+                own_re, own_im = own[0, i, part], own[1, i, part]
                 total_re[part] += own_re * wave_re + own_im * wave_im
                 total_im[part] += own_re * wave_im - own_im * wave_re
-        return carry
-
-    lax.fori_loop(0, kernels // BATCH, step, 0)
+
     pos_re, neg_re = total_re[:half], total_re[half:]
     pos_im, neg_im = total_im[:half], total_im[half:]
-    back_rows = pair(tables, 8, period, period)
+    back_rows = pair(tables, 4, period, period)
     back_rows = (back_rows[0], stacked(back_rows))
     for_re = jnp.concatenate([pos_re + neg_re, neg_im - pos_im], axis=0)
     for_im = jnp.concatenate([pos_im + neg_im, pos_re - neg_re], axis=0)
     re_pos, re_neg = halves(dot3_stacked(back_rows, split(for_re)))
     im_pos, im_neg = halves(dot3_stacked(back_rows, split(for_im)))
     last = jnp.concatenate([re_pos + re_neg, im_neg - im_pos], axis=1)
-    framed = dot3(split(last), pair(tables, 4, 2 * LANES, period)) * (2.0 / (period * period))
+    framed = dot3(split(last), pair(tables, 2, 2 * LANES, period)) * (2.0 / (period * period))
     grad[...] = framed
     lower, _ = place_in_pair("ty")
     rim[...] = jnp.where(lower, framed[:radius], framed[radius + tile :])
@@ -502,14 +503,13 @@
     return jax.ShapeDtypeStruct(dims, F32)
 
 
-def call(kernel, name, out_shape, in_specs, scratch=(), aliases=None, micros=1):
+def call(kernel, name, out_shape, in_specs, scratch=(), micros=1):
     return pl.pallas_call(
         kernel,
         out_shape=out_shape,
         in_specs=in_specs,
         out_specs=[VMEM] * len(out_shape),
         scratch_shapes=scratch,
-        input_output_aliases=aliases or {},
         compiler_params=pltpu.CompilerParams(vmem_limit_bytes=10 * 1024 * 1024),
         cost_estimate=pl.CostEstimate(
             flops=micros * 10**9, bytes_accessed=2**20, transcendentals=0
@@ -529,53 +529,55 @@
     radius = (taps - 1) // 2
     period = tile + 2 * radius
     half = period // 2
-    tables = jnp.asarray(wave_tables(period, tile))
+    tables = wave_tables(period, tile)
+    last_tables = jnp.asarray(tables[[0, 1, 4, 5, 8, 9, 11]])
+    tables = jnp.asarray(tables)
     token = shape(8, LANES)
     packed = shape(tile // 2, 2 * radius)
     devices = lax.axis_size("ty") * lax.axis_size("tx")
 
     spec = []
 
-    def spectra(start, parts, *after):
-        given = spec + list(after)
+    def spectra(groups, after):
         *out, done = call(
-            functools.partial(spectra_kernel, start, parts),
+            functools.partial(spectra_kernel, len(spec) * BATCH, groups),
             "spectra",
-            [shape(count, period, 2 * LANES)] * 2 + [token],
-            [VMEM] * 2 + [ANY] * len(given),
+            [shape(2, BATCH, period, 2 * LANES)] * groups + [token],
+            [VMEM] * 2 + [ANY],
             scratch=[pltpu.VMEM((period, LANES), F32)],
-            aliases={2: 0, 3: 1} if spec else None,
-            micros=2,
-        )(kernels[:, start : start + parts], tables, *given)
-        spec[:] = out
+            micros=groups,
+        )(kernels, tables, after)
+        spec.extend(out)
         return done
 
     partner, outside = swap("tx", latent), swap_outside("tx", latent)
-    quarter = count // 4
-    done = spectra(0, quarter)
+    transmit, done = call(
+        own_kernel, "own", [shape(tile, tile), token], [VMEM], micros=4
+    )(latent)
+    done = spectra(1, done)
     band, done = call(
         band_kernel, "band", [shape(tile, period), token], [VMEM] * 3 + [ANY]
-    )(latent, partner, outside, done)
+    )(transmit, partner, outside, done)
     partner = swap("ty", band)
-    done = spectra(quarter, quarter, done)
+    done = spectra(1, done)
     rim, done = call(
         relay_rows_kernel, "relay", [shape(radius, period), token], [VMEM, ANY]
     )(partner, done)
     rim = ring("ty", rim)
-    spectra(2 * quarter, count - 2 * quarter, done)
+    spectra(count // BATCH - len(spec), done)
 
     field_re, field_im, sampled, copies = call(
         field_kernel,
         "field",
         [shape(count, tile, LANES)] * 2
         + [shape(1, 2 * samples), shape(devices, 1, 2 * samples)],
-        [SMEM] + [VMEM] * 8,
+        [SMEM] + [VMEM] * (6 + len(spec)),
         scratch=[
             pltpu.VMEM((period, period), F32),
             pltpu.VMEM((4, half, 2 * LANES), F32),
         ],
         micros=7,
-    )(socs_weights, *spec, band, partner, rim, edge_pixels, inv_slope, tables)
+    )(socs_weights, band, partner, rim, edge_pixels, inv_slope, tables, *spec)
 
     gathered = gather_all(copies).reshape(devices, 2 * samples)
     grid, tail_mean = call(
@@ -589,10 +591,10 @@
         gradient_kernel,
         "gradient",
         [shape(period, period), shape(radius, period)],
-        [SMEM] + [VMEM] * 6,
+        [SMEM] + [VMEM] * (4 + len(spec)),
         scratch=[pltpu.VMEM((period, 2 * LANES), F32)] * 2,
         micros=6,
-    )(socs_weights, grid, *spec, field_re, field_im, tables)
+    )(socs_weights, grid, field_re, field_im, last_tables, *spec)
 
     rim = ring("ty", rim, back=True)
     (partner,) = call(fold_rows_kernel, "fold", [shape(tile, period)], [VMEM] * 2)(
@@ -605,8 +607,9 @@
     far = swap_outside("tx", far)
     (near,) = call(near_rim_kernel, "near", [packed], [VMEM])(band)
     near = swap("tx", near)
-    (steering,) = call(finish_kernel, "finish", [shape(tile, tile)], [VMEM] * 4)(
-        band, near, far, latent
+    (total,) = call(far_side_kernel, "far", [shape(tile, tile)], [VMEM] * 2)(band, far)
+    (steering,) = call(finish_kernel, "finish", [shape(tile, tile)], [VMEM] * 3)(
+        total, near, latent
     )
     return (steering, tail_mean.reshape(1))
 

time: 56 us -> 55.7 us (level)
  the two profiles are of different devices: /device:TPU:4 before, /device:TPU:0 now
where the time goes in v9:
time: 55.7 us; the launch traced here: 55.3 us
  starting transfers between devices  17.8 us (32%)
  Pallas kernels  16.4 us (29%)
  waiting for transfers between devices  14.1 us (25%)
  local copies, waits for them, and re-layouts  5.58 us (10%)
  between operations  1.48 us (3%)
    all_to_all x1, starting transfers between devices, gather_all(): return lax.all_to_all(copies, ('ty', 'tx'), 0, 0, tiled=True)  7.7 us
    all_to_all x1, waiting for transfers between devices, gather_all(): return lax.all_to_all(copies, ('ty', 'tx'), 0, 0, tiled=True)  6.63 us
    ppermute x4, starting transfers between devices, swap(): lax.ppermute(x, axis, [(i, i ^ 1) for i in range(lax.axis_size(axis))])  6.38 us
    unnamed x32, local copies, waits for them, and re-layouts  5.58 us
    pallas_call x1, Pallas kernels, body(): call(field_kernel, 'field', [shape(count, tile, LANES)] * 2 + [shape(1, 2...  4.79 us
    pallas_call x1, Pallas kernels, body(): call(gradient_kernel, 'gradient', [shape(period, period), shape(radius, p...  4.74 us
    ppermute x2, waiting for transfers between devices, ring(): return lax.ppermute(x, axis, [(b, a) if back else (a, b) for a, b in pairs])  4.31 us
    pallas_call x3, Pallas kernels, spectra(): call(functools.partial(spectra_kernel, len(spec) * BATCH, groups), 'spect...  3.96 us
  transfers between devices with their start and end apart: 9, of which 6 were waited for; matrix products, arithmetic and copies ran while one was open for 1% of the time, Pallas kernels for 8%

profile of v9, /device:TPU:0, one launch (start us, length us, event | category | flops | bytes accessed | tf_op | source)
XLA Modules:
  0.0 55.3 jit_solution(6959735585537340809)
XLA Ops:
  0.6 3.0 %collective-permute-start = (f32[96,96]{1,0:T(8,128)}, f32[96,96]{1,0:T(8,128)S(1)}, u32[]{:S(2)}, u32[]{:S(2)}) collective-permute-start(f32[96,96]{1,0:T(8,128)} %latent.3), channel_id=1, source_target_pairs={{0,1},{1,0},{2,3},{3,2},{4,5},{5,4},{6,7},{7,6},{8,9},{9,8},{10,11... | collective-permute-start | bytes 110600 | tf_op jit(solution)/shard_map/ppermute | solution.py:107
  3.7 1.4 %collective-permute-start.1 = (f32[96,96]{1,0:T(8,128)}, f32[96,96]{1,0:T(8,128)S(1)}, u32[]{:S(2)}, u32[]{:S(2)}) collective-permute-start(f32[96,96]{1,0:T(8,128)} %latent.3), channel_id=1, source_target_pairs={{0,0},{7,7},{1,2},{2,1},{3,4},{4,3},{5,6},{6,5},{8,8},{15,15},{9,1... | collective-permute-start | bytes 110600 | tf_op jit(solution)/shard_map/ppermute | solution.py:115
  5.1 0.8 %copy-done.1 = f32[96,96]{1,0:T(8,128)S(1)} copy-done((f32[96,96]{1,0:T(8,128)S(1)}, f32[96,96]{1,0:T(8,128)}, u32[]{:S(2)}) %copy-start.1) | copy-done | bytes 36888
  5.9 1.9 %copy-done.14 = f32[2,12,129,129]{3,0,2,1:T(2,128)S(1)} copy-done((f32[2,12,129,129]{3,0,2,1:T(2,128)S(1)}, f32[2,12,129,129]{3,0,2,1:T(2,128)}, u32[]{:S(2)}) %copy-start.14) | copy-done | bytes 1597560
  7.8 0.3 copy.15.kern
  8.1 1.1 %copy-done = bf16[12,256,256]{2,1,0:T(8,128)(2,1)S(1)} copy-done((bf16[12,256,256]{2,1,0:T(8,128)(2,1)S(1)}, bf16[12,256,256]{2,1,0:T(8,128)(2,1)}, u32[]{:S(2)}) %copy-start) | copy-done | bytes 1572888
  9.2 1.1 %spectra.3 = (f32[2,3,224,256]{3,2,1,0:T(8,128)S(1)}, f32[8,128]{1,0:T(8,128)S(1)}) custom-call(f32[2,12,129,129]{3,2,1,0:T(8,128)S(1)} %copy.15.kern, bf16[12,256,256]{2,1,0:T(8,128)(2,1)S(1)} %copy-done, f32[8,128]{1,0:T(8,128)S(1)} %get-tuple-element.25.rest_0_), custom_call_target="tpu_custom_call" | custom-call | flops 1000000000 | bytes 1048576 | tf_op jit(solution)/shard_map/spectra/pallas_call | solution.py:542
  10.4 0.2 band.1
  10.7 1.1 %spectra.4 = (f32[2,3,224,256]{3,2,1,0:T(8,128)S(1)}, f32[8,128]{1,0:T(8,128)S(1)}) custom-call(f32[2,12,129,129]{3,2,1,0:T(8,128)S(1)} %copy.15.kern, bf16[12,256,256]{2,1,0:T(8,128)(2,1)S(1)} %copy-done, f32[8,128]{1,0:T(8,128)S(1)} %get-tuple-element.28.rest_0_), custom_call_target="tpu_custom_call" | custom-call | flops 1000000000 | bytes 1048576 | tf_op jit(solution)/shard_map/spectra/pallas_call | solution.py:542
  12.0 1.5 %collective-permute-start.3 = (f32[64,224]{1,0:T(8,128)S(1)}, f32[64,224]{1,0:T(8,128)S(1)}, u32[]{:S(2)}, u32[]{:S(2)}) collective-permute-start(f32[64,224]{1,0:T(8,128)S(1)} %get-tuple-element.30), channel_id=1, source_target_pairs={{0,16},{16,24},{24,8},{8,0},{1,17},{17,25},{25,9},{9,1},{2,18},{18... | collective-permute-start | bytes 172040 | tf_op jit(solution)/shard_map/ppermute | solution.py:122
  13.5 1.7 %spectra.5 = (f32[2,3,224,256]{3,2,1,0:T(8,128)S(1)}, f32[2,3,224,256]{3,2,1,0:T(8,128)S(1)}, f32[8,128]{1,0:T(8,128)}) custom-call(f32[2,12,129,129]{3,2,1,0:T(8,128)S(1)} %copy.15.kern, bf16[12,256,256]{2,1,0:T(8,128)(2,1)S(1)} %copy-done, f32[8,128]{1,0:T(8,128)S(1)} %get-tuple-element.33.rest_0_), custom_call_target="tpu_custom_call" | custom-call | flops 2000000000 | bytes 1048576 | tf_op jit(solution)/shard_map/spectra/pallas_call | solution.py:542
  15.4 4.8 %field.1 = (f32[12,96,128]{2,1,0:T(8,128)S(1)}, f32[12,96,128]{2,1,0:T(8,128)S(1)}, f32[1,512]{1,0:T(1,128)S(1)}, f32[32,1,512]{2,1,0:T(1,128)}) custom-call(f32[12]{0:T(128)S(1)} %copy-done.6, f32[96,224]{1,0:T(8,128)S(1)} %get-tuple-element.27.band, f32[96,224]{1,0:T(8,128)S(1)} %collective-permute-done.2.partner, ...), custom_call_target="tpu_custom_call" | custom-call | flops 7000000000 | bytes 1048576 | tf_op jit(solution)/shard_map/field/pallas_call | solution.py:569
  20.2 0.8 %copy-done.12 = f32[12,96,128]{2,1,0:T(8,128)} copy-done((f32[12,96,128]{2,1,0:T(8,128)}, f32[12,96,128]{2,1,0:T(8,128)S(1)}, u32[]{:S(2)}) %copy-start.12) | copy-done | bytes 589848
  21.0 7.7 %all-to-all-start = ((f32[32,1,512]{2,1,0:T(1,128)}), f32[32,1,512]{2,1,0:T(1,128)S(1)}, u32[]{:S(2)}, u32[]{:S(2)}) async-start(f32[32,1,512]{2,1,0:T(1,128)} %get-tuple-element.36), calls=%async_computation | async-start | bytes 131072 | tf_op jit(solution)/shard_map/all_to_all | solution.py:522
  29.4 6.6 %all-to-all-done = f32[32,1,512]{2,1,0:T(1,128)S(1)} async-done(((f32[32,1,512]{2,1,0:T(1,128)}), f32[32,1,512]{2,1,0:T(1,128)S(1)}, u32[]{:S(2)}, u32[]{:S(2)}) %all-to-all-start) | async-done | bytes 65568 | tf_op jit(solution)/shard_map/all_to_all | solution.py:522
  36.1 1.5 %source.1 = (f32[96,128]{1,0:T(8,128)S(1)}, f32[1,1]{1,0:T(1,128)}) custom-call(f32[12]{0:T(128)S(1)} %copy-done.6, f32[8]{0:T(128)S(1)} %copy-done.5, s32[1]{0:T(128)S(6)} %copy.21.pick, f32[32,512]{1,0:T(8,128)S(1)} %bitcast.4, f32[1,512]{1,0:T(1,128)S(1)} %get-tuple-element.37.sampled, s32[1,256]{1,0:T(1,128)S(1)} %copy-done.4), custom_call_target="tpu_custom_call" | custom-call | flops 2000000000 | bytes 1048576 | tf_op jit(solution)/shard_map/source/pallas_call | solution.py:583
  37.7 0.4 copy-done.11
  38.2 4.7 %gradient.1 = (f32[224,224]{1,0:T(8,128)S(1)}, f32[64,224]{1,0:T(8,128)S(1)}) custom-call(f32[12]{0:T(128)S(1)} %copy-done.6, f32[96,128]{1,0:T(8,128)S(1)} %get-tuple-element.38.grid, f32[12,96,128]{2,1,0:T(8,128)S(1)} %get-tuple-element.39.field_re, f32[12,96,128]{2,1,0:T(8,128)S(1)} %copy-done.13, bf16[7,256,256]{2,1,0:T(8,128)(2,1)S(1)} %copy-done.7, ...), custom_call_target="tpu_custom_call" | custom-call | flops 6000000000 | bytes 1048576 | tf_op jit(solution)/shard_map/gradient/pallas_call | solution.py:590
  43.1 4.2 %collective-permute-done.4.rim = f32[64,224]{1,0:T(8,128)S(1)} collective-permute-done((f32[64,224]{1,0:T(8,128)S(1)}, f32[64,224]{1,0:T(8,128)S(1)}, u32[]{:S(2)}, u32[]{:S(2)}) %collective-permute-start.4) | collective-permute-done | bytes 57376 | tf_op jit(solution)/shard_map/ppermute | solution.py:122
  47.3 1.3 %collective-permute-done.5.partner = f32[96,224]{1,0:T(8,128)S(1)} collective-permute-done((f32[96,224]{1,0:T(8,128)S(1)}, f32[96,224]{1,0:T(8,128)S(1)}, u32[]{:S(2)}, u32[]{:S(2)}) %collective-permute-start.5) | collective-permute-done | bytes 86048 | tf_op jit(solution)/shard_map/ppermute | solution.py:107
  48.7 0.7 %collective-permute-start.6 = (f32[48,128]{1,0:T(8,128)S(1)}, f32[48,128]{1,0:T(8,128)S(1)}, u32[]{:S(2)}, u32[]{:S(2)}) collective-permute-start(f32[48,128]{1,0:T(8,128)S(1)} %get-tuple-element.44), channel_id=1, source_target_pairs={{0,0},{7,7},{1,2},{2,1},{3,4},{4,3},{5,6},{6,5},{8,8},{15,15},{9,1... | collective-permute-start | bytes 73736 | tf_op jit(solution)/shard_map/ppermute | solution.py:115
  49.5 3.2 %collective-permute-start.7 = (f32[48,128]{1,0:T(8,128)S(1)}, f32[48,128]{1,0:T(8,128)S(1)}, u32[]{:S(2)}, u32[]{:S(2)}) collective-permute-start(f32[48,128]{1,0:T(8,128)S(1)} %near.1), channel_id=1, source_target_pairs={{0,1},{1,0},{2,3},{3,2},{4,5},{5,4},{6,7},{7,6},{8,9},{9,8},{10,11... | collective-permute-start | bytes 73736 | tf_op jit(solution)/shard_map/ppermute | solution.py:107
  52.8 1.7 %collective-permute-done.7.near = f32[48,128]{1,0:T(8,128)S(1)} collective-permute-done((f32[48,128]{1,0:T(8,128)S(1)}, f32[48,128]{1,0:T(8,128)S(1)}, u32[]{:S(2)}, u32[]{:S(2)}) %collective-permute-start.7) | collective-permute-done | bytes 24608 | tf_op jit(solution)/shard_map/ppermute | solution.py:107
  54.5 0.8 %finish.1 = f32[96,96]{1,0:T(8,128)} custom-call(f32[96,96]{1,0:T(8,128)S(1)} %far.1.total, f32[48,128]{1,0:T(8,128)S(1)} %collective-permute-done.7.near, f32[96,96]{1,0:T(8,128)S(1)} %copy-done.2), custom_call_target="tpu_custom_call" | custom-call | flops 1000000000 | bytes 1048576 | tf_op jit(solution)/shard_map/finish/pallas_call | solution.py:611
  (40 shorter events, 1.2 us)
Async XLA Ops:
  0.6 9.7 %collective-permute-start = (f32[96,96]{1,0:T(8,128)}, f32[96,96]{1,0:T(8,128)S(1)}, u32[]{:S(2)}, u32[]{:S(2)}) collective-permute-start(f32[96,96]{1,0:T(8,128)} %latent.3), channel_id=1, source_target_pairs={{0,1},{1,0},{2,3},{3,2},{4,5},{5,4},{6,7},{7,6},{8,9},{9,8},{10,11... | collective-permute-start | bytes 110600 | tf_op jit(solution)/shard_map/ppermute | solution.py:107
  3.7 6.7 %collective-permute-start.1 = (f32[96,96]{1,0:T(8,128)}, f32[96,96]{1,0:T(8,128)S(1)}, u32[]{:S(2)}, u32[]{:S(2)}) collective-permute-start(f32[96,96]{1,0:T(8,128)} %latent.3), channel_id=1, source_target_pairs={{0,0},{7,7},{1,2},{2,1},{3,4},{4,3},{5,6},{6,5},{8,8},{15,15},{9,1... | collective-permute-start | bytes 110600 | tf_op jit(solution)/shard_map/ppermute | solution.py:115
  5.1 0.8 %copy-start.1 = (f32[96,96]{1,0:T(8,128)S(1)}, f32[96,96]{1,0:T(8,128)}, u32[]{:S(2)}) copy-start(f32[96,96]{1,0:T(8,128)} %latent.3) | copy-start | bytes 110596
  5.9 1.9 %copy-start.14 = (f32[2,12,129,129]{3,0,2,1:T(2,128)S(1)}, f32[2,12,129,129]{3,0,2,1:T(2,128)}, u32[]{:S(2)}) copy-start(f32[2,12,129,129]{3,0,2,1:T(2,128)} %param.10) | copy-start | bytes 4792612
  7.8 1.4 %copy-start = (bf16[12,256,256]{2,1,0:T(8,128)(2,1)S(1)}, bf16[12,256,256]{2,1,0:T(8,128)(2,1)}, u32[]{:S(2)}) copy-start(bf16[12,256,256]{2,1,0:T(8,128)(2,1)} %constant.5.clone.tables) | copy-start | bytes 4718596
  10.6 1.4 %collective-permute-start.2 = (f32[96,224]{1,0:T(8,128)S(1)}, f32[96,224]{1,0:T(8,128)S(1)}, u32[]{:S(2)}, u32[]{:S(2)}) collective-permute-start(f32[96,224]{1,0:T(8,128)S(1)} %get-tuple-element.27.band), channel_id=1, source_target_pairs={{0,8},{8,0},{16,24},{24,16},{1,9},{9,1},{17,25},{25,17},{2,10},{10... | collective-permute-start | bytes 258056 | tf_op jit(solution)/shard_map/ppermute | solution.py:107
  12.0 3.4 %collective-permute-start.3 = (f32[64,224]{1,0:T(8,128)S(1)}, f32[64,224]{1,0:T(8,128)S(1)}, u32[]{:S(2)}, u32[]{:S(2)}) collective-permute-start(f32[64,224]{1,0:T(8,128)S(1)} %get-tuple-element.30), channel_id=1, source_target_pairs={{0,16},{16,24},{24,8},{8,0},{1,17},{17,25},{25,9},{9,1},{2,18},{18... | collective-permute-start | bytes 172040 | tf_op jit(solution)/shard_map/ppermute | solution.py:122
  13.5 1.9 %copy-start.3 = (f32[1,256]{1,0:T(1,128)S(1)}, f32[1,256]{1,0:T(1,128)}, u32[]{:S(2)}) copy-start(f32[1,256]{1,0:T(1,128)} %slopes.1) | copy-start | bytes 3076
  13.5 1.9 %copy-start.4 = (s32[1,256]{1,0:T(1,128)S(1)}, s32[1,256]{1,0:T(1,128)}, u32[]{:S(2)}) copy-start(s32[1,256]{1,0:T(1,128)} %pixels.3) | copy-start | bytes 3076
  13.5 1.9 %copy-start.6 = (f32[12]{0:T(128)S(1)}, f32[12]{0:T(128)}, u32[]{:S(2)}) copy-start(f32[12]{0:T(128)} %weights.5) | copy-start | bytes 148
  15.2 5.0 %copy-start.8 = (f32[2,3,224,256]{3,2,1,0:T(8,128)}, f32[2,3,224,256]{3,2,1,0:T(8,128)S(1)}, u32[]{:S(2)}) copy-start(f32[2,3,224,256]{3,2,1,0:T(8,128)S(1)} %get-tuple-element.34.rest_2_) | copy-start | bytes 4128772
  15.2 5.0 %copy-start.10 = (f32[2,3,224,256]{3,2,1,0:T(8,128)}, f32[2,3,224,256]{3,2,1,0:T(8,128)S(1)}, u32[]{:S(2)}) copy-start(f32[2,3,224,256]{3,2,1,0:T(8,128)S(1)} %get-tuple-element.35.rest_3_) | copy-start | bytes 4128772
  15.4 20.6 %copy-start.5 = (f32[8]{0:T(128)S(1)}, f32[8]{0:T(128)}, u32[]{:S(2)}) copy-start(f32[8]{0:T(128)} %doses.1) | copy-start | bytes 100
  20.2 0.8 %copy-start.12 = (f32[12,96,128]{2,1,0:T(8,128)}, f32[12,96,128]{2,1,0:T(8,128)S(1)}, u32[]{:S(2)}) copy-start(f32[12,96,128]{2,1,0:T(8,128)S(1)} %get-tuple-element.40.field_im) | copy-start | bytes 1769476
  21.0 15.0 %all-to-all-start = ((f32[32,1,512]{2,1,0:T(1,128)}), f32[32,1,512]{2,1,0:T(1,128)S(1)}, u32[]{:S(2)}, u32[]{:S(2)}) async-start(f32[32,1,512]{2,1,0:T(1,128)} %get-tuple-element.36), calls=%async_computation | async-start | bytes 131072 | tf_op jit(solution)/shard_map/all_to_all | solution.py:522
  36.0 1.5 %copy-start.7 = (bf16[7,256,256]{2,1,0:T(8,128)(2,1)S(1)}, bf16[7,256,256]{2,1,0:T(8,128)(2,1)}, u32[]{:S(2)}) copy-start(bf16[7,256,256]{2,1,0:T(8,128)(2,1)} %constant.4.clone.tables) | copy-start | bytes 2752516
  36.0 1.6 %copy-start.9 = (f32[2,3,224,256]{3,2,1,0:T(8,128)S(1)}, f32[2,3,224,256]{3,2,1,0:T(8,128)}, u32[]{:S(2)}) copy-start(f32[2,3,224,256]{3,2,1,0:T(8,128)} %copy-done.8) | copy-start | bytes 4128772
  36.1 2.0 %copy-start.11 = (f32[2,3,224,256]{3,2,1,0:T(8,128)S(1)}, f32[2,3,224,256]{3,2,1,0:T(8,128)}, u32[]{:S(2)}) copy-start(f32[2,3,224,256]{3,2,1,0:T(8,128)} %copy-done.10) | copy-start | bytes 4128772
  36.1 2.1 %copy-start.13 = (f32[12,96,128]{2,1,0:T(8,128)S(1)}, f32[12,96,128]{2,1,0:T(8,128)}, u32[]{:S(2)}) copy-start(f32[12,96,128]{2,1,0:T(8,128)} %copy-done.12) | copy-start | bytes 1769476
  43.0 4.3 %collective-permute-start.4 = (f32[64,224]{1,0:T(8,128)S(1)}, f32[64,224]{1,0:T(8,128)S(1)}, u32[]{:S(2)}, u32[]{:S(2)}) collective-permute-start(f32[64,224]{1,0:T(8,128)S(1)} %get-tuple-element.42), channel_id=1, source_target_pairs={{16,0},{24,16},{8,24},{0,8},{17,1},{25,17},{9,25},{1,9},{18,2},{26... | collective-permute-start | bytes 172040 | tf_op jit(solution)/shard_map/ppermute | solution.py:122
  47.3 1.4 %collective-permute-start.5 = (f32[96,224]{1,0:T(8,128)S(1)}, f32[96,224]{1,0:T(8,128)S(1)}, u32[]{:S(2)}, u32[]{:S(2)}) collective-permute-start(f32[96,224]{1,0:T(8,128)S(1)} %fold.2), channel_id=1, source_target_pairs={{0,8},{8,0},{16,24},{24,16},{1,9},{9,1},{17,25},{25,17},{2,10},{10... | collective-permute-start | bytes 258056 | tf_op jit(solution)/shard_map/ppermute | solution.py:107
  48.7 4.0 %collective-permute-start.6 = (f32[48,128]{1,0:T(8,128)S(1)}, f32[48,128]{1,0:T(8,128)S(1)}, u32[]{:S(2)}, u32[]{:S(2)}) collective-permute-start(f32[48,128]{1,0:T(8,128)S(1)} %get-tuple-element.44), channel_id=1, source_target_pairs={{0,0},{7,7},{1,2},{2,1},{3,4},{4,3},{5,6},{6,5},{8,8},{15,15},{9,1... | collective-permute-start | bytes 73736 | tf_op jit(solution)/shard_map/ppermute | solution.py:115
  49.5 5.0 %copy-start.2 = (f32[96,96]{1,0:T(8,128)S(1)}, f32[96,96]{1,0:T(8,128)}, u32[]{:S(2)}) copy-start(f32[96,96]{1,0:T(8,128)} %latent.3) | copy-start | bytes 110596
  49.5 5.0 %collective-permute-start.7 = (f32[48,128]{1,0:T(8,128)S(1)}, f32[48,128]{1,0:T(8,128)S(1)}, u32[]{:S(2)}, u32[]{:S(2)}) collective-permute-start(f32[48,128]{1,0:T(8,128)S(1)} %near.1), channel_id=1, source_target_pairs={{0,1},{1,0},{2,3},{3,2},{4,5},{5,4},{6,7},{7,6},{8,9},{9,8},{10,11... | collective-permute-start | bytes 73736 | tf_op jit(solution)/shard_map/ppermute | solution.py:107

commit v10 on v9

--- a/solution.py
+++ b/solution.py
@@ -14,7 +14,7 @@
 RESIST_LEVEL = 0.7
 SOFTNESS = 0.25
 LANES = 128
-BATCH = 3
+BATCH = 4
 F32 = jnp.float32
 BF16 = jnp.bfloat16
 
@@ -24,6 +24,21 @@
     return high, (x - high.astype(F32)).astype(BF16)
 
 
+def split3(x):
+    first = x.astype(BF16)
+    rest = x - first.astype(F32)
+    second = rest.astype(BF16)
+    return first, second, (rest - second.astype(F32)).astype(BF16)
+
+
+def table_parts(table):
+    parts = []
+    for _ in range(3):
+        parts.append(table.astype(ml_dtypes.bfloat16))
+        table = table - parts[-1].astype(np.float64)
+    return parts
+
+
 def dot(a, b):
     return jnp.dot(a, b, preferred_element_type=F32)
 
@@ -34,6 +49,11 @@
 
 def stacked(pair):
     return jnp.concatenate(pair, axis=0)
+
+
+def dot6(a, b):
+    small = dot(a[0], b[2]) + dot(a[1], b[1]) + dot(a[2], b[0])
+    return small + (dot(a[0], b[1]) + dot(a[1], b[0])) + dot(a[0], b[0])
 
 
 def dot3_stacked(a, b):
@@ -43,54 +63,67 @@
     return tall[:count] + tall[count:] + dot(high, b[1])
 
 
-def wave_tables(period, tile):
+def waves(period, places):
+    turn = (np.arange(period // 2) + 0.5) * (2.0 * math.pi / period)
+    angle = turn[:, None] * places[None, :]
+    return np.cos(angle), np.sin(angle)
+
+
+def wave_table(period, places, by_lane=False):
     half = period // 2
-    turn = (np.arange(half) + 0.5) * (2.0 * math.pi / period)
-    size = 2 * LANES
-
-    def parts(table):
-        high = table.astype(ml_dtypes.bfloat16)
-        return high, (table - high.astype(np.float64)).astype(ml_dtypes.bfloat16)
-
-    def both(places):
-        angle = turn[:, None] * places[None, :]
-        return np.cos(angle), np.sin(angle)
-
-    def whole_table(places, by_lane):
-        cos, sin = both(places)
-        out = np.zeros((size, size))
-        out[:half, : len(places)] = cos
-        start = LANES if by_lane else half
-        out[start : start + half, : len(places)] = sin
-        return out
-
+    out = np.zeros((2 * LANES, 2 * LANES))
+    for first, table in zip((0, LANES if by_lane else half), waves(period, places)):
+        out[first : first + half, : len(places)] = table
+    return out
+
+
+def spectra_tables(period, last):
+    taps = np.arange(last + 1)
+    wide = wave_table(period, taps, True)
+    tall = wave_table(period, taps)
+    c1, c2, c3 = (part[:, :last].T for part in table_parts(wide))
+    lanes = np.stack([np.concatenate(two) for two in ((c1, c1), (c2, c2), (c1, c3))])
+    c1, c2, c3 = (part[:period, :last] for part in table_parts(tall))
+    rows = [np.concatenate(two, axis=1) for two in ((c1, c1), (c2, c2), (c1, c3))]
+    ends = np.zeros((period + 8, 2 * LANES), np.float32)
+    ends[:period] = tall[:period, last : last + 1]
+    ends[period] = wide[:, last]
+    return lanes, np.concatenate(rows), ends
+
+
+def field_tables(period, tile):
+    half, rows = period // 2, tile // 2
     place = np.arange(period)
-    wide = whole_table(place, True)
-    tall = whole_table(place, False)
-    centred = whole_table(place - (tile - 1) / 2, False)
-    out = np.zeros((12, size, size), ml_dtypes.bfloat16)
-    for first, table in ((0, wide.T), (2, tall), (4, wide), (6, centred), (8, centred.T)):
-        out[first], out[first + 1] = parts(table)
-    rows = tile // 2
-    for i, table in enumerate(both(np.arange(rows) + 0.5)):
-        high, low = parts(table)
-        top = 2 * rows * i
-        out[10, top : top + rows, :half] = high.T
-        out[10, top : top + rows, half:period] = high.T
-        out[10, top + rows : top + 2 * rows, :half] = low.T
-        top = half * i
-        out[11, top : top + half, :rows] = high
-        out[11, top : top + half, rows : 2 * rows] = high
-        out[11, top : top + half, 2 * rows : 3 * rows] = low
-    return out
+    wide = table_parts(wave_table(period, place, True))
+    centred = table_parts(wave_table(period, place - (tile - 1) / 2))
+    out = [part.T for part in wide] + centred + wide
+    for table in waves(period, np.arange(rows) + 0.5):
+        c1, c2, c3 = table_parts(table.T)
+        slot = np.zeros((2 * LANES, 2 * LANES), ml_dtypes.bfloat16)
+        for i, two in enumerate(((c1, c1), (c2, c2), (c1, c3))):
+            slot[i * rows : (i + 1) * rows, :period] = np.concatenate(two, axis=1)
+        out.append(slot)
+    return np.stack(out)
+
+
+def gradient_tables(period, tile):
+    half, rows = period // 2, tile // 2
+    place = np.arange(period)
+    wide = table_parts(wave_table(period, place, True))[:2]
+    centred = table_parts(wave_table(period, place - (tile - 1) / 2))[:2]
+    slot = np.zeros((2 * LANES, 2 * LANES), ml_dtypes.bfloat16)
+    for i, table in enumerate(waves(period, np.arange(rows) + 0.5)):
+        high, low, _ = table_parts(table)
+        slot[i * half : (i + 1) * half, : 3 * rows] = np.concatenate([high, high, low], axis=1)
+    return np.stack([part.T for part in wide] + wide + [part.T for part in centred] + [slot])
 
 
 def pair(tables, first, rows, cols):
     return tables[first, :rows, :cols], tables[first + 1, :rows, :cols]
 
 
-def whole(parts):
-    return parts[0].astype(F32) + parts[1].astype(F32)
+def triple(tables, first, rows, cols):
+    return [tables[first + i, :rows, :cols] for i in range(3)]
 
 
 def halves(x):
@@ -122,32 +155,23 @@
     return lax.ppermute(x, axis, [(b, a) if back else (a, b) for a, b in pairs])
 
 
-def spectra_kernel(start, groups, kern, tables, *rest):
-    *outs, token, edge = rest[-2 - groups :]
-    period = outs[0].shape[2]
+def spectra_kernel(start, first_out, groups, kern, lanes, rows, ends, *rest):
+    out, token = rest[-2:]
+    period = out.shape[2]
     half = period // 2
     last = kern.shape[-1] - 1
-    cols = pair(tables, 0, last, 2 * LANES)
-    cols = (stacked((cols[0], cols[0])), cols[1])
-    end_row = whole((tables[0, last : last + 16, :], tables[1, last : last + 16, :]))[:1]
-    high, low = pair(tables, 2, period, last)
-    rows = stacked(
-        (
-            jnp.concatenate([high, high], axis=1),
-            jnp.concatenate([low, jnp.zeros_like(low)], axis=1),
-        )
-    )
-    end_col = whole(pair(tables, 2, period, 2 * LANES))[:, last : last + 1]
-    edge[...] = jnp.broadcast_to(end_col, edge.shape)
+    end_row = ends[period : period + 1]
+    token[...] = jnp.zeros(token.shape, F32)
 
     def along_lanes(planes):
         main = stacked([plane[:last] for plane in planes])
         tail = stacked([plane[last:] for plane in planes])
         tail = jnp.concatenate([tail, jnp.zeros((-tail.shape[0] % 16, last + 1), F32)], axis=0)
         both = stacked((main, tail))
-        high, low = split(both[:, :last])
-        out = dot(jnp.concatenate([high, low], axis=1), cols[0]) + dot(high, cols[1])
-        out = out + both[:, last:] * end_row
+        x1, x2, x3 = split3(both[:, :last])
+        most = jnp.concatenate([x1, x2], axis=1)
+        out = dot(jnp.concatenate([x3, x1], axis=1), lanes[2]) + dot(most, lanes[1])
+        out = out + dot(most, lanes[0]) + both[:, last:] * end_row
         first = len(planes) * last
         return [
             (out[i * last : (i + 1) * last], out[first + i : first + i + 1])
@@ -155,9 +179,10 @@
         ]
 
     def along_rows(wide, tail):
-        tall = dot(rows, stacked(split(wide)))
-        outer = [edge[...] * tail[:, :LANES], edge[...] * tail[:, LANES:]]
-        return tall[:period] + tall[period:] + jnp.concatenate(outer, axis=1)
+        x1, x2, x3 = split3(wide)
+        tall = dot(rows[: 2 * period], stacked((x1, x2)))
+        small = dot(rows[2 * period :], stacked((x3, x1)))
+        return tall[:period] + (tall[period:] + small) + ends[:period] * tail
 
     def mixed(real, imag):
         real_cos, real_sin = halves(real)
@@ -167,19 +192,20 @@
             jnp.concatenate([real_sin + imag_cos, imag_cos - real_sin], axis=1),
         )
 
-    for group, out in enumerate(outs):
+    for group in range(groups):
         first = start + group * BATCH
         planes = along_lanes([kern[c, first + k] for k in range(BATCH) for c in range(2)])
         for k in range(BATCH):
+            to = first_out + group * BATCH + k
             (real, real_tail), (imag, imag_tail) = planes[2 * k : 2 * k + 2]
             wide_re, wide_im = mixed(real, imag)
             tail_re, tail_im = mixed(real_tail, imag_tail)
             tall_re = along_rows(wide_re, tail_re)
             tall_im = along_rows(wide_im, tail_im)
-            out[0, k, :half] = tall_re[:half] - tall_im[half:]
-            out[0, k, half:] = tall_re[:half] + tall_im[half:]
-            out[1, k, :half] = tall_im[:half] + tall_re[half:]
-            out[1, k, half:] = tall_im[:half] - tall_re[half:]
+            out[0, to, :half] = tall_re[:half] - tall_im[half:]
+            out[0, to, half:] = tall_re[:half] + tall_im[half:]
+            out[1, to, :half] = tall_im[:half] + tall_re[half:]
+            out[1, to, half:] = tall_im[:half] - tall_re[half:]
 
 
 def pack(x):
@@ -202,11 +228,8 @@
     radius = (band.shape[1] - tile) // 2
     lower, other = place_in_pair("tx")
 
-    def transmit(x):
-        return 0.5 * (1.0 + jnp.tanh(x))
-
-    near = transmit(jnp.where(lower, partner[:, :radius], partner[:, tile - radius :]))
-    far = transmit(jnp.where(lower, outside[:, tile - radius :], outside[:, :radius]))
+    near = jnp.where(lower, partner[:, :radius], partner[:, tile - radius :])
+    far = jnp.where(lower, outside[:, tile - radius :], outside[:, :radius])
     far = jnp.where(other, far, 0.0)
     band[:, :radius] = jnp.where(lower, far, near)
     band[:, radius : radius + tile] = middle[...]
@@ -298,8 +321,8 @@
     framed[:radius] = jnp.where(lower, outer, partner[tile - radius :])
     framed[radius + tile :] = jnp.where(lower, partner[:radius], outer)
     framed[radius : radius + tile] = band[...]
-    wide = dot3(split(framed[...]), pair(tables, 0, period, 2 * LANES))
-    tall = dot3(pair(tables, 6, period, period), split(wide)) * (1.0 / (period * period))
+    wide = dot6(split3(framed[...]), triple(tables, 0, period, 2 * LANES))
+    tall = dot6(triple(tables, 3, period, period), split3(wide)) * (1.0 / (period * period))
     cos_cos, cos_sin = halves(tall[:half])
     sin_cos, sin_sin = halves(tall[half:])
     same, other = cos_cos - sin_sin, cos_cos + sin_sin
@@ -308,16 +331,16 @@
     mask[1, :, :LANES], mask[1, :, LANES:] = -joint, -cross
     mask[2, :, :LANES], mask[2, :, LANES:] = other, same
     mask[3, :, :LANES], mask[3, :, LANES:] = cross, joint
-    cos_lift = tables[10, :tile, :period]
-    sin_lift = tables[10, tile : 2 * tile, :period]
     rows = tile // 2
 
-    def lift(table, x):
-        out = dot(table, stacked(split(x)))
-        return out[:rows] + out[rows:]
-
-    across = pair(tables, 4, 2 * LANES, LANES)
-    across = (across[0], jnp.concatenate(across, axis=1))
+    def lift(slot, x):
+        x1, x2, x3 = split3(x)
+        out = dot(tables[slot, :tile, :period], stacked((x1, x2)))
+        small = dot(tables[slot, tile : tile + rows, :period], stacked((x3, x1)))
+        return out[:rows] + (out[rows:] + small)
+
+    across = triple(tables, 6, 2 * LANES, LANES)
+    across = (across[0], jnp.concatenate(across[:2], axis=1), across[2])
 
     def lifted(own, k):
         pos_re, pos_im = own[0, k, :half], own[1, k, :half]
@@ -326,10 +349,10 @@
         up_im = mask[0] * pos_im + mask[1] * pos_re
         down_re = mask[2] * neg_re - mask[3] * neg_im
         down_im = mask[2] * neg_im + mask[3] * neg_re
-        even_re = lift(cos_lift, up_re + down_re)
-        even_im = lift(cos_lift, up_im + down_im)
-        odd_re = lift(sin_lift, up_im - down_im)
-        odd_im = lift(sin_lift, up_re - down_re)
+        even_re = lift(9, up_re + down_re)
+        even_im = lift(9, up_im + down_im)
+        odd_re = lift(10, up_im - down_im)
+        odd_im = lift(10, up_re - down_re)
         re_pos, re_neg = halves(stacked((even_re - odd_re, even_re + odd_re)))
         im_pos, im_neg = halves(stacked((even_im + odd_im, even_im - odd_im)))
         rows_re = jnp.concatenate([re_pos + re_neg, im_neg - im_pos], axis=1)
@@ -337,12 +360,13 @@
         return [rows_re, rows_im]
 
     intensity = jnp.zeros((tile, LANES), F32)
-    for group, own in enumerate(spec):
-        first = group * BATCH
-        lines = stacked([line for i in range(BATCH) for line in lifted(own, i)])
-        high, low = split(lines)
-        by_high, by_low = halves(dot(high, across[1]))
-        both = by_high + by_low + dot(low, across[0])
+    places = [(own, k) for own in spec for k in range(own.shape[1])]
+    for first in range(0, kernels, BATCH):
+        lines = stacked([line for i in range(BATCH) for line in lifted(*places[first + i])])
+        x1, x2, x3 = split3(lines)
+        most, more = halves(dot(x1, across[1]))
+        some, small = halves(dot(x2, across[1]))
+        both = small + dot(x1, across[2]) + dot(x3, across[0]) + (more + some) + most
         for i in range(BATCH):
             real = both[2 * i * tile : (2 * i + 1) * tile]
             imag = both[(2 * i + 1) * tile : (2 * i + 2) * tile]
@@ -395,7 +419,7 @@
 
     zero = jnp.zeros((devices, samples), F32)
     soft_sum, error_sum = lax.fori_loop(
-        0, corners, corner, (zero, zero), unroll=4 if devices <= 32 else 1
+        0, corners, corner, (zero, zero), unroll=8 if devices <= 32 else 1
     )
     soft_total = jnp.sum(soft_sum, keepdims=True)
     tail_mean = jnp.sum(error_sum, keepdims=True) / soft_total
@@ -455,7 +479,8 @@
     total_re[...] = jnp.zeros((period, 2 * LANES), F32)
     total_im[...] = jnp.zeros((period, 2 * LANES), F32)
 
-    for group, own in enumerate(spec):
+    places = [(own, k) for own in spec for k in range(own.shape[1])]
+    for group in range(len(places) // BATCH):
         sources = []
         for i in range(BATCH):
             k = group * BATCH + i
@@ -464,7 +489,7 @@
         high, low = split(stacked(sources))
         both = dot(jnp.concatenate([high, low], axis=1), cols[0]) + dot(high, cols[1])
         for i in range(BATCH):
-            k = group * BATCH + i
+            own, at = places[group * BATCH + i]
             real_cos, real_sin = halves(both[2 * i * tile : (2 * i + 1) * tile])
             imag_cos, imag_sin = halves(both[(2 * i + 1) * tile : (2 * i + 2) * tile])
             wide_re = jnp.concatenate([real_cos + imag_sin, real_cos - imag_sin], axis=1)
@@ -475,7 +500,7 @@
                 part = slice(start, start + half)
                 wave_re = cos_re + sign * sin_im
                 wave_im = cos_im - sign * sin_re
-                own_re, own_im = own[0, i, part], own[1, i, part]
+                own_re, own_im = own[0, at, part], own[1, at, part]
                 total_re[part] += own_re * wave_re + own_im * wave_im
                 total_im[part] += own_re * wave_im - own_im * wave_re
 
@@ -503,13 +528,14 @@
     return jax.ShapeDtypeStruct(dims, F32)
 
 
-def call(kernel, name, out_shape, in_specs, scratch=(), micros=1):
+def call(kernel, name, out_shape, in_specs, scratch=(), aliases=None, micros=1):
     return pl.pallas_call(
         kernel,
         out_shape=out_shape,
         in_specs=in_specs,
         out_specs=[VMEM] * len(out_shape),
         scratch_shapes=scratch,
+        input_output_aliases=aliases or {},
         compiler_params=pltpu.CompilerParams(vmem_limit_bytes=10 * 1024 * 1024),
         cost_estimate=pl.CostEstimate(
             flops=micros * 10**9, bytes_accessed=2**20, transcendentals=0
@@ -529,42 +555,41 @@
     radius = (taps - 1) // 2
     period = tile + 2 * radius
     half = period // 2
-    tables = wave_tables(period, tile)
-    last_tables = jnp.asarray(tables[[0, 1, 4, 5, 8, 9, 11]])
-    tables = jnp.asarray(tables)
+    first_tables = [jnp.asarray(x) for x in spectra_tables(period, taps - 1)]
+    tables = jnp.asarray(field_tables(period, tile))
+    last_tables = jnp.asarray(gradient_tables(period, tile))
     token = shape(8, LANES)
     packed = shape(tile // 2, 2 * radius)
     devices = lax.axis_size("ty") * lax.axis_size("tx")
 
-    spec = []
-
-    def spectra(groups, after):
-        *out, done = call(
-            functools.partial(spectra_kernel, len(spec) * BATCH, groups),
+    def spectra(start, first_out, groups, size, after, into=()):
+        return call(
+            functools.partial(spectra_kernel, start, first_out, groups),
             "spectra",
-            [shape(2, BATCH, period, 2 * LANES)] * groups + [token],
-            [VMEM] * 2 + [ANY],
-            scratch=[pltpu.VMEM((period, LANES), F32)],
+            [shape(2, size, period, 2 * LANES), token],
+            [VMEM] * 4 + [ANY] * (1 + len(into)),
+            aliases={5: 0} if into else None,
             micros=groups,
-        )(kernels, tables, after)
-        spec.extend(out)
-        return done
-
-    partner, outside = swap("tx", latent), swap_outside("tx", latent)
+        )(kernels, *first_tables, after, *into)
+
     transmit, done = call(
-        own_kernel, "own", [shape(tile, tile), token], [VMEM], micros=4
+        own_kernel, "own", [shape(tile, tile), token], [VMEM], micros=3
     )(latent)
-    done = spectra(1, done)
+    partner, outside = swap("tx", transmit), swap_outside("tx", transmit)
+    small, large = BATCH, count - BATCH
+    spec_a, done = spectra(0, 0, 1, small, done)
     band, done = call(
         band_kernel, "band", [shape(tile, period), token], [VMEM] * 3 + [ANY]
     )(transmit, partner, outside, done)
     partner = swap("ty", band)
-    done = spectra(1, done)
+    spec_b, done = spectra(small, 0, 1, large, done)
     rim, done = call(
         relay_rows_kernel, "relay", [shape(radius, period), token], [VMEM, ANY]
     )(partner, done)
     rim = ring("ty", rim)
-    spectra(count // BATCH - len(spec), done)
+    groups = large // BATCH - 1
+    spec_b, _ = spectra(2 * small, small, groups, large, done, (spec_b,))
+    spec = [spec_a, spec_b]
 
     field_re, field_im, sampled, copies = call(
         field_kernel,

time: 55.7 us -> 55.7 us (level)
  local copies, waits for them, and re-layouts: 5.58 us -> 2.05 us
  Pallas kernels: 16.4 us -> 19.4 us
  starting transfers between devices: 17.8 us -> 18.9 us
    unnamed x32 -> x30, local copies, waits for them, and re-layouts: 5.58 us -> 2.05 us
    pallas_call x4, Pallas kernels: 3.97 us -> 6.02 us  [the longest x3 6.01 us: spectra(): call(functools.partial(spectra_kernel, start, first_out, groups), 'spectr...]
    all_to_all x1, starting transfers between devices: 7.7 us -> 9.58 us  [gather_all(): return lax.all_to_all(copies, ('ty', 'tx'), 0, 0, tiled=True)]
    pallas_call x1, Pallas kernels: 4.79 us -> 6.51 us  [body(): call(field_kernel, 'field', [shape(count, tile, LANES)] * 2 + [shape(1, 2...]
    ppermute x2, starting transfers between devices: 2.11 us -> 1.31 us  [swap_outside(): return lax.ppermute(x, axis, pairs)]
    pallas_call x1, Pallas kernels: 4.74 us -> 4.07 us  [body(): call(gradient_kernel, 'gradient', [shape(period, period), shape(radius, p...]
  transfers between devices with their start and end apart: 9 -> 9, of which waited for: 6 -> 4; matrix products, arithmetic and copies ran while one was open for 1% -> 1% of each run, Pallas kernels for 8% -> 11%
where the time goes in v10:
time: 55.7 us; the launch traced here: 55.4 us
  Pallas kernels  19.4 us (35%)
  starting transfers between devices  18.9 us (34%)
  waiting for transfers between devices  13.6 us (24%)
  local copies, waits for them, and re-layouts  2.05 us (4%)
  between operations  1.57 us (3%)
    all_to_all x1, starting transfers between devices, gather_all(): return lax.all_to_all(copies, ('ty', 'tx'), 0, 0, tiled=True)  9.58 us
    pallas_call x1, Pallas kernels, body(): call(field_kernel, 'field', [shape(count, tile, LANES)] * 2 + [shape(1, 2...  6.51 us
    all_to_all x1, waiting for transfers between devices, gather_all(): return lax.all_to_all(copies, ('ty', 'tx'), 0, 0, tiled=True)  6.45 us
    ppermute x4, starting transfers between devices, swap(): lax.ppermute(x, axis, [(i, i ^ 1) for i in range(lax.axis_size(axis))])  6.35 us
    pallas_call x3, Pallas kernels, spectra(): call(functools.partial(spectra_kernel, start, first_out, groups), 'spectr...  6.01 us
    ppermute x2, waiting for transfers between devices, ring(): return lax.ppermute(x, axis, [(b, a) if back else (a, b) for a, b in pairs])  4.16 us
    pallas_call x1, Pallas kernels, body(): call(gradient_kernel, 'gradient', [shape(period, period), shape(radius, p...  4.07 us
    ppermute x4, waiting for transfers between devices, swap(): lax.ppermute(x, axis, [(i, i ^ 1) for i in range(lax.axis_size(axis))])  2.96 us
  transfers between devices with their start and end apart: 9, of which 4 were waited for; matrix products, arithmetic and copies ran while one was open for 1% of the time, Pallas kernels for 11%

profile of v10, /device:TPU:0, one launch (start us, length us, event | category | flops | bytes accessed | tf_op | source)
XLA Modules:
  0.0 55.4 jit_solution(3684562093903326732)
XLA Ops:
  0.6 0.8 %copy-done.5 = f32[96,96]{1,0:T(8,128)S(1)} copy-done((f32[96,96]{1,0:T(8,128)S(1)}, f32[96,96]{1,0:T(8,128)}, u32[]{:S(2)}) %copy-start.5) | copy-done | bytes 36888
  1.5 3.0 %collective-permute-start = (f32[96,96]{1,0:T(8,128)S(1)}, f32[96,96]{1,0:T(8,128)S(1)}, u32[]{:S(2)}, u32[]{:S(2)}) collective-permute-start(f32[96,96]{1,0:T(8,128)S(1)} %get-tuple-element.23.middle), channel_id=1, source_target_pairs={{0,1},{1,0},{2,3},{3,2},{4,5},{5,4},{6,7},{7,6},{8,9},{9,8},{10,11... | collective-permute-start | bytes 110600 | tf_op jit(solution)/shard_map/ppermute | solution.py:140
  4.5 0.7 %collective-permute-start.1 = (f32[96,96]{1,0:T(8,128)S(1)}, f32[96,96]{1,0:T(8,128)S(1)}, u32[]{:S(2)}, u32[]{:S(2)}) collective-permute-start(f32[96,96]{1,0:T(8,128)S(1)} %get-tuple-element.23.middle), channel_id=1, source_target_pairs={{0,0},{7,7},{1,2},{2,1},{3,4},{4,3},{5,6},{6,5},{8,8},{15,15},{9,1... | collective-permute-start | bytes 110600 | tf_op jit(solution)/shard_map/ppermute | solution.py:148
  5.2 0.3 copy.19.kern
  5.6 2.0 %spectra.3 = (f32[2,4,224,256]{3,2,1,0:T(8,128)S(1)}, f32[8,128]{1,0:T(8,128)S(1)}) custom-call(f32[2,12,129,129]{3,2,1,0:T(8,128)S(1)} %copy.19.kern, bf16[3,256,256]{2,1,0:T(8,128)(2,1)S(1)} %copy-done.2, bf16[672,256]{1,0:T(8,128)(2,1)S(1)} %copy-done.3, f32[232,256]{1,0:T(8,128)S(1)} %copy-done.4, f32[8,128]{1,0:T(8,128)S(1)} %get-tuple-element.24.rest_0_), custom_call_target="tpu_custom_call" | custom-call | flops 1000000000 | bytes 1048576 | tf_op jit(solution)/shard_map/spectra/pallas_call | solution.py:566
  7.6 0.2 band.1
  7.9 2.0 %spectra.4 = (f32[2,8,224,256]{3,2,1,0:T(8,128)S(1)}, f32[8,128]{1,0:T(8,128)S(1)}) custom-call(f32[2,12,129,129]{3,2,1,0:T(8,128)S(1)} %copy.19.kern, bf16[3,256,256]{2,1,0:T(8,128)(2,1)S(1)} %copy-done.2, bf16[672,256]{1,0:T(8,128)(2,1)S(1)} %copy-done.3, f32[232,256]{1,0:T(8,128)S(1)} %copy-done.4, f32[8,128]{1,0:T(8,128)S(1)} %get-tuple-element.27.rest_0_), custom_call_target="tpu_custom_call" | custom-call | flops 1000000000 | bytes 1048576 | tf_op jit(solution)/shard_map/spectra/pallas_call | solution.py:566
  9.9 1.5 %collective-permute-start.3 = (f32[64,224]{1,0:T(8,128)S(1)}, f32[64,224]{1,0:T(8,128)S(1)}, u32[]{:S(2)}, u32[]{:S(2)}) collective-permute-start(f32[64,224]{1,0:T(8,128)S(1)} %get-tuple-element.29), channel_id=1, source_target_pairs={{0,16},{16,24},{24,8},{8,0},{1,17},{17,25},{25,9},{9,1},{2,18},{18... | collective-permute-start | bytes 172040 | tf_op jit(solution)/shard_map/ppermute | solution.py:155
  11.4 2.0 %spectra.5 = (f32[2,8,224,256]{3,2,1,0:T(8,128)S(1)}, f32[8,128]{1,0:T(8,128)}) custom-call(f32[2,12,129,129]{3,2,1,0:T(8,128)S(1)} %copy.19.kern, bf16[3,256,256]{2,1,0:T(8,128)(2,1)S(1)} %copy-done.2, bf16[672,256]{1,0:T(8,128)(2,1)S(1)} %copy-done.3, f32[232,256]{1,0:T(8,128)S(1)} %copy-done.4, ...), custom_call_target="tpu_custom_call", output_to_operand_aliasing={{0}: (5, {})} | custom-call | flops 1000000000 | bytes 1048576 | tf_op jit(solution)/shard_map/spectra/pallas_call | solution.py:566
  13.5 6.5 %field.1 = (f32[12,96,128]{2,1,0:T(8,128)S(1)}, f32[12,96,128]{2,1,0:T(8,128)S(1)}, f32[1,512]{1,0:T(1,128)S(1)}, f32[32,1,512]{2,1,0:T(1,128)}) custom-call(f32[12]{0:T(128)S(1)} %copy-done.10, f32[96,224]{1,0:T(8,128)S(1)} %get-tuple-element.26.band, f32[96,224]{1,0:T(8,128)S(1)} %collective-permute-done.2.partner, ...), custom_call_target="tpu_custom_call" | custom-call | flops 7000000000 | bytes 1048576 | tf_op jit(solution)/shard_map/field/pallas_call | solution.py:594
  20.0 9.6 %all-to-all-start = ((f32[32,1,512]{2,1,0:T(1,128)}), f32[32,1,512]{2,1,0:T(1,128)S(1)}, u32[]{:S(2)}, u32[]{:S(2)}) async-start(f32[32,1,512]{2,1,0:T(1,128)} %get-tuple-element.34), calls=%async_computation | async-start | bytes 131072 | tf_op jit(solution)/shard_map/all_to_all | solution.py:548
  30.3 6.4 %all-to-all-done = f32[32,1,512]{2,1,0:T(1,128)S(1)} async-done(((f32[32,1,512]{2,1,0:T(1,128)}), f32[32,1,512]{2,1,0:T(1,128)S(1)}, u32[]{:S(2)}, u32[]{:S(2)}) %all-to-all-start) | async-done | bytes 65568 | tf_op jit(solution)/shard_map/all_to_all | solution.py:548
  36.7 1.4 %source.1 = (f32[96,128]{1,0:T(8,128)S(1)}, f32[1,1]{1,0:T(1,128)}) custom-call(f32[12]{0:T(128)S(1)} %copy-done.10, f32[8]{0:T(128)S(1)} %copy-done.9, s32[1]{0:T(128)S(6)} %copy.26.pick, f32[32,512]{1,0:T(8,128)S(1)} %bitcast.4, f32[1,512]{1,0:T(1,128)S(1)} %get-tuple-element.35.sampled, s32[1,256]{1,0:T(1,128)S(1)} %copy-done.8), custom_call_target="tpu_custom_call" | custom-call | flops 2000000000 | bytes 1048576 | tf_op jit(solution)/shard_map/source/pallas_call | solution.py:608
  38.2 0.6 %copy-done.1 = f32[2,8,224,256]{3,2,1,0:T(8,128)S(1)} copy-done((f32[2,8,224,256]{3,2,1,0:T(8,128)S(1)}, f32[2,8,224,256]{3,2,1,0:T(8,128)}, u32[]{:S(2)}) %copy-start.1) | copy-done | bytes 3670040
  38.8 0.2 copy-done.12
  39.0 4.1 %gradient.1 = (f32[224,224]{1,0:T(8,128)S(1)}, f32[64,224]{1,0:T(8,128)S(1)}) custom-call(f32[12]{0:T(128)S(1)} %copy-done.10, f32[96,128]{1,0:T(8,128)S(1)} %get-tuple-element.36.grid, f32[12,96,128]{2,1,0:T(8,128)S(1)} %get-tuple-element.37.field_re, f32[12,96,128]{2,1,0:T(8,128)S(1)} %get-tuple-element.38.field_im, bf16[7,256,256]{2,1,0:T(8,128)(2,1)S(1)} %copy-done.12, ...), custom_call_target="tpu_custom_call" | custom-call | flops 6000000000 | bytes 1048576 | tf_op jit(solution)/shard_map/gradient/pallas_call | solution.py:615
  43.1 0.1 collective-permute-start.4
  43.2 4.2 %collective-permute-done.4.rim = f32[64,224]{1,0:T(8,128)S(1)} collective-permute-done((f32[64,224]{1,0:T(8,128)S(1)}, f32[64,224]{1,0:T(8,128)S(1)}, u32[]{:S(2)}, u32[]{:S(2)}) %collective-permute-start.4) | collective-permute-done | bytes 57376 | tf_op jit(solution)/shard_map/ppermute | solution.py:155
  47.5 1.3 %collective-permute-done.5.partner = f32[96,224]{1,0:T(8,128)S(1)} collective-permute-done((f32[96,224]{1,0:T(8,128)S(1)}, f32[96,224]{1,0:T(8,128)S(1)}, u32[]{:S(2)}, u32[]{:S(2)}) %collective-permute-start.5) | collective-permute-done | bytes 86048 | tf_op jit(solution)/shard_map/ppermute | solution.py:140
  48.9 0.7 %collective-permute-start.6 = (f32[48,128]{1,0:T(8,128)S(1)}, f32[48,128]{1,0:T(8,128)S(1)}, u32[]{:S(2)}, u32[]{:S(2)}) collective-permute-start(f32[48,128]{1,0:T(8,128)S(1)} %get-tuple-element.42), channel_id=1, source_target_pairs={{0,0},{7,7},{1,2},{2,1},{3,4},{4,3},{5,6},{6,5},{8,8},{15,15},{9,1... | collective-permute-start | bytes 73736 | tf_op jit(solution)/shard_map/ppermute | solution.py:148
  49.6 3.2 %collective-permute-start.7 = (f32[48,128]{1,0:T(8,128)S(1)}, f32[48,128]{1,0:T(8,128)S(1)}, u32[]{:S(2)}, u32[]{:S(2)}) collective-permute-start(f32[48,128]{1,0:T(8,128)S(1)} %near.1), channel_id=1, source_target_pairs={{0,1},{1,0},{2,3},{3,2},{4,5},{5,4},{6,7},{7,6},{8,9},{9,8},{10,11... | collective-permute-start | bytes 73736 | tf_op jit(solution)/shard_map/ppermute | solution.py:140
  52.8 0.1 far.1.total
  53.0 1.7 %collective-permute-done.7.near = f32[48,128]{1,0:T(8,128)S(1)} collective-permute-done((f32[48,128]{1,0:T(8,128)S(1)}, f32[48,128]{1,0:T(8,128)S(1)}, u32[]{:S(2)}, u32[]{:S(2)}) %collective-permute-start.7) | collective-permute-done | bytes 24608 | tf_op jit(solution)/shard_map/ppermute | solution.py:140
  54.6 0.8 %finish.1 = f32[96,96]{1,0:T(8,128)} custom-call(f32[96,96]{1,0:T(8,128)S(1)} %far.1.total, f32[48,128]{1,0:T(8,128)S(1)} %collective-permute-done.7.near, f32[96,96]{1,0:T(8,128)S(1)} %copy-done.6), custom_call_target="tpu_custom_call" | custom-call | flops 1000000000 | bytes 1048576 | tf_op jit(solution)/shard_map/finish/pallas_call | solution.py:636
  (38 shorter events, 0.4 us)
Async XLA Ops:
  0.6 0.8 %copy-start.5 = (f32[96,96]{1,0:T(8,128)S(1)}, f32[96,96]{1,0:T(8,128)}, u32[]{:S(2)}) copy-start(f32[96,96]{1,0:T(8,128)} %latent.3) | copy-start | bytes 110596
  1.4 3.8 %copy-start.13 = (f32[2,12,129,129]{3,0,2,1:T(2,128)S(1)}, f32[2,12,129,129]{3,0,2,1:T(2,128)}, u32[]{:S(2)}) copy-start(f32[2,12,129,129]{3,0,2,1:T(2,128)} %param.13) | copy-start | bytes 4792612
  1.5 4.1 %copy-start.2 = (bf16[3,256,256]{2,1,0:T(8,128)(2,1)S(1)}, bf16[3,256,256]{2,1,0:T(8,128)(2,1)}, u32[]{:S(2)}) copy-start(bf16[3,256,256]{2,1,0:T(8,128)(2,1)} %constant.10.clone.lanes) | copy-start | bytes 1179652
  1.5 4.1 %copy-start.3 = (bf16[672,256]{1,0:T(8,128)(2,1)S(1)}, bf16[672,256]{1,0:T(8,128)(2,1)}, u32[]{:S(2)}) copy-start(bf16[672,256]{1,0:T(8,128)(2,1)} %constant.11.clone.rows) | copy-start | bytes 1032196
  1.5 4.1 %copy-start.4 = (f32[232,256]{1,0:T(8,128)S(1)}, f32[232,256]{1,0:T(8,128)}, u32[]{:S(2)}) copy-start(f32[232,256]{1,0:T(8,128)} %constant.12.clone.ends) | copy-start | bytes 712708
  1.5 6.1 %collective-permute-start = (f32[96,96]{1,0:T(8,128)S(1)}, f32[96,96]{1,0:T(8,128)S(1)}, u32[]{:S(2)}, u32[]{:S(2)}) collective-permute-start(f32[96,96]{1,0:T(8,128)S(1)} %get-tuple-element.23.middle), channel_id=1, source_target_pairs={{0,1},{1,0},{2,3},{3,2},{4,5},{5,4},{6,7},{7,6},{8,9},{9,8},{10,11... | collective-permute-start | bytes 110600 | tf_op jit(solution)/shard_map/ppermute | solution.py:140
  4.5 3.1 %collective-permute-start.1 = (f32[96,96]{1,0:T(8,128)S(1)}, f32[96,96]{1,0:T(8,128)S(1)}, u32[]{:S(2)}, u32[]{:S(2)}) collective-permute-start(f32[96,96]{1,0:T(8,128)S(1)} %get-tuple-element.23.middle), channel_id=1, source_target_pairs={{0,0},{7,7},{1,2},{2,1},{3,4},{4,3},{5,6},{6,5},{8,8},{15,15},{9,1... | collective-permute-start | bytes 110600 | tf_op jit(solution)/shard_map/ppermute | solution.py:148
  7.8 2.1 %collective-permute-start.2 = (f32[96,224]{1,0:T(8,128)S(1)}, f32[96,224]{1,0:T(8,128)S(1)}, u32[]{:S(2)}, u32[]{:S(2)}) collective-permute-start(f32[96,224]{1,0:T(8,128)S(1)} %get-tuple-element.26.band), channel_id=1, source_target_pairs={{0,8},{8,0},{16,24},{24,16},{1,9},{9,1},{17,25},{25,17},{2,10},{10... | collective-permute-start | bytes 258056 | tf_op jit(solution)/shard_map/ppermute | solution.py:140
  9.9 3.5 %collective-permute-start.3 = (f32[64,224]{1,0:T(8,128)S(1)}, f32[64,224]{1,0:T(8,128)S(1)}, u32[]{:S(2)}, u32[]{:S(2)}) collective-permute-start(f32[64,224]{1,0:T(8,128)S(1)} %get-tuple-element.29), channel_id=1, source_target_pairs={{0,16},{16,24},{24,8},{8,0},{1,17},{17,25},{25,9},{9,1},{2,18},{18... | collective-permute-start | bytes 172040 | tf_op jit(solution)/shard_map/ppermute | solution.py:155
  11.4 2.0 %copy-start.7 = (f32[1,256]{1,0:T(1,128)S(1)}, f32[1,256]{1,0:T(1,128)}, u32[]{:S(2)}) copy-start(f32[1,256]{1,0:T(1,128)} %slopes.1) | copy-start | bytes 3076
  11.4 2.1 %copy-start.8 = (s32[1,256]{1,0:T(1,128)S(1)}, s32[1,256]{1,0:T(1,128)}, u32[]{:S(2)}) copy-start(s32[1,256]{1,0:T(1,128)} %pixels.3) | copy-start | bytes 3076
  11.4 2.1 %copy-start.10 = (f32[12]{0:T(128)S(1)}, f32[12]{0:T(128)}, u32[]{:S(2)}) copy-start(f32[12]{0:T(128)} %weights.5) | copy-start | bytes 148
  11.4 2.1 %copy-start.11 = (bf16[11,256,256]{2,1,0:T(8,128)(2,1)S(1)}, bf16[11,256,256]{2,1,0:T(8,128)(2,1)}, u32[]{:S(2)}) copy-start(bf16[11,256,256]{2,1,0:T(8,128)(2,1)} %constant.13.clone.tables) | copy-start | bytes 4325380
  13.4 6.6 %copy-start = (f32[2,8,224,256]{3,2,1,0:T(8,128)}, f32[2,8,224,256]{3,2,1,0:T(8,128)S(1)}, u32[]{:S(2)}) copy-start(f32[2,8,224,256]{3,2,1,0:T(8,128)S(1)} %get-tuple-element.33.rest_1_) | copy-start | bytes 11010052
  13.5 23.2 %copy-start.9 = (f32[8]{0:T(128)S(1)}, f32[8]{0:T(128)}, u32[]{:S(2)}) copy-start(f32[8]{0:T(128)} %doses.1) | copy-start | bytes 100
  20.0 16.7 %all-to-all-start = ((f32[32,1,512]{2,1,0:T(1,128)}), f32[32,1,512]{2,1,0:T(1,128)S(1)}, u32[]{:S(2)}, u32[]{:S(2)}) async-start(f32[32,1,512]{2,1,0:T(1,128)} %get-tuple-element.34), calls=%async_computation | async-start | bytes 131072 | tf_op jit(solution)/shard_map/all_to_all | solution.py:548
  36.7 2.0 %copy-start.1 = (f32[2,8,224,256]{3,2,1,0:T(8,128)S(1)}, f32[2,8,224,256]{3,2,1,0:T(8,128)}, u32[]{:S(2)}) copy-start(f32[2,8,224,256]{3,2,1,0:T(8,128)} %copy-done) | copy-start | bytes 11010052
  36.7 2.3 %copy-start.12 = (bf16[7,256,256]{2,1,0:T(8,128)(2,1)S(1)}, bf16[7,256,256]{2,1,0:T(8,128)(2,1)}, u32[]{:S(2)}) copy-start(bf16[7,256,256]{2,1,0:T(8,128)(2,1)} %constant.14.clone.tables) | copy-start | bytes 2752516
  43.1 4.3 %collective-permute-start.4 = (f32[64,224]{1,0:T(8,128)S(1)}, f32[64,224]{1,0:T(8,128)S(1)}, u32[]{:S(2)}, u32[]{:S(2)}) collective-permute-start(f32[64,224]{1,0:T(8,128)S(1)} %get-tuple-element.40), channel_id=1, source_target_pairs={{16,0},{24,16},{8,24},{0,8},{17,1},{25,17},{9,25},{1,9},{18,2},{26... | collective-permute-start | bytes 172040 | tf_op jit(solution)/shard_map/ppermute | solution.py:155
  47.4 1.4 %collective-permute-start.5 = (f32[96,224]{1,0:T(8,128)S(1)}, f32[96,224]{1,0:T(8,128)S(1)}, u32[]{:S(2)}, u32[]{:S(2)}) collective-permute-start(f32[96,224]{1,0:T(8,128)S(1)} %fold.2), channel_id=1, source_target_pairs={{0,8},{8,0},{16,24},{24,16},{1,9},{9,1},{17,25},{25,17},{2,10},{10... | collective-permute-start | bytes 258056 | tf_op jit(solution)/shard_map/ppermute | solution.py:140
  48.9 4.0 %collective-permute-start.6 = (f32[48,128]{1,0:T(8,128)S(1)}, f32[48,128]{1,0:T(8,128)S(1)}, u32[]{:S(2)}, u32[]{:S(2)}) collective-permute-start(f32[48,128]{1,0:T(8,128)S(1)} %get-tuple-element.42), channel_id=1, source_target_pairs={{0,0},{7,7},{1,2},{2,1},{3,4},{4,3},{5,6},{6,5},{8,8},{15,15},{9,1... | collective-permute-start | bytes 73736 | tf_op jit(solution)/shard_map/ppermute | solution.py:148
  49.5 5.1 %copy-start.6 = (f32[96,96]{1,0:T(8,128)S(1)}, f32[96,96]{1,0:T(8,128)}, u32[]{:S(2)}) copy-start(f32[96,96]{1,0:T(8,128)} %latent.3) | copy-start | bytes 110596
  49.6 5.0 %collective-permute-start.7 = (f32[48,128]{1,0:T(8,128)S(1)}, f32[48,128]{1,0:T(8,128)S(1)}, u32[]{:S(2)}, u32[]{:S(2)}) collective-permute-start(f32[48,128]{1,0:T(8,128)S(1)} %near.1), channel_id=1, source_target_pairs={{0,1},{1,0},{2,3},{3,2},{4,5},{5,4},{6,7},{7,6},{8,9},{9,8},{10,11... | collective-permute-start | bytes 73736 | tf_op jit(solution)/shard_map/ppermute | solution.py:140

commit v11 on v10

--- a/solution.py
+++ b/solution.py
@@ -100,7 +100,7 @@
     for table in waves(period, np.arange(rows) + 0.5):
         c1, c2, c3 = table_parts(table.T)
         slot = np.zeros((2 * LANES, 2 * LANES), ml_dtypes.bfloat16)
-        for i, two in enumerate(((c1, c1), (c2, c2), (c1, c3))):
+        for i, two in enumerate(((c1, c1), (c2, c2), (c3, 0 * c3), (c1, 0 * c1))):
             slot[i * rows : (i + 1) * rows, :period] = np.concatenate(two, axis=1)
         out.append(slot)
     return np.stack(out)
@@ -155,7 +155,7 @@
     return lax.ppermute(x, axis, [(b, a) if back else (a, b) for a, b in pairs])
 
 
-def spectra_kernel(start, first_out, groups, kern, lanes, rows, ends, *rest):
+def spectra_kernel(start, first_out, parts, kern, lanes, rows, ends, *rest):
     out, token = rest[-2:]
     period = out.shape[2]
     half = period // 2
@@ -192,20 +192,18 @@
             jnp.concatenate([real_sin + imag_cos, imag_cos - real_sin], axis=1),
         )
 
-    for group in range(groups):
-        first = start + group * BATCH
-        planes = along_lanes([kern[c, first + k] for k in range(BATCH) for c in range(2)])
-        for k in range(BATCH):
-            to = first_out + group * BATCH + k
-            (real, real_tail), (imag, imag_tail) = planes[2 * k : 2 * k + 2]
-            wide_re, wide_im = mixed(real, imag)
-            tail_re, tail_im = mixed(real_tail, imag_tail)
-            tall_re = along_rows(wide_re, tail_re)
-            tall_im = along_rows(wide_im, tail_im)
-            out[0, to, :half] = tall_re[:half] - tall_im[half:]
-            out[0, to, half:] = tall_re[:half] + tall_im[half:]
-            out[1, to, :half] = tall_im[:half] + tall_re[half:]
-            out[1, to, half:] = tall_im[:half] - tall_re[half:]
+    planes = along_lanes([kern[c, start + k] for k in range(parts) for c in range(2)])
+    for k in range(parts):
+        to = first_out + k
+        (real, real_tail), (imag, imag_tail) = planes[2 * k : 2 * k + 2]
+        wide_re, wide_im = mixed(real, imag)
+        tail_re, tail_im = mixed(real_tail, imag_tail)
+        tall_re = along_rows(wide_re, tail_re)
+        tall_im = along_rows(wide_im, tail_im)
+        out[0, to, :half] = tall_re[:half] - tall_im[half:]
+        out[0, to, half:] = tall_re[:half] + tall_im[half:]
+        out[1, to, :half] = tall_im[:half] + tall_re[half:]
+        out[1, to, half:] = tall_im[:half] - tall_re[half:]
 
 
 def pack(x):
@@ -335,9 +333,9 @@
 
     def lift(slot, x):
         x1, x2, x3 = split3(x)
-        out = dot(tables[slot, :tile, :period], stacked((x1, x2)))
-        small = dot(tables[slot, tile : tile + rows, :period], stacked((x3, x1)))
-        return out[:rows] + (out[rows:] + small)
+        out = dot(tables[slot, : 3 * rows, :period], stacked((x1, x2)))
+        small = dot(tables[slot, 3 * rows : 4 * rows, :half], x3)
+        return out[:rows] + (out[rows:tile] + (out[tile:] + small))
 
     across = triple(tables, 6, 2 * LANES, LANES)
     across = (across[0], jnp.concatenate(across[:2], axis=1), across[2])
@@ -562,33 +560,33 @@
     packed = shape(tile // 2, 2 * radius)
     devices = lax.axis_size("ty") * lax.axis_size("tx")
 
-    def spectra(start, first_out, groups, size, after, into=()):
+    def spectra(start, first_out, parts, size, after, into=()):
         return call(
-            functools.partial(spectra_kernel, start, first_out, groups),
+            functools.partial(spectra_kernel, start, first_out, parts),
             "spectra",
             [shape(2, size, period, 2 * LANES), token],
             [VMEM] * 4 + [ANY] * (1 + len(into)),
             aliases={5: 0} if into else None,
-            micros=groups,
+            micros=parts // 2,
         )(kernels, *first_tables, after, *into)
 
     transmit, done = call(
         own_kernel, "own", [shape(tile, tile), token], [VMEM], micros=3
     )(latent)
     partner, outside = swap("tx", transmit), swap_outside("tx", transmit)
-    small, large = BATCH, count - BATCH
-    spec_a, done = spectra(0, 0, 1, small, done)
+    small, few = count // 3, count // 6
+    large = count - small
+    spec_a, done = spectra(0, 0, small, small, done)
     band, done = call(
         band_kernel, "band", [shape(tile, period), token], [VMEM] * 3 + [ANY]
     )(transmit, partner, outside, done)
     partner = swap("ty", band)
-    spec_b, done = spectra(small, 0, 1, large, done)
+    spec_b, done = spectra(small, 0, few, large, done)
     rim, done = call(
         relay_rows_kernel, "relay", [shape(radius, period), token], [VMEM, ANY]
     )(partner, done)
     rim = ring("ty", rim)
-    groups = large // BATCH - 1
-    spec_b, _ = spectra(2 * small, small, groups, large, done, (spec_b,))
+    spec_b, _ = spectra(small + few, few, large - few, large, done, (spec_b,))
     spec = [spec_a, spec_b]
 
     field_re, field_im, sampled, copies = call(

time: 55.7 us -> 55.1 us (0.989)
  starting transfers between devices: 18.9 us -> 17.6 us
  Pallas kernels: 19.4 us -> 20.1 us
    all_to_all x1, starting transfers between devices: 9.58 us -> 8.33 us  [gather_all(): return lax.all_to_all(copies, ('ty', 'tx'), 0, 0, tiled=True)]
  transfers between devices with their start and end apart: 9 -> 9, of which waited for: 4 -> 5; matrix products, arithmetic and copies ran while one was open for 1% -> 1% of each run, Pallas kernels for 11% -> 12%
where the time goes in v11:
time: 55.1 us; the launch traced here: 54.9 us
  Pallas kernels  20.1 us (36%)
  starting transfers between devices  17.6 us (32%)
  waiting for transfers between devices  13.6 us (25%)
  local copies, waits for them, and re-layouts  2.05 us (4%)
  between operations  1.52 us (3%)
    all_to_all x1, starting transfers between devices, gather_all(): return lax.all_to_all(copies, ('ty', 'tx'), 0, 0, tiled=True)  8.33 us
    pallas_call x1, Pallas kernels, body(): call(field_kernel, 'field', [shape(count, tile, LANES)] * 2 + [shape(1, 2...  6.66 us
    pallas_call x3, Pallas kernels, spectra(): call(functools.partial(spectra_kernel, start, first_out, parts), 'spectra...  6.51 us
    all_to_all x1, waiting for transfers between devices, gather_all(): return lax.all_to_all(copies, ('ty', 'tx'), 0, 0, tiled=True)  6.45 us
    ppermute x4, starting transfers between devices, swap(): lax.ppermute(x, axis, [(i, i ^ 1) for i in range(lax.axis_size(axis))])  6.35 us
    ppermute x2, waiting for transfers between devices, ring(): return lax.ppermute(x, axis, [(b, a) if back else (a, b) for a, b in pairs])  4.15 us
    pallas_call x1, Pallas kernels, body(): call(gradient_kernel, 'gradient', [shape(period, period), shape(radius, p...  4.13 us
    ppermute x4, waiting for transfers between devices, swap(): lax.ppermute(x, axis, [(i, i ^ 1) for i in range(lax.axis_size(axis))])  3 us
  transfers between devices with their start and end apart: 9, of which 5 were waited for; matrix products, arithmetic and copies ran while one was open for 1% of the time, Pallas kernels for 12%

profile of v11, /device:TPU:0, one launch (start us, length us, event | category | flops | bytes accessed | tf_op | source)
XLA Modules:
  0.0 54.9 jit_solution(6925926323077435000)
XLA Ops:
  0.6 0.8 %copy-done.5 = f32[96,96]{1,0:T(8,128)S(1)} copy-done((f32[96,96]{1,0:T(8,128)S(1)}, f32[96,96]{1,0:T(8,128)}, u32[]{:S(2)}) %copy-start.5) | copy-done | bytes 36888
  1.5 3.0 %collective-permute-start = (f32[96,96]{1,0:T(8,128)S(1)}, f32[96,96]{1,0:T(8,128)S(1)}, u32[]{:S(2)}, u32[]{:S(2)}) collective-permute-start(f32[96,96]{1,0:T(8,128)S(1)} %get-tuple-element.23.middle), channel_id=1, source_target_pairs={{0,1},{1,0},{2,3},{3,2},{4,5},{5,4},{6,7},{7,6},{8,9},{9,8},{10,11... | collective-permute-start | bytes 110600 | tf_op jit(solution)/shard_map/ppermute | solution.py:140
  4.5 0.7 %collective-permute-start.1 = (f32[96,96]{1,0:T(8,128)S(1)}, f32[96,96]{1,0:T(8,128)S(1)}, u32[]{:S(2)}, u32[]{:S(2)}) collective-permute-start(f32[96,96]{1,0:T(8,128)S(1)} %get-tuple-element.23.middle), channel_id=1, source_target_pairs={{0,0},{7,7},{1,2},{2,1},{3,4},{4,3},{5,6},{6,5},{8,8},{15,15},{9,1... | collective-permute-start | bytes 110600 | tf_op jit(solution)/shard_map/ppermute | solution.py:148
  5.2 0.3 copy.19.kern
  5.6 2.0 %spectra.3 = (f32[2,4,224,256]{3,2,1,0:T(8,128)S(1)}, f32[8,128]{1,0:T(8,128)S(1)}) custom-call(f32[2,12,129,129]{3,2,1,0:T(8,128)S(1)} %copy.19.kern, bf16[3,256,256]{2,1,0:T(8,128)(2,1)S(1)} %copy-done, bf16[672,256]{1,0:T(8,128)(2,1)S(1)} %copy-done.1, f32[232,256]{1,0:T(8,128)S(1)} %copy-done.2, f32[8,128]{1,0:T(8,128)S(1)} %get-tuple-element.24.rest_0_), custom_call_target="tpu_custom_call" | custom-call | flops 2000000000 | bytes 1048576 | tf_op jit(solution)/shard_map/spectra/pallas_call | solution.py:564
  7.6 0.2 band.1
  7.9 1.2 %spectra.4 = (f32[2,8,224,256]{3,2,1,0:T(8,128)S(1)}, f32[8,128]{1,0:T(8,128)S(1)}) custom-call(f32[2,12,129,129]{3,2,1,0:T(8,128)S(1)} %copy.19.kern, bf16[3,256,256]{2,1,0:T(8,128)(2,1)S(1)} %copy-done, bf16[672,256]{1,0:T(8,128)(2,1)S(1)} %copy-done.1, f32[232,256]{1,0:T(8,128)S(1)} %copy-done.2, f32[8,128]{1,0:T(8,128)S(1)} %get-tuple-element.27.rest_0_), custom_call_target="tpu_custom_call" | custom-call | flops 1000000000 | bytes 1048576 | tf_op jit(solution)/shard_map/spectra/pallas_call | solution.py:564
  9.2 1.5 %collective-permute-start.3 = (f32[64,224]{1,0:T(8,128)S(1)}, f32[64,224]{1,0:T(8,128)S(1)}, u32[]{:S(2)}, u32[]{:S(2)}) collective-permute-start(f32[64,224]{1,0:T(8,128)S(1)} %get-tuple-element.29), channel_id=1, source_target_pairs={{0,16},{16,24},{24,8},{8,0},{1,17},{17,25},{25,9},{9,1},{2,18},{18... | collective-permute-start | bytes 172040 | tf_op jit(solution)/shard_map/ppermute | solution.py:155
  10.7 3.3 %spectra.5 = (f32[2,8,224,256]{3,2,1,0:T(8,128)S(1)}, f32[8,128]{1,0:T(8,128)}) custom-call(f32[2,12,129,129]{3,2,1,0:T(8,128)S(1)} %copy.19.kern, bf16[3,256,256]{2,1,0:T(8,128)(2,1)S(1)} %copy-done, bf16[672,256]{1,0:T(8,128)(2,1)S(1)} %copy-done.1, f32[232,256]{1,0:T(8,128)S(1)} %copy-done.2, ...), custom_call_target="tpu_custom_call", output_to_operand_aliasing={{0}: (5, {})} | custom-call | flops 3000000000 | bytes 1048576 | tf_op jit(solution)/shard_map/spectra/pallas_call | solution.py:564
  14.0 6.7 %field.1 = (f32[12,96,128]{2,1,0:T(8,128)S(1)}, f32[12,96,128]{2,1,0:T(8,128)S(1)}, f32[1,512]{1,0:T(1,128)S(1)}, f32[32,1,512]{2,1,0:T(1,128)}) custom-call(f32[12]{0:T(128)S(1)} %copy-done.10, f32[96,224]{1,0:T(8,128)S(1)} %get-tuple-element.26.band, f32[96,224]{1,0:T(8,128)S(1)} %collective-permute-done.2.partner, ...), custom_call_target="tpu_custom_call" | custom-call | flops 7000000000 | bytes 1048576 | tf_op jit(solution)/shard_map/field/pallas_call | solution.py:592
  20.7 8.3 %all-to-all-start = ((f32[32,1,512]{2,1,0:T(1,128)}), f32[32,1,512]{2,1,0:T(1,128)S(1)}, u32[]{:S(2)}, u32[]{:S(2)}) async-start(f32[32,1,512]{2,1,0:T(1,128)} %get-tuple-element.34), calls=%async_computation | async-start | bytes 131072 | tf_op jit(solution)/shard_map/all_to_all | solution.py:546
  29.7 6.4 %all-to-all-done = f32[32,1,512]{2,1,0:T(1,128)S(1)} async-done(((f32[32,1,512]{2,1,0:T(1,128)}), f32[32,1,512]{2,1,0:T(1,128)S(1)}, u32[]{:S(2)}, u32[]{:S(2)}) %all-to-all-start) | async-done | bytes 65568 | tf_op jit(solution)/shard_map/all_to_all | solution.py:546
  36.1 1.4 %source.1 = (f32[96,128]{1,0:T(8,128)S(1)}, f32[1,1]{1,0:T(1,128)}) custom-call(f32[12]{0:T(128)S(1)} %copy-done.10, f32[8]{0:T(128)S(1)} %copy-done.9, s32[1]{0:T(128)S(6)} %copy.26.pick, f32[32,512]{1,0:T(8,128)S(1)} %bitcast.4, f32[1,512]{1,0:T(1,128)S(1)} %get-tuple-element.35.sampled, s32[1,256]{1,0:T(1,128)S(1)} %copy-done.8), custom_call_target="tpu_custom_call" | custom-call | flops 2000000000 | bytes 1048576 | tf_op jit(solution)/shard_map/source/pallas_call | solution.py:606
  37.5 0.6 %copy-done.4 = f32[2,8,224,256]{3,2,1,0:T(8,128)S(1)} copy-done((f32[2,8,224,256]{3,2,1,0:T(8,128)S(1)}, f32[2,8,224,256]{3,2,1,0:T(8,128)}, u32[]{:S(2)}) %copy-start.4) | copy-done | bytes 3670040
  38.2 0.2 copy-done.12
  38.4 4.1 %gradient.1 = (f32[224,224]{1,0:T(8,128)S(1)}, f32[64,224]{1,0:T(8,128)S(1)}) custom-call(f32[12]{0:T(128)S(1)} %copy-done.10, f32[96,128]{1,0:T(8,128)S(1)} %get-tuple-element.36.grid, f32[12,96,128]{2,1,0:T(8,128)S(1)} %get-tuple-element.37.field_re, f32[12,96,128]{2,1,0:T(8,128)S(1)} %get-tuple-element.38.field_im, bf16[7,256,256]{2,1,0:T(8,128)(2,1)S(1)} %copy-done.12, ...), custom_call_target="tpu_custom_call" | custom-call | flops 6000000000 | bytes 1048576 | tf_op jit(solution)/shard_map/gradient/pallas_call | solution.py:613
  42.5 0.1 collective-permute-start.4
  42.7 4.2 %collective-permute-done.4.rim = f32[64,224]{1,0:T(8,128)S(1)} collective-permute-done((f32[64,224]{1,0:T(8,128)S(1)}, f32[64,224]{1,0:T(8,128)S(1)}, u32[]{:S(2)}, u32[]{:S(2)}) %collective-permute-start.4) | collective-permute-done | bytes 57376 | tf_op jit(solution)/shard_map/ppermute | solution.py:155
  46.9 1.3 %collective-permute-done.5.partner = f32[96,224]{1,0:T(8,128)S(1)} collective-permute-done((f32[96,224]{1,0:T(8,128)S(1)}, f32[96,224]{1,0:T(8,128)S(1)}, u32[]{:S(2)}, u32[]{:S(2)}) %collective-permute-start.5) | collective-permute-done | bytes 86048 | tf_op jit(solution)/shard_map/ppermute | solution.py:140
  48.3 0.7 %collective-permute-start.6 = (f32[48,128]{1,0:T(8,128)S(1)}, f32[48,128]{1,0:T(8,128)S(1)}, u32[]{:S(2)}, u32[]{:S(2)}) collective-permute-start(f32[48,128]{1,0:T(8,128)S(1)} %get-tuple-element.42), channel_id=1, source_target_pairs={{0,0},{7,7},{1,2},{2,1},{3,4},{4,3},{5,6},{6,5},{8,8},{15,15},{9,1... | collective-permute-start | bytes 73736 | tf_op jit(solution)/shard_map/ppermute | solution.py:148
  49.1 3.2 %collective-permute-start.7 = (f32[48,128]{1,0:T(8,128)S(1)}, f32[48,128]{1,0:T(8,128)S(1)}, u32[]{:S(2)}, u32[]{:S(2)}) collective-permute-start(f32[48,128]{1,0:T(8,128)S(1)} %near.1), channel_id=1, source_target_pairs={{0,1},{1,0},{2,3},{3,2},{4,5},{5,4},{6,7},{7,6},{8,9},{9,8},{10,11... | collective-permute-start | bytes 73736 | tf_op jit(solution)/shard_map/ppermute | solution.py:140
  52.3 0.1 far.1.total
  52.4 1.7 %collective-permute-done.7.near = f32[48,128]{1,0:T(8,128)S(1)} collective-permute-done((f32[48,128]{1,0:T(8,128)S(1)}, f32[48,128]{1,0:T(8,128)S(1)}, u32[]{:S(2)}, u32[]{:S(2)}) %collective-permute-start.7) | collective-permute-done | bytes 24608 | tf_op jit(solution)/shard_map/ppermute | solution.py:140
  54.1 0.8 %finish.1 = f32[96,96]{1,0:T(8,128)} custom-call(f32[96,96]{1,0:T(8,128)S(1)} %far.1.total, f32[48,128]{1,0:T(8,128)S(1)} %collective-permute-done.7.near, f32[96,96]{1,0:T(8,128)S(1)} %copy-done.6), custom_call_target="tpu_custom_call" | custom-call | flops 1000000000 | bytes 1048576 | tf_op jit(solution)/shard_map/finish/pallas_call | solution.py:634
  (38 shorter events, 0.5 us)
Async XLA Ops:
  0.6 0.8 %copy-start.5 = (f32[96,96]{1,0:T(8,128)S(1)}, f32[96,96]{1,0:T(8,128)}, u32[]{:S(2)}) copy-start(f32[96,96]{1,0:T(8,128)} %latent.3) | copy-start | bytes 110596
  1.4 3.8 %copy-start.13 = (f32[2,12,129,129]{3,0,2,1:T(2,128)S(1)}, f32[2,12,129,129]{3,0,2,1:T(2,128)}, u32[]{:S(2)}) copy-start(f32[2,12,129,129]{3,0,2,1:T(2,128)} %param.13) | copy-start | bytes 4792612
  1.5 4.1 %copy-start = (bf16[3,256,256]{2,1,0:T(8,128)(2,1)S(1)}, bf16[3,256,256]{2,1,0:T(8,128)(2,1)}, u32[]{:S(2)}) copy-start(bf16[3,256,256]{2,1,0:T(8,128)(2,1)} %constant.10.clone.lanes) | copy-start | bytes 1179652
  1.5 4.1 %copy-start.1 = (bf16[672,256]{1,0:T(8,128)(2,1)S(1)}, bf16[672,256]{1,0:T(8,128)(2,1)}, u32[]{:S(2)}) copy-start(bf16[672,256]{1,0:T(8,128)(2,1)} %constant.11.clone.rows) | copy-start | bytes 1032196
  1.5 4.1 %copy-start.2 = (f32[232,256]{1,0:T(8,128)S(1)}, f32[232,256]{1,0:T(8,128)}, u32[]{:S(2)}) copy-start(f32[232,256]{1,0:T(8,128)} %constant.12.clone.ends) | copy-start | bytes 712708
  1.5 6.1 %collective-permute-start = (f32[96,96]{1,0:T(8,128)S(1)}, f32[96,96]{1,0:T(8,128)S(1)}, u32[]{:S(2)}, u32[]{:S(2)}) collective-permute-start(f32[96,96]{1,0:T(8,128)S(1)} %get-tuple-element.23.middle), channel_id=1, source_target_pairs={{0,1},{1,0},{2,3},{3,2},{4,5},{5,4},{6,7},{7,6},{8,9},{9,8},{10,11... | collective-permute-start | bytes 110600 | tf_op jit(solution)/shard_map/ppermute | solution.py:140
  4.5 3.1 %collective-permute-start.1 = (f32[96,96]{1,0:T(8,128)S(1)}, f32[96,96]{1,0:T(8,128)S(1)}, u32[]{:S(2)}, u32[]{:S(2)}) collective-permute-start(f32[96,96]{1,0:T(8,128)S(1)} %get-tuple-element.23.middle), channel_id=1, source_target_pairs={{0,0},{7,7},{1,2},{2,1},{3,4},{4,3},{5,6},{6,5},{8,8},{15,15},{9,1... | collective-permute-start | bytes 110600 | tf_op jit(solution)/shard_map/ppermute | solution.py:148
  7.8 1.3 %collective-permute-start.2 = (f32[96,224]{1,0:T(8,128)S(1)}, f32[96,224]{1,0:T(8,128)S(1)}, u32[]{:S(2)}, u32[]{:S(2)}) collective-permute-start(f32[96,224]{1,0:T(8,128)S(1)} %get-tuple-element.26.band), channel_id=1, source_target_pairs={{0,8},{8,0},{16,24},{24,16},{1,9},{9,1},{17,25},{25,17},{2,10},{10... | collective-permute-start | bytes 258056 | tf_op jit(solution)/shard_map/ppermute | solution.py:140
  9.2 4.8 %collective-permute-start.3 = (f32[64,224]{1,0:T(8,128)S(1)}, f32[64,224]{1,0:T(8,128)S(1)}, u32[]{:S(2)}, u32[]{:S(2)}) collective-permute-start(f32[64,224]{1,0:T(8,128)S(1)} %get-tuple-element.29), channel_id=1, source_target_pairs={{0,16},{16,24},{24,8},{8,0},{1,17},{17,25},{25,9},{9,1},{2,18},{18... | collective-permute-start | bytes 172040 | tf_op jit(solution)/shard_map/ppermute | solution.py:155
  10.7 3.3 %copy-start.7 = (f32[1,256]{1,0:T(1,128)S(1)}, f32[1,256]{1,0:T(1,128)}, u32[]{:S(2)}) copy-start(f32[1,256]{1,0:T(1,128)} %slopes.1) | copy-start | bytes 3076
  10.7 3.3 %copy-start.8 = (s32[1,256]{1,0:T(1,128)S(1)}, s32[1,256]{1,0:T(1,128)}, u32[]{:S(2)}) copy-start(s32[1,256]{1,0:T(1,128)} %pixels.3) | copy-start | bytes 3076
  10.7 3.3 %copy-start.10 = (f32[12]{0:T(128)S(1)}, f32[12]{0:T(128)}, u32[]{:S(2)}) copy-start(f32[12]{0:T(128)} %weights.5) | copy-start | bytes 148
  10.7 3.3 %copy-start.11 = (bf16[11,256,256]{2,1,0:T(8,128)(2,1)S(1)}, bf16[11,256,256]{2,1,0:T(8,128)(2,1)}, u32[]{:S(2)}) copy-start(bf16[11,256,256]{2,1,0:T(8,128)(2,1)} %constant.13.clone.tables) | copy-start | bytes 4325380
  14.0 6.7 %copy-start.3 = (f32[2,8,224,256]{3,2,1,0:T(8,128)}, f32[2,8,224,256]{3,2,1,0:T(8,128)S(1)}, u32[]{:S(2)}) copy-start(f32[2,8,224,256]{3,2,1,0:T(8,128)S(1)} %get-tuple-element.33.rest_1_) | copy-start | bytes 11010052
  14.0 22.1 %copy-start.9 = (f32[8]{0:T(128)S(1)}, f32[8]{0:T(128)}, u32[]{:S(2)}) copy-start(f32[8]{0:T(128)} %doses.1) | copy-start | bytes 100
  20.7 15.4 %all-to-all-start = ((f32[32,1,512]{2,1,0:T(1,128)}), f32[32,1,512]{2,1,0:T(1,128)S(1)}, u32[]{:S(2)}, u32[]{:S(2)}) async-start(f32[32,1,512]{2,1,0:T(1,128)} %get-tuple-element.34), calls=%async_computation | async-start | bytes 131072 | tf_op jit(solution)/shard_map/all_to_all | solution.py:546
  36.1 2.0 %copy-start.4 = (f32[2,8,224,256]{3,2,1,0:T(8,128)S(1)}, f32[2,8,224,256]{3,2,1,0:T(8,128)}, u32[]{:S(2)}) copy-start(f32[2,8,224,256]{3,2,1,0:T(8,128)} %copy-done.3) | copy-start | bytes 11010052
  36.1 2.3 %copy-start.12 = (bf16[7,256,256]{2,1,0:T(8,128)(2,1)S(1)}, bf16[7,256,256]{2,1,0:T(8,128)(2,1)}, u32[]{:S(2)}) copy-start(bf16[7,256,256]{2,1,0:T(8,128)(2,1)} %constant.14.clone.tables) | copy-start | bytes 2752516
  42.5 4.3 %collective-permute-start.4 = (f32[64,224]{1,0:T(8,128)S(1)}, f32[64,224]{1,0:T(8,128)S(1)}, u32[]{:S(2)}, u32[]{:S(2)}) collective-permute-start(f32[64,224]{1,0:T(8,128)S(1)} %get-tuple-element.40), channel_id=1, source_target_pairs={{16,0},{24,16},{8,24},{0,8},{17,1},{25,17},{9,25},{1,9},{18,2},{26... | collective-permute-start | bytes 172040 | tf_op jit(solution)/shard_map/ppermute | solution.py:155
  46.8 1.4 %collective-permute-start.5 = (f32[96,224]{1,0:T(8,128)S(1)}, f32[96,224]{1,0:T(8,128)S(1)}, u32[]{:S(2)}, u32[]{:S(2)}) collective-permute-start(f32[96,224]{1,0:T(8,128)S(1)} %fold.2), channel_id=1, source_target_pairs={{0,8},{8,0},{16,24},{24,16},{1,9},{9,1},{17,25},{25,17},{2,10},{10... | collective-permute-start | bytes 258056 | tf_op jit(solution)/shard_map/ppermute | solution.py:140
  48.3 4.0 %collective-permute-start.6 = (f32[48,128]{1,0:T(8,128)S(1)}, f32[48,128]{1,0:T(8,128)S(1)}, u32[]{:S(2)}, u32[]{:S(2)}) collective-permute-start(f32[48,128]{1,0:T(8,128)S(1)} %get-tuple-element.42), channel_id=1, source_target_pairs={{0,0},{7,7},{1,2},{2,1},{3,4},{4,3},{5,6},{6,5},{8,8},{15,15},{9,1... | collective-permute-start | bytes 73736 | tf_op jit(solution)/shard_map/ppermute | solution.py:148
  49.0 5.1 %copy-start.6 = (f32[96,96]{1,0:T(8,128)S(1)}, f32[96,96]{1,0:T(8,128)}, u32[]{:S(2)}) copy-start(f32[96,96]{1,0:T(8,128)} %latent.3) | copy-start | bytes 110596
  49.1 5.0 %collective-permute-start.7 = (f32[48,128]{1,0:T(8,128)S(1)}, f32[48,128]{1,0:T(8,128)S(1)}, u32[]{:S(2)}, u32[]{:S(2)}) collective-permute-start(f32[48,128]{1,0:T(8,128)S(1)} %near.1), channel_id=1, source_target_pairs={{0,1},{1,0},{2,3},{3,2},{4,5},{5,4},{6,7},{7,6},{8,9},{9,8},{10,11... | collective-permute-start | bytes 73736 | tf_op jit(solution)/shard_map/ppermute | solution.py:140

commit v12 on v11

--- a/solution.py
+++ b/solution.py
@@ -227,6 +227,7 @@
     lower, other = place_in_pair("tx")
 
     near = jnp.where(lower, partner[:, :radius], partner[:, tile - radius :])
+    near = 0.5 * (1.0 + jnp.tanh(near))
     far = jnp.where(lower, outside[:, tile - radius :], outside[:, :radius])
     far = jnp.where(other, far, 0.0)
     band[:, :radius] = jnp.where(lower, far, near)
@@ -395,10 +396,30 @@
     return resist, offset, offset * offset
 
 
-def source_kernel(weights, doses, pick, gathered, sampled, pixels, placed_sum, tail):
+def own_samples_kernel(doses, sampled, pixels, own_error, chain, in_row, one_hot):
+    corners, samples = own_error.shape
+    tile = in_row.shape[0]
+    own, slope = sampled[:, :samples], sampled[:, samples:]
+    which = lax.broadcasted_iota(jnp.int32, (corners, samples), 0)
+    dose = jnp.zeros((corners, samples), F32)
+    for c in range(corners):
+        dose = jnp.where(which == c, doses[c], dose)
+    resist, offset, error = errors(own, slope, dose)
+    own_error[...] = error
+    chain[...] = 2.0 * STEEPNESS * offset * slope * dose * (0.25 - resist * resist)
+    row, col = sample_places(pixels[...], tile)
+    place = lax.broadcasted_iota(jnp.int32, (tile, samples), 0)
+    in_row[...] = jnp.where(place == row, 1.0, 0.0)
+    place = lax.broadcasted_iota(jnp.int32, (LANES, samples), 0)
+    one_hot[...] = jnp.where(place == col, 1.0, 0.0).astype(BF16)
+
+
+def source_kernel(
+    weights, doses, pick, gathered, own_error, chain, in_row, one_hot, placed_sum, tail
+):
     kernels = weights.shape[0]
     tile = placed_sum.shape[0]
-    samples = pixels.shape[1]
+    samples = own_error.shape[1]
     devices = gathered.shape[0]
     corners = doses.shape[0]
     per_corner = devices * samples
@@ -423,30 +444,20 @@
     tail_mean = jnp.sum(error_sum, keepdims=True) / soft_total
     tail[...] = tail_mean
 
-    own, slope = sampled[:, :samples], sampled[:, samples:]
-    which = lax.broadcasted_iota(jnp.int32, (corners, samples), 0)
-    dose = jnp.zeros((corners, samples), F32)
-    for c in range(corners):
-        dose = jnp.where(which == c, doses[c], dose)
-    resist, offset, error = errors(own, slope, dose)
+    error = own_error[...]
     soft = sigmoid((error - threshold) * (1.0 / SOFTNESS))
     slope_soft = soft * (1.0 - soft) * (1.0 / SOFTNESS)
-    chain = 2.0 * STEEPNESS * offset * slope * dose * (0.25 - resist * resist)
     coefficient = (soft + (error - tail_mean) * slope_soft) * (corners * per_corner / soft_total)
-    summed = jnp.sum(coefficient * chain, axis=0, keepdims=True)
+    summed = jnp.sum(coefficient * chain[...], axis=0, keepdims=True)
     summed = summed / total_weight(weights, kernels)
 
-    row, col = sample_places(pixels[...], tile)
-    in_row = lax.broadcasted_iota(jnp.int32, (tile, samples), 0) == row
-    in_col = lax.broadcasted_iota(jnp.int32, (LANES, samples), 0) == col
-    one_hot = jnp.where(in_col, 1.0, 0.0).astype(BF16)
-    placed = jnp.where(in_row, summed, 0.0)
+    placed = in_row[...] * summed
     high, rest = split(placed)
     low = (placed - high.astype(F32) - rest.astype(F32)).astype(BF16)
     grid = jnp.zeros((tile, LANES), F32)
     for part in (high, rest, low):
         grid = grid + lax.dot_general(
-            part, one_hot, (((1,), (1,)), ((), ())), preferred_element_type=F32
+            part, one_hot[...], (((1,), (1,)), ((), ())), preferred_element_type=F32
         )
 
     placed_sum[...] = grid
@@ -570,10 +581,11 @@
             micros=parts // 2,
         )(kernels, *first_tables, after, *into)
 
+    partner = swap("tx", latent)
     transmit, done = call(
         own_kernel, "own", [shape(tile, tile), token], [VMEM], micros=3
     )(latent)
-    partner, outside = swap("tx", transmit), swap_outside("tx", transmit)
+    outside = swap_outside("tx", transmit)
     small, few = count // 3, count // 6
     large = count - small
     spec_a, done = spectra(0, 0, small, small, done)
@@ -603,13 +615,22 @@
     )(socs_weights, band, partner, rim, edge_pixels, inv_slope, tables, *spec)
 
     gathered = gather_all(copies).reshape(devices, 2 * samples)
+    corners = dose_scale.shape[0]
+    own = call(
+        own_samples_kernel,
+        "samples",
+        [shape(corners, samples)] * 2
+        + [shape(tile, samples), jax.ShapeDtypeStruct((LANES, samples), BF16)],
+        [SMEM] + [VMEM] * 2,
+        micros=2,
+    )(dose_scale, sampled, edge_pixels)
     grid, tail_mean = call(
         source_kernel,
         "source",
         [shape(tile, LANES), shape(1, 1)],
-        [SMEM] * 3 + [VMEM] * 3,
+        [SMEM] * 3 + [VMEM] * 5,
         micros=2,
-    )(socs_weights, dose_scale, threshold_pick, gathered, sampled, edge_pixels)
+    )(socs_weights, dose_scale, threshold_pick, gathered, *own)
     grad, rim = call(
         gradient_kernel,
         "gradient",

time: 55.1 us -> 55.5 us (level)
  starting transfers between devices: 17.6 us -> 16.3 us
  local copies, waits for them, and re-layouts: 2.05 us -> 3.09 us
  Pallas kernels: 20.1 us -> 20.7 us
    all_to_all x1, starting transfers between devices: 8.33 us -> 6.79 us  [gather_all(): return lax.all_to_all(copies, ('ty', 'tx'), 0, 0, tiled=True)]
    unnamed x30, local copies, waits for them, and re-layouts: 2.05 us -> 3.09 us
    pallas_call x0 -> x1, Pallas kernels: none -> 0.57 us  [body(): call(own_samples_kernel, 'samples', [shape(corners, samples)] * 2 + [shap...]
  transfers between devices with their start and end apart: 9 -> 9, of which waited for: 5 -> 5; matrix products, arithmetic and copies ran while one was open for 1% -> 1% of each run, Pallas kernels for 12% -> 13%
where the time goes in v12:
time: 55.5 us; the launch traced here: 55.2 us
  Pallas kernels  20.7 us (37%)
  starting transfers between devices  16.3 us (29%)
  waiting for transfers between devices  13.7 us (25%)
  local copies, waits for them, and re-layouts  3.09 us (6%)
  between operations  1.52 us (3%)
    all_to_all x1, starting transfers between devices, gather_all(): return lax.all_to_all(copies, ('ty', 'tx'), 0, 0, tiled=True)  6.79 us
    pallas_call x1, Pallas kernels, body(): call(field_kernel, 'field', [shape(count, tile, LANES)] * 2 + [shape(1, 2...  6.65 us
    pallas_call x3, Pallas kernels, spectra(): call(functools.partial(spectra_kernel, start, first_out, parts), 'spectra...  6.51 us
    all_to_all x1, waiting for transfers between devices, gather_all(): return lax.all_to_all(copies, ('ty', 'tx'), 0, 0, tiled=True)  6.51 us
    ppermute x4, starting transfers between devices, swap(): lax.ppermute(x, axis, [(i, i ^ 1) for i in range(lax.axis_size(axis))])  6.38 us
    ppermute x2, waiting for transfers between devices, ring(): return lax.ppermute(x, axis, [(b, a) if back else (a, b) for a, b in pairs])  4.15 us
    pallas_call x1, Pallas kernels, body(): call(gradient_kernel, 'gradient', [shape(period, period), shape(radius, p...  4.12 us
    unnamed x30, local copies, waits for them, and re-layouts  3.09 us
  transfers between devices with their start and end apart: 9, of which 5 were waited for; matrix products, arithmetic and copies ran while one was open for 1% of the time, Pallas kernels for 13%

profile of v12, /device:TPU:0, one launch (start us, length us, event | category | flops | bytes accessed | tf_op | source)
XLA Modules:
  0.0 55.2 jit_solution(17545180627628398575)
XLA Ops:
  0.6 3.0 %collective-permute-start = (f32[96,96]{1,0:T(8,128)}, f32[96,96]{1,0:T(8,128)S(1)}, u32[]{:S(2)}, u32[]{:S(2)}) collective-permute-start(f32[96,96]{1,0:T(8,128)} %latent.3), channel_id=1, source_target_pairs={{0,1},{1,0},{2,3},{3,2},{4,5},{5,4},{6,7},{7,6},{8,9},{9,8},{10,11... | collective-permute-start | bytes 110600 | tf_op jit(solution)/shard_map/ppermute | solution.py:140
  3.7 0.8 %copy-done.5 = f32[96,96]{1,0:T(8,128)S(1)} copy-done((f32[96,96]{1,0:T(8,128)S(1)}, f32[96,96]{1,0:T(8,128)}, u32[]{:S(2)}) %copy-start.5) | copy-done | bytes 36888
  4.6 0.8 %collective-permute-start.1 = (f32[96,96]{1,0:T(8,128)S(1)}, f32[96,96]{1,0:T(8,128)S(1)}, u32[]{:S(2)}, u32[]{:S(2)}) collective-permute-start(f32[96,96]{1,0:T(8,128)S(1)} %get-tuple-element.27.middle), channel_id=1, source_target_pairs={{0,0},{7,7},{1,2},{2,1},{3,4},{4,3},{5,6},{6,5},{8,8},{15,15},{9,1... | collective-permute-start | bytes 110600 | tf_op jit(solution)/shard_map/ppermute | solution.py:148
  5.4 1.0 %copy-done.13 = f32[2,12,129,129]{3,0,2,1:T(2,128)S(1)} copy-done((f32[2,12,129,129]{3,0,2,1:T(2,128)S(1)}, f32[2,12,129,129]{3,0,2,1:T(2,128)}, u32[]{:S(2)}) %copy-start.13) | copy-done | bytes 1597560
  6.4 0.3 copy.19.kern
  6.8 2.0 %spectra.3 = (f32[2,4,224,256]{3,2,1,0:T(8,128)S(1)}, f32[8,128]{1,0:T(8,128)S(1)}) custom-call(f32[2,12,129,129]{3,2,1,0:T(8,128)S(1)} %copy.19.kern, bf16[3,256,256]{2,1,0:T(8,128)(2,1)S(1)} %copy-done, bf16[672,256]{1,0:T(8,128)(2,1)S(1)} %copy-done.1, f32[232,256]{1,0:T(8,128)S(1)} %copy-done.2, f32[8,128]{1,0:T(8,128)S(1)} %get-tuple-element.28.rest_0_), custom_call_target="tpu_custom_call" | custom-call | flops 2000000000 | bytes 1048576 | tf_op jit(solution)/shard_map/spectra/pallas_call | solution.py:575
  9.4 0.2 band.1
  9.8 1.2 %spectra.4 = (f32[2,8,224,256]{3,2,1,0:T(8,128)S(1)}, f32[8,128]{1,0:T(8,128)S(1)}) custom-call(f32[2,12,129,129]{3,2,1,0:T(8,128)S(1)} %copy.19.kern, bf16[3,256,256]{2,1,0:T(8,128)(2,1)S(1)} %copy-done, bf16[672,256]{1,0:T(8,128)(2,1)S(1)} %copy-done.1, f32[232,256]{1,0:T(8,128)S(1)} %copy-done.2, f32[8,128]{1,0:T(8,128)S(1)} %get-tuple-element.31.rest_0_), custom_call_target="tpu_custom_call" | custom-call | flops 1000000000 | bytes 1048576 | tf_op jit(solution)/shard_map/spectra/pallas_call | solution.py:575
  11.1 1.5 %collective-permute-start.3 = (f32[64,224]{1,0:T(8,128)S(1)}, f32[64,224]{1,0:T(8,128)S(1)}, u32[]{:S(2)}, u32[]{:S(2)}) collective-permute-start(f32[64,224]{1,0:T(8,128)S(1)} %get-tuple-element.33), channel_id=1, source_target_pairs={{0,16},{16,24},{24,8},{8,0},{1,17},{17,25},{25,9},{9,1},{2,18},{18... | collective-permute-start | bytes 172040 | tf_op jit(solution)/shard_map/ppermute | solution.py:155
  12.6 3.3 %spectra.5 = (f32[2,8,224,256]{3,2,1,0:T(8,128)S(1)}, f32[8,128]{1,0:T(8,128)}) custom-call(f32[2,12,129,129]{3,2,1,0:T(8,128)S(1)} %copy.19.kern, bf16[3,256,256]{2,1,0:T(8,128)(2,1)S(1)} %copy-done, bf16[672,256]{1,0:T(8,128)(2,1)S(1)} %copy-done.1, f32[232,256]{1,0:T(8,128)S(1)} %copy-done.2, ...), custom_call_target="tpu_custom_call", output_to_operand_aliasing={{0}: (5, {})} | custom-call | flops 3000000000 | bytes 1048576 | tf_op jit(solution)/shard_map/spectra/pallas_call | solution.py:575
  15.9 6.6 %field.1 = (f32[12,96,128]{2,1,0:T(8,128)S(1)}, f32[12,96,128]{2,1,0:T(8,128)S(1)}, f32[1,512]{1,0:T(1,128)S(1)}, f32[32,1,512]{2,1,0:T(1,128)}) custom-call(f32[12]{0:T(128)S(1)} %copy-done.10, f32[96,224]{1,0:T(8,128)S(1)} %get-tuple-element.30.band, f32[96,224]{1,0:T(8,128)S(1)} %collective-permute-done.2.partner, ...), custom_call_target="tpu_custom_call" | custom-call | flops 7000000000 | bytes 1048576 | tf_op jit(solution)/shard_map/field/pallas_call | solution.py:604
  22.6 6.8 %all-to-all-start = ((f32[32,1,512]{2,1,0:T(1,128)}), f32[32,1,512]{2,1,0:T(1,128)S(1)}, u32[]{:S(2)}, u32[]{:S(2)}) async-start(f32[32,1,512]{2,1,0:T(1,128)} %get-tuple-element.38), calls=%async_computation | async-start | bytes 131072 | tf_op jit(solution)/shard_map/all_to_all | solution.py:557
  29.4 0.6 %samples.1 = (f32[8,256]{1,0:T(8,128)S(1)}, f32[8,256]{1,0:T(8,128)S(1)}, f32[96,256]{1,0:T(8,128)S(1)}, bf16[128,256]{1,0:T(8,128)(2,1)S(1)}) custom-call(f32[8]{0:T(128)S(1)} %copy-done.9, f32[1,512]{1,0:T(1,128)S(1)} %get-tuple-element.39.sampled, s32[1,256]{1,0:T(1,128)S(1)} %copy-done.8), custom_call_target="tpu_custom_call" | custom-call | flops 2000000000 | bytes 1048576 | tf_op jit(solution)/shard_map/samples/pallas_call | solution.py:619
  30.0 6.5 %all-to-all-done = f32[32,1,512]{2,1,0:T(1,128)S(1)} async-done(((f32[32,1,512]{2,1,0:T(1,128)}), f32[32,1,512]{2,1,0:T(1,128)S(1)}, u32[]{:S(2)}, u32[]{:S(2)}) %all-to-all-start) | async-done | bytes 65568 | tf_op jit(solution)/shard_map/all_to_all | solution.py:557
  36.5 1.4 %source.1 = (f32[96,128]{1,0:T(8,128)S(1)}, f32[1,1]{1,0:T(1,128)}) custom-call(f32[12]{0:T(128)S(1)} %copy-done.10, f32[8]{0:T(128)S(1)} %copy-done.9, s32[1]{0:T(128)S(6)} %copy.26.pick, f32[32,512]{1,0:T(8,128)S(1)} %bitcast.4, f32[8,256]{1,0:T(8,128)S(1)} %get-tuple-element.40.own_error, f32[8,256]{1,0:T(8,128)S(1)} %get-tuple-element.41.chain, ...), custom_call_target="tpu_custom_call" | custom-call | flops 2000000000 | bytes 1048576 | tf_op jit(solution)/shard_map/source/pallas_call | solution.py:627
  37.9 0.6 %copy-done.4 = f32[2,8,224,256]{3,2,1,0:T(8,128)S(1)} copy-done((f32[2,8,224,256]{3,2,1,0:T(8,128)S(1)}, f32[2,8,224,256]{3,2,1,0:T(8,128)}, u32[]{:S(2)}) %copy-start.4) | copy-done | bytes 3670040
  38.5 0.2 copy-done.12
  38.8 4.1 %gradient.1 = (f32[224,224]{1,0:T(8,128)S(1)}, f32[64,224]{1,0:T(8,128)S(1)}) custom-call(f32[12]{0:T(128)S(1)} %copy-done.10, f32[96,128]{1,0:T(8,128)S(1)} %get-tuple-element.44.grid, f32[12,96,128]{2,1,0:T(8,128)S(1)} %get-tuple-element.45.field_re, f32[12,96,128]{2,1,0:T(8,128)S(1)} %get-tuple-element.46.field_im, bf16[7,256,256]{2,1,0:T(8,128)(2,1)S(1)} %copy-done.12, ...), custom_call_target="tpu_custom_call" | custom-call | flops 6000000000 | bytes 1048576 | tf_op jit(solution)/shard_map/gradient/pallas_call | solution.py:634
  43.0 4.2 %collective-permute-done.4.rim = f32[64,224]{1,0:T(8,128)S(1)} collective-permute-done((f32[64,224]{1,0:T(8,128)S(1)}, f32[64,224]{1,0:T(8,128)S(1)}, u32[]{:S(2)}, u32[]{:S(2)}) %collective-permute-start.4) | collective-permute-done | bytes 57376 | tf_op jit(solution)/shard_map/ppermute | solution.py:155
  47.3 1.3 %collective-permute-done.5.partner = f32[96,224]{1,0:T(8,128)S(1)} collective-permute-done((f32[96,224]{1,0:T(8,128)S(1)}, f32[96,224]{1,0:T(8,128)S(1)}, u32[]{:S(2)}, u32[]{:S(2)}) %collective-permute-start.5) | collective-permute-done | bytes 86048 | tf_op jit(solution)/shard_map/ppermute | solution.py:140
  48.7 0.7 %collective-permute-start.6 = (f32[48,128]{1,0:T(8,128)S(1)}, f32[48,128]{1,0:T(8,128)S(1)}, u32[]{:S(2)}, u32[]{:S(2)}) collective-permute-start(f32[48,128]{1,0:T(8,128)S(1)} %get-tuple-element.50), channel_id=1, source_target_pairs={{0,0},{7,7},{1,2},{2,1},{3,4},{4,3},{5,6},{6,5},{8,8},{15,15},{9,1... | collective-permute-start | bytes 73736 | tf_op jit(solution)/shard_map/ppermute | solution.py:148
  49.4 3.2 %collective-permute-start.7 = (f32[48,128]{1,0:T(8,128)S(1)}, f32[48,128]{1,0:T(8,128)S(1)}, u32[]{:S(2)}, u32[]{:S(2)}) collective-permute-start(f32[48,128]{1,0:T(8,128)S(1)} %near.1), channel_id=1, source_target_pairs={{0,1},{1,0},{2,3},{3,2},{4,5},{5,4},{6,7},{7,6},{8,9},{9,8},{10,11... | collective-permute-start | bytes 73736 | tf_op jit(solution)/shard_map/ppermute | solution.py:140
  52.8 1.7 %collective-permute-done.7.near = f32[48,128]{1,0:T(8,128)S(1)} collective-permute-done((f32[48,128]{1,0:T(8,128)S(1)}, f32[48,128]{1,0:T(8,128)S(1)}, u32[]{:S(2)}, u32[]{:S(2)}) %collective-permute-start.7) | collective-permute-done | bytes 24608 | tf_op jit(solution)/shard_map/ppermute | solution.py:140
  54.4 0.8 %finish.1 = f32[96,96]{1,0:T(8,128)} custom-call(f32[96,96]{1,0:T(8,128)S(1)} %far.1.total, f32[48,128]{1,0:T(8,128)S(1)} %collective-permute-done.7.near, f32[96,96]{1,0:T(8,128)S(1)} %copy-done.6), custom_call_target="tpu_custom_call" | custom-call | flops 1000000000 | bytes 1048576 | tf_op jit(solution)/shard_map/finish/pallas_call | solution.py:655
  (39 shorter events, 0.8 us)
Async XLA Ops:
  0.6 8.8 %collective-permute-start = (f32[96,96]{1,0:T(8,128)}, f32[96,96]{1,0:T(8,128)S(1)}, u32[]{:S(2)}, u32[]{:S(2)}) collective-permute-start(f32[96,96]{1,0:T(8,128)} %latent.3), channel_id=1, source_target_pairs={{0,1},{1,0},{2,3},{3,2},{4,5},{5,4},{6,7},{7,6},{8,9},{9,8},{10,11... | collective-permute-start | bytes 110600 | tf_op jit(solution)/shard_map/ppermute | solution.py:140
  3.7 0.8 %copy-start.5 = (f32[96,96]{1,0:T(8,128)S(1)}, f32[96,96]{1,0:T(8,128)}, u32[]{:S(2)}) copy-start(f32[96,96]{1,0:T(8,128)} %latent.3) | copy-start | bytes 110596
  4.5 1.9 %copy-start.13 = (f32[2,12,129,129]{3,0,2,1:T(2,128)S(1)}, f32[2,12,129,129]{3,0,2,1:T(2,128)}, u32[]{:S(2)}) copy-start(f32[2,12,129,129]{3,0,2,1:T(2,128)} %param.13) | copy-start | bytes 4792612
  4.5 2.2 %copy-start = (bf16[3,256,256]{2,1,0:T(8,128)(2,1)S(1)}, bf16[3,256,256]{2,1,0:T(8,128)(2,1)}, u32[]{:S(2)}) copy-start(bf16[3,256,256]{2,1,0:T(8,128)(2,1)} %constant.10.clone.lanes) | copy-start | bytes 1179652
  4.5 2.2 %copy-start.1 = (bf16[672,256]{1,0:T(8,128)(2,1)S(1)}, bf16[672,256]{1,0:T(8,128)(2,1)}, u32[]{:S(2)}) copy-start(bf16[672,256]{1,0:T(8,128)(2,1)} %constant.11.clone.rows) | copy-start | bytes 1032196
  4.5 2.2 %copy-start.2 = (f32[232,256]{1,0:T(8,128)S(1)}, f32[232,256]{1,0:T(8,128)}, u32[]{:S(2)}) copy-start(f32[232,256]{1,0:T(8,128)} %constant.12.clone.ends) | copy-start | bytes 712708
  4.6 4.9 %collective-permute-start.1 = (f32[96,96]{1,0:T(8,128)S(1)}, f32[96,96]{1,0:T(8,128)S(1)}, u32[]{:S(2)}, u32[]{:S(2)}) collective-permute-start(f32[96,96]{1,0:T(8,128)S(1)} %get-tuple-element.27.middle), channel_id=1, source_target_pairs={{0,0},{7,7},{1,2},{2,1},{3,4},{4,3},{5,6},{6,5},{8,8},{15,15},{9,1... | collective-permute-start | bytes 110600 | tf_op jit(solution)/shard_map/ppermute | solution.py:148
  9.7 1.4 %collective-permute-start.2 = (f32[96,224]{1,0:T(8,128)S(1)}, f32[96,224]{1,0:T(8,128)S(1)}, u32[]{:S(2)}, u32[]{:S(2)}) collective-permute-start(f32[96,224]{1,0:T(8,128)S(1)} %get-tuple-element.30.band), channel_id=1, source_target_pairs={{0,8},{8,0},{16,24},{24,16},{1,9},{9,1},{17,25},{25,17},{2,10},{10... | collective-permute-start | bytes 258056 | tf_op jit(solution)/shard_map/ppermute | solution.py:140
  11.1 4.8 %collective-permute-start.3 = (f32[64,224]{1,0:T(8,128)S(1)}, f32[64,224]{1,0:T(8,128)S(1)}, u32[]{:S(2)}, u32[]{:S(2)}) collective-permute-start(f32[64,224]{1,0:T(8,128)S(1)} %get-tuple-element.33), channel_id=1, source_target_pairs={{0,16},{16,24},{24,8},{8,0},{1,17},{17,25},{25,9},{9,1},{2,18},{18... | collective-permute-start | bytes 172040 | tf_op jit(solution)/shard_map/ppermute | solution.py:155
  12.6 3.3 %copy-start.7 = (f32[1,256]{1,0:T(1,128)S(1)}, f32[1,256]{1,0:T(1,128)}, u32[]{:S(2)}) copy-start(f32[1,256]{1,0:T(1,128)} %slopes.1) | copy-start | bytes 3076
  12.6 3.3 %copy-start.8 = (s32[1,256]{1,0:T(1,128)S(1)}, s32[1,256]{1,0:T(1,128)}, u32[]{:S(2)}) copy-start(s32[1,256]{1,0:T(1,128)} %pixels.3) | copy-start | bytes 3076
  12.6 3.3 %copy-start.10 = (f32[12]{0:T(128)S(1)}, f32[12]{0:T(128)}, u32[]{:S(2)}) copy-start(f32[12]{0:T(128)} %weights.5) | copy-start | bytes 148
  12.6 3.3 %copy-start.11 = (bf16[11,256,256]{2,1,0:T(8,128)(2,1)S(1)}, bf16[11,256,256]{2,1,0:T(8,128)(2,1)}, u32[]{:S(2)}) copy-start(bf16[11,256,256]{2,1,0:T(8,128)(2,1)} %constant.13.clone.tables) | copy-start | bytes 4325380
  15.9 6.7 %copy-start.3 = (f32[2,8,224,256]{3,2,1,0:T(8,128)}, f32[2,8,224,256]{3,2,1,0:T(8,128)S(1)}, u32[]{:S(2)}) copy-start(f32[2,8,224,256]{3,2,1,0:T(8,128)S(1)} %get-tuple-element.37.rest_1_) | copy-start | bytes 11010052
  15.9 13.5 %copy-start.9 = (f32[8]{0:T(128)S(1)}, f32[8]{0:T(128)}, u32[]{:S(2)}) copy-start(f32[8]{0:T(128)} %doses.3) | copy-start | bytes 100
  22.6 13.9 %all-to-all-start = ((f32[32,1,512]{2,1,0:T(1,128)}), f32[32,1,512]{2,1,0:T(1,128)S(1)}, u32[]{:S(2)}, u32[]{:S(2)}) async-start(f32[32,1,512]{2,1,0:T(1,128)} %get-tuple-element.38), calls=%async_computation | async-start | bytes 131072 | tf_op jit(solution)/shard_map/all_to_all | solution.py:557
  36.5 2.0 %copy-start.4 = (f32[2,8,224,256]{3,2,1,0:T(8,128)S(1)}, f32[2,8,224,256]{3,2,1,0:T(8,128)}, u32[]{:S(2)}) copy-start(f32[2,8,224,256]{3,2,1,0:T(8,128)} %copy-done.3) | copy-start | bytes 11010052
  36.5 2.3 %copy-start.12 = (bf16[7,256,256]{2,1,0:T(8,128)(2,1)S(1)}, bf16[7,256,256]{2,1,0:T(8,128)(2,1)}, u32[]{:S(2)}) copy-start(bf16[7,256,256]{2,1,0:T(8,128)(2,1)} %constant.14.clone.tables) | copy-start | bytes 2752516
  42.9 4.3 %collective-permute-start.4 = (f32[64,224]{1,0:T(8,128)S(1)}, f32[64,224]{1,0:T(8,128)S(1)}, u32[]{:S(2)}, u32[]{:S(2)}) collective-permute-start(f32[64,224]{1,0:T(8,128)S(1)} %get-tuple-element.48), channel_id=1, source_target_pairs={{16,0},{24,16},{8,24},{0,8},{17,1},{25,17},{9,25},{1,9},{18,2},{26... | collective-permute-start | bytes 172040 | tf_op jit(solution)/shard_map/ppermute | solution.py:155
  47.2 1.4 %collective-permute-start.5 = (f32[96,224]{1,0:T(8,128)S(1)}, f32[96,224]{1,0:T(8,128)S(1)}, u32[]{:S(2)}, u32[]{:S(2)}) collective-permute-start(f32[96,224]{1,0:T(8,128)S(1)} %fold.2), channel_id=1, source_target_pairs={{0,8},{8,0},{16,24},{24,16},{1,9},{9,1},{17,25},{25,17},{2,10},{10... | collective-permute-start | bytes 258056 | tf_op jit(solution)/shard_map/ppermute | solution.py:140
  48.7 4.0 %collective-permute-start.6 = (f32[48,128]{1,0:T(8,128)S(1)}, f32[48,128]{1,0:T(8,128)S(1)}, u32[]{:S(2)}, u32[]{:S(2)}) collective-permute-start(f32[48,128]{1,0:T(8,128)S(1)} %get-tuple-element.50), channel_id=1, source_target_pairs={{0,0},{7,7},{1,2},{2,1},{3,4},{4,3},{5,6},{6,5},{8,8},{15,15},{9,1... | collective-permute-start | bytes 73736 | tf_op jit(solution)/shard_map/ppermute | solution.py:148
  49.3 5.1 %copy-start.6 = (f32[96,96]{1,0:T(8,128)S(1)}, f32[96,96]{1,0:T(8,128)}, u32[]{:S(2)}) copy-start(f32[96,96]{1,0:T(8,128)} %latent.3) | copy-start | bytes 110596
  49.4 5.0 %collective-permute-start.7 = (f32[48,128]{1,0:T(8,128)S(1)}, f32[48,128]{1,0:T(8,128)S(1)}, u32[]{:S(2)}, u32[]{:S(2)}) collective-permute-start(f32[48,128]{1,0:T(8,128)S(1)} %near.1), channel_id=1, source_target_pairs={{0,1},{1,0},{2,3},{3,2},{4,5},{5,4},{6,7},{7,6},{8,9},{9,8},{10,11... | collective-permute-start | bytes 73736 | tf_op jit(solution)/shard_map/ppermute | solution.py:140

commit v13 on v12

--- a/solution.py
+++ b/solution.py
@@ -227,7 +227,6 @@
     lower, other = place_in_pair("tx")
 
     near = jnp.where(lower, partner[:, :radius], partner[:, tile - radius :])
-    near = 0.5 * (1.0 + jnp.tanh(near))
     far = jnp.where(lower, outside[:, tile - radius :], outside[:, :radius])
     far = jnp.where(other, far, 0.0)
     band[:, :radius] = jnp.where(lower, far, near)
@@ -411,7 +410,7 @@
     place = lax.broadcasted_iota(jnp.int32, (tile, samples), 0)
     in_row[...] = jnp.where(place == row, 1.0, 0.0)
     place = lax.broadcasted_iota(jnp.int32, (LANES, samples), 0)
-    one_hot[...] = jnp.where(place == col, 1.0, 0.0).astype(BF16)
+    one_hot[...] = jnp.where(place == col, 1.0, 0.0).T.astype(BF16)
 
 
 def source_kernel(
@@ -452,23 +451,15 @@
     summed = summed / total_weight(weights, kernels)
 
     placed = in_row[...] * summed
-    high, rest = split(placed)
-    low = (placed - high.astype(F32) - rest.astype(F32)).astype(BF16)
-    grid = jnp.zeros((tile, LANES), F32)
-    for part in (high, rest, low):
-        grid = grid + lax.dot_general(
-            part, one_hot[...], (((1,), (1,)), ((), ())), preferred_element_type=F32
-        )
-
+    tall = dot(stacked(split3(placed)), one_hot[...])
+    grid = tall[:tile] + (tall[tile : 2 * tile] + tall[2 * tile :])
     placed_sum[...] = grid
 
 
-def gradient_kernel(weights, grid, field_re, field_im, tables, *rest):
-    *spec, grad, rim, total_re, total_im = rest
-    period = grad.shape[0]
+def add_waves(first, weights, grid, field_re, field_im, tables, own, total_re, total_im):
+    period = total_re.shape[0]
     half = period // 2
     tile = field_re.shape[1]
-    radius = (period - tile) // 2
     cols = pair(tables, 0, LANES, 2 * LANES)
     cols = (stacked((cols[0], cols[0])), cols[1])
     rows = tile // 2
@@ -485,34 +476,47 @@
             out.append(dot(table, stacked((high, low, high))))
         return out
 
-    total_re[...] = jnp.zeros((period, 2 * LANES), F32)
-    total_im[...] = jnp.zeros((period, 2 * LANES), F32)
-
-    places = [(own, k) for own in spec for k in range(own.shape[1])]
-    for group in range(len(places) // BATCH):
+    for start in range(0, own.shape[1], BATCH):
         sources = []
-        for i in range(BATCH):
-            k = group * BATCH + i
-            weighted = grid[...] * weights[k]
-            sources += [weighted * field_re[k], weighted * field_im[k]]
+        for at in range(start, start + BATCH):
+            weighted = grid[...] * weights[first + at]
+            sources += [weighted * field_re[first + at], weighted * field_im[first + at]]
         high, low = split(stacked(sources))
         both = dot(jnp.concatenate([high, low], axis=1), cols[0]) + dot(high, cols[1])
         for i in range(BATCH):
-            own, at = places[group * BATCH + i]
+            at = start + i
             real_cos, real_sin = halves(both[2 * i * tile : (2 * i + 1) * tile])
             imag_cos, imag_sin = halves(both[(2 * i + 1) * tile : (2 * i + 2) * tile])
             wide_re = jnp.concatenate([real_cos + imag_sin, real_cos - imag_sin], axis=1)
             wide_im = jnp.concatenate([imag_cos - real_sin, imag_cos + real_sin], axis=1)
             cos_re, sin_re = along_rows(wide_re)
             cos_im, sin_im = along_rows(wide_im)
-            for start, sign in ((0, 1.0), (half, -1.0)):
-                part = slice(start, start + half)
+            for begin, sign in ((0, 1.0), (half, -1.0)):
+                part = slice(begin, begin + half)
                 wave_re = cos_re + sign * sin_im
                 wave_im = cos_im - sign * sin_re
                 own_re, own_im = own[0, at, part], own[1, at, part]
                 total_re[part] += own_re * wave_re + own_im * wave_im
                 total_im[part] += own_re * wave_im - own_im * wave_re
 
+
+def first_waves_kernel(weights, grid, field_re, field_im, tables, own, total_re, total_im):
+    total_re[...] = jnp.zeros(total_re.shape, F32)
+    total_im[...] = jnp.zeros(total_im.shape, F32)
+    add_waves(0, weights, grid, field_re, field_im, tables, own, total_re, total_im)
+
+
+def gradient_kernel(
+    first, weights, grid, field_re, field_im, tables, own, sum_re, sum_im,
+    grad, rim, total_re, total_im,
+):
+    period = grad.shape[0]
+    half = period // 2
+    tile = field_re.shape[1]
+    radius = (period - tile) // 2
+    total_re[...] = sum_re[...]
+    total_im[...] = sum_im[...]
+    add_waves(first, weights, grid, field_re, field_im, tables, own, total_re, total_im)
     pos_re, neg_re = total_re[:half], total_re[half:]
     pos_im, neg_im = total_im[:half], total_im[half:]
     back_rows = pair(tables, 4, period, period)
@@ -581,11 +585,10 @@
             micros=parts // 2,
         )(kernels, *first_tables, after, *into)
 
-    partner = swap("tx", latent)
     transmit, done = call(
         own_kernel, "own", [shape(tile, tile), token], [VMEM], micros=3
     )(latent)
-    outside = swap_outside("tx", transmit)
+    partner, outside = swap("tx", transmit), swap_outside("tx", transmit)
     small, few = count // 3, count // 6
     large = count - small
     spec_a, done = spectra(0, 0, small, small, done)
@@ -620,7 +623,7 @@
         own_samples_kernel,
         "samples",
         [shape(corners, samples)] * 2
-        + [shape(tile, samples), jax.ShapeDtypeStruct((LANES, samples), BF16)],
+        + [shape(tile, samples), jax.ShapeDtypeStruct((samples, LANES), BF16)],
         [SMEM] + [VMEM] * 2,
         micros=2,
     )(dose_scale, sampled, edge_pixels)
@@ -631,14 +634,22 @@
         [SMEM] * 3 + [VMEM] * 5,
         micros=2,
     )(socs_weights, dose_scale, threshold_pick, gathered, *own)
+    known = (socs_weights, grid, field_re, field_im, last_tables)
+    sums = call(
+        first_waves_kernel,
+        "waves",
+        [shape(period, 2 * LANES)] * 2,
+        [SMEM] + [VMEM] * 5,
+        micros=2,
+    )(*known, spec_a)
     grad, rim = call(
-        gradient_kernel,
+        functools.partial(gradient_kernel, small),
         "gradient",
         [shape(period, period), shape(radius, period)],
-        [SMEM] + [VMEM] * (4 + len(spec)),
+        [SMEM] + [VMEM] * 7,
         scratch=[pltpu.VMEM((period, 2 * LANES), F32)] * 2,
-        micros=6,
-    )(socs_weights, grid, field_re, field_im, last_tables, *spec)
+        micros=5,
+    )(*known, spec_b, *sums)
 
     rim = ring("ty", rim, back=True)
     (partner,) = call(fold_rows_kernel, "fold", [shape(tile, period)], [VMEM] * 2)(

time: 55.5 us -> 55.4 us (level)
  local copies, waits for them, and re-layouts: 3.09 us -> 1.45 us
  Pallas kernels: 20.7 us -> 21.6 us
  starting transfers between devices: 16.3 us -> 17 us
    unnamed x30, local copies, waits for them, and re-layouts: 3.09 us -> 1.45 us
    all_to_all x1, starting transfers between devices: 6.79 us -> 7.69 us  [gather_all(): return lax.all_to_all(copies, ('ty', 'tx'), 0, 0, tiled=True)]
    pallas_call x1 -> x2, Pallas kernels: 4.12 us -> 4.99 us  [the longest x1 3.22 us: body(): call(functools.partial(gradient_kernel, small), 'gradient', [shape(period...]
where the time goes in v13:
time: 55.4 us; the launch traced here: 55.1 us
  Pallas kernels  21.6 us (39%)
  starting transfers between devices  17 us (31%)
  waiting for transfers between devices  13.6 us (25%)
  between operations  1.53 us (3%)
  local copies, waits for them, and re-layouts  1.45 us (3%)
    all_to_all x1, starting transfers between devices, gather_all(): return lax.all_to_all(copies, ('ty', 'tx'), 0, 0, tiled=True)  7.69 us
    pallas_call x1, Pallas kernels, body(): call(field_kernel, 'field', [shape(count, tile, LANES)] * 2 + [shape(1, 2...  6.64 us
    pallas_call x3, Pallas kernels, spectra(): call(functools.partial(spectra_kernel, start, first_out, parts), 'spectra...  6.51 us
    all_to_all x1, waiting for transfers between devices, gather_all(): return lax.all_to_all(copies, ('ty', 'tx'), 0, 0, tiled=True)  6.43 us
    ppermute x4, starting transfers between devices, swap(): lax.ppermute(x, axis, [(i, i ^ 1) for i in range(lax.axis_size(axis))])  6.35 us
    ppermute x2, waiting for transfers between devices, ring(): return lax.ppermute(x, axis, [(b, a) if back else (a, b) for a, b in pairs])  4.15 us
    pallas_call x1, Pallas kernels, body(): call(functools.partial(gradient_kernel, small), 'gradient', [shape(period...  3.22 us
    ppermute x4, waiting for transfers between devices, swap(): lax.ppermute(x, axis, [(i, i ^ 1) for i in range(lax.axis_size(axis))])  3 us
  transfers between devices with their start and end apart: 9, of which 5 were waited for; matrix products, arithmetic and copies ran while one was open for 1% of the time, Pallas kernels for 13%

profile of v13, /device:TPU:0, one launch (start us, length us, event | category | flops | bytes accessed | tf_op | source)
XLA Modules:
  0.0 55.1 jit_solution(9360484090461919301)
XLA Ops:
  0.6 0.8 %copy-done.5 = f32[96,96]{1,0:T(8,128)S(1)} copy-done((f32[96,96]{1,0:T(8,128)S(1)}, f32[96,96]{1,0:T(8,128)}, u32[]{:S(2)}) %copy-start.5) | copy-done | bytes 36888
  1.5 3.0 %collective-permute-start = (f32[96,96]{1,0:T(8,128)S(1)}, f32[96,96]{1,0:T(8,128)S(1)}, u32[]{:S(2)}, u32[]{:S(2)}) collective-permute-start(f32[96,96]{1,0:T(8,128)S(1)} %get-tuple-element.29.middle), channel_id=1, source_target_pairs={{0,1},{1,0},{2,3},{3,2},{4,5},{5,4},{6,7},{7,6},{8,9},{9,8},{10,11... | collective-permute-start | bytes 110600 | tf_op jit(solution)/shard_map/ppermute | solution.py:140
  4.5 0.7 %collective-permute-start.1 = (f32[96,96]{1,0:T(8,128)S(1)}, f32[96,96]{1,0:T(8,128)S(1)}, u32[]{:S(2)}, u32[]{:S(2)}) collective-permute-start(f32[96,96]{1,0:T(8,128)S(1)} %get-tuple-element.29.middle), channel_id=1, source_target_pairs={{0,0},{7,7},{1,2},{2,1},{3,4},{4,3},{5,6},{6,5},{8,8},{15,15},{9,1... | collective-permute-start | bytes 110600 | tf_op jit(solution)/shard_map/ppermute | solution.py:148
  5.2 0.3 copy.19.kern
  5.6 2.0 %spectra.3 = (f32[2,4,224,256]{3,2,1,0:T(8,128)S(1)}, f32[8,128]{1,0:T(8,128)S(1)}) custom-call(f32[2,12,129,129]{3,2,1,0:T(8,128)S(1)} %copy.19.kern, bf16[3,256,256]{2,1,0:T(8,128)(2,1)S(1)} %copy-done, bf16[672,256]{1,0:T(8,128)(2,1)S(1)} %copy-done.1, f32[232,256]{1,0:T(8,128)S(1)} %copy-done.2, f32[8,128]{1,0:T(8,128)S(1)} %get-tuple-element.30.rest_0_), custom_call_target="tpu_custom_call" | custom-call | flops 2000000000 | bytes 1048576 | tf_op jit(solution)/shard_map/spectra/pallas_call | solution.py:579
  8.2 0.2 band.1
  8.5 1.2 %spectra.4 = (f32[2,8,224,256]{3,2,1,0:T(8,128)S(1)}, f32[8,128]{1,0:T(8,128)S(1)}) custom-call(f32[2,12,129,129]{3,2,1,0:T(8,128)S(1)} %copy.19.kern, bf16[3,256,256]{2,1,0:T(8,128)(2,1)S(1)} %copy-done, bf16[672,256]{1,0:T(8,128)(2,1)S(1)} %copy-done.1, f32[232,256]{1,0:T(8,128)S(1)} %copy-done.2, f32[8,128]{1,0:T(8,128)S(1)} %get-tuple-element.33.rest_0_), custom_call_target="tpu_custom_call" | custom-call | flops 1000000000 | bytes 1048576 | tf_op jit(solution)/shard_map/spectra/pallas_call | solution.py:579
  9.8 1.5 %collective-permute-start.3 = (f32[64,224]{1,0:T(8,128)S(1)}, f32[64,224]{1,0:T(8,128)S(1)}, u32[]{:S(2)}, u32[]{:S(2)}) collective-permute-start(f32[64,224]{1,0:T(8,128)S(1)} %get-tuple-element.35), channel_id=1, source_target_pairs={{0,16},{16,24},{24,8},{8,0},{1,17},{17,25},{25,9},{9,1},{2,18},{18... | collective-permute-start | bytes 172040 | tf_op jit(solution)/shard_map/ppermute | solution.py:155
  11.3 3.3 %spectra.5 = (f32[2,8,224,256]{3,2,1,0:T(8,128)S(1)}, f32[8,128]{1,0:T(8,128)}) custom-call(f32[2,12,129,129]{3,2,1,0:T(8,128)S(1)} %copy.19.kern, bf16[3,256,256]{2,1,0:T(8,128)(2,1)S(1)} %copy-done, bf16[672,256]{1,0:T(8,128)(2,1)S(1)} %copy-done.1, f32[232,256]{1,0:T(8,128)S(1)} %copy-done.2, ...), custom_call_target="tpu_custom_call", output_to_operand_aliasing={{0}: (5, {})} | custom-call | flops 3000000000 | bytes 1048576 | tf_op jit(solution)/shard_map/spectra/pallas_call | solution.py:579
  14.7 6.6 %field.1 = (f32[12,96,128]{2,1,0:T(8,128)S(1)}, f32[12,96,128]{2,1,0:T(8,128)S(1)}, f32[1,512]{1,0:T(1,128)S(1)}, f32[32,1,512]{2,1,0:T(1,128)}) custom-call(f32[12]{0:T(128)S(1)} %copy-done.10, f32[96,224]{1,0:T(8,128)S(1)} %get-tuple-element.32.band, f32[96,224]{1,0:T(8,128)S(1)} %collective-permute-done.2.partner, ...), custom_call_target="tpu_custom_call" | custom-call | flops 7000000000 | bytes 1048576 | tf_op jit(solution)/shard_map/field/pallas_call | solution.py:607
  21.3 7.7 %all-to-all-start = ((f32[32,1,512]{2,1,0:T(1,128)}), f32[32,1,512]{2,1,0:T(1,128)S(1)}, u32[]{:S(2)}, u32[]{:S(2)}) async-start(f32[32,1,512]{2,1,0:T(1,128)} %get-tuple-element.40), calls=%async_computation | async-start | bytes 131072 | tf_op jit(solution)/shard_map/all_to_all | solution.py:561
  29.0 0.6 %samples.1 = (f32[8,256]{1,0:T(8,128)S(1)}, f32[8,256]{1,0:T(8,128)S(1)}, f32[96,256]{1,0:T(8,128)S(1)}, bf16[256,128]{1,0:T(8,128)(2,1)S(1)}) custom-call(f32[8]{0:T(128)S(1)} %copy-done.9, f32[1,512]{1,0:T(1,128)S(1)} %get-tuple-element.41.sampled, s32[1,256]{1,0:T(1,128)S(1)} %copy-done.8), custom_call_target="tpu_custom_call" | custom-call | flops 2000000000 | bytes 1048576 | tf_op jit(solution)/shard_map/samples/pallas_call | solution.py:622
  29.7 6.4 %all-to-all-done = f32[32,1,512]{2,1,0:T(1,128)S(1)} async-done(((f32[32,1,512]{2,1,0:T(1,128)}), f32[32,1,512]{2,1,0:T(1,128)S(1)}, u32[]{:S(2)}, u32[]{:S(2)}) %all-to-all-start) | async-done | bytes 65568 | tf_op jit(solution)/shard_map/all_to_all | solution.py:561
  36.1 1.4 %source.1 = (f32[96,128]{1,0:T(8,128)S(1)}, f32[1,1]{1,0:T(1,128)}) custom-call(f32[12]{0:T(128)S(1)} %copy-done.10, f32[8]{0:T(128)S(1)} %copy-done.9, s32[1]{0:T(128)S(6)} %copy.26.pick, f32[32,512]{1,0:T(8,128)S(1)} %bitcast.4, f32[8,256]{1,0:T(8,128)S(1)} %get-tuple-element.42.own_error, f32[8,256]{1,0:T(8,128)S(1)} %get-tuple-element.43.chain, ...), custom_call_target="tpu_custom_call" | custom-call | flops 2000000000 | bytes 1048576 | tf_op jit(solution)/shard_map/source/pallas_call | solution.py:630
  37.5 1.8 %waves.1 = (f32[224,256]{1,0:T(8,128)S(1)}, f32[224,256]{1,0:T(8,128)S(1)}) custom-call(f32[12]{0:T(128)S(1)} %copy-done.10, f32[96,128]{1,0:T(8,128)S(1)} %get-tuple-element.46.grid, f32[12,96,128]{2,1,0:T(8,128)S(1)} %get-tuple-element.47.field_re, f32[12,96,128]{2,1,0:T(8,128)S(1)} %get-tuple-element.48.field_im, bf16[7,256,256]{2,1,0:T(8,128)(2,1)S(1)} %copy-done.12, ...), custom_call_target="tpu_custom_call" | custom-call | flops 2000000000 | bytes 1048576 | tf_op jit(solution)/shard_map/waves/pallas_call | solution.py:638
  39.3 0.3 copy-done.4
  39.6 3.2 %gradient.1 = (f32[224,224]{1,0:T(8,128)S(1)}, f32[64,224]{1,0:T(8,128)S(1)}) custom-call(f32[12]{0:T(128)S(1)} %copy-done.10, f32[96,128]{1,0:T(8,128)S(1)} %get-tuple-element.46.grid, f32[12,96,128]{2,1,0:T(8,128)S(1)} %get-tuple-element.47.field_re, f32[12,96,128]{2,1,0:T(8,128)S(1)} %get-tuple-element.48.field_im, bf16[7,256,256]{2,1,0:T(8,128)(2,1)S(1)} %copy-done.12, ...), custom_call_target="tpu_custom_call" | custom-call | flops 5000000000 | bytes 1048576 | tf_op jit(solution)/shard_map/gradient/pallas_call | solution.py:645
  42.9 4.2 %collective-permute-done.4.rim = f32[64,224]{1,0:T(8,128)S(1)} collective-permute-done((f32[64,224]{1,0:T(8,128)S(1)}, f32[64,224]{1,0:T(8,128)S(1)}, u32[]{:S(2)}, u32[]{:S(2)}) %collective-permute-start.4) | collective-permute-done | bytes 57376 | tf_op jit(solution)/shard_map/ppermute | solution.py:155
  47.2 1.3 %collective-permute-done.5.partner = f32[96,224]{1,0:T(8,128)S(1)} collective-permute-done((f32[96,224]{1,0:T(8,128)S(1)}, f32[96,224]{1,0:T(8,128)S(1)}, u32[]{:S(2)}, u32[]{:S(2)}) %collective-permute-start.5) | collective-permute-done | bytes 86048 | tf_op jit(solution)/shard_map/ppermute | solution.py:140
  48.6 0.7 %collective-permute-start.6 = (f32[48,128]{1,0:T(8,128)S(1)}, f32[48,128]{1,0:T(8,128)S(1)}, u32[]{:S(2)}, u32[]{:S(2)}) collective-permute-start(f32[48,128]{1,0:T(8,128)S(1)} %get-tuple-element.54), channel_id=1, source_target_pairs={{0,0},{7,7},{1,2},{2,1},{3,4},{4,3},{5,6},{6,5},{8,8},{15,15},{9,1... | collective-permute-start | bytes 73736 | tf_op jit(solution)/shard_map/ppermute | solution.py:148
  49.3 3.2 %collective-permute-start.7 = (f32[48,128]{1,0:T(8,128)S(1)}, f32[48,128]{1,0:T(8,128)S(1)}, u32[]{:S(2)}, u32[]{:S(2)}) collective-permute-start(f32[48,128]{1,0:T(8,128)S(1)} %near.1), channel_id=1, source_target_pairs={{0,1},{1,0},{2,3},{3,2},{4,5},{5,4},{6,7},{7,6},{8,9},{9,8},{10,11... | collective-permute-start | bytes 73736 | tf_op jit(solution)/shard_map/ppermute | solution.py:140
  52.5 0.1 far.1.total
  52.7 1.7 %collective-permute-done.7.near = f32[48,128]{1,0:T(8,128)S(1)} collective-permute-done((f32[48,128]{1,0:T(8,128)S(1)}, f32[48,128]{1,0:T(8,128)S(1)}, u32[]{:S(2)}, u32[]{:S(2)}) %collective-permute-start.7) | collective-permute-done | bytes 24608 | tf_op jit(solution)/shard_map/ppermute | solution.py:140
  54.4 0.8 %finish.1 = f32[96,96]{1,0:T(8,128)} custom-call(f32[96,96]{1,0:T(8,128)S(1)} %far.1.total, f32[48,128]{1,0:T(8,128)S(1)} %collective-permute-done.7.near, f32[96,96]{1,0:T(8,128)S(1)} %copy-done.6), custom_call_target="tpu_custom_call" | custom-call | flops 1000000000 | bytes 1048576 | tf_op jit(solution)/shard_map/finish/pallas_call | solution.py:666
  (40 shorter events, 0.6 us)
Async XLA Ops:
  0.6 0.8 %copy-start.5 = (f32[96,96]{1,0:T(8,128)S(1)}, f32[96,96]{1,0:T(8,128)}, u32[]{:S(2)}) copy-start(f32[96,96]{1,0:T(8,128)} %latent.3) | copy-start | bytes 110596
  1.4 3.8 %copy-start.13 = (f32[2,12,129,129]{3,0,2,1:T(2,128)S(1)}, f32[2,12,129,129]{3,0,2,1:T(2,128)}, u32[]{:S(2)}) copy-start(f32[2,12,129,129]{3,0,2,1:T(2,128)} %param.13) | copy-start | bytes 4792612
  1.5 4.1 %copy-start = (bf16[3,256,256]{2,1,0:T(8,128)(2,1)S(1)}, bf16[3,256,256]{2,1,0:T(8,128)(2,1)}, u32[]{:S(2)}) copy-start(bf16[3,256,256]{2,1,0:T(8,128)(2,1)} %constant.10.clone.lanes) | copy-start | bytes 1179652
  1.5 4.1 %copy-start.1 = (bf16[672,256]{1,0:T(8,128)(2,1)S(1)}, bf16[672,256]{1,0:T(8,128)(2,1)}, u32[]{:S(2)}) copy-start(bf16[672,256]{1,0:T(8,128)(2,1)} %constant.11.clone.rows) | copy-start | bytes 1032196
  1.5 4.1 %copy-start.2 = (f32[232,256]{1,0:T(8,128)S(1)}, f32[232,256]{1,0:T(8,128)}, u32[]{:S(2)}) copy-start(f32[232,256]{1,0:T(8,128)} %constant.12.clone.ends) | copy-start | bytes 712708
  1.5 6.7 %collective-permute-start = (f32[96,96]{1,0:T(8,128)S(1)}, f32[96,96]{1,0:T(8,128)S(1)}, u32[]{:S(2)}, u32[]{:S(2)}) collective-permute-start(f32[96,96]{1,0:T(8,128)S(1)} %get-tuple-element.29.middle), channel_id=1, source_target_pairs={{0,1},{1,0},{2,3},{3,2},{4,5},{5,4},{6,7},{7,6},{8,9},{9,8},{10,11... | collective-permute-start | bytes 110600 | tf_op jit(solution)/shard_map/ppermute | solution.py:140
  4.5 3.7 %collective-permute-start.1 = (f32[96,96]{1,0:T(8,128)S(1)}, f32[96,96]{1,0:T(8,128)S(1)}, u32[]{:S(2)}, u32[]{:S(2)}) collective-permute-start(f32[96,96]{1,0:T(8,128)S(1)} %get-tuple-element.29.middle), channel_id=1, source_target_pairs={{0,0},{7,7},{1,2},{2,1},{3,4},{4,3},{5,6},{6,5},{8,8},{15,15},{9,1... | collective-permute-start | bytes 110600 | tf_op jit(solution)/shard_map/ppermute | solution.py:148
  8.5 1.3 %collective-permute-start.2 = (f32[96,224]{1,0:T(8,128)S(1)}, f32[96,224]{1,0:T(8,128)S(1)}, u32[]{:S(2)}, u32[]{:S(2)}) collective-permute-start(f32[96,224]{1,0:T(8,128)S(1)} %get-tuple-element.32.band), channel_id=1, source_target_pairs={{0,8},{8,0},{16,24},{24,16},{1,9},{9,1},{17,25},{25,17},{2,10},{10... | collective-permute-start | bytes 258056 | tf_op jit(solution)/shard_map/ppermute | solution.py:140
  9.8 4.8 %collective-permute-start.3 = (f32[64,224]{1,0:T(8,128)S(1)}, f32[64,224]{1,0:T(8,128)S(1)}, u32[]{:S(2)}, u32[]{:S(2)}) collective-permute-start(f32[64,224]{1,0:T(8,128)S(1)} %get-tuple-element.35), channel_id=1, source_target_pairs={{0,16},{16,24},{24,8},{8,0},{1,17},{17,25},{25,9},{9,1},{2,18},{18... | collective-permute-start | bytes 172040 | tf_op jit(solution)/shard_map/ppermute | solution.py:155
  11.3 3.3 %copy-start.7 = (f32[1,256]{1,0:T(1,128)S(1)}, f32[1,256]{1,0:T(1,128)}, u32[]{:S(2)}) copy-start(f32[1,256]{1,0:T(1,128)} %slopes.1) | copy-start | bytes 3076
  11.3 3.3 %copy-start.8 = (s32[1,256]{1,0:T(1,128)S(1)}, s32[1,256]{1,0:T(1,128)}, u32[]{:S(2)}) copy-start(s32[1,256]{1,0:T(1,128)} %pixels.3) | copy-start | bytes 3076
  11.3 3.3 %copy-start.10 = (f32[12]{0:T(128)S(1)}, f32[12]{0:T(128)}, u32[]{:S(2)}) copy-start(f32[12]{0:T(128)} %weights.7) | copy-start | bytes 148
  11.3 3.3 %copy-start.11 = (bf16[11,256,256]{2,1,0:T(8,128)(2,1)S(1)}, bf16[11,256,256]{2,1,0:T(8,128)(2,1)}, u32[]{:S(2)}) copy-start(bf16[11,256,256]{2,1,0:T(8,128)(2,1)} %constant.13.clone.tables) | copy-start | bytes 4325380
  14.6 6.7 %copy-start.3 = (f32[2,8,224,256]{3,2,1,0:T(8,128)}, f32[2,8,224,256]{3,2,1,0:T(8,128)S(1)}, u32[]{:S(2)}) copy-start(f32[2,8,224,256]{3,2,1,0:T(8,128)S(1)} %get-tuple-element.39.rest_1_.own) | copy-start | bytes 11010052
  14.6 14.3 %copy-start.9 = (f32[8]{0:T(128)S(1)}, f32[8]{0:T(128)}, u32[]{:S(2)}) copy-start(f32[8]{0:T(128)} %doses.3) | copy-start | bytes 100
  21.3 14.8 %all-to-all-start = ((f32[32,1,512]{2,1,0:T(1,128)}), f32[32,1,512]{2,1,0:T(1,128)S(1)}, u32[]{:S(2)}, u32[]{:S(2)}) async-start(f32[32,1,512]{2,1,0:T(1,128)} %get-tuple-element.40), calls=%async_computation | async-start | bytes 131072 | tf_op jit(solution)/shard_map/all_to_all | solution.py:561
  36.1 1.4 %copy-start.12 = (bf16[7,256,256]{2,1,0:T(8,128)(2,1)S(1)}, bf16[7,256,256]{2,1,0:T(8,128)(2,1)}, u32[]{:S(2)}) copy-start(bf16[7,256,256]{2,1,0:T(8,128)(2,1)} %constant.14.clone.tables) | copy-start | bytes 2752516
  37.5 2.0 %copy-start.4 = (f32[2,8,224,256]{3,2,1,0:T(8,128)S(1)}, f32[2,8,224,256]{3,2,1,0:T(8,128)}, u32[]{:S(2)}) copy-start(f32[2,8,224,256]{3,2,1,0:T(8,128)} %copy-done.3) | copy-start | bytes 11010052
  42.8 4.3 %collective-permute-start.4 = (f32[64,224]{1,0:T(8,128)S(1)}, f32[64,224]{1,0:T(8,128)S(1)}, u32[]{:S(2)}, u32[]{:S(2)}) collective-permute-start(f32[64,224]{1,0:T(8,128)S(1)} %get-tuple-element.52), channel_id=1, source_target_pairs={{16,0},{24,16},{8,24},{0,8},{17,1},{25,17},{9,25},{1,9},{18,2},{26... | collective-permute-start | bytes 172040 | tf_op jit(solution)/shard_map/ppermute | solution.py:155
  47.1 1.4 %collective-permute-start.5 = (f32[96,224]{1,0:T(8,128)S(1)}, f32[96,224]{1,0:T(8,128)S(1)}, u32[]{:S(2)}, u32[]{:S(2)}) collective-permute-start(f32[96,224]{1,0:T(8,128)S(1)} %fold.2), channel_id=1, source_target_pairs={{0,8},{8,0},{16,24},{24,16},{1,9},{9,1},{17,25},{25,17},{2,10},{10... | collective-permute-start | bytes 258056 | tf_op jit(solution)/shard_map/ppermute | solution.py:140
  48.6 4.0 %collective-permute-start.6 = (f32[48,128]{1,0:T(8,128)S(1)}, f32[48,128]{1,0:T(8,128)S(1)}, u32[]{:S(2)}, u32[]{:S(2)}) collective-permute-start(f32[48,128]{1,0:T(8,128)S(1)} %get-tuple-element.54), channel_id=1, source_target_pairs={{0,0},{7,7},{1,2},{2,1},{3,4},{4,3},{5,6},{6,5},{8,8},{15,15},{9,1... | collective-permute-start | bytes 73736 | tf_op jit(solution)/shard_map/ppermute | solution.py:148
  49.2 5.1 %copy-start.6 = (f32[96,96]{1,0:T(8,128)S(1)}, f32[96,96]{1,0:T(8,128)}, u32[]{:S(2)}) copy-start(f32[96,96]{1,0:T(8,128)} %latent.3) | copy-start | bytes 110596
  49.3 5.0 %collective-permute-start.7 = (f32[48,128]{1,0:T(8,128)S(1)}, f32[48,128]{1,0:T(8,128)S(1)}, u32[]{:S(2)}, u32[]{:S(2)}) collective-permute-start(f32[48,128]{1,0:T(8,128)S(1)} %near.1), channel_id=1, source_target_pairs={{0,1},{1,0},{2,3},{3,2},{4,5},{5,4},{6,7},{7,6},{8,9},{9,8},{10,11... | collective-permute-start | bytes 73736 | tf_op jit(solution)/shard_map/ppermute | solution.py:140

commit v14 on v11

--- a/solution.py
+++ b/solution.py
@@ -14,7 +14,7 @@
 RESIST_LEVEL = 0.7
 SOFTNESS = 0.25
 LANES = 128
-BATCH = 4
+BATCH = 6
 F32 = jnp.float32
 BF16 = jnp.bfloat16
 
@@ -362,8 +362,9 @@
     for first in range(0, kernels, BATCH):
         lines = stacked([line for i in range(BATCH) for line in lifted(*places[first + i])])
         x1, x2, x3 = split3(lines)
-        most, more = halves(dot(x1, across[1]))
-        some, small = halves(dot(x2, across[1]))
+        leading = dot(stacked((x1, x2)), across[1])
+        most, more = halves(leading[: x1.shape[0]])
+        some, small = halves(leading[x1.shape[0] :])
         both = small + dot(x1, across[2]) + dot(x3, across[0]) + (more + some) + most
         for i in range(BATCH):
             real = both[2 * i * tile : (2 * i + 1) * tile]

time: 55.1 us -> 55.1 us (level)
  no operation moved by 1% of the time
where the time goes in v14:
time: 55.1 us; the launch traced here: 54.9 us
  Pallas kernels  20.1 us (36%)
  starting transfers between devices  17.6 us (32%)
  waiting for transfers between devices  13.6 us (25%)
  local copies, waits for them, and re-layouts  2.05 us (4%)
  between operations  1.52 us (3%)
    all_to_all x1, starting transfers between devices, gather_all(): return lax.all_to_all(copies, ('ty', 'tx'), 0, 0, tiled=True)  8.34 us
    pallas_call x1, Pallas kernels, body(): call(field_kernel, 'field', [shape(count, tile, LANES)] * 2 + [shape(1, 2...  6.53 us
    pallas_call x3, Pallas kernels, spectra(): call(functools.partial(spectra_kernel, start, first_out, parts), 'spectra...  6.51 us
    all_to_all x1, waiting for transfers between devices, gather_all(): return lax.all_to_all(copies, ('ty', 'tx'), 0, 0, tiled=True)  6.45 us
    ppermute x4, starting transfers between devices, swap(): lax.ppermute(x, axis, [(i, i ^ 1) for i in range(lax.axis_size(axis))])  6.35 us
    pallas_call x1, Pallas kernels, body(): call(gradient_kernel, 'gradient', [shape(period, period), shape(radius, p...  4.27 us
    ppermute x2, waiting for transfers between devices, ring(): return lax.ppermute(x, axis, [(b, a) if back else (a, b) for a, b in pairs])  4.15 us
    ppermute x4, waiting for transfers between devices, swap(): lax.ppermute(x, axis, [(i, i ^ 1) for i in range(lax.axis_size(axis))])  3 us
  transfers between devices with their start and end apart: 9, of which 5 were waited for; matrix products, arithmetic and copies ran while one was open for 1% of the time, Pallas kernels for 12%

profile of v14, /device:TPU:0, one launch (start us, length us, event | category | flops | bytes accessed | tf_op | source)
XLA Modules:
  0.0 54.9 jit_solution(11635827871281426093)
XLA Ops:
  0.6 0.8 %copy-done.5 = f32[96,96]{1,0:T(8,128)S(1)} copy-done((f32[96,96]{1,0:T(8,128)S(1)}, f32[96,96]{1,0:T(8,128)}, u32[]{:S(2)}) %copy-start.5) | copy-done | bytes 36888
  1.5 3.0 %collective-permute-start = (f32[96,96]{1,0:T(8,128)S(1)}, f32[96,96]{1,0:T(8,128)S(1)}, u32[]{:S(2)}, u32[]{:S(2)}) collective-permute-start(f32[96,96]{1,0:T(8,128)S(1)} %get-tuple-element.23.middle), channel_id=1, source_target_pairs={{0,1},{1,0},{2,3},{3,2},{4,5},{5,4},{6,7},{7,6},{8,9},{9,8},{10,11... | collective-permute-start | bytes 110600 | tf_op jit(solution)/shard_map/ppermute | solution.py:140
  4.5 0.7 %collective-permute-start.1 = (f32[96,96]{1,0:T(8,128)S(1)}, f32[96,96]{1,0:T(8,128)S(1)}, u32[]{:S(2)}, u32[]{:S(2)}) collective-permute-start(f32[96,96]{1,0:T(8,128)S(1)} %get-tuple-element.23.middle), channel_id=1, source_target_pairs={{0,0},{7,7},{1,2},{2,1},{3,4},{4,3},{5,6},{6,5},{8,8},{15,15},{9,1... | collective-permute-start | bytes 110600 | tf_op jit(solution)/shard_map/ppermute | solution.py:148
  5.2 0.3 copy.19.kern
  5.6 2.0 %spectra.3 = (f32[2,4,224,256]{3,2,1,0:T(8,128)S(1)}, f32[8,128]{1,0:T(8,128)S(1)}) custom-call(f32[2,12,129,129]{3,2,1,0:T(8,128)S(1)} %copy.19.kern, bf16[3,256,256]{2,1,0:T(8,128)(2,1)S(1)} %copy-done, bf16[672,256]{1,0:T(8,128)(2,1)S(1)} %copy-done.1, f32[232,256]{1,0:T(8,128)S(1)} %copy-done.2, f32[8,128]{1,0:T(8,128)S(1)} %get-tuple-element.24.rest_0_), custom_call_target="tpu_custom_call" | custom-call | flops 2000000000 | bytes 1048576 | tf_op jit(solution)/shard_map/spectra/pallas_call | solution.py:565
  7.6 0.2 band.1
  7.9 1.2 %spectra.4 = (f32[2,8,224,256]{3,2,1,0:T(8,128)S(1)}, f32[8,128]{1,0:T(8,128)S(1)}) custom-call(f32[2,12,129,129]{3,2,1,0:T(8,128)S(1)} %copy.19.kern, bf16[3,256,256]{2,1,0:T(8,128)(2,1)S(1)} %copy-done, bf16[672,256]{1,0:T(8,128)(2,1)S(1)} %copy-done.1, f32[232,256]{1,0:T(8,128)S(1)} %copy-done.2, f32[8,128]{1,0:T(8,128)S(1)} %get-tuple-element.27.rest_0_), custom_call_target="tpu_custom_call" | custom-call | flops 1000000000 | bytes 1048576 | tf_op jit(solution)/shard_map/spectra/pallas_call | solution.py:565
  9.2 1.5 %collective-permute-start.3 = (f32[64,224]{1,0:T(8,128)S(1)}, f32[64,224]{1,0:T(8,128)S(1)}, u32[]{:S(2)}, u32[]{:S(2)}) collective-permute-start(f32[64,224]{1,0:T(8,128)S(1)} %get-tuple-element.29), channel_id=1, source_target_pairs={{0,16},{16,24},{24,8},{8,0},{1,17},{17,25},{25,9},{9,1},{2,18},{18... | collective-permute-start | bytes 172040 | tf_op jit(solution)/shard_map/ppermute | solution.py:155
  10.7 3.3 %spectra.5 = (f32[2,8,224,256]{3,2,1,0:T(8,128)S(1)}, f32[8,128]{1,0:T(8,128)}) custom-call(f32[2,12,129,129]{3,2,1,0:T(8,128)S(1)} %copy.19.kern, bf16[3,256,256]{2,1,0:T(8,128)(2,1)S(1)} %copy-done, bf16[672,256]{1,0:T(8,128)(2,1)S(1)} %copy-done.1, f32[232,256]{1,0:T(8,128)S(1)} %copy-done.2, ...), custom_call_target="tpu_custom_call", output_to_operand_aliasing={{0}: (5, {})} | custom-call | flops 3000000000 | bytes 1048576 | tf_op jit(solution)/shard_map/spectra/pallas_call | solution.py:565
  14.0 6.5 %field.1 = (f32[12,96,128]{2,1,0:T(8,128)S(1)}, f32[12,96,128]{2,1,0:T(8,128)S(1)}, f32[1,512]{1,0:T(1,128)S(1)}, f32[32,1,512]{2,1,0:T(1,128)}) custom-call(f32[12]{0:T(128)S(1)} %copy-done.10, f32[96,224]{1,0:T(8,128)S(1)} %get-tuple-element.26.band, f32[96,224]{1,0:T(8,128)S(1)} %collective-permute-done.2.partner, ...), custom_call_target="tpu_custom_call" | custom-call | flops 7000000000 | bytes 1048576 | tf_op jit(solution)/shard_map/field/pallas_call | solution.py:593
  20.5 8.3 %all-to-all-start = ((f32[32,1,512]{2,1,0:T(1,128)}), f32[32,1,512]{2,1,0:T(1,128)S(1)}, u32[]{:S(2)}, u32[]{:S(2)}) async-start(f32[32,1,512]{2,1,0:T(1,128)} %get-tuple-element.34), calls=%async_computation | async-start | bytes 131072 | tf_op jit(solution)/shard_map/all_to_all | solution.py:547
  29.5 6.4 %all-to-all-done = f32[32,1,512]{2,1,0:T(1,128)S(1)} async-done(((f32[32,1,512]{2,1,0:T(1,128)}), f32[32,1,512]{2,1,0:T(1,128)S(1)}, u32[]{:S(2)}, u32[]{:S(2)}) %all-to-all-start) | async-done | bytes 65568 | tf_op jit(solution)/shard_map/all_to_all | solution.py:547
  36.0 1.4 %source.1 = (f32[96,128]{1,0:T(8,128)S(1)}, f32[1,1]{1,0:T(1,128)}) custom-call(f32[12]{0:T(128)S(1)} %copy-done.10, f32[8]{0:T(128)S(1)} %copy-done.9, s32[1]{0:T(128)S(6)} %copy.26.pick, f32[32,512]{1,0:T(8,128)S(1)} %bitcast.4, f32[1,512]{1,0:T(1,128)S(1)} %get-tuple-element.35.sampled, s32[1,256]{1,0:T(1,128)S(1)} %copy-done.8), custom_call_target="tpu_custom_call" | custom-call | flops 2000000000 | bytes 1048576 | tf_op jit(solution)/shard_map/source/pallas_call | solution.py:607
  37.4 0.6 %copy-done.4 = f32[2,8,224,256]{3,2,1,0:T(8,128)S(1)} copy-done((f32[2,8,224,256]{3,2,1,0:T(8,128)S(1)}, f32[2,8,224,256]{3,2,1,0:T(8,128)}, u32[]{:S(2)}) %copy-start.4) | copy-done | bytes 3670040
  38.0 0.2 copy-done.12
  38.3 4.3 %gradient.1 = (f32[224,224]{1,0:T(8,128)S(1)}, f32[64,224]{1,0:T(8,128)S(1)}) custom-call(f32[12]{0:T(128)S(1)} %copy-done.10, f32[96,128]{1,0:T(8,128)S(1)} %get-tuple-element.36.grid, f32[12,96,128]{2,1,0:T(8,128)S(1)} %get-tuple-element.37.field_re, f32[12,96,128]{2,1,0:T(8,128)S(1)} %get-tuple-element.38.field_im, bf16[7,256,256]{2,1,0:T(8,128)(2,1)S(1)} %copy-done.12, ...), custom_call_target="tpu_custom_call" | custom-call | flops 6000000000 | bytes 1048576 | tf_op jit(solution)/shard_map/gradient/pallas_call | solution.py:614
  42.6 0.1 collective-permute-start.4
  42.7 4.2 %collective-permute-done.4.rim = f32[64,224]{1,0:T(8,128)S(1)} collective-permute-done((f32[64,224]{1,0:T(8,128)S(1)}, f32[64,224]{1,0:T(8,128)S(1)}, u32[]{:S(2)}, u32[]{:S(2)}) %collective-permute-start.4) | collective-permute-done | bytes 57376 | tf_op jit(solution)/shard_map/ppermute | solution.py:155
  47.0 1.3 %collective-permute-done.5.partner = f32[96,224]{1,0:T(8,128)S(1)} collective-permute-done((f32[96,224]{1,0:T(8,128)S(1)}, f32[96,224]{1,0:T(8,128)S(1)}, u32[]{:S(2)}, u32[]{:S(2)}) %collective-permute-start.5) | collective-permute-done | bytes 86048 | tf_op jit(solution)/shard_map/ppermute | solution.py:140
  48.3 0.7 %collective-permute-start.6 = (f32[48,128]{1,0:T(8,128)S(1)}, f32[48,128]{1,0:T(8,128)S(1)}, u32[]{:S(2)}, u32[]{:S(2)}) collective-permute-start(f32[48,128]{1,0:T(8,128)S(1)} %get-tuple-element.42), channel_id=1, source_target_pairs={{0,0},{7,7},{1,2},{2,1},{3,4},{4,3},{5,6},{6,5},{8,8},{15,15},{9,1... | collective-permute-start | bytes 73736 | tf_op jit(solution)/shard_map/ppermute | solution.py:148
  49.1 3.2 %collective-permute-start.7 = (f32[48,128]{1,0:T(8,128)S(1)}, f32[48,128]{1,0:T(8,128)S(1)}, u32[]{:S(2)}, u32[]{:S(2)}) collective-permute-start(f32[48,128]{1,0:T(8,128)S(1)} %near.1), channel_id=1, source_target_pairs={{0,1},{1,0},{2,3},{3,2},{4,5},{5,4},{6,7},{7,6},{8,9},{9,8},{10,11... | collective-permute-start | bytes 73736 | tf_op jit(solution)/shard_map/ppermute | solution.py:140
  52.3 0.1 far.1.total
  52.5 1.7 %collective-permute-done.7.near = f32[48,128]{1,0:T(8,128)S(1)} collective-permute-done((f32[48,128]{1,0:T(8,128)S(1)}, f32[48,128]{1,0:T(8,128)S(1)}, u32[]{:S(2)}, u32[]{:S(2)}) %collective-permute-start.7) | collective-permute-done | bytes 24608 | tf_op jit(solution)/shard_map/ppermute | solution.py:140
  54.1 0.8 %finish.1 = f32[96,96]{1,0:T(8,128)} custom-call(f32[96,96]{1,0:T(8,128)S(1)} %far.1.total, f32[48,128]{1,0:T(8,128)S(1)} %collective-permute-done.7.near, f32[96,96]{1,0:T(8,128)S(1)} %copy-done.6), custom_call_target="tpu_custom_call" | custom-call | flops 1000000000 | bytes 1048576 | tf_op jit(solution)/shard_map/finish/pallas_call | solution.py:635
  (38 shorter events, 0.5 us)
Async XLA Ops:
  0.6 0.8 %copy-start.5 = (f32[96,96]{1,0:T(8,128)S(1)}, f32[96,96]{1,0:T(8,128)}, u32[]{:S(2)}) copy-start(f32[96,96]{1,0:T(8,128)} %latent.3) | copy-start | bytes 110596
  1.4 3.8 %copy-start.13 = (f32[2,12,129,129]{3,0,2,1:T(2,128)S(1)}, f32[2,12,129,129]{3,0,2,1:T(2,128)}, u32[]{:S(2)}) copy-start(f32[2,12,129,129]{3,0,2,1:T(2,128)} %param.13) | copy-start | bytes 4792612
  1.5 4.1 %copy-start = (bf16[3,256,256]{2,1,0:T(8,128)(2,1)S(1)}, bf16[3,256,256]{2,1,0:T(8,128)(2,1)}, u32[]{:S(2)}) copy-start(bf16[3,256,256]{2,1,0:T(8,128)(2,1)} %constant.10.clone.lanes) | copy-start | bytes 1179652
  1.5 4.1 %copy-start.1 = (bf16[672,256]{1,0:T(8,128)(2,1)S(1)}, bf16[672,256]{1,0:T(8,128)(2,1)}, u32[]{:S(2)}) copy-start(bf16[672,256]{1,0:T(8,128)(2,1)} %constant.11.clone.rows) | copy-start | bytes 1032196
  1.5 4.1 %copy-start.2 = (f32[232,256]{1,0:T(8,128)S(1)}, f32[232,256]{1,0:T(8,128)}, u32[]{:S(2)}) copy-start(f32[232,256]{1,0:T(8,128)} %constant.12.clone.ends) | copy-start | bytes 712708
  1.5 6.1 %collective-permute-start = (f32[96,96]{1,0:T(8,128)S(1)}, f32[96,96]{1,0:T(8,128)S(1)}, u32[]{:S(2)}, u32[]{:S(2)}) collective-permute-start(f32[96,96]{1,0:T(8,128)S(1)} %get-tuple-element.23.middle), channel_id=1, source_target_pairs={{0,1},{1,0},{2,3},{3,2},{4,5},{5,4},{6,7},{7,6},{8,9},{9,8},{10,11... | collective-permute-start | bytes 110600 | tf_op jit(solution)/shard_map/ppermute | solution.py:140
  4.5 3.1 %collective-permute-start.1 = (f32[96,96]{1,0:T(8,128)S(1)}, f32[96,96]{1,0:T(8,128)S(1)}, u32[]{:S(2)}, u32[]{:S(2)}) collective-permute-start(f32[96,96]{1,0:T(8,128)S(1)} %get-tuple-element.23.middle), channel_id=1, source_target_pairs={{0,0},{7,7},{1,2},{2,1},{3,4},{4,3},{5,6},{6,5},{8,8},{15,15},{9,1... | collective-permute-start | bytes 110600 | tf_op jit(solution)/shard_map/ppermute | solution.py:148
  7.8 1.3 %collective-permute-start.2 = (f32[96,224]{1,0:T(8,128)S(1)}, f32[96,224]{1,0:T(8,128)S(1)}, u32[]{:S(2)}, u32[]{:S(2)}) collective-permute-start(f32[96,224]{1,0:T(8,128)S(1)} %get-tuple-element.26.band), channel_id=1, source_target_pairs={{0,8},{8,0},{16,24},{24,16},{1,9},{9,1},{17,25},{25,17},{2,10},{10... | collective-permute-start | bytes 258056 | tf_op jit(solution)/shard_map/ppermute | solution.py:140
  9.2 4.8 %collective-permute-start.3 = (f32[64,224]{1,0:T(8,128)S(1)}, f32[64,224]{1,0:T(8,128)S(1)}, u32[]{:S(2)}, u32[]{:S(2)}) collective-permute-start(f32[64,224]{1,0:T(8,128)S(1)} %get-tuple-element.29), channel_id=1, source_target_pairs={{0,16},{16,24},{24,8},{8,0},{1,17},{17,25},{25,9},{9,1},{2,18},{18... | collective-permute-start | bytes 172040 | tf_op jit(solution)/shard_map/ppermute | solution.py:155
  10.7 3.3 %copy-start.7 = (f32[1,256]{1,0:T(1,128)S(1)}, f32[1,256]{1,0:T(1,128)}, u32[]{:S(2)}) copy-start(f32[1,256]{1,0:T(1,128)} %slopes.1) | copy-start | bytes 3076
  10.7 3.3 %copy-start.8 = (s32[1,256]{1,0:T(1,128)S(1)}, s32[1,256]{1,0:T(1,128)}, u32[]{:S(2)}) copy-start(s32[1,256]{1,0:T(1,128)} %pixels.3) | copy-start | bytes 3076
  10.7 3.3 %copy-start.10 = (f32[12]{0:T(128)S(1)}, f32[12]{0:T(128)}, u32[]{:S(2)}) copy-start(f32[12]{0:T(128)} %weights.5) | copy-start | bytes 148
  10.7 3.3 %copy-start.11 = (bf16[11,256,256]{2,1,0:T(8,128)(2,1)S(1)}, bf16[11,256,256]{2,1,0:T(8,128)(2,1)}, u32[]{:S(2)}) copy-start(bf16[11,256,256]{2,1,0:T(8,128)(2,1)} %constant.13.clone.tables) | copy-start | bytes 4325380
  14.0 6.6 %copy-start.3 = (f32[2,8,224,256]{3,2,1,0:T(8,128)}, f32[2,8,224,256]{3,2,1,0:T(8,128)S(1)}, u32[]{:S(2)}) copy-start(f32[2,8,224,256]{3,2,1,0:T(8,128)S(1)} %get-tuple-element.33.rest_1_) | copy-start | bytes 11010052
  14.0 22.0 %copy-start.9 = (f32[8]{0:T(128)S(1)}, f32[8]{0:T(128)}, u32[]{:S(2)}) copy-start(f32[8]{0:T(128)} %doses.1) | copy-start | bytes 100
  20.5 15.4 %all-to-all-start = ((f32[32,1,512]{2,1,0:T(1,128)}), f32[32,1,512]{2,1,0:T(1,128)S(1)}, u32[]{:S(2)}, u32[]{:S(2)}) async-start(f32[32,1,512]{2,1,0:T(1,128)} %get-tuple-element.34), calls=%async_computation | async-start | bytes 131072 | tf_op jit(solution)/shard_map/all_to_all | solution.py:547
  36.0 2.0 %copy-start.4 = (f32[2,8,224,256]{3,2,1,0:T(8,128)S(1)}, f32[2,8,224,256]{3,2,1,0:T(8,128)}, u32[]{:S(2)}) copy-start(f32[2,8,224,256]{3,2,1,0:T(8,128)} %copy-done.3) | copy-start | bytes 11010052
  36.0 2.3 %copy-start.12 = (bf16[7,256,256]{2,1,0:T(8,128)(2,1)S(1)}, bf16[7,256,256]{2,1,0:T(8,128)(2,1)}, u32[]{:S(2)}) copy-start(bf16[7,256,256]{2,1,0:T(8,128)(2,1)} %constant.14.clone.tables) | copy-start | bytes 2752516
  42.6 4.3 %collective-permute-start.4 = (f32[64,224]{1,0:T(8,128)S(1)}, f32[64,224]{1,0:T(8,128)S(1)}, u32[]{:S(2)}, u32[]{:S(2)}) collective-permute-start(f32[64,224]{1,0:T(8,128)S(1)} %get-tuple-element.40), channel_id=1, source_target_pairs={{16,0},{24,16},{8,24},{0,8},{17,1},{25,17},{9,25},{1,9},{18,2},{26... | collective-permute-start | bytes 172040 | tf_op jit(solution)/shard_map/ppermute | solution.py:155
  46.9 1.4 %collective-permute-start.5 = (f32[96,224]{1,0:T(8,128)S(1)}, f32[96,224]{1,0:T(8,128)S(1)}, u32[]{:S(2)}, u32[]{:S(2)}) collective-permute-start(f32[96,224]{1,0:T(8,128)S(1)} %fold.2), channel_id=1, source_target_pairs={{0,8},{8,0},{16,24},{24,16},{1,9},{9,1},{17,25},{25,17},{2,10},{10... | collective-permute-start | bytes 258056 | tf_op jit(solution)/shard_map/ppermute | solution.py:140
  48.3 4.0 %collective-permute-start.6 = (f32[48,128]{1,0:T(8,128)S(1)}, f32[48,128]{1,0:T(8,128)S(1)}, u32[]{:S(2)}, u32[]{:S(2)}) collective-permute-start(f32[48,128]{1,0:T(8,128)S(1)} %get-tuple-element.42), channel_id=1, source_target_pairs={{0,0},{7,7},{1,2},{2,1},{3,4},{4,3},{5,6},{6,5},{8,8},{15,15},{9,1... | collective-permute-start | bytes 73736 | tf_op jit(solution)/shard_map/ppermute | solution.py:148
  49.0 5.1 %copy-start.6 = (f32[96,96]{1,0:T(8,128)S(1)}, f32[96,96]{1,0:T(8,128)}, u32[]{:S(2)}) copy-start(f32[96,96]{1,0:T(8,128)} %latent.3) | copy-start | bytes 110596
  49.1 5.0 %collective-permute-start.7 = (f32[48,128]{1,0:T(8,128)S(1)}, f32[48,128]{1,0:T(8,128)S(1)}, u32[]{:S(2)}, u32[]{:S(2)}) collective-permute-start(f32[48,128]{1,0:T(8,128)S(1)} %near.1), channel_id=1, source_target_pairs={{0,1},{1,0},{2,3},{3,2},{4,5},{5,4},{6,7},{7,6},{8,9},{9,8},{10,11... | collective-permute-start | bytes 73736 | tf_op jit(solution)/shard_map/ppermute | solution.py:140

commit v15 on v11

--- a/solution.py
+++ b/solution.py
@@ -15,6 +15,7 @@
 SOFTNESS = 0.25
 LANES = 128
 BATCH = 4
+FIELD_BATCH = 2
 F32 = jnp.float32
 BF16 = jnp.bfloat16
 
@@ -359,13 +360,13 @@
 
     intensity = jnp.zeros((tile, LANES), F32)
     places = [(own, k) for own in spec for k in range(own.shape[1])]
-    for first in range(0, kernels, BATCH):
-        lines = stacked([line for i in range(BATCH) for line in lifted(*places[first + i])])
+    for first in range(0, kernels, FIELD_BATCH):
+        lines = stacked([line for i in range(FIELD_BATCH) for line in lifted(*places[first + i])])
         x1, x2, x3 = split3(lines)
         most, more = halves(dot(x1, across[1]))
         some, small = halves(dot(x2, across[1]))
         both = small + dot(x1, across[2]) + dot(x3, across[0]) + (more + some) + most
-        for i in range(BATCH):
+        for i in range(FIELD_BATCH):
             real = both[2 * i * tile : (2 * i + 1) * tile]
             imag = both[(2 * i + 1) * tile : (2 * i + 2) * tile]
             field_re[first + i] = real

time: 55.1 us -> 55.3 us (level)
  no operation moved by 1% of the time
where the time goes in v15:
time: 55.3 us; the launch traced here: 55.1 us
  Pallas kernels  20.3 us (37%)
  starting transfers between devices  17.6 us (32%)
  waiting for transfers between devices  13.6 us (25%)
  local copies, waits for them, and re-layouts  2.05 us (4%)
  between operations  1.52 us (3%)
    all_to_all x1, starting transfers between devices, gather_all(): return lax.all_to_all(copies, ('ty', 'tx'), 0, 0, tiled=True)  8.34 us
    pallas_call x1, Pallas kernels, body(): call(field_kernel, 'field', [shape(count, tile, LANES)] * 2 + [shape(1, 2...  6.85 us
    pallas_call x3, Pallas kernels, spectra(): call(functools.partial(spectra_kernel, start, first_out, parts), 'spectra...  6.51 us
    all_to_all x1, waiting for transfers between devices, gather_all(): return lax.all_to_all(copies, ('ty', 'tx'), 0, 0, tiled=True)  6.45 us
    ppermute x4, starting transfers between devices, swap(): lax.ppermute(x, axis, [(i, i ^ 1) for i in range(lax.axis_size(axis))])  6.35 us
    ppermute x2, waiting for transfers between devices, ring(): return lax.ppermute(x, axis, [(b, a) if back else (a, b) for a, b in pairs])  4.16 us
    pallas_call x1, Pallas kernels, body(): call(gradient_kernel, 'gradient', [shape(period, period), shape(radius, p...  4.13 us
    ppermute x4, waiting for transfers between devices, swap(): lax.ppermute(x, axis, [(i, i ^ 1) for i in range(lax.axis_size(axis))])  3 us
  transfers between devices with their start and end apart: 9, of which 5 were waited for; matrix products, arithmetic and copies ran while one was open for 1% of the time, Pallas kernels for 12%

profile of v15, /device:TPU:0, one launch (start us, length us, event | category | flops | bytes accessed | tf_op | source)
XLA Modules:
  0.0 55.1 jit_solution(10963879458423426704)
XLA Ops:
  0.6 0.8 %copy-done.5 = f32[96,96]{1,0:T(8,128)S(1)} copy-done((f32[96,96]{1,0:T(8,128)S(1)}, f32[96,96]{1,0:T(8,128)}, u32[]{:S(2)}) %copy-start.5) | copy-done | bytes 36888
  1.5 3.0 %collective-permute-start = (f32[96,96]{1,0:T(8,128)S(1)}, f32[96,96]{1,0:T(8,128)S(1)}, u32[]{:S(2)}, u32[]{:S(2)}) collective-permute-start(f32[96,96]{1,0:T(8,128)S(1)} %get-tuple-element.23.middle), channel_id=1, source_target_pairs={{0,1},{1,0},{2,3},{3,2},{4,5},{5,4},{6,7},{7,6},{8,9},{9,8},{10,11... | collective-permute-start | bytes 110600 | tf_op jit(solution)/shard_map/ppermute | solution.py:141
  4.5 0.7 %collective-permute-start.1 = (f32[96,96]{1,0:T(8,128)S(1)}, f32[96,96]{1,0:T(8,128)S(1)}, u32[]{:S(2)}, u32[]{:S(2)}) collective-permute-start(f32[96,96]{1,0:T(8,128)S(1)} %get-tuple-element.23.middle), channel_id=1, source_target_pairs={{0,0},{7,7},{1,2},{2,1},{3,4},{4,3},{5,6},{6,5},{8,8},{15,15},{9,1... | collective-permute-start | bytes 110600 | tf_op jit(solution)/shard_map/ppermute | solution.py:149
  5.2 0.3 copy.19.kern
  5.6 2.0 %spectra.3 = (f32[2,4,224,256]{3,2,1,0:T(8,128)S(1)}, f32[8,128]{1,0:T(8,128)S(1)}) custom-call(f32[2,12,129,129]{3,2,1,0:T(8,128)S(1)} %copy.19.kern, bf16[3,256,256]{2,1,0:T(8,128)(2,1)S(1)} %copy-done, bf16[672,256]{1,0:T(8,128)(2,1)S(1)} %copy-done.1, f32[232,256]{1,0:T(8,128)S(1)} %copy-done.2, f32[8,128]{1,0:T(8,128)S(1)} %get-tuple-element.24.rest_0_), custom_call_target="tpu_custom_call" | custom-call | flops 2000000000 | bytes 1048576 | tf_op jit(solution)/shard_map/spectra/pallas_call | solution.py:565
  7.6 0.2 band.1
  7.9 1.2 %spectra.4 = (f32[2,8,224,256]{3,2,1,0:T(8,128)S(1)}, f32[8,128]{1,0:T(8,128)S(1)}) custom-call(f32[2,12,129,129]{3,2,1,0:T(8,128)S(1)} %copy.19.kern, bf16[3,256,256]{2,1,0:T(8,128)(2,1)S(1)} %copy-done, bf16[672,256]{1,0:T(8,128)(2,1)S(1)} %copy-done.1, f32[232,256]{1,0:T(8,128)S(1)} %copy-done.2, f32[8,128]{1,0:T(8,128)S(1)} %get-tuple-element.27.rest_0_), custom_call_target="tpu_custom_call" | custom-call | flops 1000000000 | bytes 1048576 | tf_op jit(solution)/shard_map/spectra/pallas_call | solution.py:565
  9.2 1.5 %collective-permute-start.3 = (f32[64,224]{1,0:T(8,128)S(1)}, f32[64,224]{1,0:T(8,128)S(1)}, u32[]{:S(2)}, u32[]{:S(2)}) collective-permute-start(f32[64,224]{1,0:T(8,128)S(1)} %get-tuple-element.29), channel_id=1, source_target_pairs={{0,16},{16,24},{24,8},{8,0},{1,17},{17,25},{25,9},{9,1},{2,18},{18... | collective-permute-start | bytes 172040 | tf_op jit(solution)/shard_map/ppermute | solution.py:156
  10.7 3.3 %spectra.5 = (f32[2,8,224,256]{3,2,1,0:T(8,128)S(1)}, f32[8,128]{1,0:T(8,128)}) custom-call(f32[2,12,129,129]{3,2,1,0:T(8,128)S(1)} %copy.19.kern, bf16[3,256,256]{2,1,0:T(8,128)(2,1)S(1)} %copy-done, bf16[672,256]{1,0:T(8,128)(2,1)S(1)} %copy-done.1, f32[232,256]{1,0:T(8,128)S(1)} %copy-done.2, ...), custom_call_target="tpu_custom_call", output_to_operand_aliasing={{0}: (5, {})} | custom-call | flops 3000000000 | bytes 1048576 | tf_op jit(solution)/shard_map/spectra/pallas_call | solution.py:565
  14.0 6.9 %field.1 = (f32[12,96,128]{2,1,0:T(8,128)S(1)}, f32[12,96,128]{2,1,0:T(8,128)S(1)}, f32[1,512]{1,0:T(1,128)S(1)}, f32[32,1,512]{2,1,0:T(1,128)}) custom-call(f32[12]{0:T(128)S(1)} %copy-done.10, f32[96,224]{1,0:T(8,128)S(1)} %get-tuple-element.26.band, f32[96,224]{1,0:T(8,128)S(1)} %collective-permute-done.2.partner, ...), custom_call_target="tpu_custom_call" | custom-call | flops 7000000000 | bytes 1048576 | tf_op jit(solution)/shard_map/field/pallas_call | solution.py:593
  20.9 8.3 %all-to-all-start = ((f32[32,1,512]{2,1,0:T(1,128)}), f32[32,1,512]{2,1,0:T(1,128)S(1)}, u32[]{:S(2)}, u32[]{:S(2)}) async-start(f32[32,1,512]{2,1,0:T(1,128)} %get-tuple-element.34), calls=%async_computation | async-start | bytes 131072 | tf_op jit(solution)/shard_map/all_to_all | solution.py:547
  29.9 6.4 %all-to-all-done = f32[32,1,512]{2,1,0:T(1,128)S(1)} async-done(((f32[32,1,512]{2,1,0:T(1,128)}), f32[32,1,512]{2,1,0:T(1,128)S(1)}, u32[]{:S(2)}, u32[]{:S(2)}) %all-to-all-start) | async-done | bytes 65568 | tf_op jit(solution)/shard_map/all_to_all | solution.py:547
  36.3 1.4 %source.1 = (f32[96,128]{1,0:T(8,128)S(1)}, f32[1,1]{1,0:T(1,128)}) custom-call(f32[12]{0:T(128)S(1)} %copy-done.10, f32[8]{0:T(128)S(1)} %copy-done.9, s32[1]{0:T(128)S(6)} %copy.26.pick, f32[32,512]{1,0:T(8,128)S(1)} %bitcast.4, f32[1,512]{1,0:T(1,128)S(1)} %get-tuple-element.35.sampled, s32[1,256]{1,0:T(1,128)S(1)} %copy-done.8), custom_call_target="tpu_custom_call" | custom-call | flops 2000000000 | bytes 1048576 | tf_op jit(solution)/shard_map/source/pallas_call | solution.py:607
  37.8 0.6 %copy-done.4 = f32[2,8,224,256]{3,2,1,0:T(8,128)S(1)} copy-done((f32[2,8,224,256]{3,2,1,0:T(8,128)S(1)}, f32[2,8,224,256]{3,2,1,0:T(8,128)}, u32[]{:S(2)}) %copy-start.4) | copy-done | bytes 3670040
  38.4 0.2 copy-done.12
  38.6 4.1 %gradient.1 = (f32[224,224]{1,0:T(8,128)S(1)}, f32[64,224]{1,0:T(8,128)S(1)}) custom-call(f32[12]{0:T(128)S(1)} %copy-done.10, f32[96,128]{1,0:T(8,128)S(1)} %get-tuple-element.36.grid, f32[12,96,128]{2,1,0:T(8,128)S(1)} %get-tuple-element.37.field_re, f32[12,96,128]{2,1,0:T(8,128)S(1)} %get-tuple-element.38.field_im, bf16[7,256,256]{2,1,0:T(8,128)(2,1)S(1)} %copy-done.12, ...), custom_call_target="tpu_custom_call" | custom-call | flops 6000000000 | bytes 1048576 | tf_op jit(solution)/shard_map/gradient/pallas_call | solution.py:614
  42.7 0.1 collective-permute-start.4
  42.9 4.2 %collective-permute-done.4.rim = f32[64,224]{1,0:T(8,128)S(1)} collective-permute-done((f32[64,224]{1,0:T(8,128)S(1)}, f32[64,224]{1,0:T(8,128)S(1)}, u32[]{:S(2)}, u32[]{:S(2)}) %collective-permute-start.4) | collective-permute-done | bytes 57376 | tf_op jit(solution)/shard_map/ppermute | solution.py:156
  47.1 1.3 %collective-permute-done.5.partner = f32[96,224]{1,0:T(8,128)S(1)} collective-permute-done((f32[96,224]{1,0:T(8,128)S(1)}, f32[96,224]{1,0:T(8,128)S(1)}, u32[]{:S(2)}, u32[]{:S(2)}) %collective-permute-start.5) | collective-permute-done | bytes 86048 | tf_op jit(solution)/shard_map/ppermute | solution.py:141
  48.5 0.7 %collective-permute-start.6 = (f32[48,128]{1,0:T(8,128)S(1)}, f32[48,128]{1,0:T(8,128)S(1)}, u32[]{:S(2)}, u32[]{:S(2)}) collective-permute-start(f32[48,128]{1,0:T(8,128)S(1)} %get-tuple-element.42), channel_id=1, source_target_pairs={{0,0},{7,7},{1,2},{2,1},{3,4},{4,3},{5,6},{6,5},{8,8},{15,15},{9,1... | collective-permute-start | bytes 73736 | tf_op jit(solution)/shard_map/ppermute | solution.py:149
  49.3 3.2 %collective-permute-start.7 = (f32[48,128]{1,0:T(8,128)S(1)}, f32[48,128]{1,0:T(8,128)S(1)}, u32[]{:S(2)}, u32[]{:S(2)}) collective-permute-start(f32[48,128]{1,0:T(8,128)S(1)} %near.1), channel_id=1, source_target_pairs={{0,1},{1,0},{2,3},{3,2},{4,5},{5,4},{6,7},{7,6},{8,9},{9,8},{10,11... | collective-permute-start | bytes 73736 | tf_op jit(solution)/shard_map/ppermute | solution.py:141
  52.5 0.1 far.1.total
  52.6 1.7 %collective-permute-done.7.near = f32[48,128]{1,0:T(8,128)S(1)} collective-permute-done((f32[48,128]{1,0:T(8,128)S(1)}, f32[48,128]{1,0:T(8,128)S(1)}, u32[]{:S(2)}, u32[]{:S(2)}) %collective-permute-start.7) | collective-permute-done | bytes 24608 | tf_op jit(solution)/shard_map/ppermute | solution.py:141
  54.3 0.8 %finish.1 = f32[96,96]{1,0:T(8,128)} custom-call(f32[96,96]{1,0:T(8,128)S(1)} %far.1.total, f32[48,128]{1,0:T(8,128)S(1)} %collective-permute-done.7.near, f32[96,96]{1,0:T(8,128)S(1)} %copy-done.6), custom_call_target="tpu_custom_call" | custom-call | flops 1000000000 | bytes 1048576 | tf_op jit(solution)/shard_map/finish/pallas_call | solution.py:635
  (38 shorter events, 0.5 us)
Async XLA Ops:
  0.6 0.8 %copy-start.5 = (f32[96,96]{1,0:T(8,128)S(1)}, f32[96,96]{1,0:T(8,128)}, u32[]{:S(2)}) copy-start(f32[96,96]{1,0:T(8,128)} %latent.3) | copy-start | bytes 110596
  1.4 3.8 %copy-start.13 = (f32[2,12,129,129]{3,0,2,1:T(2,128)S(1)}, f32[2,12,129,129]{3,0,2,1:T(2,128)}, u32[]{:S(2)}) copy-start(f32[2,12,129,129]{3,0,2,1:T(2,128)} %param.13) | copy-start | bytes 4792612
  1.5 4.1 %copy-start = (bf16[3,256,256]{2,1,0:T(8,128)(2,1)S(1)}, bf16[3,256,256]{2,1,0:T(8,128)(2,1)}, u32[]{:S(2)}) copy-start(bf16[3,256,256]{2,1,0:T(8,128)(2,1)} %constant.10.clone.lanes) | copy-start | bytes 1179652
  1.5 4.1 %copy-start.1 = (bf16[672,256]{1,0:T(8,128)(2,1)S(1)}, bf16[672,256]{1,0:T(8,128)(2,1)}, u32[]{:S(2)}) copy-start(bf16[672,256]{1,0:T(8,128)(2,1)} %constant.11.clone.rows) | copy-start | bytes 1032196
  1.5 4.1 %copy-start.2 = (f32[232,256]{1,0:T(8,128)S(1)}, f32[232,256]{1,0:T(8,128)}, u32[]{:S(2)}) copy-start(f32[232,256]{1,0:T(8,128)} %constant.12.clone.ends) | copy-start | bytes 712708
  1.5 6.1 %collective-permute-start = (f32[96,96]{1,0:T(8,128)S(1)}, f32[96,96]{1,0:T(8,128)S(1)}, u32[]{:S(2)}, u32[]{:S(2)}) collective-permute-start(f32[96,96]{1,0:T(8,128)S(1)} %get-tuple-element.23.middle), channel_id=1, source_target_pairs={{0,1},{1,0},{2,3},{3,2},{4,5},{5,4},{6,7},{7,6},{8,9},{9,8},{10,11... | collective-permute-start | bytes 110600 | tf_op jit(solution)/shard_map/ppermute | solution.py:141
  4.5 3.1 %collective-permute-start.1 = (f32[96,96]{1,0:T(8,128)S(1)}, f32[96,96]{1,0:T(8,128)S(1)}, u32[]{:S(2)}, u32[]{:S(2)}) collective-permute-start(f32[96,96]{1,0:T(8,128)S(1)} %get-tuple-element.23.middle), channel_id=1, source_target_pairs={{0,0},{7,7},{1,2},{2,1},{3,4},{4,3},{5,6},{6,5},{8,8},{15,15},{9,1... | collective-permute-start | bytes 110600 | tf_op jit(solution)/shard_map/ppermute | solution.py:149
  7.8 1.3 %collective-permute-start.2 = (f32[96,224]{1,0:T(8,128)S(1)}, f32[96,224]{1,0:T(8,128)S(1)}, u32[]{:S(2)}, u32[]{:S(2)}) collective-permute-start(f32[96,224]{1,0:T(8,128)S(1)} %get-tuple-element.26.band), channel_id=1, source_target_pairs={{0,8},{8,0},{16,24},{24,16},{1,9},{9,1},{17,25},{25,17},{2,10},{10... | collective-permute-start | bytes 258056 | tf_op jit(solution)/shard_map/ppermute | solution.py:141
  9.2 4.8 %collective-permute-start.3 = (f32[64,224]{1,0:T(8,128)S(1)}, f32[64,224]{1,0:T(8,128)S(1)}, u32[]{:S(2)}, u32[]{:S(2)}) collective-permute-start(f32[64,224]{1,0:T(8,128)S(1)} %get-tuple-element.29), channel_id=1, source_target_pairs={{0,16},{16,24},{24,8},{8,0},{1,17},{17,25},{25,9},{9,1},{2,18},{18... | collective-permute-start | bytes 172040 | tf_op jit(solution)/shard_map/ppermute | solution.py:156
  10.7 3.3 %copy-start.7 = (f32[1,256]{1,0:T(1,128)S(1)}, f32[1,256]{1,0:T(1,128)}, u32[]{:S(2)}) copy-start(f32[1,256]{1,0:T(1,128)} %slopes.1) | copy-start | bytes 3076
  10.7 3.3 %copy-start.8 = (s32[1,256]{1,0:T(1,128)S(1)}, s32[1,256]{1,0:T(1,128)}, u32[]{:S(2)}) copy-start(s32[1,256]{1,0:T(1,128)} %pixels.3) | copy-start | bytes 3076
  10.7 3.3 %copy-start.10 = (f32[12]{0:T(128)S(1)}, f32[12]{0:T(128)}, u32[]{:S(2)}) copy-start(f32[12]{0:T(128)} %weights.5) | copy-start | bytes 148
  10.7 3.3 %copy-start.11 = (bf16[11,256,256]{2,1,0:T(8,128)(2,1)S(1)}, bf16[11,256,256]{2,1,0:T(8,128)(2,1)}, u32[]{:S(2)}) copy-start(bf16[11,256,256]{2,1,0:T(8,128)(2,1)} %constant.13.clone.tables) | copy-start | bytes 4325380
  14.0 6.9 %copy-start.3 = (f32[2,8,224,256]{3,2,1,0:T(8,128)}, f32[2,8,224,256]{3,2,1,0:T(8,128)S(1)}, u32[]{:S(2)}) copy-start(f32[2,8,224,256]{3,2,1,0:T(8,128)S(1)} %get-tuple-element.33.rest_1_) | copy-start | bytes 11010052
  14.0 22.3 %copy-start.9 = (f32[8]{0:T(128)S(1)}, f32[8]{0:T(128)}, u32[]{:S(2)}) copy-start(f32[8]{0:T(128)} %doses.1) | copy-start | bytes 100
  20.9 15.4 %all-to-all-start = ((f32[32,1,512]{2,1,0:T(1,128)}), f32[32,1,512]{2,1,0:T(1,128)S(1)}, u32[]{:S(2)}, u32[]{:S(2)}) async-start(f32[32,1,512]{2,1,0:T(1,128)} %get-tuple-element.34), calls=%async_computation | async-start | bytes 131072 | tf_op jit(solution)/shard_map/all_to_all | solution.py:547
  36.3 2.0 %copy-start.4 = (f32[2,8,224,256]{3,2,1,0:T(8,128)S(1)}, f32[2,8,224,256]{3,2,1,0:T(8,128)}, u32[]{:S(2)}) copy-start(f32[2,8,224,256]{3,2,1,0:T(8,128)} %copy-done.3) | copy-start | bytes 11010052
  36.3 2.3 %copy-start.12 = (bf16[7,256,256]{2,1,0:T(8,128)(2,1)S(1)}, bf16[7,256,256]{2,1,0:T(8,128)(2,1)}, u32[]{:S(2)}) copy-start(bf16[7,256,256]{2,1,0:T(8,128)(2,1)} %constant.14.clone.tables) | copy-start | bytes 2752516
  42.7 4.3 %collective-permute-start.4 = (f32[64,224]{1,0:T(8,128)S(1)}, f32[64,224]{1,0:T(8,128)S(1)}, u32[]{:S(2)}, u32[]{:S(2)}) collective-permute-start(f32[64,224]{1,0:T(8,128)S(1)} %get-tuple-element.40), channel_id=1, source_target_pairs={{16,0},{24,16},{8,24},{0,8},{17,1},{25,17},{9,25},{1,9},{18,2},{26... | collective-permute-start | bytes 172040 | tf_op jit(solution)/shard_map/ppermute | solution.py:156
  47.1 1.4 %collective-permute-start.5 = (f32[96,224]{1,0:T(8,128)S(1)}, f32[96,224]{1,0:T(8,128)S(1)}, u32[]{:S(2)}, u32[]{:S(2)}) collective-permute-start(f32[96,224]{1,0:T(8,128)S(1)} %fold.2), channel_id=1, source_target_pairs={{0,8},{8,0},{16,24},{24,16},{1,9},{9,1},{17,25},{25,17},{2,10},{10... | collective-permute-start | bytes 258056 | tf_op jit(solution)/shard_map/ppermute | solution.py:141
  48.5 4.0 %collective-permute-start.6 = (f32[48,128]{1,0:T(8,128)S(1)}, f32[48,128]{1,0:T(8,128)S(1)}, u32[]{:S(2)}, u32[]{:S(2)}) collective-permute-start(f32[48,128]{1,0:T(8,128)S(1)} %get-tuple-element.42), channel_id=1, source_target_pairs={{0,0},{7,7},{1,2},{2,1},{3,4},{4,3},{5,6},{6,5},{8,8},{15,15},{9,1... | collective-permute-start | bytes 73736 | tf_op jit(solution)/shard_map/ppermute | solution.py:149
  49.2 5.1 %copy-start.6 = (f32[96,96]{1,0:T(8,128)S(1)}, f32[96,96]{1,0:T(8,128)}, u32[]{:S(2)}) copy-start(f32[96,96]{1,0:T(8,128)} %latent.3) | copy-start | bytes 110596
  49.3 5.0 %collective-permute-start.7 = (f32[48,128]{1,0:T(8,128)S(1)}, f32[48,128]{1,0:T(8,128)S(1)}, u32[]{:S(2)}, u32[]{:S(2)}) collective-permute-start(f32[48,128]{1,0:T(8,128)S(1)} %near.1), channel_id=1, source_target_pairs={{0,1},{1,0},{2,3},{3,2},{4,5},{5,4},{6,7},{7,6},{8,9},{9,8},{10,11... | collective-permute-start | bytes 73736 | tf_op jit(solution)/shard_map/ppermute | solution.py:141
